TPU v7x, 32 devices: a whole 2x2x4 slice. The times are simulated.
32 devices in a mesh: dp: 16 (over z, x, core), ctx: 2 (over y).
Axes of the slice: x: 2, y: 2, z: 4, core: 2. Of those that a mesh axis runs over, the one named last changes fastest.
Arguments:
- tokens: bfloat16 [32, 1024, 1024], P('dp', 'ctx'), may hold values from -6 to 6
- w_in: bfloat16 [1024, 3072], P('dp', 'ctx'), may hold values from -0.1875 to 0.1875
- w_out: bfloat16 [1024, 1024], P('dp', 'ctx'), may hold values from -0.1875 to 0.1875
- w_gate: bfloat16 [1024, 4608], P('dp', 'ctx'), may hold values from -0.1875 to 0.1875
- w_up: bfloat16 [1024, 4608], P('dp', 'ctx'), may hold values from -0.1875 to 0.1875
- w_down: bfloat16 [4608, 1024], P('dp', 'ctx'), may hold values from -0.09375 to 0.09375
- gain_mix: bfloat16 [1024], P('dp'), may hold values from 0.099609375 to 1.8984375
- gain_ffn: bfloat16 [1024], P('dp'), may hold values from 0.099609375 to 1.8984375
- kernel: bfloat16 [3, 1024], P(None, 'dp'), may hold values from -3.5 to 3.5
- cotangent: bfloat16 [32, 1024, 1024], P('dp', 'ctx'), may hold values from -6 to 6
Outputs:
- result: bfloat16 [32, 1024, 1024], P('dp', 'ctx')
- grad_tokens: float32 [32, 1024, 1024], P('dp', 'ctx')
- grad_w_in: float32 [1024, 3072], P('dp', 'ctx')
- grad_w_out: float32 [1024, 1024], P('dp', 'ctx')
- grad_w_gate: float32 [1024, 4608], P('dp', 'ctx')
- grad_w_up: float32 [1024, 4608], P('dp', 'ctx')
- grad_w_down: float32 [4608, 1024], P('dp', 'ctx')
- grad_gain_mix: float32 [1024], P('dp')
- grad_gain_ffn: float32 [1024], P('dp')
- grad_kernel: float32 [3, 1024], P(None, 'dp')
All inputs are finite; a program needn't handle non-finite values.
Results may differ from a plain program's by a relative error of at most 0.0092.
Values may be sent and summed in bfloat16 or wider, within the bound.
No kernel may reach another device: no remote copies, remote signals or barrier semaphores. Data moves between devices by JAX's collectives and lax.ppermute only.
A program may use at most 256 MiB of HBM per device.

v0:
```python
import jax
import jax.numpy as jnp
from jax import lax
from jax.sharding import PartitionSpec as P

EPSILON = 1e-05


def passed_along(block, axis, distance):
    devices = range(lax.axis_size(axis))
    route = [(i - distance, i) for i in devices if i - distance in devices]
    return lax.ppermute(block, axis, route)


def cross_rows(left_operand, right_operand):
    return lax.dot_general(
        left_operand, right_operand, (((0,), (0,)), ((), ())), preferred_element_type=jnp.float32
    )


def cross_cols(left_operand, right_operand):
    return lax.dot_general(
        left_operand, right_operand, (((1,), (1,)), ((), ())), preferred_element_type=jnp.float32
    )


def norm_forward(values, gain):
    scale = lax.rsqrt(jnp.mean(values * values, axis=-1, keepdims=True) + EPSILON)
    return (values * scale * gain, scale)


def norm_backward(values, scale, gain, incoming):
    weighted = incoming * gain
    gain_grad = jnp.sum(incoming * values * scale, axis=0)
    inner = jnp.mean(weighted * values, axis=-1, keepdims=True)
    return (scale * weighted - values * (scale * scale * scale) * inner, gain_grad)


def shards(tokens, w_in, w_out, w_gate, w_up, w_down, gain_mix, gain_ffn, kernel, cotangent):
    seq_count, piece_len, model_width = tokens.shape
    row_count = seq_count * piece_len
    small_params = jnp.concatenate([gain_mix[None], gain_ffn[None], kernel], axis=0)
    input_columns, out_cols, gate_cols, up_cols, down_cols = (
        lax.all_gather(w_in, "ctx", axis=1, tiled=True),
        lax.all_gather(w_out, "ctx", axis=1, tiled=True),
        lax.all_gather(w_gate, "ctx", axis=1, tiled=True),
        lax.all_gather(w_up, "ctx", axis=1, tiled=True),
        lax.all_gather(w_down, "ctx", axis=1, tiled=True),
    )
    full_in, full_out, full_gate, full_up, full_down, small_full = (
        lax.all_gather(input_columns, "dp", axis=0, tiled=True),
        lax.all_gather(out_cols, "dp", axis=0, tiled=True),
        lax.all_gather(gate_cols, "dp", axis=0, tiled=True),
        lax.all_gather(up_cols, "dp", axis=0, tiled=True),
        lax.all_gather(down_cols, "dp", axis=0, tiled=True),
        lax.all_gather(small_params, "dp", axis=1, tiled=True),
    )
    small_float = small_full.astype(jnp.float32)
    first_gain = small_float[0]
    second_gain = small_float[1]
    taps = small_float[2:5]
    inputs = tokens.reshape(row_count, model_width).astype(jnp.float32)
    normed, scale_mix = norm_forward(inputs, first_gain)
    normed_low = normed.astype(jnp.bfloat16)
    projected = jnp.dot(normed_low, full_in, preferred_element_type=jnp.float32)
    gate_b = projected[:, :model_width]
    gate_c = projected[:, model_width : 2 * model_width]
    values = projected[:, 2 * model_width :]
    product = (gate_b * values).reshape(seq_count, piece_len, model_width)
    previous = passed_along(product[:, piece_len - 2 :].astype(jnp.bfloat16), "ctx", 1).astype(
        jnp.float32
    )
    padded = jnp.concatenate([previous, product], axis=1)
    convolved = taps[0] * padded[:, :-2] + taps[1] * padded[:, 1:-1] + taps[2] * padded[:, 2:]
    convolved = convolved.reshape(row_count, model_width)
    mixer_out = (gate_c * convolved).astype(jnp.bfloat16)
    residual = inputs + jnp.dot(mixer_out, full_out, preferred_element_type=jnp.float32)
    feedforward_normed, scale_ffn = norm_forward(residual, second_gain)
    nffn_low = feedforward_normed.astype(jnp.bfloat16)
    gate = jnp.dot(nffn_low, full_gate, preferred_element_type=jnp.float32)
    up_value = jnp.dot(nffn_low, full_up, preferred_element_type=jnp.float32)
    sigmoid_gate = jax.nn.sigmoid(gate)
    activated = gate * sigmoid_gate
    hidden = (activated * up_value).astype(jnp.bfloat16)
    result = residual + jnp.dot(hidden, full_down, preferred_element_type=jnp.float32)
    result = result.astype(jnp.bfloat16).reshape(seq_count, piece_len, model_width)
    back_in, output_backward, back_gate, back_up, back_down = (
        lax.all_gather(w_in, "ctx", axis=1, tiled=True),
        lax.all_gather(w_out, "ctx", axis=1, tiled=True),
        lax.all_gather(w_gate, "ctx", axis=1, tiled=True),
        lax.all_gather(w_up, "ctx", axis=1, tiled=True),
        lax.all_gather(w_down, "ctx", axis=1, tiled=True),
    )
    input_weight_used, use_out, use_gate, use_up, use_down = (
        lax.all_gather(back_in, "dp", axis=0, tiled=True),
        lax.all_gather(output_backward, "dp", axis=0, tiled=True),
        lax.all_gather(back_gate, "dp", axis=0, tiled=True),
        lax.all_gather(back_up, "dp", axis=0, tiled=True),
        lax.all_gather(back_down, "dp", axis=0, tiled=True),
    )
    grad_out = cotangent.reshape(row_count, model_width)
    grad_out_float = grad_out.astype(jnp.float32)
    grad_w_down = cross_rows(hidden, grad_out)
    grad_hidden = cross_cols(grad_out, use_down)
    grad_gate = (
        grad_hidden * up_value * sigmoid_gate * (1.0 + gate * (1.0 - sigmoid_gate))
    ).astype(jnp.bfloat16)
    grad_up = (grad_hidden * activated).astype(jnp.bfloat16)
    grad_w_gate = cross_rows(nffn_low, grad_gate)
    grad_w_up = cross_rows(nffn_low, grad_up)
    grad_nffn = cross_cols(grad_gate, use_gate) + cross_cols(grad_up, use_up)
    residual_norm_gradient, grad_gain_ffn = norm_backward(
        residual, scale_ffn, second_gain, grad_nffn
    )
    grad_residual = grad_out_float + residual_norm_gradient
    grad_branch = grad_residual.astype(jnp.bfloat16)
    grad_w_out = cross_rows(mixer_out, grad_branch)
    grad_mix = cross_cols(grad_branch, use_out)
    grad_c = grad_mix * convolved
    grad_conv = (grad_mix * gate_c).reshape(seq_count, piece_len, model_width)
    following = passed_along(grad_conv[:, :2].astype(jnp.bfloat16), "ctx", -1).astype(jnp.float32)
    extended = jnp.concatenate([grad_conv, following], axis=1)
    grad_product = (
        taps[2] * extended[:, :-2] + taps[1] * extended[:, 1:-1] + taps[0] * extended[:, 2:]
    )
    grad_kernel = jnp.stack(
        [
            jnp.sum(grad_conv * padded[:, shift_at : shift_at + piece_len], axis=(0, 1))
            for shift_at in range(3)
        ],
        axis=0,
    )
    grad_product = grad_product.reshape(row_count, model_width)
    grad_projected = jnp.concatenate(
        [grad_product * values, grad_c, grad_product * gate_b], axis=1
    ).astype(jnp.bfloat16)
    grad_w_in = cross_rows(normed_low, grad_projected)
    grad_normed = cross_cols(grad_projected, input_weight_used)
    grad_in_norm, grad_gain_mix = norm_backward(inputs, scale_mix, first_gain, grad_normed)
    grad_tokens = (grad_residual + grad_in_norm).reshape(seq_count, piece_len, model_width)
    small_grad = jnp.concatenate([grad_gain_mix[None], grad_gain_ffn[None], grad_kernel], axis=0)
    part_in, part_out, part_gate, part_up, part_down, small_part = (
        lax.psum_scatter(grad_w_in, "dp", scatter_dimension=0, tiled=True),
        lax.psum_scatter(grad_w_out, "dp", scatter_dimension=0, tiled=True),
        lax.psum_scatter(grad_w_gate, "dp", scatter_dimension=0, tiled=True),
        lax.psum_scatter(grad_w_up, "dp", scatter_dimension=0, tiled=True),
        lax.psum_scatter(grad_w_down, "dp", scatter_dimension=0, tiled=True),
        lax.psum_scatter(small_grad, "dp", scatter_dimension=1, tiled=True),
    )
    final_in, final_out, final_gate, final_up, final_down = (
        lax.psum_scatter(part_in, "ctx", scatter_dimension=1, tiled=True),
        lax.psum_scatter(part_out, "ctx", scatter_dimension=1, tiled=True),
        lax.psum_scatter(part_gate, "ctx", scatter_dimension=1, tiled=True),
        lax.psum_scatter(part_up, "ctx", scatter_dimension=1, tiled=True),
        lax.psum_scatter(part_down, "ctx", scatter_dimension=1, tiled=True),
    )
    small_total = lax.psum(small_part, "ctx")
    return (
        result,
        grad_tokens,
        final_in,
        final_out,
        final_gate,
        final_up,
        final_down,
        small_total[0],
        small_total[1],
        small_total[2:5],
    )


def solution(mesh):
    placed = (
        P("dp", "ctx", None),
        P("dp", "ctx"),
        P("dp", "ctx"),
        P("dp", "ctx"),
        P("dp", "ctx"),
        P("dp", "ctx"),
        P("dp"),
        P("dp"),
        P(None, "dp"),
        P("dp", "ctx", None),
    )
    return jax.shard_map(
        shards,
        mesh=mesh,
        in_specs=placed,
        out_specs=(
            P("dp", "ctx", None),
            P("dp", "ctx", None),
            P("dp", "ctx"),
            P("dp", "ctx"),
            P("dp", "ctx"),
            P("dp", "ctx"),
            P("dp", "ctx"),
            P("dp"),
            P("dp"),
            P(None, "dp"),
        ),
        check_vma=False,
    )
```

profile of v0, /device:TPU:0, one launch (start us, length us, event | category | flops | bytes accessed | tf_op | source)
XLA Modules:
  0.0 1420.3 jit_solution(17588494703714501852)
XLA Ops:
  7.3 10.6 all_gather.44
  17.9 5.3 all_gather.46
  23.3 9.6 all_gather.48
  33.0 7.7 all_gather.50
  40.8 7.5 all_gather.52
  48.4 22.7 %all-gather = bf16[16,64,5]{1,2,0:T(8,128)(2,1)S(1)} all-gather(bf16[1,64,5]{1,2,0:T(8,128)(2,1)S(1)} %maximum_bitcast_fusion), channel_id=1, replica_groups=mesh['dp'=16,'ctx'=2] {'dp'}, dimensions={0}, use_global_device_ids=true | all-gather | bytes 10880 | tf_op jit(solution)/shard_map/all_gather | solution.py:56
  71.7 1.9 fusion.13
  73.6 6.9 all-gather.7.cloned.1.call-done
  80.5 9.4 fusion.29
  91.3 3.6 collective-permute-start
  97.8 2.0 copy-done.3
  99.7 2.5 fusion.9
  102.2 20.5 %all-gather.9.cloned.1.call-done = bf16[1024,1024]{1,0:T(8,128)(2,1)} async-done(((bf16[64,1024]{1,0:T(8,128)(2,1)}), bf16[1024,1024]{1,0:T(8,128)(2,1)}) %all-gather.9.cloned.1.call-update) | async-done | bytes 2097168 | tf_op jit(solution)/shard_map/all_gather | solution.py:52
  122.7 4.7 multiply_reduce_fusion.5
  127.4 2.0 copy-done.8
  129.8 75.4 %all-gather.11.cloned.1.call-done = bf16[1024,4608]{1,0:T(8,128)(2,1)} async-done(((bf16[64,4608]{1,0:T(8,128)(2,1)}), bf16[1024,4608]{1,0:T(8,128)(2,1)}) %all-gather.11.cloned.1.call-update) | async-done | bytes 9437200 | tf_op jit(solution)/shard_map/all_gather | solution.py:53
  205.3 16.0 %fusion.30 = f32[1024,4608]{1,0:T(8,128)} fusion(bf16[1024,1024]{1,0:T(8,128)(2,1)S(1)} %multiply_convert_fusion.3, bf16[1024,4608]{1,0:T(8,128)(2,1)} %all-gather.11.cloned.1.call-done), kind=kOutput, calls=%fused_computation.76 | convolution fusion | flops 9663676416 | bytes 30408704 | tf_op jit(solution)/shard_map/dot_general | solution.py:80
  221.3 65.7 %all-gather.13.cloned.1.call-done = bf16[1024,4608]{1,0:T(8,128)(2,1)} async-done(((bf16[64,4608]{1,0:T(8,128)(2,1)}), bf16[1024,4608]{1,0:T(8,128)(2,1)}) %all-gather.13.cloned.1.call-update) | async-done | bytes 9437200 | tf_op jit(solution)/shard_map/all_gather | solution.py:54
  287.0 16.1 %fusion.31 = f32[1024,4608]{1,0:T(8,128)} fusion(bf16[1024,1024]{1,0:T(8,128)(2,1)S(1)} %multiply_convert_fusion.3, bf16[1024,4608]{1,0:T(8,128)(2,1)} %all-gather.13.cloned.1.call-done), kind=kOutput, calls=%fused_computation.77 | convolution fusion | flops 9663676416 | bytes 30408704 | tf_op jit(solution)/shard_map/dot_general | solution.py:81
  303.1 65.7 %all-gather.15.cloned.1.call-done = bf16[4608,1024]{1,0:T(8,128)(2,1)} async-done(((bf16[288,1024]{1,0:T(8,128)(2,1)}), bf16[4608,1024]{1,0:T(8,128)(2,1)}) %all-gather.15.cloned.1.call-update) | async-done | bytes 9437200 | tf_op jit(solution)/shard_map/all_gather | solution.py:55
  368.7 31.9 %multiply_convert_fusion = (bf16[1024,4608]{1,0:T(8,128)(2,1)}, bf16[1024,4608]{1,0:T(8,128)(2,1)}, bf16[1024,4608]{1,0:T(8,128)(2,1)}) fusion(f32[1024,4608]{1,0:T(8,128)} %fusion.30, f32[1024,4608]{1,0:T(8,128)} %fusion.31, bf16[1024,1024]{1,0:T(8,128)(2,1)} %bitcast.105, bf16[4608,1024]{1,0:T(8,128)(2,1)} %all-gather.15.cloned.1.call-done), kind=kOutput, calls=%fused_computation | convolution fusion | flops 9734455296 | bytes 77594624 | tf_op jit(solution)/shard_map/dot_general | solution.py:22
  400.7 16.1 %fusion.32 = f32[1024,1024]{1,0:T(8,128)} fusion(bf16[1024,4608]{1,0:T(8,128)(2,1)} %get-tuple-element.19, bf16[1024,4608]{1,0:T(8,128)(2,1)} %all-gather.11.cloned.1.call-done), kind=kOutput, calls=%fused_computation.78 | convolution fusion | flops 9663676416 | bytes 23068672 | tf_op jit(solution)/shard_map/dot_general | solution.py:22
  416.8 16.5 %multiply_reduce_fusion.3 = (f32[1024]{0:T(1024)S(1)}, f32[1024]{0:T(1024)S(1)}, f32[1024,1024]{1,0:T(8,128)S(1)}) fusion(f32[1024,1024]{1,0:T(8,128)S(1)} %copy-done.9, f32[1024]{0:T(1024)S(1)} %get-tuple-element.32, f32[1024]{0:T(1024)S(1)} %bitcast.119, f32[1024,1024]{1,0:T(8,128)} %fusion.32, bf16[1024,4608]{1,0:T(8,128)(2,1)} %get-tuple-element.18, ...), kind=kOutput, calls=%fused_computation.44 | convolution fusion | flops 9671014400 | bytes 31473664 | tf_op jit(solution)/shard_map/dot_general | solution.py:22
  433.3 2.8 subtract_add_fusion
  436.1 2.0 copy-done.4
  438.1 4.4 fusion.22
  442.6 9.5 multiply_reduce_fusion
  453.4 4.2 collective-permute-done.1
  459.3 5.9 fusion.7
  467.3 10.1 fusion.20
  477.4 16.5 %fusion.33 = f32[1024,4608]{1,0:T(8,128)} fusion(bf16[1024,1024]{1,0:T(8,128)(2,1)S(1)} %multiply_convert_fusion.3, bf16[1024,4608]{1,0:T(8,128)(2,1)} %get-tuple-element.19), kind=kOutput, calls=%fused_computation.79 | convolution fusion | flops 9663676416 | bytes 30408704 | tf_op jit(solution)/shard_map/dot_general | solution.py:16
  494.0 16.3 %fusion.34 = f32[1024,4608]{1,0:T(8,128)} fusion(bf16[1024,1024]{1,0:T(8,128)(2,1)S(1)} %multiply_convert_fusion.3, bf16[1024,4608]{1,0:T(8,128)(2,1)} %get-tuple-element.18), kind=kOutput, calls=%fused_computation.80 | convolution fusion | flops 9663676416 | bytes 30408704 | tf_op jit(solution)/shard_map/dot_general | solution.py:16
  511.9 17.5 %fusion.35 = f32[4608,1024]{1,0:T(8,128)} fusion(bf16[1024,4608]{1,0:T(8,128)(2,1)} %get-tuple-element.20, bf16[1024,1024]{1,0:T(8,128)(2,1)S(1)} %bitcast.106), kind=kOutput, calls=%fused_computation.81 | convolution fusion | flops 9663676416 | bytes 30408704 | tf_op jit(solution)/shard_map/dot_general | solution.py:16
  530.1 7.5 multiply_reduce_fusion.1
  539.7 12.7 fusion.19
  554.1 97.5 %reduce-scatter.14.cloned.1.call-done = f32[64,3072]{1,0:T(8,128)} async-done(((f32[1024,3072]{1,0:T(8,128)}), f32[64,3072]{1,0:T(8,128)}) %reduce-scatter.14.cloned.1.call-update) | async-done | bytes 786448 | tf_op jit(solution)/shard_map/reduce_scatter | solution.py:143
  651.7 198.5 %reduce-scatter.22.cloned.1.call-done = f32[64,4608]{1,0:T(8,128)} async-done(((f32[1024,4608]{1,0:T(8,128)}), f32[64,4608]{1,0:T(8,128)}) %reduce-scatter.22.cloned.1.call-update) | async-done | bytes 1179664 | tf_op jit(solution)/shard_map/reduce_scatter | solution.py:145
  850.3 198.5 %reduce-scatter.26.cloned.1.call-done = f32[64,4608]{1,0:T(8,128)} async-done(((f32[1024,4608]{1,0:T(8,128)}), f32[64,4608]{1,0:T(8,128)}) %reduce-scatter.26.cloned.1.call-update) | async-done | bytes 1179664 | tf_op jit(solution)/shard_map/reduce_scatter | solution.py:146
  1048.9 198.3 %reduce-scatter.30.cloned.1.call-done = f32[288,1024]{1,0:T(8,128)} async-done(((f32[4608,1024]{1,0:T(8,128)}), f32[288,1024]{1,0:T(8,128)}) %reduce-scatter.30.cloned.1.call-update) | async-done | bytes 1179664 | tf_op jit(solution)/shard_map/reduce_scatter | solution.py:147
  1247.3 17.2 %add_convert_fusion = bf16[1024,1024]{1,0:T(8,128)(2,1)} fusion(f32[1024,1024]{1,0:T(8,128)} %copy-done.8, bf16[1024,4608]{1,0:T(8,128)(2,1)} %get-tuple-element.20, bf16[4608,1024]{1,0:T(8,128)(2,1)} %all-gather.15.cloned.1.call-done), kind=kOutput, calls=%fused_computation.47 | convolution fusion | flops 9665773568 | bytes 25165824 | tf_op jit(solution)/shard_map/dot_general | solution.py:85
  1264.5 2.6 fusion.16
  1267.1 39.0 %reduce-scatter.34.cloned.1.call-done = f32[64,5]{1,0:T(8,128)} async-done(((f32[1024,5]{1,0:T(8,128)}), f32[64,5]{1,0:T(8,128)}) %reduce-scatter.34.cloned.1.call-update) | async-done | bytes 1296
  1306.9 4.9 psum.7
  1312.9 6.5 reduce-scatter.20.cloned.1.call-done
  1319.5 20.4 %reduce-scatter.16.cloned.1.call-done = f32[64,1536]{1,0:T(8,128)} async-done(((f32[64,3072]{1,0:T(8,128)}), f32[64,1536]{1,0:T(8,128)}) %reduce-scatter.16.cloned.1.call-update) | async-done | bytes 393232 | tf_op jit(solution)/shard_map/reduce_scatter | solution.py:151
  1339.8 24.5 %reduce-scatter.24.cloned.1.call-done = f32[64,2304]{1,0:T(8,128)} async-done(((f32[64,4608]{1,0:T(8,128)}), f32[64,2304]{1,0:T(8,128)}) %reduce-scatter.24.cloned.1.call-update) | async-done | bytes 589840 | tf_op jit(solution)/shard_map/reduce_scatter | solution.py:153
  1364.3 24.5 %reduce-scatter.28.cloned.1.call-done = f32[64,2304]{1,0:T(8,128)} async-done(((f32[64,4608]{1,0:T(8,128)}), f32[64,2304]{1,0:T(8,128)}) %reduce-scatter.28.cloned.1.call-update) | async-done | bytes 589840 | tf_op jit(solution)/shard_map/reduce_scatter | solution.py:154
  1388.8 24.5 %reduce-scatter.32.cloned.1.call-done = f32[288,512]{1,0:T(8,128)} async-done(((f32[288,1024]{1,0:T(8,128)}), f32[288,512]{1,0:T(8,128)}) %reduce-scatter.32.cloned.1.call-update) | async-done | bytes 589840 | tf_op jit(solution)/shard_map/reduce_scatter | solution.py:155
  (128 shorter events, 18.7 us)
Async XLA Ops:
  7.2 33.6 %copy-start.20 = (bf16[288,512]{1,0:T(8,128)(2,1)S(1)}, bf16[288,512]{1,0:T(8,128)(2,1)}, u32[]{:S(2)}) copy-start(bf16[288,512]{1,0:T(8,128)(2,1)} %param.15) | copy-start | bytes 884740
  7.2 41.2 %copy-start.35 = (bf16[64]{0:T(256)(128)(2,1)S(1)}, bf16[64]{0:T(256)(128)(2,1)}, u32[]{:S(2)}) copy-start(bf16[64]{0:T(256)(128)(2,1)} %param.16) | copy-start | bytes 388
  7.2 41.2 %copy-start.34 = (bf16[64]{0:T(256)(128)(2,1)S(1)}, bf16[64]{0:T(256)(128)(2,1)}, u32[]{:S(2)}) copy-start(bf16[64]{0:T(256)(128)(2,1)} %param.17) | copy-start | bytes 388
  7.2 41.2 %copy-start.33 = (bf16[3,64]{1,0:T(4,128)(2,1)S(1)}, bf16[3,64]{1,0:T(4,128)(2,1)}, u32[]{:S(2)}) copy-start(bf16[3,64]{1,0:T(4,128)(2,1)} %param.18) | copy-start | bytes 1156
  7.2 63.9 %copy-start.6 = (bf16[2,512,1024]{2,1,0:T(8,128)(2,1)S(1)}, bf16[2,512,1024]{2,1,0:T(8,128)(2,1)}, u32[]{:S(2)}) copy-start(bf16[2,512,1024]{2,1,0:T(8,128)(2,1)} %param.10) | copy-start | bytes 6291460
  7.2 73.2 %all-gather.7.cloned.1.call-start = ((), (), s32[]{:S(2)}) async-start(), calls=%async_computation.11 | async-start | bytes 6684672 | tf_op jit(solution)/shard_map/all_gather | solution.py:51
  17.9 104.9 %all-gather.9.cloned.1.call-start = ((), (), s32[]{:S(2)}) async-start(), calls=%async_computation.12 | async-start | bytes 2228224 | tf_op jit(solution)/shard_map/all_gather | solution.py:52
  23.2 182.1 %all-gather.11.cloned.1.call-start = ((), (), s32[]{:S(2)}) async-start(), calls=%async_computation.13 | async-start | bytes 10027008 | tf_op jit(solution)/shard_map/all_gather | solution.py:53
  32.9 254.1 %all-gather.13.cloned.1.call-start = ((), (), s32[]{:S(2)}) async-start(), calls=%async_computation.14 | async-start | bytes 10027008 | tf_op jit(solution)/shard_map/all_gather | solution.py:54
  40.7 328.0 %all-gather.15.cloned.1.call-start = ((), (), s32[]{:S(2)}) async-start(), calls=%async_computation.15 | async-start | bytes 10027008 | tf_op jit(solution)/shard_map/all_gather | solution.py:55
  48.3 505.2 %reduce-scatter.18.cloned.1.call-start = ((), (), s32[]{:S(2)}) async-start(), calls=%async_computation.18 | async-start | bytes 4456448 | tf_op jit(solution)/shard_map/reduce_scatter | solution.py:144
  71.7 18.2 %copy-start.23 = (f32[1,4,2,128]{3,1,2,0:T(4,128)}, f32[1,4,2,128]{3,1,2,0:T(4,128)S(1)}, u32[]{:S(2)}) copy-start(f32[1,4,2,128]{3,1,2,0:T(4,128)S(1)} %copy.25) | copy-start | bytes 12292
  71.7 18.2 %copy-start.31 = (f32[1,1024]{1,0:T(1,128)}, f32[1,1024]{1,0:T(1,128)S(1)}, u32[]{:S(2)}) copy-start(f32[1,1024]{1,0:T(1,128)S(1)} %get-tuple-element.28) | copy-start | bytes 12292
  71.7 24.3 %copy-start.25 = (f32[1,1024]{1,0:T(1,128)}, f32[1,1024]{1,0:T(1,128)S(1)}, u32[]{:S(2)}) copy-start(f32[1,1024]{1,0:T(1,128)S(1)} %get-tuple-element.25) | copy-start | bytes 12292
  71.7 24.3 %copy-start.27 = (f32[1,1024]{1,0:T(1,128)}, f32[1,1024]{1,0:T(1,128)S(1)}, u32[]{:S(2)}) copy-start(f32[1,1024]{1,0:T(1,128)S(1)} %get-tuple-element.26) | copy-start | bytes 12292
  71.7 24.3 %copy-start.29 = (f32[1,1024]{1,0:T(1,128)}, f32[1,1024]{1,0:T(1,128)S(1)}, u32[]{:S(2)}) copy-start(f32[1,1024]{1,0:T(1,128)S(1)} %get-tuple-element.27) | copy-start | bytes 12292
  89.9 7.8 copy-start.1
  91.3 6.5 copy-start
  91.3 4.7 collective-permute-start
  127.4 2.0 copy-start.8
  400.7 16.1 %copy-start.9 = (f32[1024,1024]{1,0:T(8,128)S(1)}, f32[1024,1024]{1,0:T(8,128)}, u32[]{:S(2)}) copy-start(f32[1024,1024]{1,0:T(8,128)} %copy-done.8) | copy-start | bytes 12582916
  433.3 4.8 copy-start.11
  442.5 15.2 %copy-start.26 = (f32[1,1024]{1,0:T(1,128)S(1)}, f32[1,1024]{1,0:T(1,128)}, u32[]{:S(2)}) copy-start(f32[1,1024]{1,0:T(1,128)} %copy-done.25) | copy-start | bytes 12292
  442.5 15.2 %copy-start.28 = (f32[1,1024]{1,0:T(1,128)S(1)}, f32[1,1024]{1,0:T(1,128)}, u32[]{:S(2)}) copy-start(f32[1,1024]{1,0:T(1,128)} %copy-done.27) | copy-start | bytes 12292
  442.5 15.1 %copy-start.30 = (f32[1,1024]{1,0:T(1,128)S(1)}, f32[1,1024]{1,0:T(1,128)}, u32[]{:S(2)}) copy-start(f32[1,1024]{1,0:T(1,128)} %copy-done.29) | copy-start | bytes 12292
  442.6 209.0 %reduce-scatter.14.cloned.1.call-start = ((), (), s32[]{:S(2)}) async-start(), calls=%async_computation.16 | async-start | bytes 13369344 | tf_op jit(solution)/shard_map/reduce_scatter | solution.py:143
  452.1 5.6 copy-start.2
  452.1 13.1 copy-start.14
  452.1 5.5 collective-permute-start.1
  459.3 8.0 copy-start.12
  465.2 2.1 copy-start.18
  477.3 372.8 %reduce-scatter.22.cloned.1.call-start = ((), (), s32[]{:S(2)}) async-start(), calls=%async_computation.20 | async-start | bytes 20054016 | tf_op jit(solution)/shard_map/reduce_scatter | solution.py:145
  493.9 554.8 %reduce-scatter.26.cloned.1.call-start = ((), (), s32[]{:S(2)}) async-start(), calls=%async_computation.22 | async-start | bytes 20054016 | tf_op jit(solution)/shard_map/reduce_scatter | solution.py:146
  510.3 736.9 %reduce-scatter.30.cloned.1.call-start = ((), (), s32[]{:S(2)}) async-start(), calls=%async_computation.24 | async-start | bytes 20054016 | tf_op jit(solution)/shard_map/reduce_scatter | solution.py:147
  529.4 8.3 copy-start.7
  529.4 8.3 copy-start.24
  529.5 8.3 copy-start.32
  529.5 776.6 %reduce-scatter.34.cloned.1.call-start = ((), (), s32[]{:S(2)}) async-start(), calls=%async_computation.26 | async-start | bytes 557056
  530.1 7.7 copy-start.15
  530.1 8.6 copy-start.17
  530.1 9.5 copy-start.19
  553.5 766.0 %reduce-scatter.20.cloned.1.call-start = ((), (), s32[]{:S(2)}) async-start(), calls=%async_computation.19 | async-start | bytes 393216 | tf_op jit(solution)/shard_map/reduce_scatter | solution.py:152
  554.0 785.8 %reduce-scatter.16.cloned.1.call-start = ((), (), s32[]{:S(2)}) async-start(), calls=%async_computation.17 | async-start | bytes 1179648 | tf_op jit(solution)/shard_map/reduce_scatter | solution.py:151
  651.6 712.7 %reduce-scatter.24.cloned.1.call-start = ((), (), s32[]{:S(2)}) async-start(), calls=%async_computation.21 | async-start | bytes 1769472 | tf_op jit(solution)/shard_map/reduce_scatter | solution.py:153
  850.2 538.6 %reduce-scatter.28.cloned.1.call-start = ((), (), s32[]{:S(2)}) async-start(), calls=%async_computation.23 | async-start | bytes 1769472 | tf_op jit(solution)/shard_map/reduce_scatter | solution.py:154
  1048.8 364.5 %reduce-scatter.32.cloned.1.call-start = ((), (), s32[]{:S(2)}) async-start(), calls=%async_computation.25 | async-start | bytes 1769472 | tf_op jit(solution)/shard_map/reduce_scatter | solution.py:155
  1247.2 17.2 %copy-start.5 = (f32[1024,1024]{1,0:T(8,128)S(1)}, f32[1024,1024]{1,0:T(8,128)}, u32[]{:S(2)}) copy-start(f32[1024,1024]{1,0:T(8,128)} %copy-done.4) | copy-start | bytes 12582916
  1247.3 17.2 %copy-start.10 = (f32[1024,1024]{1,0:T(8,128)S(1)}, f32[1024,1024]{1,0:T(8,128)}, u32[]{:S(2)}) copy-start(f32[1024,1024]{1,0:T(8,128)} %get-tuple-element.36) | copy-start | bytes 12582916
  (6 other events, 9.3 us)
Sparse Core Ops, SparseCore 0:
  18.0 62.4 all-gather.6
  82.6 40.0 all-gather.8
  125.0 80.2 all-gather.10
  207.4 79.5 all-gather.12
  289.1 79.5 all-gather.14
  442.6 70.5 reduce-scatter.17
  517.8 133.7 reduce-scatter.13
  656.2 193.9 reduce-scatter.21
  854.9 193.8 reduce-scatter.25
  1053.3 193.8 reduce-scatter.29
  1251.2 54.8 reduce-scatter.33
  1308.7 10.6 reduce-scatter.19
  1322.4 17.4 reduce-scatter.15
  1342.5 21.7 reduce-scatter.23
  1367.1 21.7 reduce-scatter.27
  1391.5 21.7 reduce-scatter.31
where the time goes:
time: 1430 us; the launch traced here: 1420 us
  waiting for transfers between devices  1070 us (75%)
  matrix products  215 us (15%)
  blocking collectives  68.3 us (5%)
  other arithmetic  28.7 us (2%)
  local copies, waits for them, and re-layouts  15.3 us (1%)
  between operations  15.1 us (1%)
    reduce_scatter x1, waiting for transfers between devices, shards(): lax.psum_scatter(grad_w_gate, 'dp', scatter_dimension=0, tiled=True)  199 us
    reduce_scatter x1, waiting for transfers between devices, shards(): lax.psum_scatter(grad_w_up, 'dp', scatter_dimension=0, tiled=True)  199 us
    reduce_scatter x1, waiting for transfers between devices, shards(): lax.psum_scatter(grad_w_down, 'dp', scatter_dimension=0, tiled=True)  198 us
    reduce_scatter x1, waiting for transfers between devices, shards(): lax.psum_scatter(grad_w_in, 'dp', scatter_dimension=0, tiled=True)  97.5 us
    dot_general x5, matrix products, cross_cols(): lax.dot_general(left_operand, right_operand, (((1,), (1,)), ((), ())), pr...  86.7 us
    all_gather x1, waiting for transfers between devices, shards(): lax.all_gather(gate_cols, 'dp', axis=0, tiled=True)  75.4 us
    all_gather x1, waiting for transfers between devices, shards(): lax.all_gather(up_cols, 'dp', axis=0, tiled=True)  65.7 us
    all_gather x1, waiting for transfers between devices, shards(): lax.all_gather(down_cols, 'dp', axis=0, tiled=True)  65.7 us
  transfers between devices with their start and end apart: 18, of which 17 were waited for; matrix products, arithmetic and copies ran while one was open for 12% of the time, Pallas kernels for 0%

commit v1 on v0

--- a/solution.py
+++ b/solution.py
@@ -1,9 +1,16 @@
+import functools
 import jax
 import jax.numpy as jnp
 from jax import lax
+from jax.experimental import pallas as pl
+from jax.experimental.pallas import tpu as pltpu
+from jax.sharding import Mesh
 from jax.sharding import PartitionSpec as P
 
 EPSILON = 1e-05
+CHUNKS = 3
+f32 = jnp.float32
+bf16 = jnp.bfloat16
 
 
 def passed_along(block, axis, distance):
@@ -36,7 +43,7 @@
     return (scale * weighted - values * (scale * scale * scale) * inner, gain_grad)
 
 
-def shards(tokens, w_in, w_out, w_gate, w_up, w_down, gain_mix, gain_ffn, kernel, cotangent):
+def plain_shards(tokens, w_in, w_out, w_gate, w_up, w_down, gain_mix, gain_ffn, kernel, cotangent):
     seq_count, piece_len, model_width = tokens.shape
     row_count = seq_count * piece_len
     small_params = jnp.concatenate([gain_mix[None], gain_ffn[None], kernel], axis=0)
@@ -169,34 +176,513 @@
     )
 
 
+NT = (((1,), (1,)), ((), ()))
+TN = (((0,), (0,)), ((), ()))
+
+
+def swap(block):
+    return lax.ppermute(block, "core", [(0, 1), (1, 0)])
+
+
+def across(block, mask):
+    count = lax.axis_size("chip") * lax.axis_size("ctx")
+    return lax.ppermute(block, ("chip", "ctx"), [(i, i ^ mask) for i in range(count)])
+
+
+def bit_masks():
+    n_chip, n_ctx = lax.axis_size("chip"), lax.axis_size("ctx")
+    ctx_bits = [1 << b for b in range(n_ctx.bit_length() - 1)]
+    near = [n_ctx]
+    far = [n_ctx << b for b in range(1, n_chip.bit_length() - 1)]
+    return far, near + ctx_bits, ctx_bits + near
+
+
+def after(value, *done):
+    return lax.optimization_barrier((value, *done))[0]
+
+
+def gather_plan(cut, total):
+    far, first_order, second_order = bit_masks()
+    plan = []
+    for operand, order, row0, rows in ((0, first_order, 0, cut), (2, second_order, cut, total - cut)):
+        masks = [0]
+        for mask in far + order[:-1]:
+            masks = masks + [m ^ mask for m in masks]
+        for index, mask in enumerate(masks):
+            plan.append((operand, index, mask, row0, rows))
+            plan.append((operand + 1, index, mask ^ order[-1], row0, rows))
+    return plan
+
+
+def gather(block, cut):
+    far, first_order, second_order = bit_masks()
+    hold = block[None]
+    for mask in far:
+        hold = jnp.concatenate([hold, across(hold, mask)], axis=0)
+    parts = []
+    for order, half in ((first_order, hold[:, :cut]), (second_order, hold[:, cut:])):
+        for mask in order[:-1]:
+            half = jnp.concatenate([half, across(half, mask)], axis=0)
+        parts += [half, across(half, order[-1])]
+    return parts
+
+
+def scatter_sum(parts, ties=()):
+    far, first_order, second_order = bit_masks()
+    ties = dict(enumerate(ties))
+
+    def sent(block, mask, step):
+        block = block.astype(bf16)
+        if ties.get(step) is not None:
+            block = after(block, ties[step])
+        return across(block, mask).astype(f32)
+
+    halves = []
+    for order, keep, send in ((first_order, parts[0], parts[1]), (second_order, parts[2], parts[3])):
+        keep = keep.astype(f32) + sent(send, order[-1], 0)
+        for step, mask in enumerate(reversed(order[:-1])):
+            mid = keep.shape[0] // 2
+            keep = keep[:mid] + sent(keep[mid:], mask, step + 1)
+        halves.append(keep)
+    keep = jnp.concatenate(halves, axis=1)
+    for step, mask in enumerate(reversed(far)):
+        mid = keep.shape[0] // 2
+        keep = keep[:mid] + sent(keep[mid:], mask, len(first_order) + step)
+    return keep[0]
+
+
+def slot_pairs(own, plan, refs, segments, n_ctx, targets):
+    pairs = []
+    for operand, index, mask, row0, nrows in plan:
+        slot = index if mask is None else jnp.bitwise_xor(own, mask)
+        y = lax.rem(slot, n_ctx)
+        chip = lax.div(slot, n_ctx)
+        src = refs[operand].at[index]
+        for seg_row, seg_rows, lane0, lanes, target, row_step, row_add, lane_step, lane_add in segments:
+            low, high = max(seg_row, row0), min(seg_row + seg_rows, row0 + nrows)
+            if low >= high:
+                continue
+            row = pl.multiple_of(chip * row_step + row_add + (low - seg_row), 16)
+            lane = pl.multiple_of(y * lane_step + lane_add, 128)
+            pairs.append(
+                (
+                    src.at[pl.ds(low - row0, high - low), pl.ds(lane0, lanes)],
+                    targets[target].at[pl.ds(row, high - low), pl.ds(lane, lanes)],
+                )
+            )
+    return pairs
+
+
+def copy_all(pairs, sems):
+    copies = [pltpu.make_async_copy(a, b, sems.at[i]) for i, (a, b) in enumerate(pairs)]
+    for copy in copies:
+        copy.start()
+    for copy in copies:
+        copy.wait()
+
+
+def part_count(plan):
+    return 1 + max(entry[0] for entry in plan)
+
+
+def part_shapes(plan, lanes):
+    shapes = {}
+    for operand, index, _, _, rows in plan:
+        shapes[operand] = (max(index + 1, shapes.get(operand, (0,))[0]), rows, lanes)
+    return [shapes[operand] for operand in sorted(shapes)]
+
+
+def ffn_kernel(geometry, out_geometry, first, own_ref, n_ref, go_ref, *refs):
+    plan, segments, n_ctx = geometry
+    out_plan = out_geometry[0]
+    count, out_count = part_count(plan), part_count(out_plan)
+    weights, refs = refs[:count], refs[count:]
+    if not first:
+        res_in, gn_in = refs[:2]
+        refs = refs[2:]
+    res_ref, gn_ref = refs[:2]
+    grads, refs = refs[2 : 2 + out_count], refs[2 + out_count :]
+    gate_m, up_m, down_m, d_gate, d_up, d_down, h_m, gg_m, gu_m, sems = refs
+    own = own_ref[0]
+    targets = (gate_m, up_m, down_m)
+
+    @pl.when(pl.program_id(0) == 0)
+    def _():
+        d_gate[...] = jnp.zeros_like(d_gate)
+        d_up[...] = jnp.zeros_like(d_up)
+        d_down[...] = jnp.zeros_like(d_down)
+        copy_all(slot_pairs(own, plan, weights, segments, n_ctx, targets), sems)
+
+    n = n_ref[...]
+    go = go_ref[...]
+    hidden_count = gate_m.shape[1]
+    step = 256
+    for start in range(0, hidden_count, step):
+        cols = slice(start, start + step)
+        g = jnp.dot(n, gate_m[:, cols], preferred_element_type=f32)
+        u = jnp.dot(n, up_m[:, cols], preferred_element_type=f32)
+        gh = lax.dot_general(go, down_m[cols, :], NT, preferred_element_type=f32)
+        s = jax.nn.sigmoid(g)
+        act = g * s
+        h_m[:, cols] = (act * u).astype(bf16)
+        gg_m[:, cols] = (gh * u * s * (1.0 + g * (1.0 - s))).astype(bf16)
+        gu_m[:, cols] = (gh * act).astype(bf16)
+    res = jnp.dot(h_m[...], down_m[...], preferred_element_type=f32)
+    gn = lax.dot_general(gg_m[...], gate_m[...], NT, preferred_element_type=f32)
+    gn = gn + lax.dot_general(gu_m[...], up_m[...], NT, preferred_element_type=f32)
+    if not first:
+        res = res_in[...] + res
+        gn = gn_in[...] + gn
+    res_ref[...] = res
+    gn_ref[...] = gn
+    d_gate[...] += lax.dot_general(n, gg_m[...], TN, preferred_element_type=f32)
+    d_up[...] += lax.dot_general(n, gu_m[...], TN, preferred_element_type=f32)
+    d_down[...] += lax.dot_general(h_m[...], go, TN, preferred_element_type=f32)
+
+    @pl.when(pl.program_id(0) == pl.num_programs(0) - 1)
+    def _():
+        gate_m[...] = d_gate[...].astype(bf16)
+        up_m[...] = d_up[...].astype(bf16)
+        down_m[...] = d_down[...].astype(bf16)
+        pairs = slot_pairs(own, out_plan, grads, segments, n_ctx, targets)
+        copy_all([(b, a) for a, b in pairs], sems)
+
+
+def ffn_chunk(own, nffn, go, weights, totals, geometry, out_geometry, hidden_count, rows=256):
+    total, width = nffn.shape
+    first = totals is None
+    plan, segments, _ = geometry
+    out_plan = out_geometry[0]
+    count, out_count = part_count(plan), part_count(out_plan)
+    lanes = weights[0].shape[-1]
+    row_spec = pl.BlockSpec((rows, width), lambda i, o: (i, 0))
+    any_spec = pl.BlockSpec(memory_space=pl.ANY)
+    outs = pl.pallas_call(
+        functools.partial(ffn_kernel, geometry, out_geometry, first),
+        out_shape=[jax.ShapeDtypeStruct((total, width), f32)] * 2
+        + [jax.ShapeDtypeStruct(s, bf16) for s in part_shapes(out_plan, lanes)],
+        grid_spec=pltpu.PrefetchScalarGridSpec(
+            num_scalar_prefetch=1,
+            grid=(total // rows,),
+            in_specs=[row_spec] * 2 + [any_spec] * count + [row_spec] * (0 if first else 2),
+            out_specs=[row_spec] * 2 + [any_spec] * out_count,
+            scratch_shapes=[
+                pltpu.VMEM((width, hidden_count), bf16),
+                pltpu.VMEM((width, hidden_count), bf16),
+                pltpu.VMEM((hidden_count, width), bf16),
+                pltpu.VMEM((width, hidden_count), f32),
+                pltpu.VMEM((width, hidden_count), f32),
+                pltpu.VMEM((hidden_count, width), f32),
+                pltpu.VMEM((rows, hidden_count), bf16),
+                pltpu.VMEM((rows, hidden_count), bf16),
+                pltpu.VMEM((rows, hidden_count), bf16),
+                pltpu.SemaphoreType.DMA((max(len(plan), len(out_plan)) * len(segments),)),
+            ],
+        ),
+        input_output_aliases={} if first else {3 + count: 0, 4 + count: 1},
+        compiler_params=pltpu.CompilerParams(
+            vmem_limit_bytes=56 * 1024 * 1024, dimension_semantics=("arbitrary",)
+        ),
+        cost_estimate=pl.CostEstimate(
+            flops=18 * total * width * hidden_count,
+            bytes_accessed=20 * total * width,
+            transcendentals=total * hidden_count,
+        ),
+    )(own, nffn, go, *weights, *(() if first else totals))
+    return (outs[0], outs[1]), outs[2:]
+
+
+def move_kernel(geometry, count, outward, own_ref, *refs):
+    plan, segments, n_ctx = geometry
+    sems = refs[-1]
+    refs = refs[:-1]
+    if outward:
+        targets, parts = refs[: len(refs) - count], refs[len(refs) - count :]
+    else:
+        parts, targets = refs[:count], refs[count:]
+    pairs = slot_pairs(own_ref[0], plan, parts, segments, n_ctx, targets)
+    copy_all([(b, a) for a, b in pairs] if outward else pairs, sems)
+
+
+def move(own, arrays, shapes, geometry, count, outward):
+    plan, segments, _ = geometry
+    any_spec = pl.BlockSpec(memory_space=pl.ANY)
+    vmem_spec = pl.BlockSpec(memory_space=pltpu.VMEM)
+    return pl.pallas_call(
+        functools.partial(move_kernel, geometry, count, outward),
+        out_shape=[jax.ShapeDtypeStruct(s, bf16) for s in shapes],
+        in_specs=[pl.BlockSpec(memory_space=pltpu.SMEM)]
+        + [vmem_spec if outward else any_spec] * len(arrays),
+        out_specs=[any_spec if outward else vmem_spec] * len(shapes),
+        scratch_shapes=[pltpu.SemaphoreType.DMA((len(plan) * len(segments),))],
+        compiler_params=pltpu.CompilerParams(vmem_limit_bytes=24 * 1024 * 1024),
+        cost_estimate=pl.CostEstimate(flops=0, bytes_accessed=1 << 24, transcendentals=0),
+    )(own, *arrays)
+
+
+def fits(tokens, w_in, w_out, w_gate, w_down, n_dp, n_ctx):
+    width, hidden = w_gate.shape
+    if n_dp % 2 or n_dp % (2 * n_ctx) or n_dp & (n_dp - 1) or n_ctx & (n_ctx - 1) or n_ctx < 2:
+        return False
+    depth = width // n_dp
+    if width % n_dp or hidden % (n_dp * CHUNKS * 48) or w_in.shape[1] % (2 * n_ctx * 256):
+        return False
+    lanes = hidden // n_dp // CHUNKS * (n_dp // n_ctx // 2)
+    wide = width // n_ctx
+    return (
+        lanes % 128 == 0
+        and wide == lanes + 128
+        and lanes == 384
+        and wide % 256 == 0
+        and depth % 16 == 0
+        and 2 * depth <= 256
+        and (w_in.shape[1] // n_ctx) % (2 * depth) == 0
+        and width % (2 * depth) == 0
+        and tokens.shape[1] % n_ctx == 0
+    )
+
+
+def fast_shards(tokens, w_in, w_out, w_gate, w_up, w_down, gain_mix, gain_ffn, kernel, cotangent):
+    seqs, piece, width = tokens.shape
+    rows = seqs * piece
+    n_chip, n_ctx = lax.axis_size("chip"), lax.axis_size("ctx")
+    slots = n_chip * n_ctx
+    core = lax.axis_index("core")
+    own_slot = lax.axis_index("chip") * n_ctx + lax.axis_index("ctx")
+    own = own_slot.astype(jnp.int32)[None]
+    depth = w_in.shape[0]
+    groups = n_chip // n_ctx
+    sub = w_down.shape[0] // CHUNKS
+    lanes = groups * sub
+    wide = w_out.shape[1]
+    in_cols = w_in.shape[1] // 2
+    in_parts, out_parts = in_cols // 256, wide // 256
+    hidden_count = n_chip * sub
+    channels = width // 2
+
+    def mine_other(pair):
+        return jnp.where(core == 0, pair[0], pair[1]), jnp.where(core == 0, pair[1], pair[0])
+
+    def in_core_order(mine, other, axis):
+        return jnp.where(
+            core == 0,
+            jnp.concatenate([mine, other], axis=axis),
+            jnp.concatenate([other, mine], axis=axis),
+        )
+
+    small = jnp.concatenate([gain_mix[None], gain_ffn[None], kernel], axis=0)
+    in_pair = w_in.reshape(depth, in_cols // depth, 2, depth).transpose(2, 0, 1, 3)
+    in_pair = in_pair.reshape(2, depth, in_parts, 256).transpose(0, 2, 1, 3)
+    in_mine, in_other = mine_other(in_pair)
+    small_rows = jnp.pad(small, ((0, 11), (0, 256 - depth)))
+    swapped = swap(jnp.concatenate([in_other.reshape(in_parts * depth, 256), small_rows], axis=0))
+    in_got = swapped[: in_parts * depth].reshape(in_parts, depth, 256)
+    in_block = in_core_order(in_mine, in_got, 1).reshape(in_parts * 2 * depth, 256)
+    small_block = in_core_order(small, swapped[in_parts * depth :][:5, :depth], 1)
+    small_block = jnp.pad(small_block, ((0, 11), (0, 256 - 2 * depth)))
+    out_block = w_out.reshape(depth, out_parts, 256).transpose(1, 0, 2).reshape(-1, 256)
+    mix_block = jnp.concatenate([in_block, out_block, small_block], axis=0)
+
+    both = jnp.stack([w_gate, w_up]).reshape(2, depth, groups, 2, CHUNKS, sub)
+    both = both.transpose(3, 4, 0, 1, 2, 5).reshape(2, CHUNKS, 2, depth, lanes)
+    both_mine, both_other = mine_other(both)
+    both_block = in_core_order(both_mine, swap(both_other), 2)
+    both_block = both_block.reshape(CHUNKS, 4 * depth, lanes)
+    down = w_down.reshape(CHUNKS, sub, wide)
+    down_rest = down[:, :, lanes:].reshape(CHUNKS, 3, sub // 3, 128).transpose(0, 2, 1, 3)
+    chunk_blocks = jnp.concatenate(
+        [both_block, down[:, :, :lanes], down_rest.reshape(CHUNKS, sub // 3, lanes)], axis=1
+    )
+
+    mix_rows = mix_block.shape[0]
+    mix_cut = 256
+    in_rows = in_parts * 2 * depth
+    mix_segments = [
+        (k * 2 * depth, 2 * depth, 0, 256, 0, 2 * depth, 0, in_cols, 256 * k)
+        for k in range(in_parts)
+    ]
+    mix_segments += [
+        (in_rows + k * depth, depth, 0, 256, 1, depth, 0, wide, 256 * k) for k in range(out_parts)
+    ]
+    small_segment = (in_rows + out_parts * depth, 16, 0, 256, 2, 16, 0, 256, 0)
+    mix_plan = gather_plan(mix_cut, mix_rows)
+    chunk_rows = chunk_blocks.shape[1]
+    chunk_cut = chunk_rows // 2
+    chunk_segments = [
+        (0, 2 * depth, 0, lanes, 0, 2 * depth, 0, lanes, 0),
+        (2 * depth, 2 * depth, 0, lanes, 1, 2 * depth, 0, lanes, 0),
+        (4 * depth, sub, 0, lanes, 2, sub, 0, wide, 0),
+    ] + [
+        (4 * depth + sub, sub // 3, 128 * k, 128, 2, sub, k * (sub // 3), wide, lanes)
+        for k in range(3)
+    ]
+    whole_plan = [(0, i, None, 0, chunk_rows) for i in range(slots)]
+    whole_geometry = (whole_plan, chunk_segments, n_ctx)
+    step_geometry = (gather_plan(chunk_cut, chunk_rows), chunk_segments, n_ctx)
+
+    mix_parts = gather(mix_block, mix_cut)
+    chunk_weights = [[lax.all_gather(chunk_blocks[q], ("chip", "ctx"))] for q in range(CHUNKS)]
+    in_half, out_half, small_all = move(
+        own,
+        mix_parts,
+        [(width, n_ctx * in_cols), (channels, width), (n_chip * 16, n_ctx * 256)],
+        (mix_plan, mix_segments + [small_segment], n_ctx),
+        4,
+        False,
+    )
+    small_all = small_all.reshape(n_chip, 16, n_ctx * 256)[:, :5, : 2 * depth].astype(f32)
+    first_gain = small_all[:, 0].reshape(width)
+    second_gain = small_all[:, 1].reshape(width)
+    taps = small_all[:, 2:].reshape(n_chip, 3, 2, depth)
+    taps = jnp.where(core == 0, taps[:, :, 0], taps[:, :, 1]).transpose(1, 0, 2)
+    taps = taps.reshape(3, channels)
+
+    token_rows = tokens.reshape(rows, width)
+    inputs = jnp.concatenate([token_rows, swap(token_rows)], axis=0).astype(f32)
+    go_rows = cotangent.reshape(rows, width)
+    go = jnp.concatenate([go_rows, swap(go_rows)], axis=0)
+    normed, scale_mix = norm_forward(inputs, first_gain)
+    normed_low = normed.astype(bf16)
+    projected = jnp.dot(normed_low, in_half, preferred_element_type=f32)
+    gate_b = projected[:, :channels]
+    gate_c = projected[:, channels : 2 * channels]
+    values = projected[:, 2 * channels :]
+    product = (gate_b * values).reshape(2 * seqs, piece, channels)
+    previous = passed_along(product[:, piece - 2 :].astype(bf16), "ctx", 1).astype(f32)
+    padded = jnp.concatenate([previous, product], axis=1)
+    convolved = taps[0] * padded[:, :-2] + taps[1] * padded[:, 1:-1] + taps[2] * padded[:, 2:]
+    convolved = convolved.reshape(2 * rows, channels)
+    mixer_out = (gate_c * convolved).astype(bf16)
+    branch = jnp.dot(mixer_out, out_half, preferred_element_type=f32)
+
+    def swap_rows(block):
+        got = swap(block.astype(bf16)).astype(f32)
+        return jnp.concatenate([got[rows:], got[:rows]], axis=0)
+
+    residual = inputs + (branch + swap_rows(branch))
+    feedforward_normed, scale_ffn = norm_forward(residual, second_gain)
+    nffn_low = feedforward_normed.astype(bf16)
+
+    totals = None
+    chunk_parts = []
+    for q in range(CHUNKS):
+        steps = q == CHUNKS - 1
+        totals, parts = ffn_chunk(
+            own, nffn_low, go, chunk_weights[q], totals, whole_geometry,
+            step_geometry if steps else whole_geometry, hidden_count,
+        )
+        chunk_parts.append(parts)
+    chunk_grads = [
+        lax.psum_scatter(parts[0], ("chip", "ctx"), scatter_dimension=0).astype(f32)
+        for parts in chunk_parts[:-1]
+    ]
+    ffn_out, grad_nffn = totals
+    grad_nffn = grad_nffn + swap_rows(grad_nffn)
+    result = residual[:rows] + (ffn_out[:rows] + swap(ffn_out[rows:].astype(bf16)).astype(f32))
+    result = result.astype(bf16).reshape(seqs, piece, width)
+
+    weighted = grad_nffn * second_gain
+    grad_gain_ffn = jnp.sum((grad_nffn * residual * scale_ffn)[:rows], axis=0)
+    inner = jnp.mean(weighted * residual, axis=-1, keepdims=True)
+    grad_residual = go.astype(f32) + (
+        scale_ffn * weighted - residual * (scale_ffn * scale_ffn * scale_ffn) * inner
+    )
+    grad_branch = grad_residual.astype(bf16)
+    grad_w_out = cross_rows(mixer_out, grad_branch).astype(bf16)
+    grad_mix = cross_cols(grad_branch, out_half)
+    grad_c = grad_mix * convolved
+    grad_conv = (grad_mix * gate_c).reshape(2 * seqs, piece, channels)
+    following = passed_along(grad_conv[:, :2].astype(bf16), "ctx", -1).astype(f32)
+    extended = jnp.concatenate([grad_conv, following], axis=1)
+    grad_product = (
+        taps[2] * extended[:, :-2] + taps[1] * extended[:, 1:-1] + taps[0] * extended[:, 2:]
+    )
+    grad_kernel = jnp.stack(
+        [jnp.sum(grad_conv * padded[:, k : k + piece], axis=(0, 1)) for k in range(3)], axis=0
+    )
+    grad_product = grad_product.reshape(2 * rows, channels)
+    grad_projected = jnp.concatenate(
+        [grad_product * values, grad_c, grad_product * gate_b], axis=1
+    ).astype(bf16)
+    last_sum = scatter_sum(chunk_parts[-1], (None, grad_branch, grad_conv, grad_projected))
+    grad_w_in = cross_rows(normed_low, grad_projected).astype(bf16)
+    mix_grad_parts = move(
+        own,
+        [grad_w_in, grad_w_out],
+        [(slots // 2, mix_cut, 256)] * 2 + [(slots // 2, in_rows + out_parts * depth - mix_cut, 256)] * 2,
+        (gather_plan(mix_cut, in_rows + out_parts * depth), mix_segments, n_ctx),
+        4,
+        True,
+    )
+    mix_sum = scatter_sum(mix_grad_parts)
+    grad_normed = cross_cols(grad_projected, in_half)
+    grad_normed = grad_normed[:rows] + swap(grad_normed[rows:].astype(bf16)).astype(f32)
+    grad_in_norm, grad_gain_mix = norm_backward(
+        inputs[:rows], scale_mix[:rows], first_gain, grad_normed
+    )
+    grad_tokens = (grad_residual[:rows] + grad_in_norm).reshape(seqs, piece, width)
+
+    chunk_sum = jnp.stack(chunk_grads + [last_sum])
+    both_sum = chunk_sum[:, : 4 * depth].reshape(CHUNKS, 2, 2, depth, lanes).transpose(2, 0, 1, 3, 4)
+    both_mine, both_other = mine_other(both_sum)
+    both_got = swap(both_other)
+    both_sum = in_core_order(both_mine[None], both_got[None], 0)
+    both_sum = both_sum.reshape(2, CHUNKS, 2, depth, groups, sub).transpose(2, 3, 4, 0, 1, 5)
+    both_sum = both_sum.reshape(2, depth, 2 * CHUNKS * lanes)
+    down_rest = chunk_sum[:, 4 * depth + sub :].reshape(CHUNKS, sub // 3, 3, 128)
+    down_rest = down_rest.transpose(0, 2, 1, 3).reshape(CHUNKS, sub, 128)
+    final_down = jnp.concatenate([chunk_sum[:, 4 * depth : 4 * depth + sub], down_rest], axis=2)
+    final_down = final_down.reshape(CHUNKS * sub, wide)
+
+    in_sum = mix_sum[:in_rows].reshape(in_parts, 2, depth, 256).transpose(1, 0, 2, 3)
+    in_mine, in_other = mine_other(in_sum)
+    in_sum = in_core_order(in_mine[None], swap(in_other)[None], 0)
+    in_sum = in_sum.transpose(0, 2, 1, 3).reshape(2, depth, in_cols // depth, depth)
+    final_in = in_sum.transpose(1, 2, 0, 3).reshape(depth, 2 * in_cols)
+    final_out = mix_sum[in_rows:].reshape(out_parts, depth, 256).transpose(1, 0, 2)
+    final_out = final_out.reshape(depth, wide)
+
+    grad_taps = grad_kernel.reshape(3, n_chip, 1, depth)
+    grad_taps = jnp.where(
+        jnp.arange(2).reshape(1, 1, 2, 1) == core, grad_taps, jnp.zeros_like(grad_taps)
+    ).reshape(3, width)
+    small_grad = jnp.concatenate([grad_gain_mix[None], grad_gain_ffn[None], grad_taps], axis=0)
+    small_sum = lax.psum_scatter(small_grad, ("chip", "core"), scatter_dimension=1, tiled=True)
+    for bit in range(n_ctx.bit_length() - 1):
+        route = [(i, i ^ (1 << bit)) for i in range(n_ctx)]
+        small_sum = small_sum + lax.ppermute(small_sum, "ctx", route)
+    return (
+        result,
+        grad_tokens,
+        final_in,
+        final_out,
+        both_sum[0],
+        both_sum[1],
+        final_down,
+        small_sum[0],
+        small_sum[1],
+        small_sum[2:5],
+    )
+
+
 def solution(mesh):
-    placed = (
-        P("dp", "ctx", None),
-        P("dp", "ctx"),
-        P("dp", "ctx"),
-        P("dp", "ctx"),
-        P("dp", "ctx"),
-        P("dp", "ctx"),
-        P("dp"),
-        P("dp"),
-        P(None, "dp"),
-        P("dp", "ctx", None),
-    )
-    return jax.shard_map(
-        shards,
-        mesh=mesh,
-        in_specs=placed,
-        out_specs=(
-            P("dp", "ctx", None),
-            P("dp", "ctx", None),
-            P("dp", "ctx"),
-            P("dp", "ctx"),
-            P("dp", "ctx"),
-            P("dp", "ctx"),
-            P("dp", "ctx"),
-            P("dp"),
-            P("dp"),
-            P(None, "dp"),
-        ),
-        check_vma=False,
-    )
+    n_dp, n_ctx = mesh.shape["dp"], mesh.shape["ctx"]
+
+    def placed(dp):
+        whole, cut = P(dp, "ctx", None), P(dp, "ctx")
+        ins = (whole, cut, cut, cut, cut, cut, P(dp), P(dp), P(None, dp), whole)
+        outs = (whole, whole, cut, cut, cut, cut, cut, P(dp), P(dp), P(None, dp))
+        return ins, outs
+
+    def run(tokens, w_in, w_out, w_gate, w_up, w_down, gain_mix, gain_ffn, kernel, cotangent):
+        if fits(tokens, w_in, w_out, w_gate, w_down, n_dp, n_ctx):
+            cut_mesh = Mesh(mesh.devices.reshape(n_dp // 2, 2, n_ctx), ("chip", "core", "ctx"))
+            body, on, (ins, outs) = fast_shards, cut_mesh, placed(("chip", "core"))
+        else:
+            body, on, (ins, outs) = plain_shards, mesh, placed("dp")
+        call = jax.shard_map(body, mesh=on, in_specs=ins, out_specs=outs, check_vma=False)
+        return call(
+            tokens, w_in, w_out, w_gate, w_up, w_down, gain_mix, gain_ffn, kernel, cotangent
+        )
+
+    return run

time: 1430 us -> 822 us (0.57)
  waiting for transfers between devices: 1070 us -> 428 us
  matrix products: 215 us -> 47.5 us
  Pallas kernels: 0 us -> 130 us
  other arithmetic: 28.7 us -> 102 us
  blocking collectives: 68.3 us -> 0 us
  local copies, waits for them, and re-layouts: 15.3 us -> 55.4 us
  starting transfers between devices: 5.54 us -> 37 us
    reduce_scatter x10 -> x2, waiting for transfers between devices: 793 us -> 186 us  [fast_shards(): lax.psum_scatter(parts[0], ('chip', 'ctx'), scatter_dimension=0).astype(f32)]
    ppermute x0 -> x29, waiting for transfers between devices: none -> 222 us  [the longest x18 209 us: across(): lax.ppermute(block, ('chip', 'ctx'), [(i, i ^ mask) for i in range(count)])]
    all_gather x5 -> x3, waiting for transfers between devices: 234 us -> 18.8 us  [fast_shards(): lax.all_gather(chunk_blocks[q], ('chip', 'ctx'))]
    pallas_call x0 -> x5, Pallas kernels: none -> 130 us  [the longest x3 124 us: ffn_chunk(): pl.pallas_call(functools.partial(ffn_kernel, geometry, out_geometry, firs...]
    dot_general x5 -> x2, matrix products: 86.7 us -> 15.9 us  [cross_cols(): lax.dot_general(left_operand, right_operand, (((1,), (1,)), ((), ())), pr...]
    all_gather x6 -> x0, blocking collectives: 63.4 us -> none  [the longest x1 22.7 us: shards(): lax.all_gather(small_params, 'dp', axis=1, tiled=True)]
    dot_general x5 -> x2, matrix products: 64.8 us -> 13.6 us  [cross_rows(): lax.dot_general(left_operand, right_operand, (((0,), (0,)), ((), ())), pr...]
    dot_general x5 -> x2, matrix products: 63.4 us -> 18 us  [the longest x1 10.9 us: fast_shards(): projected = jnp.dot(normed_low, in_half, preferred_element_type=f32)]
  transfers between devices with their start and end apart: 18 -> 37, of which waited for: 17 -> 18; matrix products, arithmetic and copies ran while one was open for 12% -> 20% of each run, Pallas kernels for 0% -> 11%
where the time goes in v1:
time: 822 us; the launch traced here: 816 us
  waiting for transfers between devices  428 us (52%)
  Pallas kernels  130 us (16%)
  other arithmetic  102 us (12%)
  local copies, waits for them, and re-layouts  55.4 us (7%)
  matrix products  47.5 us (6%)
  starting transfers between devices  37 us (5%)
  between operations  15.6 us (2%)
    ppermute x18, waiting for transfers between devices, across(): lax.ppermute(block, ('chip', 'ctx'), [(i, i ^ mask) for i in range(count)])  209 us
    reduce_scatter x2, waiting for transfers between devices, fast_shards(): lax.psum_scatter(parts[0], ('chip', 'ctx'), scatter_dimension=0).astype(f32)  186 us
    pallas_call x3, Pallas kernels, ffn_chunk(): pl.pallas_call(functools.partial(ffn_kernel, geometry, out_geometry, firs...  124 us
    ppermute x18, starting transfers between devices, across(): lax.ppermute(block, ('chip', 'ctx'), [(i, i ^ mask) for i in range(count)])  28.1 us
    unnamed x90, local copies, waits for them, and re-layouts  20.6 us
    all_gather x3, waiting for transfers between devices, fast_shards(): lax.all_gather(chunk_blocks[q], ('chip', 'ctx'))  18.8 us
  transfers between devices with their start and end apart: 37, of which 18 were waited for; matrix products, arithmetic and copies ran while one was open for 20% of the time, Pallas kernels for 11%

profile of v1, /device:TPU:0, one launch (start us, length us, event | category | flops | bytes accessed | tf_op | source)
XLA Modules:
  0.0 815.9 jit_solution(3692738579114960999)
XLA Ops:
  19.0 3.0 collective-permute-start.2
  22.0 6.8 collective-permute-done.2
  28.9 2.8 collective-permute-start.3
  31.7 29.7 %collective-permute-done.3 = bf16[2,528,256]{2,1,0:T(8,128)(2,1)S(1)} collective-permute-done((bf16[2,528,256]{2,1,0:T(8,128)(2,1)S(1)}, bf16[2,528,256]{2,1,0:T(8,128)(2,1)S(1)}, u32[]{:S(2)}, u32[]{:S(2)}) %collective-permute-start.3) | collective-permute-done | bytes 540704 | tf_op jit(solution)/shard_map/ppermute | solution.py:189
  65.1 10.4 %collective-permute-done.6 = bf16[4,272,256]{2,1,0:T(8,128)(2,1)S(1)} collective-permute-done((bf16[4,272,256]{2,1,0:T(8,128)(2,1)S(1)}, bf16[4,272,256]{2,1,0:T(8,128)(2,1)S(1)}, u32[]{:S(2)}, u32[]{:S(2)}) %collective-permute-start.6) | collective-permute-done | bytes 557088 | tf_op jit(solution)/shard_map/ppermute | solution.py:189
  77.2 2.8 collective-permute-done.4
  81.7 2.7 multiply_reduce_fusion.2
  84.4 36.2 %collective-permute-done.5.refs_1_ = bf16[8,256,256]{2,1,0:T(8,128)(2,1)} collective-permute-done((bf16[8,256,256]{2,1,0:T(8,128)(2,1)S(1)}, bf16[8,256,256]{2,1,0:T(8,128)(2,1)}, u32[]{:S(2)}, u32[]{:S(2)}) %collective-permute-start.5) | collective-permute-done | bytes 1048608 | tf_op jit(solution)/shard_map/ppermute | solution.py:189
  120.5 3.2 shard_map.177
  124.8 10.9 %fusion.14 = f32[2048,1536]{1,0:T(8,128)S(1)} fusion(bf16[1024,1536]{1,0:T(8,128)(2,1)S(1)} %get-tuple-element.34, f32[1024]{0:T(1024)S(1)} %get-tuple-element.89, f32[2048]{0:T(1024)S(1)} %add_rsqrt_fusion.1, bf16[1024,1024]{1,0:T(8,128)(2,1)} %collective-permute-done, bf16[1024,1024]{1,0:T(8,128)(2,1)} %bitcast), kind=kOutput, calls=%fused_computation.61 | convolution fusion | flops 6457131008 | bytes 19935232 | tf_op jit(solution)/shard_map/dot_general | solution.py:546
  136.7 3.5 copy-done.5
  142.3 3.5 collective-permute-start.8
  147.2 5.5 multiply_add_fusion
  152.7 4.6 fusion.11
  157.4 7.1 fusion.42
  165.1 9.3 %collective-permute-done.10 = bf16[1024,1024]{1,0:T(8,128)(2,1)} collective-permute-done((bf16[1024,1024]{1,0:T(8,128)(2,1)S(1)}, bf16[1024,1024]{1,0:T(8,128)(2,1)}, u32[]{:S(2)}, u32[]{:S(2)}) %collective-permute-start.10) | collective-permute-done | bytes 2097184 | tf_op jit(solution)/shard_map/ppermute | solution.py:184
  174.4 4.0 pad_maximum_fusion.4.go_ref
  178.4 5.1 fusion.38
  183.5 7.1 multiply_reduce_fusion.1
  190.6 3.3 copy-done.4
  196.5 40.5 %shard_map.178 = (f32[2048,1024]{1,0:T(8,128)}, f32[2048,1024]{1,0:T(8,128)}, bf16[16,384,384]{2,1,0:T(8,128)(2,1)}) custom-call(s32[1]{0:T(128)} %bitcast.1.own_ref, bf16[2048,1024]{1,0:T(8,128)(2,1)} %multiply_convert_fusion.n_ref, bf16[2048,1024]{1,0:T(8,128)(2,1)} %pad_maximum_fusion.4.go_ref, bf16[16,384,384]{2,1,0:T(8,128)(2,1)} %all-gather.8.cloned.1.call-done.refs_0_), custom_call_target="tpu_custom_call" | custom-call | flops 28991029248 | bytes 41943040 | tf_op jit(solution)/shard_map/pallas_call | solution.py:360
  237.0 41.6 %shard_map.179 = (f32[2048,1024]{1,0:T(8,128)}, f32[2048,1024]{1,0:T(8,128)}, bf16[16,384,384]{2,1,0:T(8,128)(2,1)}) custom-call(s32[1]{0:T(128)} %bitcast.1.own_ref, bf16[2048,1024]{1,0:T(8,128)(2,1)} %multiply_convert_fusion.n_ref, bf16[2048,1024]{1,0:T(8,128)(2,1)} %pad_maximum_fusion.4.go_ref, ...), custom_call_target="tpu_custom_call", output_to_operand_aliasing={{0}: (4, {}), {1}: (5, {})} | custom-call | flops 28991029248 | bytes 41943040 | tf_op jit(solution)/shard_map/pallas_call | solution.py:360
  278.6 18.8 %all-gather.4.cloned.1.call-done.refs_0_ = bf16[16,384,384]{2,1,0:T(8,128)(2,1)} async-done(((bf16[1,384,384]{2,1,0:T(8,128)(2,1)}), bf16[16,384,384]{2,1,0:T(8,128)(2,1)}) %all-gather.4.cloned.1.call-update) | async-done | bytes 4718608 | tf_op jit(solution)/shard_map/all_gather | solution.py:524
  297.4 42.0 %shard_map.180 = (f32[2048,1024]{1,0:T(8,128)}, f32[2048,1024]{1,0:T(8,128)}, bf16[8,192,384]{2,1,0:T(8,128)(2,1)}, bf16[8,192,384]{2,1,0:T(8,128)(2,1)}, bf16[8...) custom-call(s32[1]{0:T(128)} %bitcast.1.own_ref, ...), custom_call_target="tpu_custom_call", output_to_operand_aliasing={{0}: (4, {}), {1}: (5, {})} | custom-call | flops 28991029248 | bytes 41943040 | tf_op jit(solution)/shard_map/pallas_call | solution.py:360
  339.4 4.0 convert_element_type.138
  343.5 4.0 slice.510
  348.0 2.7 collective-permute-done.13
  350.7 4.2 fusion.37
  354.9 10.0 %multiply_reduce_fusion = (f32[2048]{0:T(1024)S(1)}, f32[2048,1024]{1,0:T(8,128)}) fusion(f32[2048,1024]{1,0:T(8,128)S(1)} %bitcast.114, f32[1024]{0:T(1024)S(1)} %get-tuple-element.88, f32[2048,1024]{1,0:T(8,128)} %get-tuple-element.41, f32[1024,1024]{1,0:T(8,128)} %get-tuple-element.72, f32[1024,1024]{1,0:T(8,128)} %get-tuple-element.71), kind=kLoop, calls=%fused_computation.4 | loop fusion | flops 10483712 | bytes 33566720 | tf_op jit(solution)/shard_map/reduce_sum | solution.py:586
  364.9 10.2 %fusion.35 = (bf16[2048,1024]{1,0:T(8,128)(2,1)S(1)}, f32[2048,1024]{1,0:T(8,128)}) fusion(f32[2048]{0:T(1024)S(1)} %broadcast_multiply_fusion, f32[2048,1024]{1,0:T(8,128)S(1)} %bitcast.114, f32[2048]{0:T(1024)S(1)} %get-tuple-element.93, f32[2048,1024]{1,0:T(8,128)} %get-tuple-element.64, f32[1024]{0:T(1024)S(1)} %get-tuple-element.88, ...), kind=kLoop, calls=%fused_computation.144 | loop fusion | flops 23068672 | bytes 33583104 | tf_op jit(solution)/shard_map/convert_element_type | solution.py:590
  375.1 9.2 %multiply_reduce_fusion.5 = (f32[512]{0:T(512)S(1)}, f32[512]{0:T(512)S(1)}, f32[2048,512]{1,0:T(8,128)S(1)}, f32[2048,512]{1,0:T(8,128)}) fusion(f32[4,512,512]{2,1,0:T(8,128)S(1)} %bitcast.119, f32[4,2,512]{2,1,0:T(2,128)S(1)} %convert_element_type.130, f32[2048,1536]{1,0:T(8,128)} %copy-done.5, bf16[2048,1024]{1,0:T(8,128)(2,1)S(1)} %get-tuple-element.61, ...), kind=kOutput, calls=%fused_computation.41 | convolution fusion | flops 2154822656 | bytes 22040576 | tf_op jit(solution)/shard_map/dot_general | solution.py:29
  387.8 8.8 %fusion.12 = (bf16[2048,512]{1,0:T(8,128)(2,1)S(1)}, f32[512]{0:T(512)S(1)}) fusion(f32[2048,512]{1,0:T(8,128)} %get-tuple-element.99, f32[4,512,512]{2,1,0:T(8,128)} %copy-done.6, f32[2048,512]{1,0:T(8,128)} %copy-done.9, f32[2048,1536]{1,0:T(8,128)} %copy-done.5), kind=kLoop, calls=%fused_computation.38 | loop fusion | flops 5242368 | bytes 23070720 | tf_op jit(solution)/shard_map/convert.10 | solution.py:684
  398.2 5.8 fusion.9
  404.0 6.7 fusion.34
  410.8 3.3 copy-done.11
  416.1 6.6 fusion.33
  423.1 7.3 fusion.7
  442.2 25.0 %collective-permute-done.25 = bf16[8,192,384]{2,1,0:T(8,128)(2,1)S(1)} collective-permute-done((bf16[8,192,384]{2,1,0:T(8,128)(2,1)}, bf16[8,192,384]{2,1,0:T(8,128)(2,1)S(1)}, u32[]{:S(2)}, u32[]{:S(2)}) %collective-permute-start.25) | collective-permute-done | bytes 1179680 | tf_op jit(solution)/shard_map/ppermute | solution.py:189
  467.5 3.5 collective-permute-start.26
  473.4 11.2 %convolution_convert_fusion.refs_0_ = bf16[1024,1536]{1,0:T(8,128)(2,1)S(1)} fusion(f32[1024]{0:T(1024)S(1)} %copy-done.28, f32[2048]{0:T(1024)S(1)} %copy-done.36, bf16[1024,1024]{1,0:T(8,128)(2,1)} %collective-permute-done, bf16[1024,1024]{1,0:T(8,128)(2,1)} %bitcast, bf16[2048,512]{1,0:T(8,128)(2,1)} %copy-done.21, bf16[2048,512]{1,0:T(8,128)(2,1)} %copy-done.19, ...), kind=kOutput, calls=%fused_computation.48 | convolution fusion | flops 6477578240 | bytes 13643776 | tf_op jit(solution)/shard_map/dot_general | solution.py:23
  484.6 2.7 shard_map.181
  490.0 38.7 %collective-permute-done.24 = bf16[4,192,384]{2,1,0:T(8,128)(2,1)S(1)} collective-permute-done((bf16[4,192,384]{2,1,0:T(8,128)(2,1)S(1)}, bf16[4,192,384]{2,1,0:T(8,128)(2,1)S(1)}, u32[]{:S(2)}, u32[]{:S(2)}) %collective-permute-start.24) | collective-permute-done | bytes 589856 | tf_op jit(solution)/shard_map/ppermute | solution.py:189
  533.3 36.2 %collective-permute-done.27 = bf16[2,384,384]{2,1,0:T(8,128)(2,1)S(1)} collective-permute-done((bf16[2,384,384]{2,1,0:T(8,128)(2,1)S(1)}, bf16[2,384,384]{2,1,0:T(8,128)(2,1)S(1)}, u32[]{:S(2)}, u32[]{:S(2)}) %collective-permute-start.27) | collective-permute-done | bytes 589856 | tf_op jit(solution)/shard_map/ppermute | solution.py:189
  572.2 10.4 %collective-permute-done.28 = bf16[1,384,384]{2,1,0:T(8,128)(2,1)S(1)} collective-permute-done((bf16[1,384,384]{2,1,0:T(8,128)(2,1)S(1)}, bf16[1,384,384]{2,1,0:T(8,128)(2,1)S(1)}, u32[]{:S(2)}, u32[]{:S(2)}) %collective-permute-start.28) | collective-permute-done | bytes 294944 | tf_op jit(solution)/shard_map/ppermute | solution.py:189
  582.7 12.8 %collective-permute-done.20 = bf16[2,512,256]{2,1,0:T(8,128)(2,1)S(1)} collective-permute-done((bf16[2,512,256]{2,1,0:T(8,128)(2,1)S(1)}, bf16[2,512,256]{2,1,0:T(8,128)(2,1)S(1)}, u32[]{:S(2)}, u32[]{:S(2)}) %collective-permute-start.20) | collective-permute-done | bytes 524320 | tf_op jit(solution)/shard_map/ppermute | solution.py:189
  597.4 8.1 slice_add_fusion.1
  606.0 45.1 %reduce-scatter.8.cloned.1.call-done = bf16[1,384,384]{2,1,0:T(8,128)(2,1)} async-done(((bf16[16,384,384]{2,1,0:T(8,128)(2,1)}), bf16[1,384,384]{2,1,0:T(8,128)(2,1)}) %reduce-scatter.8.cloned.1.call-update) | async-done | bytes 294928 | tf_op jit(solution)/shard_map/reduce_scatter | solution.py:576
  652.2 140.4 %reduce-scatter.6.cloned.1.call-done = bf16[1,384,384]{2,1,0:T(8,128)(2,1)} async-done(((bf16[16,384,384]{2,1,0:T(8,128)(2,1)}), bf16[1,384,384]{2,1,0:T(8,128)(2,1)}) %reduce-scatter.6.cloned.1.call-update) | async-done | bytes 294928 | tf_op jit(solution)/shard_map/reduce_scatter | solution.py:576
  (272 shorter events, 79.0 us)
Async XLA Ops:
  7.2 189.3 %all-gather.8.cloned.1.call-start = ((), (), s32[]{:S(2)}) async-start(), calls=%async_computation.5 | async-start | bytes 5013504 | tf_op jit(solution)/shard_map/all_gather | solution.py:524
  13.0 1.7 collective-permute-start.11
  16.0 221.0 %all-gather.6.cloned.1.call-start = ((), (), s32[]{:S(2)}) async-start(), calls=%async_computation.4 | async-start | bytes 5013504 | tf_op jit(solution)/shard_map/all_gather | solution.py:524
  17.0 1.4 collective-permute-start.1
  19.0 9.8 %collective-permute-start.2 = (bf16[1,528,256]{2,1,0:T(8,128)(2,1)S(1)}, bf16[1,528,256]{2,1,0:T(8,128)(2,1)S(1)}, u32[]{:S(2)}, u32[]{:S(2)}) collective-permute-start(bf16[1,528,256]{2,1,0:T(8,128)(2,1)S(1)} %fusion.23), channel_id=1, source_target_pairs={{0,8},{1,9},{4,12},{5,13},{8,0},{9,1},{12,4},{13,5},{16,24},{17,25... | collective-permute-start | bytes 811016 | tf_op jit(solution)/shard_map/ppermute | solution.py:189
  22.0 59.6 %collective-permute-start = (bf16[1024,1024]{1,0:T(8,128)(2,1)}, bf16[1024,1024]{1,0:T(8,128)(2,1)}, u32[]{:S(2)}, u32[]{:S(2)}) collective-permute-start(bf16[1024,1024]{1,0:T(8,128)(2,1)} %bitcast), channel_id=1, source_target_pairs={{0,2},{2,0},{1,3},{3,1},{4,6},{6,4},{5,7},{7,5},{8,10},{10,8},{9,1... | collective-permute-start | bytes 6291464 | tf_op jit(solution)/shard_map/ppermute | solution.py:184
  28.9 32.5 %collective-permute-start.3 = (bf16[2,528,256]{2,1,0:T(8,128)(2,1)S(1)}, bf16[2,528,256]{2,1,0:T(8,128)(2,1)S(1)}, u32[]{:S(2)}, u32[]{:S(2)}) collective-permute-start(bf16[2,528,256]{2,1,0:T(8,128)(2,1)S(1)} %pad_maximum_fusion.14), channel_id=1, source_target_pairs={{0,16},{1,17},{4,20},{5,21},{8,24},{9,25},{12,28},{13,29},{16,0},{... | collective-permute-start | bytes 1622024 | tf_op jit(solution)/shard_map/ppermute | solution.py:189
  61.4 14.1 %collective-permute-start.6 = (bf16[4,272,256]{2,1,0:T(8,128)(2,1)S(1)}, bf16[4,272,256]{2,1,0:T(8,128)(2,1)S(1)}, u32[]{:S(2)}, u32[]{:S(2)}) collective-permute-start(bf16[4,272,256]{2,1,0:T(8,128)(2,1)S(1)} %pad_maximum_fusion.12), channel_id=1, source_target_pairs={{0,1},{1,0},{4,5},{5,4},{8,9},{9,8},{12,13},{13,12},{16,17},{17,16... | collective-permute-start | bytes 1671176 | tf_op jit(solution)/shard_map/ppermute | solution.py:189
  63.6 16.4 %collective-permute-start.4 = (bf16[4,256,256]{2,1,0:T(8,128)(2,1)S(1)}, bf16[4,256,256]{2,1,0:T(8,128)(2,1)S(1)}, u32[]{:S(2)}, u32[]{:S(2)}) collective-permute-start(bf16[4,256,256]{2,1,0:T(8,128)(2,1)S(1)} %pad_maximum_fusion.15), channel_id=1, source_target_pairs={{0,4},{1,5},{4,0},{5,1},{8,12},{9,13},{12,8},{13,9},{16,20},{17,21... | collective-permute-start | bytes 1572872 | tf_op jit(solution)/shard_map/ppermute | solution.py:189
  75.6 44.9 %collective-permute-start.7 = (bf16[8,272,256]{2,1,0:T(8,128)(2,1)S(1)}, bf16[8,272,256]{2,1,0:T(8,128)(2,1)S(1)}, u32[]{:S(2)}, u32[]{:S(2)}) collective-permute-start(bf16[8,272,256]{2,1,0:T(8,128)(2,1)S(1)} %pad_maximum_fusion.7.refs_2_), channel_id=1, source_target_pairs={{0,4},{1,5},{4,0},{5,1},{8,12},{9,13},{12,8},{13,9},{16,20},{17,21... | collective-permute-start | bytes 3342344 | tf_op jit(solution)/shard_map/ppermute | solution.py:189
  80.1 40.5 %collective-permute-start.5 = (bf16[8,256,256]{2,1,0:T(8,128)(2,1)S(1)}, bf16[8,256,256]{2,1,0:T(8,128)(2,1)}, u32[]{:S(2)}, u32[]{:S(2)}) collective-permute-start(bf16[8,256,256]{2,1,0:T(8,128)(2,1)S(1)} %pad_maximum_fusion.9.refs_0_), channel_id=1, source_target_pairs={{0,1},{1,0},{4,5},{5,4},{8,9},{9,8},{12,13},{13,12},{16,17},{17,16... | collective-permute-start | bytes 3145736 | tf_op jit(solution)/shard_map/ppermute | solution.py:189
  81.4 215.9 %all-gather.4.cloned.1.call-start = ((), (), s32[]{:S(2)}) async-start(), calls=%async_computation.3 | async-start | bytes 5013504 | tf_op jit(solution)/shard_map/all_gather | solution.py:524
  84.4 40.4 %copy-start.35 = (f32[2048]{0:T(1024)}, f32[2048]{0:T(1024)S(1)}, u32[]{:S(2)}) copy-start(f32[2048]{0:T(1024)S(1)} %add_rsqrt_fusion.1) | copy-start | bytes 24580
  124.7 11.0 %copy-start.2 = (bf16[1024,1536]{1,0:T(8,128)(2,1)}, bf16[1024,1536]{1,0:T(8,128)(2,1)S(1)}, u32[]{:S(2)}) copy-start(bf16[1024,1536]{1,0:T(8,128)(2,1)S(1)} %get-tuple-element.34) | copy-start | bytes 9437188
  124.7 10.9 %copy-start.27 = (f32[1024]{0:T(1024)}, f32[1024]{0:T(1024)S(1)}, u32[]{:S(2)}) copy-start(f32[1024]{0:T(1024)S(1)} %get-tuple-element.89) | copy-start | bytes 12292
  142.3 4.9 collective-permute-start.8
  164.5 14.0 %collective-permute-start.9 = (bf16[2048,1024]{1,0:T(8,128)(2,1)}, bf16[2048,1024]{1,0:T(8,128)(2,1)}, u32[]{:S(2)}, u32[]{:S(2)}) collective-permute-start(bf16[2048,1024]{1,0:T(8,128)(2,1)} %get-tuple-element.97), channel_id=1, source_target_pairs={{0,2},{2,0},{1,3},{3,1},{4,6},{6,4},{5,7},{7,5},{8,10},{10,8},{9,1... | collective-permute-start | bytes 12582920 | tf_op jit(solution)/shard_map/ppermute | solution.py:184
  164.5 9.9 %collective-permute-start.10 = (bf16[1024,1024]{1,0:T(8,128)(2,1)S(1)}, bf16[1024,1024]{1,0:T(8,128)(2,1)}, u32[]{:S(2)}, u32[]{:S(2)}) collective-permute-start(bf16[1024,1024]{1,0:T(8,128)(2,1)S(1)} %bitcast.122), channel_id=1, source_target_pairs={{0,2},{2,0},{1,3},{3,1},{4,6},{6,4},{5,7},{7,5},{8,10},{10,8},{9,1... | collective-permute-start | bytes 6291464 | tf_op jit(solution)/shard_map/ppermute | solution.py:184
  165.0 430.7 %reduce-scatter.10.cloned.1.call-start = ((), (), s32[]{:S(2)}) async-start(), calls=%async_computation.8 | async-start | bytes 557056
  343.4 7.2 collective-permute-start.13
  343.5 11.4 %slice-start = ((s8[8388608]{0:T(1024)(128)(4,1)}), s8[4194304]{0:T(1024)(128)(4,1)S(1)}, s32[]{:S(2)}) async-start(s8[8388608]{0:T(1024)(128)(4,1)} %bitcast.113), calls=%async_computation.9 | async-start | bytes 8388608
  347.5 75.6 %collective-permute-start.12 = (bf16[1024,1024]{1,0:T(8,128)(2,1)}, bf16[1024,1024]{1,0:T(8,128)(2,1)}, u32[]{:S(2)}, u32[]{:S(2)}) collective-permute-start(bf16[1024,1024]{1,0:T(8,128)(2,1)} %slice.510), channel_id=1, source_target_pairs={{0,2},{2,0},{1,3},{3,1},{4,6},{6,4},{5,7},{7,5},{8,10},{10,8},{9,1... | collective-permute-start | bytes 6291464 | tf_op jit(solution)/shard_map/ppermute | solution.py:184
  364.9 10.2 %copy-start.8 = (f32[2048,512]{1,0:T(8,128)S(1)}, f32[2048,512]{1,0:T(8,128)}, u32[]{:S(2)}) copy-start(f32[2048,512]{1,0:T(8,128)} %copy-done.7) | copy-start | bytes 12582916
  375.1 9.2 %copy-start.17 = (bf16[2048,1024]{1,0:T(8,128)(2,1)}, bf16[2048,1024]{1,0:T(8,128)(2,1)S(1)}, u32[]{:S(2)}) copy-start(bf16[2048,1024]{1,0:T(8,128)(2,1)S(1)} %get-tuple-element.61) | copy-start | bytes 12582916
  386.3 10.3 %collective-permute-start.14 = (bf16[4,2,512]{2,1,0:T(2,128)(2,1)S(1)}, bf16[4,2,512]{2,1,0:T(2,128)(2,1)S(1)}, u32[]{:S(2)}, u32[]{:S(2)}) collective-permute-start(bf16[4,2,512]{2,1,0:T(2,128)(2,1)S(1)} %slice.517), channel_id=1, source_target_pairs={{1,0},{3,2},{5,4},{7,6},{9,8},{11,10},{13,12},{15,14},{17,16},{19,... | collective-permute-start | bytes 24584 | tf_op jit(solution)/shard_map/ppermute | solution.py:19
  415.8 14.7 %collective-permute-start.15 = (bf16[1024,1024]{1,0:T(8,128)(2,1)}, bf16[1024,1024]{1,0:T(8,128)(2,1)S(1)}, u32[]{:S(2)}, u32[]{:S(2)}) collective-permute-start(bf16[1024,1024]{1,0:T(8,128)(2,1)} %slice.509), channel_id=1, source_target_pairs={{0,2},{2,0},{1,3},{3,1},{4,6},{6,4},{5,7},{7,5},{8,10},{10,8},{9,1... | collective-permute-start | bytes 6291464 | tf_op jit(solution)/shard_map/ppermute | solution.py:184
  423.1 10.8 %copy-start.12 = (f32[2048,1024]{1,0:T(8,128)S(1)}, f32[2048,1024]{1,0:T(8,128)}, u32[]{:S(2)}) copy-start(f32[2048,1024]{1,0:T(8,128)} %copy-done.11) | copy-start | bytes 25165828
  423.1 10.8 %copy-start.28 = (f32[1024]{0:T(1024)S(1)}, f32[1024]{0:T(1024)}, u32[]{:S(2)}) copy-start(f32[1024]{0:T(1024)} %copy-done.27) | copy-start | bytes 12292
  437.0 214.2 %reduce-scatter.8.cloned.1.call-start = ((), (), s32[]{:S(2)}) async-start(), calls=%async_computation.7 | async-start | bytes 5013504 | tf_op jit(solution)/shard_map/reduce_scatter | solution.py:576
  437.0 30.1 %copy-start.23 = (bf16[8,192,384]{2,1,0:T(8,128)(2,1)S(1)}, bf16[8,192,384]{2,1,0:T(8,128)(2,1)}, u32[]{:S(2)}) copy-start(bf16[8,192,384]{2,1,0:T(8,128)(2,1)} %get-tuple-element.51) | copy-start | bytes 3538948
  437.6 355.0 %reduce-scatter.6.cloned.1.call-start = ((), (), s32[]{:S(2)}) async-start(), calls=%async_computation.6 | async-start | bytes 5013504 | tf_op jit(solution)/shard_map/reduce_scatter | solution.py:576
  438.0 33.0 %copy-start.14 = (bf16[2048,512]{1,0:T(8,128)(2,1)S(1)}, bf16[2048,512]{1,0:T(8,128)(2,1)}, u32[]{:S(2)}) copy-start(bf16[2048,512]{1,0:T(8,128)(2,1)} %copy-done.13) | copy-start | bytes 6291460
  438.1 32.9 %copy-start.18 = (bf16[2048,1024]{1,0:T(8,128)(2,1)S(1)}, bf16[2048,1024]{1,0:T(8,128)(2,1)}, u32[]{:S(2)}) copy-start(bf16[2048,1024]{1,0:T(8,128)(2,1)} %copy-done.17) | copy-start | bytes 12582916
  438.1 29.0 %collective-permute-start.25 = (bf16[8,192,384]{2,1,0:T(8,128)(2,1)}, bf16[8,192,384]{2,1,0:T(8,128)(2,1)S(1)}, u32[]{:S(2)}, u32[]{:S(2)}) collective-permute-start(bf16[8,192,384]{2,1,0:T(8,128)(2,1)} %get-tuple-element.52), channel_id=1, source_target_pairs={{0,4},{1,5},{4,0},{5,1},{8,12},{9,13},{12,8},{13,9},{16,20},{17,21... | collective-permute-start | bytes 3538952 | tf_op jit(solution)/shard_map/ppermute | solution.py:189
  439.7 49.3 %collective-permute-start.23 = (bf16[8,192,384]{2,1,0:T(8,128)(2,1)}, bf16[8,192,384]{2,1,0:T(8,128)(2,1)S(1)}, u32[]{:S(2)}, u32[]{:S(2)}) collective-permute-start(bf16[8,192,384]{2,1,0:T(8,128)(2,1)} %get-tuple-element.49), channel_id=1, source_target_pairs={{0,1},{1,0},{4,5},{5,4},{8,9},{9,8},{12,13},{13,12},{16,17},{17,16... | collective-permute-start | bytes 3538952 | tf_op jit(solution)/shard_map/ppermute | solution.py:189
  467.5 22.4 %collective-permute-start.26 = (bf16[4,192,384]{2,1,0:T(8,128)(2,1)S(1)}, bf16[4,192,384]{2,1,0:T(8,128)(2,1)S(1)}, u32[]{:S(2)}, u32[]{:S(2)}) collective-permute-start(bf16[4,192,384]{2,1,0:T(8,128)(2,1)S(1)} %slice.511), channel_id=1, source_target_pairs={{0,1},{1,0},{4,5},{5,4},{8,9},{9,8},{12,13},{13,12},{16,17},{17,16... | collective-permute-start | bytes 1769480 | tf_op jit(solution)/shard_map/ppermute | solution.py:189
  487.4 43.1 %collective-permute-start.18 = (bf16[8,256,256]{2,1,0:T(8,128)(2,1)S(1)}, bf16[8,256,256]{2,1,0:T(8,128)(2,1)S(1)}, u32[]{:S(2)}, u32[]{:S(2)}) collective-permute-start(bf16[8,256,256]{2,1,0:T(8,128)(2,1)S(1)} %get-tuple-element.45), channel_id=1, source_target_pairs={{0,4},{1,5},{4,0},{5,1},{8,12},{9,13},{12,8},{13,9},{16,20},{17,21... | collective-permute-start | bytes 3145736 | tf_op jit(solution)/shard_map/ppermute | solution.py:189
  489.3 39.4 %collective-permute-start.24 = (bf16[4,192,384]{2,1,0:T(8,128)(2,1)S(1)}, bf16[4,192,384]{2,1,0:T(8,128)(2,1)S(1)}, u32[]{:S(2)}, u32[]{:S(2)}) collective-permute-start(bf16[4,192,384]{2,1,0:T(8,128)(2,1)S(1)} %slice.512), channel_id=1, source_target_pairs={{0,4},{1,5},{4,0},{5,1},{8,12},{9,13},{12,8},{13,9},{16,20},{17,21... | collective-permute-start | bytes 1769480 | tf_op jit(solution)/shard_map/ppermute | solution.py:189
  489.8 41.3 %collective-permute-start.16 = (bf16[8,256,256]{2,1,0:T(8,128)(2,1)S(1)}, bf16[8,256,256]{2,1,0:T(8,128)(2,1)S(1)}, u32[]{:S(2)}, u32[]{:S(2)}) collective-permute-start(bf16[8,256,256]{2,1,0:T(8,128)(2,1)S(1)} %get-tuple-element.43), channel_id=1, source_target_pairs={{0,1},{1,0},{4,5},{5,4},{8,9},{9,8},{12,13},{13,12},{16,17},{17,16... | collective-permute-start | bytes 3145736 | tf_op jit(solution)/shard_map/ppermute | solution.py:189
  528.9 40.6 %collective-permute-start.27 = (bf16[2,384,384]{2,1,0:T(8,128)(2,1)S(1)}, bf16[2,384,384]{2,1,0:T(8,128)(2,1)S(1)}, u32[]{:S(2)}, u32[]{:S(2)}) collective-permute-start(bf16[2,384,384]{2,1,0:T(8,128)(2,1)S(1)} %fusion.17), channel_id=1, source_target_pairs={{0,16},{1,17},{4,20},{5,21},{8,24},{9,25},{12,28},{13,29},{16,0},{... | collective-permute-start | bytes 1769480 | tf_op jit(solution)/shard_map/ppermute | solution.py:189
  530.8 39.0 %collective-permute-start.19 = (bf16[4,256,256]{2,1,0:T(8,128)(2,1)S(1)}, bf16[4,256,256]{2,1,0:T(8,128)(2,1)S(1)}, u32[]{:S(2)}, u32[]{:S(2)}) collective-permute-start(bf16[4,256,256]{2,1,0:T(8,128)(2,1)S(1)} %slice.513), channel_id=1, source_target_pairs={{0,1},{1,0},{4,5},{5,4},{8,9},{9,8},{12,13},{13,12},{16,17},{17,16... | collective-permute-start | bytes 1572872 | tf_op jit(solution)/shard_map/ppermute | solution.py:189
  531.5 38.4 %collective-permute-start.17 = (bf16[4,256,256]{2,1,0:T(8,128)(2,1)S(1)}, bf16[4,256,256]{2,1,0:T(8,128)(2,1)S(1)}, u32[]{:S(2)}, u32[]{:S(2)}) collective-permute-start(bf16[4,256,256]{2,1,0:T(8,128)(2,1)S(1)} %slice.514), channel_id=1, source_target_pairs={{0,4},{1,5},{4,0},{5,1},{8,12},{9,13},{12,8},{13,9},{16,20},{17,21... | collective-permute-start | bytes 1572872 | tf_op jit(solution)/shard_map/ppermute | solution.py:189
  569.7 12.9 %collective-permute-start.28 = (bf16[1,384,384]{2,1,0:T(8,128)(2,1)S(1)}, bf16[1,384,384]{2,1,0:T(8,128)(2,1)S(1)}, u32[]{:S(2)}, u32[]{:S(2)}) collective-permute-start(bf16[1,384,384]{2,1,0:T(8,128)(2,1)S(1)} %slice.515), channel_id=1, source_target_pairs={{0,8},{1,9},{4,12},{5,13},{8,0},{9,1},{12,4},{13,5},{16,24},{17,25... | collective-permute-start | bytes 884744 | tf_op jit(solution)/shard_map/ppermute | solution.py:189
  570.1 25.4 %collective-permute-start.20 = (bf16[2,512,256]{2,1,0:T(8,128)(2,1)S(1)}, bf16[2,512,256]{2,1,0:T(8,128)(2,1)S(1)}, u32[]{:S(2)}, u32[]{:S(2)}) collective-permute-start(bf16[2,512,256]{2,1,0:T(8,128)(2,1)S(1)} %fusion.20), channel_id=1, source_target_pairs={{0,16},{1,17},{4,20},{5,21},{8,24},{9,25},{12,28},{13,29},{16,0},{... | collective-permute-start | bytes 1572872 | tf_op jit(solution)/shard_map/ppermute | solution.py:189
  595.6 9.9 %collective-permute-start.21 = (bf16[1,512,256]{2,1,0:T(8,128)(2,1)S(1)}, bf16[1,512,256]{2,1,0:T(8,128)(2,1)S(1)}, u32[]{:S(2)}, u32[]{:S(2)}) collective-permute-start(bf16[1,512,256]{2,1,0:T(8,128)(2,1)S(1)} %slice.516), channel_id=1, source_target_pairs={{0,8},{1,9},{4,12},{5,13},{8,0},{9,1},{12,4},{13,5},{16,24},{17,25... | collective-permute-start | bytes 786440 | tf_op jit(solution)/shard_map/ppermute | solution.py:189
  596.6 8.9 %collective-permute-start.30 = (f32[5,64]{1,0:T(8,128)S(1)}, f32[5,64]{1,0:T(8,128)S(1)}, u32[]{:S(2)}, u32[]{:S(2)}) collective-permute-start(f32[5,64]{1,0:T(8,128)S(1)} %copy.83), channel_id=1, source_target_pairs={{0,1},{1,0},{2,3},{3,2},{4,5},{5,4},{6,7},{7,6},{8,9},{9,8},{10,11... | collective-permute-start | bytes 3848 | tf_op jit(solution)/shard_map/ppermute | solution.py:653
  605.9 190.8 %collective-permute-start.22 = (f32[3,64,256]{1,2,0:T(8,128)S(1)}, f32[3,64,256]{1,2,0:T(8,128)}, u32[]{:S(2)}, u32[]{:S(2)}) collective-permute-start(f32[3,64,256]{1,2,0:T(8,128)S(1)} %get-tuple-element.85), channel_id=1, source_target_pairs={{0,2},{2,0},{1,3},{3,1},{4,6},{6,4},{5,7},{7,5},{8,10},{10,8},{9,1... | collective-permute-start | bytes 589832 | tf_op jit(solution)/shard_map/ppermute | solution.py:184
  795.0 7.6 collective-permute-start.29
  (33 other events, 159.3 us)
Sparse Core Ops, SparseCore 0:
  16.1 115.8 all-gather.7
  135.3 79.5 all-gather.5
  218.3 79.0 all-gather.3
  437.1 56.6 reduce-scatter.9
  499.6 151.5 reduce-scatter.7
  656.2 136.3 reduce-scatter.5

commit v2 on v1

--- a/solution.py
+++ b/solution.py
@@ -420,6 +420,145 @@
     )(own, *arrays)
 
 
+def shifted_down(block, before):
+    row = lax.broadcasted_iota(jnp.int32, block.shape, 0)
+    one = jnp.where(row == 0, before[1:2], pltpu.roll(block, 1, 0))
+    two = jnp.where(row == 0, before[0:1], pltpu.roll(block, 2, 0))
+    return one, jnp.where(row == 1, before[1:2], two)
+
+
+def shifted_up(block, behind):
+    count = block.shape[0]
+    row = lax.broadcasted_iota(jnp.int32, block.shape, 0)
+    one = jnp.where(row == count - 1, behind[0:1], pltpu.roll(block, count - 1, 0))
+    two = jnp.where(row == count - 2, behind[0:1], pltpu.roll(block, count - 2, 0))
+    return one, jnp.where(row == count - 1, behind[1:2], two)
+
+
+def in_kernel(x_ref, gain_ref, w_ref, normed_ref, projected_ref):
+    x = x_ref[...].astype(f32)
+    scale = lax.rsqrt(jnp.mean(x * x, axis=-1, keepdims=True) + EPSILON)
+    normed = (x * scale * gain_ref[...]).astype(bf16)
+    normed_ref[...] = normed
+    projected_ref[...] = jnp.dot(normed, w_ref[...], preferred_element_type=f32)
+
+
+def conv_kernel(projected_ref, before_ref, taps_ref, w_ref, mixer_ref, conv_ref, branch_ref):
+    channels = conv_ref.shape[1]
+    product = projected_ref[:, :channels] * projected_ref[:, 2 * channels :]
+    one, two = shifted_down(product, before_ref[0].astype(f32))
+    conv = taps_ref[0:1] * two + taps_ref[1:2] * one + taps_ref[2:3] * product
+    conv_ref[...] = conv
+    mixer = (projected_ref[:, channels : 2 * channels] * conv).astype(bf16)
+    mixer_ref[...] = mixer
+    branch_ref[...] = jnp.dot(mixer, w_ref[...], preferred_element_type=f32).astype(bf16)
+
+
+def norm_kernel(x_ref, branch_ref, got_ref, gain_ref, residual_ref, normed_ref):
+    residual = x_ref[...].astype(f32) + (branch_ref[...].astype(f32) + got_ref[...].astype(f32))
+    residual_ref[...] = residual
+    scale = lax.rsqrt(jnp.mean(residual * residual, axis=-1, keepdims=True) + EPSILON)
+    normed_ref[...] = (residual * scale * gain_ref[...]).astype(bf16)
+
+
+def branch_grad_kernel(
+    own_first, gn_ref, got_ref, residual_ref, go_ref, gain_ref, mixer_ref, conv_ref, gate_c_ref,
+    w_ref, grad_residual_ref, grad_conv_ref, grad_c_ref, grad_w_ref, grad_gain_ref, total_ref,
+):
+    step = pl.program_id(0)
+
+    @pl.when(step == 0)
+    def _():
+        total_ref[...] = jnp.zeros_like(total_ref)
+        grad_gain_ref[...] = jnp.zeros_like(grad_gain_ref)
+
+    incoming = gn_ref[...] + got_ref[...].astype(f32)
+    residual = residual_ref[...]
+    scale = lax.rsqrt(jnp.mean(residual * residual, axis=-1, keepdims=True) + EPSILON)
+    weighted = incoming * gain_ref[...]
+
+    @pl.when(step >= own_first)
+    def _():
+        grad_gain_ref[...] += jnp.sum(incoming * residual * scale, axis=0, keepdims=True)
+
+    inner = jnp.mean(weighted * residual, axis=-1, keepdims=True)
+    grad_residual = go_ref[...].astype(f32) + (
+        scale * weighted - residual * (scale * scale * scale) * inner
+    )
+    grad_residual_ref[...] = grad_residual
+    grad_branch = grad_residual.astype(bf16)
+    grad_mix = lax.dot_general(grad_branch, w_ref[...], NT, preferred_element_type=f32)
+    grad_c_ref[...] = (grad_mix * conv_ref[...]).astype(bf16)
+    grad_conv_ref[...] = grad_mix * gate_c_ref[...]
+    total_ref[...] += lax.dot_general(mixer_ref[...], grad_branch, TN, preferred_element_type=f32)
+
+    @pl.when(step == pl.num_programs(0) - 1)
+    def _():
+        grad_w_ref[...] = total_ref[...].astype(bf16)
+
+
+def in_grad_kernel(
+    geometry, count, own_ref, grad_conv_ref, behind_ref, before_ref, projected_ref, grad_c_ref,
+    normed_ref, taps_ref, grad_out_ref, grad_projected_ref, grad_taps_ref, *refs
+):
+    parts, (total_ref, low_ref, sems) = refs[:count], refs[count:]
+    plan, segments, n_ctx = geometry
+    step = pl.program_id(0)
+
+    @pl.when(step == 0)
+    def _():
+        total_ref[...] = jnp.zeros_like(total_ref)
+        grad_taps_ref[...] = jnp.zeros_like(grad_taps_ref)
+
+    channels = grad_c_ref.shape[1]
+    grad_conv = grad_conv_ref[...]
+    gate_b = projected_ref[:, :channels]
+    values = projected_ref[:, 2 * channels :]
+    product = gate_b * values
+    one, two = shifted_down(product, before_ref[0].astype(f32))
+    for k, shifted in enumerate((two, one, product)):
+        grad_taps_ref[k : k + 1] += jnp.sum(grad_conv * shifted, axis=0, keepdims=True)
+    one, two = shifted_up(grad_conv, behind_ref[0].astype(f32))
+    grad_product = taps_ref[2:3] * grad_conv + taps_ref[1:2] * one + taps_ref[0:1] * two
+    grad_projected_ref[:, :channels] = (grad_product * values).astype(bf16)
+    grad_projected_ref[:, channels : 2 * channels] = grad_c_ref[...]
+    grad_projected_ref[:, 2 * channels :] = (grad_product * gate_b).astype(bf16)
+    total_ref[...] += lax.dot_general(
+        normed_ref[...], grad_projected_ref[...], TN, preferred_element_type=f32
+    )
+
+    @pl.when(step == pl.num_programs(0) - 1)
+    def _():
+        low_ref[...] = total_ref[...].astype(bf16)
+        pairs = slot_pairs(own_ref[0], plan, parts, segments, n_ctx, (low_ref, grad_out_ref))
+        copy_all([(b, a) for a, b in pairs], sems)
+
+
+def row_call(body, steps, ins, outs, scratch=(), flops=0, limit=48):
+    return pl.pallas_call(
+        body,
+        grid=(steps,),
+        in_specs=[
+            pl.BlockSpec(memory_space=pltpu.SMEM) if block is None else pl.BlockSpec(block, place)
+            for _, block, place in ins
+        ],
+        out_specs=[
+            pl.BlockSpec(memory_space=pl.ANY) if block is None else pl.BlockSpec(block, place)
+            for _, _, block, place in outs
+        ],
+        out_shape=[jax.ShapeDtypeStruct(shape, dtype) for shape, dtype, _, _ in outs],
+        scratch_shapes=list(scratch),
+        compiler_params=pltpu.CompilerParams(
+            vmem_limit_bytes=limit * 1024 * 1024, dimension_semantics=("arbitrary",)
+        ),
+        cost_estimate=pl.CostEstimate(
+            flops=flops,
+            bytes_accessed=sum(a.size * a.dtype.itemsize for a, _, _ in ins),
+            transcendentals=0,
+        ),
+    )(*[a for a, _, _ in ins])
+
+
 def fits(tokens, w_in, w_out, w_gate, w_down, n_dp, n_ctx):
     width, hidden = w_gate.shape
     if n_dp % 2 or n_dp % (2 * n_ctx) or n_dp & (n_dp - 1) or n_ctx & (n_ctx - 1) or n_ctx < 2:
@@ -481,7 +620,7 @@
     small_block = in_core_order(small, swapped[in_parts * depth :][:5, :depth], 1)
     small_block = jnp.pad(small_block, ((0, 11), (0, 256 - 2 * depth)))
     out_block = w_out.reshape(depth, out_parts, 256).transpose(1, 0, 2).reshape(-1, 256)
-    mix_block = jnp.concatenate([in_block, out_block, small_block], axis=0)
+    mix_block = jnp.concatenate([in_block, small_block], axis=0)
 
     both = jnp.stack([w_gate, w_up]).reshape(2, depth, groups, 2, CHUNKS, sub)
     both = both.transpose(3, 4, 0, 1, 2, 5).reshape(2, CHUNKS, 2, depth, lanes)
@@ -495,16 +634,16 @@
     )
 
     mix_rows = mix_block.shape[0]
-    mix_cut = 256
+    mix_cut = in_parts * depth
     in_rows = in_parts * 2 * depth
     mix_segments = [
         (k * 2 * depth, 2 * depth, 0, 256, 0, 2 * depth, 0, in_cols, 256 * k)
         for k in range(in_parts)
     ]
-    mix_segments += [
+    out_segments = [
         (in_rows + k * depth, depth, 0, 256, 1, depth, 0, wide, 256 * k) for k in range(out_parts)
     ]
-    small_segment = (in_rows + out_parts * depth, 16, 0, 256, 2, 16, 0, 256, 0)
+    small_segment = (in_rows, 16, 0, 256, 1, 16, 0, 256, 0)
     mix_plan = gather_plan(mix_cut, mix_rows)
     chunk_rows = chunk_blocks.shape[1]
     chunk_cut = chunk_rows // 2
@@ -520,16 +659,68 @@
     whole_geometry = (whole_plan, chunk_segments, n_ctx)
     step_geometry = (gather_plan(chunk_cut, chunk_rows), chunk_segments, n_ctx)
 
-    mix_parts = gather(mix_block, mix_cut)
-    chunk_weights = [[lax.all_gather(chunk_blocks[q], ("chip", "ctx"))] for q in range(CHUNKS)]
-    in_half, out_half, small_all = move(
+    first_block = jnp.concatenate(
+        [chunk_blocks[0], jnp.pad(out_block, ((0, 0), (0, lanes - 256)))], axis=0
+    )
+    first_all = lax.all_gather(first_block, ("chip", "ctx"))
+    last_all = lax.all_gather(chunk_blocks[2], ("chip", "ctx"))
+
+    far, first_order, second_order = bit_masks()
+
+    def doubled(hold, got):
+        return jnp.concatenate([hold, got], axis=0)
+
+    hold = mix_block[None]
+    for mask in far:
+        hold = doubled(hold, across(hold, mask))
+    mix_halves = [hold[:, :mix_cut], hold[:, mix_cut:]]
+    next_hold = after(chunk_blocks[1][None], hold)
+    far_left = list(far)
+    mix_parts = []
+    for step in range(len(first_order)):
+        got = [across(h, order[step]) for h, order in zip(mix_halves, (first_order, second_order))]
+        if far_left:
+            next_got = across(next_hold, far_left.pop(0))
+            next_hold = doubled(next_hold, next_got)
+            if step + 1 < len(first_order):
+                got = [after(g, next_got) for g in got]
+        if step + 1 < len(first_order):
+            mix_halves = [doubled(h, g) for h, g in zip(mix_halves, got)]
+            next_hold = after(next_hold, *got)
+        else:
+            mix_parts = [mix_halves[0], got[0], mix_halves[1], got[1]]
+    for mask in far_left:
+        next_hold = doubled(next_hold, across(next_hold, mask))
+    in_half, small_all = move(
         own,
         mix_parts,
-        [(width, n_ctx * in_cols), (channels, width), (n_chip * 16, n_ctx * 256)],
+        [(width, n_ctx * in_cols), (n_chip * 16, n_ctx * 256)],
         (mix_plan, mix_segments + [small_segment], n_ctx),
         4,
         False,
     )
+    (out_half,) = move(
+        own,
+        [first_all],
+        [(channels, width)],
+        (
+            [(0, i, None, 0, chunk_rows + out_parts * depth) for i in range(slots)],
+            [
+                (chunk_rows + k * depth, depth, 0, 256, 0, depth, 0, wide, 256 * k)
+                for k in range(out_parts)
+            ],
+            n_ctx,
+        ),
+        1,
+        False,
+    )
+    next_halves = [next_hold[:, :chunk_cut], next_hold[:, chunk_cut:]]
+    next_orders = (first_order, second_order)
+
+    def next_step(step, *done):
+        got = [across(after(h, *done), o[step]) for h, o in zip(next_halves, next_orders)]
+        return got
+
     small_all = small_all.reshape(n_chip, 16, n_ctx * 256)[:, :5, : 2 * depth].astype(f32)
     first_gain = small_all[:, 0].reshape(width)
     second_gain = small_all[:, 1].reshape(width)
@@ -538,91 +729,178 @@
     taps = taps.reshape(3, channels)
 
     token_rows = tokens.reshape(rows, width)
-    inputs = jnp.concatenate([token_rows, swap(token_rows)], axis=0).astype(f32)
+    inputs = jnp.concatenate([token_rows, swap(token_rows)], axis=0)
     go_rows = cotangent.reshape(rows, width)
     go = jnp.concatenate([go_rows, swap(go_rows)], axis=0)
-    normed, scale_mix = norm_forward(inputs, first_gain)
-    normed_low = normed.astype(bf16)
-    projected = jnp.dot(normed_low, in_half, preferred_element_type=f32)
-    gate_b = projected[:, :channels]
-    gate_c = projected[:, channels : 2 * channels]
-    values = projected[:, 2 * channels :]
-    product = (gate_b * values).reshape(2 * seqs, piece, channels)
-    previous = passed_along(product[:, piece - 2 :].astype(bf16), "ctx", 1).astype(f32)
-    padded = jnp.concatenate([previous, product], axis=1)
-    convolved = taps[0] * padded[:, :-2] + taps[1] * padded[:, 1:-1] + taps[2] * padded[:, 2:]
-    convolved = convolved.reshape(2 * rows, channels)
-    mixer_out = (gate_c * convolved).astype(bf16)
-    branch = jnp.dot(mixer_out, out_half, preferred_element_type=f32)
-
-    def swap_rows(block):
-        got = swap(block.astype(bf16)).astype(f32)
-        return jnp.concatenate([got[rows:], got[:rows]], axis=0)
-
-    residual = inputs + (branch + swap_rows(branch))
-    feedforward_normed, scale_ffn = norm_forward(residual, second_gain)
-    nffn_low = feedforward_normed.astype(bf16)
-
-    totals = None
-    chunk_parts = []
-    for q in range(CHUNKS):
-        steps = q == CHUNKS - 1
-        totals, parts = ffn_chunk(
-            own, nffn_low, go, chunk_weights[q], totals, whole_geometry,
-            step_geometry if steps else whole_geometry, hidden_count,
-        )
-        chunk_parts.append(parts)
-    chunk_grads = [
-        lax.psum_scatter(parts[0], ("chip", "ctx"), scatter_dimension=0).astype(f32)
-        for parts in chunk_parts[:-1]
-    ]
+    blocks = 2 * seqs
+
+    def at(i):
+        return (i, 0)
+
+    def still(i):
+        return (0, 0)
+
+    def other(i):
+        return ((i + seqs) % blocks, 0)
+
+    wide_rows, thin_rows = (piece, width), (piece, channels)
+    taps = jnp.pad(taps, ((0, 5), (0, 0)))
+    next_got = next_step(0, in_half)
+    normed_low, projected = row_call(
+        in_kernel,
+        blocks,
+        [
+            (inputs, wide_rows, at),
+            (first_gain[None], (1, width), still),
+            (in_half, in_half.shape, still),
+        ],
+        [
+            ((2 * rows, width), bf16, wide_rows, at),
+            ((2 * rows, 3 * channels), f32, (piece, 3 * channels), at),
+        ],
+        flops=12 * rows * width * channels,
+    )
+    tail = projected.reshape(blocks, piece, 3 * channels)[:, piece - 2 :]
+    tail = (tail[:, :, :channels] * tail[:, :, 2 * channels :]).astype(bf16)
+    before = passed_along(tail, "ctx", 1)
+    halo = (1, 2, channels)
+
+    def halo_at(i):
+        return (i, 0, 0)
+
+    mixer_out, convolved, branch = row_call(
+        conv_kernel,
+        blocks,
+        [
+            (projected, (piece, 3 * channels), at),
+            (before, halo, halo_at),
+            (taps, taps.shape, still),
+            (out_half, out_half.shape, still),
+        ],
+        [
+            ((2 * rows, channels), bf16, thin_rows, at),
+            ((2 * rows, channels), f32, thin_rows, at),
+            ((2 * rows, width), bf16, wide_rows, at),
+        ],
+        flops=4 * rows * width * channels,
+    )
+    branch = after(branch, *next_got)
+    for step in range(1, len(first_order)):
+        next_halves = [doubled(h, g) for h, g in zip(next_halves, next_got)]
+        next_got = next_step(step, branch)
+    next_parts = [next_halves[0], next_got[0], next_halves[1], next_got[1]]
+    residual, nffn_low = row_call(
+        norm_kernel,
+        blocks,
+        [
+            (inputs, wide_rows, at),
+            (branch, wide_rows, at),
+            (swap(branch), wide_rows, other),
+            (second_gain[None], (1, width), still),
+        ],
+        [((2 * rows, width), f32, wide_rows, at), ((2 * rows, width), bf16, wide_rows, at)],
+    )
+
+    totals, first_grads = ffn_chunk(
+        own, nffn_low, go, [first_all], None, whole_geometry, step_geometry, hidden_count
+    )
+    first_total = totals[1]
+    totals, next_grads = ffn_chunk(
+        own, nffn_low, go, next_parts, totals, step_geometry, step_geometry, hidden_count
+    )
+    next_total = totals[1]
+    totals, last_grads = ffn_chunk(
+        own, nffn_low, go, [last_all], totals, whole_geometry, step_geometry, hidden_count
+    )
     ffn_out, grad_nffn = totals
-    grad_nffn = grad_nffn + swap_rows(grad_nffn)
-    result = residual[:rows] + (ffn_out[:rows] + swap(ffn_out[rows:].astype(bf16)).astype(f32))
+    grad_got = swap(grad_nffn.astype(bf16))
+    ffn_got = swap(ffn_out[rows:].astype(bf16))
+
+    def turned(i):
+        return ((i + seqs) % blocks, 0)
+
+    def turned_back(i):
+        return (i, 0)
+
+    def own_place(i):
+        return (jnp.maximum(i - seqs, 0), 0)
+
+    def gate_c_place(i):
+        return ((i + seqs) % blocks, 1)
+
+    grad_residual, grad_conv, grad_c, grad_w_out, grad_gain_ffn = row_call(
+        functools.partial(branch_grad_kernel, seqs),
+        blocks,
+        [
+            (grad_nffn, wide_rows, turned),
+            (grad_got, wide_rows, turned_back),
+            (residual, wide_rows, turned),
+            (go, wide_rows, turned),
+            (second_gain[None], (1, width), still),
+            (mixer_out, thin_rows, turned),
+            (convolved, thin_rows, turned),
+            (projected, thin_rows, gate_c_place),
+            (out_half, out_half.shape, still),
+        ],
+        [
+            ((rows, width), f32, wide_rows, own_place),
+            ((2 * rows, channels), f32, thin_rows, turned),
+            ((2 * rows, channels), bf16, thin_rows, turned),
+            ((channels, width), bf16, (channels, width), still),
+            ((1, width), f32, (1, width), still),
+        ],
+        scratch=[pltpu.VMEM((channels, width), f32)],
+        flops=8 * rows * width * channels,
+    )
+    grad_gain_ffn = grad_gain_ffn[0]
+    head = grad_conv.reshape(blocks, piece, channels)[:, :2].astype(bf16)
+    behind = passed_along(head, "ctx", -1)
+    sum_rows = in_rows + out_parts * depth
+    sum_cut = sum_rows // 2
+    sum_plan = gather_plan(sum_cut, sum_rows)
+    sum_segments = mix_segments + out_segments
+    grad_projected, grad_kernel, *mix_grad_parts = row_call(
+        functools.partial(in_grad_kernel, (sum_plan, sum_segments, n_ctx), 4),
+        blocks,
+        [
+            (own, None, None),
+            (grad_conv, thin_rows, at),
+            (behind, halo, halo_at),
+            (before, halo, halo_at),
+            (projected, (piece, 3 * channels), at),
+            (grad_c, thin_rows, at),
+            (normed_low, wide_rows, at),
+            (taps, taps.shape, still),
+            (grad_w_out, grad_w_out.shape, still),
+        ],
+        [
+            ((2 * rows, 3 * channels), bf16, (piece, 3 * channels), at),
+            ((8, channels), f32, (8, channels), still),
+        ]
+        + [(shape, bf16, None, None) for shape in part_shapes(sum_plan, 256)],
+        scratch=[
+            pltpu.VMEM((width, 3 * channels), f32),
+            pltpu.VMEM((width, 3 * channels), bf16),
+            pltpu.SemaphoreType.DMA((len(sum_plan) * len(sum_segments),)),
+        ],
+        flops=12 * rows * width * channels,
+    )
+    grad_kernel = grad_kernel[:3]
+    first_sum = scatter_sum(first_grads, (None, next_total, grad_got, grad_c))
+    next_sum = scatter_sum(next_grads, (None, grad_got, grad_c, grad_projected))
+    last_sum = scatter_sum(last_grads, (None, grad_c, grad_projected, grad_projected))
+    mix_sum = scatter_sum(mix_grad_parts)
+    late_projected = after(grad_projected, mix_grad_parts[1])
+    grad_normed = cross_cols(late_projected[rows:], in_half).astype(bf16)
+    grad_normed = cross_cols(late_projected[:rows], in_half) + swap(grad_normed).astype(f32)
+    result = residual[:rows] + (ffn_out[:rows] + ffn_got.astype(f32))
     result = result.astype(bf16).reshape(seqs, piece, width)
-
-    weighted = grad_nffn * second_gain
-    grad_gain_ffn = jnp.sum((grad_nffn * residual * scale_ffn)[:rows], axis=0)
-    inner = jnp.mean(weighted * residual, axis=-1, keepdims=True)
-    grad_residual = go.astype(f32) + (
-        scale_ffn * weighted - residual * (scale_ffn * scale_ffn * scale_ffn) * inner
-    )
-    grad_branch = grad_residual.astype(bf16)
-    grad_w_out = cross_rows(mixer_out, grad_branch).astype(bf16)
-    grad_mix = cross_cols(grad_branch, out_half)
-    grad_c = grad_mix * convolved
-    grad_conv = (grad_mix * gate_c).reshape(2 * seqs, piece, channels)
-    following = passed_along(grad_conv[:, :2].astype(bf16), "ctx", -1).astype(f32)
-    extended = jnp.concatenate([grad_conv, following], axis=1)
-    grad_product = (
-        taps[2] * extended[:, :-2] + taps[1] * extended[:, 1:-1] + taps[0] * extended[:, 2:]
-    )
-    grad_kernel = jnp.stack(
-        [jnp.sum(grad_conv * padded[:, k : k + piece], axis=(0, 1)) for k in range(3)], axis=0
-    )
-    grad_product = grad_product.reshape(2 * rows, channels)
-    grad_projected = jnp.concatenate(
-        [grad_product * values, grad_c, grad_product * gate_b], axis=1
-    ).astype(bf16)
-    last_sum = scatter_sum(chunk_parts[-1], (None, grad_branch, grad_conv, grad_projected))
-    grad_w_in = cross_rows(normed_low, grad_projected).astype(bf16)
-    mix_grad_parts = move(
-        own,
-        [grad_w_in, grad_w_out],
-        [(slots // 2, mix_cut, 256)] * 2 + [(slots // 2, in_rows + out_parts * depth - mix_cut, 256)] * 2,
-        (gather_plan(mix_cut, in_rows + out_parts * depth), mix_segments, n_ctx),
-        4,
-        True,
-    )
-    mix_sum = scatter_sum(mix_grad_parts)
-    grad_normed = cross_cols(grad_projected, in_half)
-    grad_normed = grad_normed[:rows] + swap(grad_normed[rows:].astype(bf16)).astype(f32)
-    grad_in_norm, grad_gain_mix = norm_backward(
-        inputs[:rows], scale_mix[:rows], first_gain, grad_normed
-    )
-    grad_tokens = (grad_residual[:rows] + grad_in_norm).reshape(seqs, piece, width)
-
-    chunk_sum = jnp.stack(chunk_grads + [last_sum])
+    own_inputs = token_rows.astype(f32)
+    scale_mix = lax.rsqrt(jnp.mean(own_inputs * own_inputs, axis=-1, keepdims=True) + EPSILON)
+    grad_in_norm, grad_gain_mix = norm_backward(own_inputs, scale_mix, first_gain, grad_normed)
+    grad_tokens = (grad_residual + grad_in_norm).reshape(seqs, piece, width)
+
+    chunk_sum = jnp.stack([first_sum, next_sum, last_sum])
     both_sum = chunk_sum[:, : 4 * depth].reshape(CHUNKS, 2, 2, depth, lanes).transpose(2, 0, 1, 3, 4)
     both_mine, both_other = mine_other(both_sum)
     both_got = swap(both_other)
@@ -647,10 +925,16 @@
         jnp.arange(2).reshape(1, 1, 2, 1) == core, grad_taps, jnp.zeros_like(grad_taps)
     ).reshape(3, width)
     small_grad = jnp.concatenate([grad_gain_mix[None], grad_gain_ffn[None], grad_taps], axis=0)
-    small_sum = lax.psum_scatter(small_grad, ("chip", "core"), scatter_dimension=1, tiled=True)
+    small_sum = small_grad.reshape(5, n_chip, 2 * depth).transpose(1, 0, 2)
     for bit in range(n_ctx.bit_length() - 1):
-        route = [(i, i ^ (1 << bit)) for i in range(n_ctx)]
-        small_sum = small_sum + lax.ppermute(small_sum, "ctx", route)
+        small_sum = small_sum + across(small_sum, 1 << bit)
+    for bit in range(n_chip.bit_length() - 1):
+        mask = n_chip >> (bit + 1)
+        low, high = small_sum[: small_sum.shape[0] // 2], small_sum[small_sum.shape[0] // 2 :]
+        upper = jnp.bitwise_and(lax.axis_index("chip"), mask) != 0
+        small_sum = jnp.where(upper, high, low) + across(jnp.where(upper, low, high), mask * n_ctx)
+    small_mine, small_other = mine_other(small_sum[0].reshape(5, 2, depth).transpose(1, 0, 2))
+    small_sum = small_mine + swap(small_other)
     return (
         result,
         grad_tokens,

time: 822 us -> 617 us (0.75)
  waiting for transfers between devices: 428 us -> 218 us
  Pallas kernels: 130 us -> 193 us
  other arithmetic: 102 us -> 59.3 us
  matrix products: 47.5 us -> 15.8 us
  starting transfers between devices: 37 us -> 52.6 us
    reduce_scatter x2 -> x0, waiting for transfers between devices: 186 us -> none  [fast_shards(): lax.psum_scatter(parts[0], ('chip', 'ctx'), scatter_dimension=0).astype(f32)]
    pallas_call x0 -> x5, Pallas kernels: none -> 64.7 us  [row_call(): pl.pallas_call(body, grid=(steps,), in_specs=[pl.BlockSpec(memory_space=p...]
    dot_general x4 -> x0, matrix products: 31.6 us -> none  [the longest x2 13.6 us: cross_rows(): lax.dot_general(left_operand, right_operand, (((0,), (0,)), ((), ())), pr...]
    reduce_sum x5 -> x1, other arithmetic: 29 us -> 2.07 us  [fast_shards(): jnp.mean(own_inputs * own_inputs, axis=-1, keepdims=True) + EPSILON]
    convert_element_type x9 -> x3, other arithmetic: 30 us -> 12.4 us  [the longest x1 6.06 us: fast_shards(): grad_got = swap(grad_nffn.astype(bf16))]
    ppermute x18 -> x40, starting transfers between devices: 28.1 us -> 44.8 us  [across(): lax.ppermute(block, ('chip', 'ctx'), [(i, i ^ mask) for i in range(count)])]
    all_gather x3 -> x2, waiting for transfers between devices: 18.8 us -> 8.4 us  [the longest x1 8.4 us: fast_shards(): first_all = lax.all_gather(first_block, ('chip', 'ctx'))]
    ppermute x18 -> x40, waiting for transfers between devices: 209 us -> 199 us  [across(): lax.ppermute(block, ('chip', 'ctx'), [(i, i ^ mask) for i in range(count)])]
  transfers between devices with their start and end apart: 37 -> 55, of which waited for: 18 -> 24; matrix products, arithmetic and copies ran while one was open for 20% -> 16% of each run, Pallas kernels for 11% -> 25%
where the time goes in v2:
time: 617 us; the launch traced here: 608 us
  waiting for transfers between devices  218 us (35%)
  Pallas kernels  193 us (31%)
  other arithmetic  59.3 us (10%)
  local copies, waits for them, and re-layouts  52.9 us (9%)
  starting transfers between devices  52.6 us (9%)
  matrix products  15.8 us (3%)
  between operations  15.8 us (3%)
    ppermute x40, waiting for transfers between devices, across(): lax.ppermute(block, ('chip', 'ctx'), [(i, i ^ mask) for i in range(count)])  199 us
    pallas_call x3, Pallas kernels, ffn_chunk(): pl.pallas_call(functools.partial(ffn_kernel, geometry, out_geometry, firs...  126 us
    pallas_call x5, Pallas kernels, row_call(): pl.pallas_call(body, grid=(steps,), in_specs=[pl.BlockSpec(memory_space=p...  64.7 us
    ppermute x40, starting transfers between devices, across(): lax.ppermute(block, ('chip', 'ctx'), [(i, i ^ mask) for i in range(count)])  44.8 us
    dot_general x2, matrix products, cross_cols(): lax.dot_general(left_operand, right_operand, (((1,), (1,)), ((), ())), pr...  15.8 us
    unnamed x115, local copies, waits for them, and re-layouts  15.2 us
  transfers between devices with their start and end apart: 55, of which 24 were waited for; matrix products, arithmetic and copies ran while one was open for 16% of the time, Pallas kernels for 25%

profile of v2, /device:TPU:0, one launch (start us, length us, event | category | flops | bytes accessed | tf_op | source)
XLA Modules:
  0.0 607.6 jit_solution(16616763947211638950)
XLA Ops:
  19.7 3.0 collective-permute-start.2
  22.7 5.4 collective-permute-done.2
  28.1 2.8 collective-permute-start.3
  30.9 26.4 %collective-permute-done.3 = bf16[2,400,256]{2,1,0:T(8,128)(2,1)S(1)} collective-permute-done((bf16[2,400,256]{2,1,0:T(8,128)(2,1)S(1)}, bf16[2,400,256]{2,1,0:T(8,128)(2,1)S(1)}, u32[]{:S(2)}, u32[]{:S(2)}) %collective-permute-start.3) | collective-permute-done | bytes 409632 | tf_op jit(solution)/shard_map/ppermute | solution.py:189
  60.5 16.3 %collective-permute-done.6 = bf16[1,384,384]{2,1,0:T(8,128)(2,1)S(1)} collective-permute-done((bf16[1,384,384]{2,1,0:T(8,128)(2,1)S(1)}, bf16[1,384,384]{2,1,0:T(8,128)(2,1)S(1)}, u32[]{:S(2)}, u32[]{:S(2)}) %collective-permute-start.6) | collective-permute-done | bytes 294944 | tf_op jit(solution)/shard_map/ppermute | solution.py:189
  78.4 2.9 collective-permute-start.11
  84.8 35.2 %collective-permute-done.11 = bf16[2,384,384]{2,1,0:T(8,128)(2,1)} collective-permute-done((bf16[2,384,384]{2,1,0:T(8,128)(2,1)}, bf16[2,384,384]{2,1,0:T(8,128)(2,1)}, u32[]{:S(2)}, u32[]{:S(2)}) %collective-permute-start.11) | collective-permute-done | bytes 589856 | tf_op jit(solution)/shard_map/ppermute | solution.py:189
  122.3 2.2 shard_map.177
  127.0 4.8 pad_maximum_fusion.x_ref
  131.8 11.1 %shard_map.178 = (bf16[2048,1024]{1,0:T(8,128)(2,1)}, f32[2048,1536]{1,0:T(8,128)}) custom-call(bf16[2048,1024]{1,0:T(8,128)(2,1)} %pad_maximum_fusion.x_ref, f32[1,1024]{1,0:T(1,128)S(1)} %bitcast.111, bf16[1024,1536]{1,0:T(8,128)(2,1)S(1)} %copy-done.5), custom_call_target="tpu_custom_call" | custom-call | flops 6442450944 | bytes 7344128 | tf_op jit(solution)/shard_map/pallas_call | solution.py:538
  143.8 4.1 collective-permute-start.10
  148.0 8.4 %all-gather.6.cloned.1.call-done = bf16[8192,384]{1,0:T(8,128)(2,1)} async-done(((bf16[512,384]{1,0:T(8,128)(2,1)}), bf16[8192,384]{1,0:T(8,128)(2,1)}) %all-gather.6.cloned.1.call-update) | async-done | bytes 6291472 | tf_op jit(solution)/shard_map/all_gather | solution.py:665
  156.4 2.8 copy-done
  159.8 8.8 %shard_map.180 = (bf16[2048,512]{1,0:T(8,128)(2,1)S(1)}, f32[2048,512]{1,0:T(8,128)}, bf16[2048,1024]{1,0:T(8,128)(2,1)}) custom-call(f32[2048,1536]{1,0:T(8,128)} %get-tuple-element.75.projected_ref.gate_c_ref, bf16[4,2,512]{2,1,0:T(2,128)(2,1)S(1)} %collective-permute-done.10.before_ref, f32[8,512]{1,0:T(8,128)S(1)} %pad.18.taps_ref, ...), custom_call_target="tpu_custom_call" | custom-call | flops 2147483648 | bytes 13656064 | tf_op jit(solution)/shard_map/pallas_call | solution.py:538
  170.5 9.2 %collective-permute-done.15 = bf16[1024,1024]{1,0:T(8,128)(2,1)S(1)} collective-permute-done((bf16[1024,1024]{1,0:T(8,128)(2,1)S(1)}, bf16[1024,1024]{1,0:T(8,128)(2,1)S(1)}, u32[]{:S(2)}, u32[]{:S(2)}) %collective-permute-start.15) | collective-permute-done | bytes 2097184 | tf_op jit(solution)/shard_map/ppermute | solution.py:184
  179.7 2.4 pad_maximum_fusion.1.go_ref
  185.0 5.3 collective-permute-start.16
  190.4 8.5 %shard_map.181 = (f32[2048,1024]{1,0:T(8,128)}, bf16[2048,1024]{1,0:T(8,128)(2,1)S(1)}) custom-call(bf16[2048,1024]{1,0:T(8,128)(2,1)} %pad_maximum_fusion.x_ref, bf16[2048,1024]{1,0:T(8,128)(2,1)} %get-tuple-element.80.branch_ref, bf16[2048,1024]{1,0:T(8,128)(2,1)} %collective-permute-done.14.got_ref, f32[1,1024]{1,0:T(1,128)S(1)} %bitcast.107), custom_call_target="tpu_custom_call" | custom-call | bytes 12587008 | tf_op jit(solution)/shard_map/pallas_call | solution.py:538
  198.9 2.0 copy-done.3
  200.9 41.2 %shard_map.182 = (f32[2048,1024]{1,0:T(8,128)}, f32[2048,1024]{1,0:T(8,128)}, bf16[8,192,384]{2,1,0:T(8,128)(2,1)}, bf16[8,192,384]{2,1,0:T(8,128)(2,1)}, bf16[8...) custom-call(s32[1]{0:T(128)} %bitcast.1.own_ref, bf16[2048,1024]{1,0:T(8,128)(2,1)} %copy-done.3, ...), custom_call_target="tpu_custom_call" | custom-call | flops 28991029248 | bytes 41943040 | tf_op jit(solution)/shard_map/pallas_call | solution.py:360
  245.8 42.5 %shard_map.183 = (f32[2048,1024]{1,0:T(8,128)}, f32[2048,1024]{1,0:T(8,128)}, bf16[8,192,384]{2,1,0:T(8,128)(2,1)}, bf16[8,192,384]{2,1,0:T(8,128)(2,1)}, bf16[8...) custom-call(s32[1]{0:T(128)} %bitcast.1.own_ref, ...), custom_call_target="tpu_custom_call", output_to_operand_aliasing={{0}: (7, {}), {1}: (8, {})} | custom-call | flops 28991029248 | bytes 41943040 | tf_op jit(solution)/shard_map/pallas_call | solution.py:360
  292.1 42.2 %shard_map.184 = (f32[2048,1024]{1,0:T(8,128)}, f32[2048,1024]{1,0:T(8,128)}, bf16[8,192,384]{2,1,0:T(8,128)(2,1)}, bf16[8,192,384]{2,1,0:T(8,128)(2,1)}, bf16[8...) custom-call(s32[1]{0:T(128)} %bitcast.1.own_ref, ...), custom_call_target="tpu_custom_call", output_to_operand_aliasing={{0}: (4, {}), {1}: (5, {})} | custom-call | flops 28991029248 | bytes 41943040 | tf_op jit(solution)/shard_map/pallas_call | solution.py:360
  334.3 6.1 convert_element_type.153
  342.3 2.1 multiply_reduce_fusion
  344.4 2.0 collective-permute-start.30
  346.8 22.7 %collective-permute-done.35 = bf16[8,192,384]{2,1,0:T(8,128)(2,1)} collective-permute-done((bf16[8,192,384]{2,1,0:T(8,128)(2,1)}, bf16[8,192,384]{2,1,0:T(8,128)(2,1)}, u32[]{:S(2)}, u32[]{:S(2)}) %collective-permute-start.35) | collective-permute-done | bytes 1179680 | tf_op jit(solution)/shard_map/ppermute | solution.py:189
  373.3 4.7 slice.556
  378.0 6.0 collective-permute-done.30
  389.9 17.2 %collective-permute-done.41 = bf16[8,192,384]{2,1,0:T(8,128)(2,1)S(1)} collective-permute-done((bf16[8,192,384]{2,1,0:T(8,128)(2,1)}, bf16[8,192,384]{2,1,0:T(8,128)(2,1)S(1)}, u32[]{:S(2)}, u32[]{:S(2)}) %collective-permute-start.41) | collective-permute-done | bytes 1179680 | tf_op jit(solution)/shard_map/ppermute | solution.py:189
  410.7 19.0 %shard_map.185 = (f32[1024,1024]{1,0:T(8,128)}, f32[2048,512]{1,0:T(8,128)}, bf16[2048,512]{1,0:T(8,128)(2,1)S(1)}, bf16[512,1024]{1,0:T(8,128)(2,1)S(1)}, f32[1,1024]{1,0:T(1,128)S(1)}) custom-call(f32[2048,1024]{1,0:T(8,128)} %get-tuple-element.90.gn_ref, bf16[2048,1024]{1,0:T(8,128)(2,1)} %collective-permute-done.19.got_ref, ...), custom_call_target="tpu_custom_call" | custom-call | flops 4294967296 | bytes 45092864 | tf_op jit(solution)/shard_map/pallas_call | solution.py:538
  429.7 3.2 convert.56
  434.3 5.5 add_convert_fusion
  442.0 2.6 collective-permute-start.38
  446.4 17.3 %shard_map.186 = (bf16[2048,1536]{1,0:T(8,128)(2,1)}, f32[8,512]{1,0:T(8,128)S(1)}, bf16[8,256,256]{2,1,0:T(8,128)(2,1)S(1)}, bf16[8,256,256]{2,1,0:T(8,128)(2,1...) custom-call(s32[1]{0:T(128)} %bitcast.1.own_ref, f32[2048,512]{1,0:T(8,128)} %get-tuple-element.94.grad_conv_ref, ...), custom_call_target="tpu_custom_call" | custom-call | flops 6442450944 | bytes 24150020 | tf_op jit(solution)/shard_map/pallas_call | solution.py:538
  463.8 7.0 %fusion.12 = bf16[1024,1024]{1,0:T(8,128)(2,1)} fusion(bf16[1024,1536]{1,0:T(8,128)(2,1)S(1)} %copy-done.6, bf16[2048,1536]{1,0:T(8,128)(2,1)} %get-tuple-element.100), kind=kOutput, calls=%fused_computation.35 | convolution fusion | flops 3222274048 | bytes 8388608 | tf_op jit(solution)/shard_map/dot_general | solution.py:29
  470.9 2.0 collective-permute-start.22
  483.0 7.4 %collective-permute-done.34 = bf16[1,384,384]{2,1,0:T(8,128)(2,1)S(1)} collective-permute-done((bf16[1,384,384]{2,1,0:T(8,128)(2,1)S(1)}, bf16[1,384,384]{2,1,0:T(8,128)(2,1)S(1)}, u32[]{:S(2)}, u32[]{:S(2)}) %collective-permute-start.34) | collective-permute-done | bytes 294944 | tf_op jit(solution)/shard_map/ppermute | solution.py:189
  490.5 7.0 %collective-permute-done.24 = bf16[8,256,256]{2,1,0:T(8,128)(2,1)S(1)} collective-permute-done((bf16[8,256,256]{2,1,0:T(8,128)(2,1)S(1)}, bf16[8,256,256]{2,1,0:T(8,128)(2,1)S(1)}, u32[]{:S(2)}, u32[]{:S(2)}) %collective-permute-start.24) | collective-permute-done | bytes 1048608 | tf_op jit(solution)/shard_map/ppermute | solution.py:189
  499.1 24.1 %collective-permute-done.39 = bf16[2,384,384]{2,1,0:T(8,128)(2,1)S(1)} collective-permute-done((bf16[2,384,384]{2,1,0:T(8,128)(2,1)S(1)}, bf16[2,384,384]{2,1,0:T(8,128)(2,1)S(1)}, u32[]{:S(2)}, u32[]{:S(2)}) %collective-permute-start.39) | collective-permute-done | bytes 589856 | tf_op jit(solution)/shard_map/ppermute | solution.py:189
  523.4 12.1 %collective-permute-done.45 = bf16[2,384,384]{2,1,0:T(8,128)(2,1)S(1)} collective-permute-done((bf16[2,384,384]{2,1,0:T(8,128)(2,1)S(1)}, bf16[2,384,384]{2,1,0:T(8,128)(2,1)S(1)}, u32[]{:S(2)}, u32[]{:S(2)}) %collective-permute-start.45) | collective-permute-done | bytes 589856 | tf_op jit(solution)/shard_map/ppermute | solution.py:189
  538.5 3.3 collective-permute-done.40
  541.9 6.2 %collective-permute-done.46 = bf16[1,384,384]{2,1,0:T(8,128)(2,1)S(1)} collective-permute-done((bf16[1,384,384]{2,1,0:T(8,128)(2,1)S(1)}, bf16[1,384,384]{2,1,0:T(8,128)(2,1)S(1)}, u32[]{:S(2)}, u32[]{:S(2)}) %collective-permute-start.46) | collective-permute-done | bytes 294944 | tf_op jit(solution)/shard_map/ppermute | solution.py:189
  556.5 2.8 concatenate.139
  559.4 8.9 %fusion.5 = (f32[1024]{0:T(1024)S(1)}, f32[1024]{0:T(1024)S(1)}, f32[1024,1024]{1,0:T(8,128)}) fusion(f32[1024]{0:T(1024)S(1)} %bitcast.145, bf16[2,512,1024]{2,1,0:T(8,128)(2,1)} %param.10, f32[1024]{0:T(1024)S(1)} %copy-done.47, bf16[1024,1024]{1,0:T(8,128)(2,1)} %collective-permute-done.21, bf16[1024,1536]{1,0:T(8,128)(2,1)S(1)} %copy-done.7, ...), kind=kOutput, calls=%fused_computation.8 | convolution fusion | flops 3230660608 | bytes 14696448 | tf_op jit(solution)/shard_map/dot_general | solution.py:29
  568.9 3.2 collective-permute-done.48
  572.1 2.3 collective-permute-start.49
  581.9 3.6 collective-permute-done.50
  589.4 5.9 fusion.2
  (340 shorter events, 100.0 us)
Async XLA Ops:
  7.2 149.3 %all-gather.6.cloned.1.call-start = ((), (), s32[]{:S(2)}) async-start(), calls=%async_computation.1 | async-start | bytes 6684672 | tf_op jit(solution)/shard_map/all_gather | solution.py:665
  16.6 275.5 %all-gather.4.cloned.1.call-start = ((), (), s32[]{:S(2)}) async-start(), calls=%async_computation | async-start | bytes 5013504 | tf_op jit(solution)/shard_map/all_gather | solution.py:666
  19.7 8.4 %collective-permute-start.2 = (bf16[1,400,256]{2,1,0:T(8,128)(2,1)S(1)}, bf16[1,400,256]{2,1,0:T(8,128)(2,1)S(1)}, u32[]{:S(2)}, u32[]{:S(2)}) collective-permute-start(bf16[1,400,256]{2,1,0:T(8,128)(2,1)S(1)} %fusion.32), channel_id=1, source_target_pairs={{0,8},{1,9},{4,12},{5,13},{8,0},{9,1},{12,4},{13,5},{16,24},{17,25... | collective-permute-start | bytes 614408 | tf_op jit(solution)/shard_map/ppermute | solution.py:189
  28.1 29.2 %collective-permute-start.3 = (bf16[2,400,256]{2,1,0:T(8,128)(2,1)S(1)}, bf16[2,400,256]{2,1,0:T(8,128)(2,1)S(1)}, u32[]{:S(2)}, u32[]{:S(2)}) collective-permute-start(bf16[2,400,256]{2,1,0:T(8,128)(2,1)S(1)} %pad_maximum_fusion.16), channel_id=1, source_target_pairs={{0,16},{1,17},{4,20},{5,21},{8,24},{9,25},{12,28},{13,29},{16,0},{... | collective-permute-start | bytes 1228808 | tf_op jit(solution)/shard_map/ppermute | solution.py:189
  30.9 96.0 %collective-permute-start = (bf16[1024,1024]{1,0:T(8,128)(2,1)}, bf16[1024,1024]{1,0:T(8,128)(2,1)}, u32[]{:S(2)}, u32[]{:S(2)}) collective-permute-start(bf16[1024,1024]{1,0:T(8,128)(2,1)} %bitcast), channel_id=1, source_target_pairs={{0,2},{2,0},{1,3},{3,1},{4,6},{6,4},{5,7},{7,5},{8,10},{10,8},{9,1... | collective-permute-start | bytes 6291464 | tf_op jit(solution)/shard_map/ppermute | solution.py:184
  57.4 21.0 %collective-permute-start.8 = (bf16[4,208,256]{2,1,0:T(8,128)(2,1)S(1)}, bf16[4,208,256]{2,1,0:T(8,128)(2,1)S(1)}, u32[]{:S(2)}, u32[]{:S(2)}) collective-permute-start(bf16[4,208,256]{2,1,0:T(8,128)(2,1)S(1)} %slice.385), channel_id=1, source_target_pairs={{0,1},{1,0},{4,5},{5,4},{8,9},{9,8},{12,13},{13,12},{16,17},{17,16... | collective-permute-start | bytes 1277960 | tf_op jit(solution)/shard_map/ppermute | solution.py:189
  58.9 17.9 %collective-permute-start.6 = (bf16[1,384,384]{2,1,0:T(8,128)(2,1)S(1)}, bf16[1,384,384]{2,1,0:T(8,128)(2,1)S(1)}, u32[]{:S(2)}, u32[]{:S(2)}) collective-permute-start(bf16[1,384,384]{2,1,0:T(8,128)(2,1)S(1)} %get-tuple-element.70), channel_id=1, source_target_pairs={{0,8},{1,9},{4,12},{5,13},{8,0},{9,1},{12,4},{13,5},{16,24},{17,25... | collective-permute-start | bytes 884744 | tf_op jit(solution)/shard_map/ppermute | solution.py:189
  58.9 19.5 %collective-permute-start.4 = (bf16[4,192,256]{2,1,0:T(8,128)(2,1)S(1)}, bf16[4,192,256]{2,1,0:T(8,128)(2,1)S(1)}, u32[]{:S(2)}, u32[]{:S(2)}) collective-permute-start(bf16[4,192,256]{2,1,0:T(8,128)(2,1)S(1)} %slice.379), channel_id=1, source_target_pairs={{0,4},{1,5},{4,0},{5,1},{8,12},{9,13},{12,8},{13,9},{16,20},{17,21... | collective-permute-start | bytes 1179656 | tf_op jit(solution)/shard_map/ppermute | solution.py:189
  78.4 41.5 %collective-permute-start.11 = (bf16[2,384,384]{2,1,0:T(8,128)(2,1)}, bf16[2,384,384]{2,1,0:T(8,128)(2,1)}, u32[]{:S(2)}, u32[]{:S(2)}) collective-permute-start(bf16[2,384,384]{2,1,0:T(8,128)(2,1)} %pad_maximum_fusion.13), channel_id=1, source_target_pairs={{0,16},{1,17},{4,20},{5,21},{8,24},{9,25},{12,28},{13,29},{16,0},{... | collective-permute-start | bytes 1769480 | tf_op jit(solution)/shard_map/ppermute | solution.py:189
  81.4 40.9 %collective-permute-start.9 = (bf16[8,208,256]{2,1,0:T(8,128)(2,1)S(1)}, bf16[8,208,256]{2,1,0:T(8,128)(2,1)S(1)}, u32[]{:S(2)}, u32[]{:S(2)}) collective-permute-start(bf16[8,208,256]{2,1,0:T(8,128)(2,1)S(1)} %pad_maximum_fusion.10.refs_2_), channel_id=1, source_target_pairs={{0,4},{1,5},{4,0},{5,1},{8,12},{9,13},{12,8},{13,9},{16,20},{17,21... | collective-permute-start | bytes 2555912 | tf_op jit(solution)/shard_map/ppermute | solution.py:189
  83.0 39.2 %collective-permute-start.7 = (bf16[8,192,256]{2,1,0:T(8,128)(2,1)S(1)}, bf16[8,192,256]{2,1,0:T(8,128)(2,1)S(1)}, u32[]{:S(2)}, u32[]{:S(2)}) collective-permute-start(bf16[8,192,256]{2,1,0:T(8,128)(2,1)S(1)} %pad_maximum_fusion.12.refs_0_), channel_id=1, source_target_pairs={{0,1},{1,0},{4,5},{5,4},{8,9},{9,8},{12,13},{13,12},{16,17},{17,16... | collective-permute-start | bytes 2359304 | tf_op jit(solution)/shard_map/ppermute | solution.py:189
  126.2 43.7 %collective-permute-start.12 = (bf16[4,192,384]{2,1,0:T(8,128)(2,1)}, bf16[4,192,384]{2,1,0:T(8,128)(2,1)}, u32[]{:S(2)}, u32[]{:S(2)}) collective-permute-start(bf16[4,192,384]{2,1,0:T(8,128)(2,1)} %get-tuple-element.78), channel_id=1, source_target_pairs={{0,4},{1,5},{4,0},{5,1},{8,12},{9,13},{12,8},{13,9},{16,20},{17,21... | collective-permute-start | bytes 1769480 | tf_op jit(solution)/shard_map/ppermute | solution.py:189
  126.3 43.6 %collective-permute-start.13 = (bf16[4,192,384]{2,1,0:T(8,128)(2,1)}, bf16[4,192,384]{2,1,0:T(8,128)(2,1)}, u32[]{:S(2)}, u32[]{:S(2)}) collective-permute-start(bf16[4,192,384]{2,1,0:T(8,128)(2,1)} %get-tuple-element.79), channel_id=1, source_target_pairs={{0,1},{1,0},{4,5},{5,4},{8,9},{9,8},{12,13},{13,12},{16,17},{17,16... | collective-permute-start | bytes 1769480 | tf_op jit(solution)/shard_map/ppermute | solution.py:189
  143.8 16.0 %collective-permute-start.10 = (bf16[4,2,512]{2,1,0:T(2,128)(2,1)S(1)}, bf16[4,2,512]{2,1,0:T(2,128)(2,1)S(1)}, u32[]{:S(2)}, u32[]{:S(2)}) collective-permute-start(bf16[4,2,512]{2,1,0:T(2,128)(2,1)S(1)} %fusion.33), channel_id=1, source_target_pairs={{0,1},{2,3},{4,5},{6,7},{8,9},{10,11},{12,13},{14,15},{16,17},{18,... | collective-permute-start | bytes 24584 | tf_op jit(solution)/shard_map/ppermute | solution.py:19
  169.9 20.5 %collective-permute-start.14 = (bf16[2048,1024]{1,0:T(8,128)(2,1)}, bf16[2048,1024]{1,0:T(8,128)(2,1)}, u32[]{:S(2)}, u32[]{:S(2)}) collective-permute-start(bf16[2048,1024]{1,0:T(8,128)(2,1)} %get-tuple-element.80.branch_ref), channel_id=1, source_target_pairs={{0,2},{2,0},{1,3},{3,1},{4,6},{6,4},{5,7},{7,5},{8,10},{10,8},{9,1... | collective-permute-start | bytes 12582920 | tf_op jit(solution)/shard_map/ppermute | solution.py:184
  170.0 9.7 %collective-permute-start.15 = (bf16[1024,1024]{1,0:T(8,128)(2,1)S(1)}, bf16[1024,1024]{1,0:T(8,128)(2,1)S(1)}, u32[]{:S(2)}, u32[]{:S(2)}) collective-permute-start(bf16[1024,1024]{1,0:T(8,128)(2,1)S(1)} %bitcast.123), channel_id=1, source_target_pairs={{0,2},{2,0},{1,3},{3,1},{4,6},{6,4},{5,7},{7,5},{8,10},{10,8},{9,1... | collective-permute-start | bytes 6291464 | tf_op jit(solution)/shard_map/ppermute | solution.py:184
  185.0 59.3 %collective-permute-start.16 = (bf16[8,192,384]{2,1,0:T(8,128)(2,1)S(1)}, bf16[8,192,384]{2,1,0:T(8,128)(2,1)S(1)}, u32[]{:S(2)}, u32[]{:S(2)}) collective-permute-start(bf16[8,192,384]{2,1,0:T(8,128)(2,1)S(1)} %pad_maximum_fusion.6.refs_0_), channel_id=1, source_target_pairs={{0,1},{1,0},{4,5},{5,4},{8,9},{9,8},{12,13},{13,12},{16,17},{17,16... | collective-permute-start | bytes 3538952 | tf_op jit(solution)/shard_map/ppermute | solution.py:189
  190.4 54.0 %collective-permute-start.17 = (bf16[8,192,384]{2,1,0:T(8,128)(2,1)S(1)}, bf16[8,192,384]{2,1,0:T(8,128)(2,1)S(1)}, u32[]{:S(2)}, u32[]{:S(2)}) collective-permute-start(bf16[8,192,384]{2,1,0:T(8,128)(2,1)S(1)} %pad_maximum_fusion.7.refs_2_), channel_id=1, source_target_pairs={{0,4},{1,5},{4,0},{5,1},{8,12},{9,13},{12,8},{13,9},{16,20},{17,21... | collective-permute-start | bytes 3538952 | tf_op jit(solution)/shard_map/ppermute | solution.py:189
  242.2 46.0 %collective-permute-start.29 = (bf16[8,192,384]{2,1,0:T(8,128)(2,1)}, bf16[8,192,384]{2,1,0:T(8,128)(2,1)S(1)}, u32[]{:S(2)}, u32[]{:S(2)}) collective-permute-start(bf16[8,192,384]{2,1,0:T(8,128)(2,1)} %get-tuple-element.105), channel_id=1, source_target_pairs={{0,1},{1,0},{4,5},{5,4},{8,9},{9,8},{12,13},{13,12},{16,17},{17,16... | collective-permute-start | bytes 3538952 | tf_op jit(solution)/shard_map/ppermute | solution.py:189
  242.6 46.8 %collective-permute-start.31 = (bf16[8,192,384]{2,1,0:T(8,128)(2,1)}, bf16[8,192,384]{2,1,0:T(8,128)(2,1)S(1)}, u32[]{:S(2)}, u32[]{:S(2)}) collective-permute-start(bf16[8,192,384]{2,1,0:T(8,128)(2,1)} %get-tuple-element.108), channel_id=1, source_target_pairs={{0,4},{1,5},{4,0},{5,1},{8,12},{9,13},{12,8},{13,9},{16,20},{17,21... | collective-permute-start | bytes 3538952 | tf_op jit(solution)/shard_map/ppermute | solution.py:189
  340.4 69.8 %collective-permute-start.19 = (bf16[2048,1024]{1,0:T(8,128)(2,1)}, bf16[2048,1024]{1,0:T(8,128)(2,1)}, u32[]{:S(2)}, u32[]{:S(2)}) collective-permute-start(bf16[2048,1024]{1,0:T(8,128)(2,1)} %convert_element_type.153), channel_id=1, source_target_pairs={{0,2},{2,0},{1,3},{3,1},{4,6},{6,4},{5,7},{7,5},{8,10},{10,8},{9,1... | collective-permute-start | bytes 12582920 | tf_op jit(solution)/shard_map/ppermute | solution.py:184
  340.4 29.2 %collective-permute-start.35 = (bf16[8,192,384]{2,1,0:T(8,128)(2,1)}, bf16[8,192,384]{2,1,0:T(8,128)(2,1)}, u32[]{:S(2)}, u32[]{:S(2)}) collective-permute-start(bf16[8,192,384]{2,1,0:T(8,128)(2,1)} %get-tuple-element.113), channel_id=1, source_target_pairs={{0,1},{1,0},{4,5},{5,4},{8,9},{9,8},{12,13},{13,12},{16,17},{17,16... | collective-permute-start | bytes 3538952 | tf_op jit(solution)/shard_map/ppermute | solution.py:189
  342.3 35.7 %collective-permute-start.37 = (bf16[8,192,384]{2,1,0:T(8,128)(2,1)}, bf16[8,192,384]{2,1,0:T(8,128)(2,1)}, u32[]{:S(2)}, u32[]{:S(2)}) collective-permute-start(bf16[8,192,384]{2,1,0:T(8,128)(2,1)} %get-tuple-element.116), channel_id=1, source_target_pairs={{0,4},{1,5},{4,0},{5,1},{8,12},{9,13},{12,8},{13,9},{16,20},{17,21... | collective-permute-start | bytes 3538952 | tf_op jit(solution)/shard_map/ppermute | solution.py:189
  344.4 39.6 %collective-permute-start.30 = (bf16[4,192,384]{2,1,0:T(8,128)(2,1)}, bf16[4,192,384]{2,1,0:T(8,128)(2,1)}, u32[]{:S(2)}, u32[]{:S(2)}) collective-permute-start(bf16[4,192,384]{2,1,0:T(8,128)(2,1)} %slice.562), channel_id=1, source_target_pairs={{0,4},{1,5},{4,0},{5,1},{8,12},{9,13},{12,8},{13,9},{16,20},{17,21... | collective-permute-start | bytes 1769480 | tf_op jit(solution)/shard_map/ppermute | solution.py:189
  346.7 42.0 %collective-permute-start.32 = (bf16[4,192,384]{2,1,0:T(8,128)(2,1)}, bf16[4,192,384]{2,1,0:T(8,128)(2,1)S(1)}, u32[]{:S(2)}, u32[]{:S(2)}) collective-permute-start(bf16[4,192,384]{2,1,0:T(8,128)(2,1)} %slice.561), channel_id=1, source_target_pairs={{0,1},{1,0},{4,5},{5,4},{8,9},{9,8},{12,13},{13,12},{16,17},{17,16... | collective-permute-start | bytes 1769480 | tf_op jit(solution)/shard_map/ppermute | solution.py:189
  369.5 37.5 %collective-permute-start.41 = (bf16[8,192,384]{2,1,0:T(8,128)(2,1)}, bf16[8,192,384]{2,1,0:T(8,128)(2,1)S(1)}, u32[]{:S(2)}, u32[]{:S(2)}) collective-permute-start(bf16[8,192,384]{2,1,0:T(8,128)(2,1)} %get-tuple-element.121), channel_id=1, source_target_pairs={{0,1},{1,0},{4,5},{5,4},{8,9},{9,8},{12,13},{13,12},{16,17},{17,16... | collective-permute-start | bytes 3538952 | tf_op jit(solution)/shard_map/ppermute | solution.py:189
  378.0 30.5 %collective-permute-start.43 = (bf16[8,192,384]{2,1,0:T(8,128)(2,1)S(1)}, bf16[8,192,384]{2,1,0:T(8,128)(2,1)S(1)}, u32[]{:S(2)}, u32[]{:S(2)}) collective-permute-start(bf16[8,192,384]{2,1,0:T(8,128)(2,1)S(1)} %copy-done.51), channel_id=1, source_target_pairs={{0,4},{1,5},{4,0},{5,1},{8,12},{9,13},{12,8},{13,9},{16,20},{17,21... | collective-permute-start | bytes 3538952 | tf_op jit(solution)/shard_map/ppermute | solution.py:189
  384.1 50.2 %collective-permute-start.18 = (bf16[1024,1024]{1,0:T(8,128)(2,1)}, bf16[1024,1024]{1,0:T(8,128)(2,1)}, u32[]{:S(2)}, u32[]{:S(2)}) collective-permute-start(bf16[1024,1024]{1,0:T(8,128)(2,1)} %slice.556), channel_id=1, source_target_pairs={{0,2},{2,0},{1,3},{3,1},{4,6},{6,4},{5,7},{7,5},{8,10},{10,8},{9,1... | collective-permute-start | bytes 6291464 | tf_op jit(solution)/shard_map/ppermute | solution.py:184
  432.9 13.5 %collective-permute-start.20 = (bf16[4,2,512]{2,1,0:T(2,128)(2,1)S(1)}, bf16[4,2,512]{2,1,0:T(2,128)(2,1)S(1)}, u32[]{:S(2)}, u32[]{:S(2)}) collective-permute-start(bf16[4,2,512]{2,1,0:T(2,128)(2,1)S(1)} %slice.399), channel_id=1, source_target_pairs={{1,0},{3,2},{5,4},{7,6},{9,8},{11,10},{13,12},{15,14},{17,16},{19,... | collective-permute-start | bytes 24584 | tf_op jit(solution)/shard_map/ppermute | solution.py:19
  439.7 36.8 %collective-permute-start.33 = (bf16[2,384,384]{2,1,0:T(8,128)(2,1)}, bf16[2,384,384]{2,1,0:T(8,128)(2,1)}, u32[]{:S(2)}, u32[]{:S(2)}) collective-permute-start(bf16[2,384,384]{2,1,0:T(8,128)(2,1)} %fusion.24), channel_id=1, source_target_pairs={{0,16},{1,17},{4,20},{5,21},{8,24},{9,25},{12,28},{13,29},{16,0},{... | collective-permute-start | bytes 1769480 | tf_op jit(solution)/shard_map/ppermute | solution.py:189
  441.7 29.2 %collective-permute-start.36 = (bf16[4,192,384]{2,1,0:T(8,128)(2,1)}, bf16[4,192,384]{2,1,0:T(8,128)(2,1)}, u32[]{:S(2)}, u32[]{:S(2)}) collective-permute-start(bf16[4,192,384]{2,1,0:T(8,128)(2,1)} %slice.560), channel_id=1, source_target_pairs={{0,4},{1,5},{4,0},{5,1},{8,12},{9,13},{12,8},{13,9},{16,20},{17,21... | collective-permute-start | bytes 1769480 | tf_op jit(solution)/shard_map/ppermute | solution.py:189
  442.0 32.5 %collective-permute-start.38 = (bf16[4,192,384]{2,1,0:T(8,128)(2,1)}, bf16[4,192,384]{2,1,0:T(8,128)(2,1)}, u32[]{:S(2)}, u32[]{:S(2)}) collective-permute-start(bf16[4,192,384]{2,1,0:T(8,128)(2,1)} %slice.559), channel_id=1, source_target_pairs={{0,1},{1,0},{4,5},{5,4},{8,9},{9,8},{12,13},{13,12},{16,17},{17,16... | collective-permute-start | bytes 1769480 | tf_op jit(solution)/shard_map/ppermute | solution.py:189
  444.6 33.4 %collective-permute-start.42 = (bf16[4,192,384]{2,1,0:T(8,128)(2,1)}, bf16[4,192,384]{2,1,0:T(8,128)(2,1)}, u32[]{:S(2)}, u32[]{:S(2)}) collective-permute-start(bf16[4,192,384]{2,1,0:T(8,128)(2,1)} %slice.558), channel_id=1, source_target_pairs={{0,4},{1,5},{4,0},{5,1},{8,12},{9,13},{12,8},{13,9},{16,20},{17,21... | collective-permute-start | bytes 1769480 | tf_op jit(solution)/shard_map/ppermute | solution.py:189
  446.4 34.3 %collective-permute-start.44 = (bf16[4,192,384]{2,1,0:T(8,128)(2,1)}, bf16[4,192,384]{2,1,0:T(8,128)(2,1)}, u32[]{:S(2)}, u32[]{:S(2)}) collective-permute-start(bf16[4,192,384]{2,1,0:T(8,128)(2,1)} %slice.557), channel_id=1, source_target_pairs={{0,1},{1,0},{4,5},{5,4},{8,9},{9,8},{12,13},{13,12},{16,17},{17,16... | collective-permute-start | bytes 1769480 | tf_op jit(solution)/shard_map/ppermute | solution.py:189
  470.9 64.8 %collective-permute-start.22 = (bf16[8,256,256]{2,1,0:T(8,128)(2,1)S(1)}, bf16[8,256,256]{2,1,0:T(8,128)(2,1)S(1)}, u32[]{:S(2)}, u32[]{:S(2)}) collective-permute-start(bf16[8,256,256]{2,1,0:T(8,128)(2,1)S(1)} %get-tuple-element.99), channel_id=1, source_target_pairs={{0,1},{1,0},{4,5},{5,4},{8,9},{9,8},{12,13},{13,12},{16,17},{17,16... | collective-permute-start | bytes 3145736 | tf_op jit(solution)/shard_map/ppermute | solution.py:189
  474.5 23.0 %collective-permute-start.24 = (bf16[8,256,256]{2,1,0:T(8,128)(2,1)S(1)}, bf16[8,256,256]{2,1,0:T(8,128)(2,1)S(1)}, u32[]{:S(2)}, u32[]{:S(2)}) collective-permute-start(bf16[8,256,256]{2,1,0:T(8,128)(2,1)S(1)} %copy-done.9), channel_id=1, source_target_pairs={{0,4},{1,5},{4,0},{5,1},{8,12},{9,13},{12,8},{13,9},{16,20},{17,21... | collective-permute-start | bytes 3145736 | tf_op jit(solution)/shard_map/ppermute | solution.py:189
  476.6 82.8 %collective-permute-start.21 = (bf16[1024,1024]{1,0:T(8,128)(2,1)}, bf16[1024,1024]{1,0:T(8,128)(2,1)}, u32[]{:S(2)}, u32[]{:S(2)}) collective-permute-start(bf16[1024,1024]{1,0:T(8,128)(2,1)} %fusion.12), channel_id=1, source_target_pairs={{0,2},{2,0},{1,3},{3,1},{4,6},{6,4},{5,7},{7,5},{8,10},{10,8},{9,1... | collective-permute-start | bytes 6291464 | tf_op jit(solution)/shard_map/ppermute | solution.py:184
  478.0 12.4 %collective-permute-start.34 = (bf16[1,384,384]{2,1,0:T(8,128)(2,1)S(1)}, bf16[1,384,384]{2,1,0:T(8,128)(2,1)S(1)}, u32[]{:S(2)}, u32[]{:S(2)}) collective-permute-start(bf16[1,384,384]{2,1,0:T(8,128)(2,1)S(1)} %slice.567), channel_id=1, source_target_pairs={{0,8},{1,9},{4,12},{5,13},{8,0},{9,1},{12,4},{13,5},{16,24},{17,25... | collective-permute-start | bytes 884744 | tf_op jit(solution)/shard_map/ppermute | solution.py:189
  480.7 42.4 %collective-permute-start.39 = (bf16[2,384,384]{2,1,0:T(8,128)(2,1)S(1)}, bf16[2,384,384]{2,1,0:T(8,128)(2,1)S(1)}, u32[]{:S(2)}, u32[]{:S(2)}) collective-permute-start(bf16[2,384,384]{2,1,0:T(8,128)(2,1)S(1)} %fusion.23), channel_id=1, source_target_pairs={{0,16},{1,17},{4,20},{5,21},{8,24},{9,25},{12,28},{13,29},{16,0},{... | collective-permute-start | bytes 1769480 | tf_op jit(solution)/shard_map/ppermute | solution.py:189
  490.4 45.1 %collective-permute-start.45 = (bf16[2,384,384]{2,1,0:T(8,128)(2,1)S(1)}, bf16[2,384,384]{2,1,0:T(8,128)(2,1)S(1)}, u32[]{:S(2)}, u32[]{:S(2)}) collective-permute-start(bf16[2,384,384]{2,1,0:T(8,128)(2,1)S(1)} %fusion.22), channel_id=1, source_target_pairs={{0,16},{1,17},{4,20},{5,21},{8,24},{9,25},{12,28},{13,29},{16,0},{... | collective-permute-start | bytes 1769480 | tf_op jit(solution)/shard_map/ppermute | solution.py:189
  498.7 53.2 %collective-permute-start.25 = (bf16[4,256,256]{2,1,0:T(8,128)(2,1)}, bf16[4,256,256]{2,1,0:T(8,128)(2,1)}, u32[]{:S(2)}, u32[]{:S(2)}) collective-permute-start(bf16[4,256,256]{2,1,0:T(8,128)(2,1)} %slice.563), channel_id=1, source_target_pairs={{0,1},{1,0},{4,5},{5,4},{8,9},{9,8},{12,13},{13,12},{16,17},{17,16... | collective-permute-start | bytes 1572872 | tf_op jit(solution)/shard_map/ppermute | solution.py:189
  523.3 18.5 %collective-permute-start.40 = (bf16[1,384,384]{2,1,0:T(8,128)(2,1)S(1)}, bf16[1,384,384]{2,1,0:T(8,128)(2,1)S(1)}, u32[]{:S(2)}, u32[]{:S(2)}) collective-permute-start(bf16[1,384,384]{2,1,0:T(8,128)(2,1)S(1)} %slice.566), channel_id=1, source_target_pairs={{0,8},{1,9},{4,12},{5,13},{8,0},{9,1},{12,4},{13,5},{16,24},{17,25... | collective-permute-start | bytes 884744 | tf_op jit(solution)/shard_map/ppermute | solution.py:189
  535.6 12.4 %collective-permute-start.46 = (bf16[1,384,384]{2,1,0:T(8,128)(2,1)S(1)}, bf16[1,384,384]{2,1,0:T(8,128)(2,1)S(1)}, u32[]{:S(2)}, u32[]{:S(2)}) collective-permute-start(bf16[1,384,384]{2,1,0:T(8,128)(2,1)S(1)} %slice.565), channel_id=1, source_target_pairs={{0,8},{1,9},{4,12},{5,13},{8,0},{9,1},{12,4},{13,5},{16,24},{17,25... | collective-permute-start | bytes 884744 | tf_op jit(solution)/shard_map/ppermute | solution.py:189
  536.9 16.9 %collective-permute-start.23 = (bf16[4,256,256]{2,1,0:T(8,128)(2,1)}, bf16[4,256,256]{2,1,0:T(8,128)(2,1)}, u32[]{:S(2)}, u32[]{:S(2)}) collective-permute-start(bf16[4,256,256]{2,1,0:T(8,128)(2,1)} %slice.564), channel_id=1, source_target_pairs={{0,4},{1,5},{4,0},{5,1},{8,12},{9,13},{12,8},{13,9},{16,20},{17,21... | collective-permute-start | bytes 1572872 | tf_op jit(solution)/shard_map/ppermute | solution.py:189
  556.2 31.2 %collective-permute-start.26 = (bf16[2,512,256]{2,1,0:T(8,128)(2,1)}, bf16[2,512,256]{2,1,0:T(8,128)(2,1)}, u32[]{:S(2)}, u32[]{:S(2)}) collective-permute-start(bf16[2,512,256]{2,1,0:T(8,128)(2,1)} %fusion.27), channel_id=1, source_target_pairs={{0,16},{1,17},{4,20},{5,21},{8,24},{9,25},{12,28},{13,29},{16,0},{... | collective-permute-start | bytes 1572872 | tf_op jit(solution)/shard_map/ppermute | solution.py:189
  572.1 9.7 %collective-permute-start.49 = (f32[4,5,128]{2,0,1:T(4,128)S(1)}, f32[4,5,128]{2,0,1:T(4,128)S(1)}, u32[]{:S(2)}, u32[]{:S(2)}) collective-permute-start(f32[4,5,128]{2,0,1:T(4,128)S(1)} %slice_select_fusion.2), channel_id=1, source_target_pairs={{0,16},{1,17},{4,20},{5,21},{8,24},{9,25},{12,28},{13,29},{16,0},{... | collective-permute-start | bytes 30728 | tf_op jit(solution)/shard_map/ppermute | solution.py:189
  588.6 7.3 %collective-permute-start.27 = (bf16[1,512,256]{2,1,0:T(8,128)(2,1)S(1)}, bf16[1,512,256]{2,1,0:T(8,128)(2,1)S(1)}, u32[]{:S(2)}, u32[]{:S(2)}) collective-permute-start(bf16[1,512,256]{2,1,0:T(8,128)(2,1)S(1)} %slice.568), channel_id=1, source_target_pairs={{0,8},{1,9},{4,12},{5,13},{8,0},{9,1},{12,4},{13,5},{16,24},{17,25... | collective-permute-start | bytes 786440 | tf_op jit(solution)/shard_map/ppermute | solution.py:189
  589.3 6.0 collective-permute-start.52
  (63 other events, 460.7 us)
Sparse Core Ops, SparseCore 0:
  16.7 139.6 all-gather.5
  170.1 95.6 all-gather.3

commit v3 on v2

--- a/solution.py
+++ b/solution.py
@@ -176,6 +176,8 @@
     )
 
 
+SMALL_COST = pl.CostEstimate(flops=1 << 16, bytes_accessed=1 << 16, transcendentals=0)
+VMEM_LIMIT = 60 * 1024 * 1024
 NT = (((1,), (1,)), ((), ()))
 TN = (((0,), (0,)), ((), ()))
 
@@ -229,25 +231,35 @@
 
 def scatter_sum(parts, ties=()):
     far, first_order, second_order = bit_masks()
+    n_slots = lax.axis_size("chip") * lax.axis_size("ctx")
     ties = dict(enumerate(ties))
 
-    def sent(block, mask, step):
-        block = block.astype(bf16)
+    def got(block, mask, step, senders=range(n_slots)):
+        block = lax.ppermute(block.astype(bf16), ("chip", "ctx"), [(i, i ^ mask) for i in senders])
         if ties.get(step) is not None:
             block = after(block, ties[step])
-        return across(block, mask).astype(f32)
+        return block.astype(f32)
 
     halves = []
     for order, keep, send in ((first_order, parts[0], parts[1]), (second_order, parts[2], parts[3])):
-        keep = keep.astype(f32) + sent(send, order[-1], 0)
+        keep = keep.astype(f32) + got(send, order[-1], 0)
         for step, mask in enumerate(reversed(order[:-1])):
             mid = keep.shape[0] // 2
-            keep = keep[:mid] + sent(keep[mid:], mask, step + 1)
+            keep = keep[:mid] + got(keep[mid:], mask, step + 1)
         halves.append(keep)
     keep = jnp.concatenate(halves, axis=1)
-    for step, mask in enumerate(reversed(far)):
+    step = len(first_order)
+    if len(far) == 2:
+        low, high = far
+        outer = [i for i in range(n_slots) if (i & low == 0) == (i & high == 0)]
+        inner = [i for i in range(n_slots) if i not in outer]
+        distant = keep[2:] + got(keep[2:], low, step, outer)[::-1]
+        keep = keep[:2] + got(distant, low | high, step + 1, inner)[::-1]
+        return keep[0] + got(keep[1:], low, step + 2)[0]
+    for mask in reversed(far):
         mid = keep.shape[0] // 2
-        keep = keep[:mid] + sent(keep[mid:], mask, len(first_order) + step)
+        keep = keep[:mid] + got(keep[mid:], mask, step)
+        step += 1
     return keep[0]
 
 
@@ -381,13 +393,9 @@
         ),
         input_output_aliases={} if first else {3 + count: 0, 4 + count: 1},
         compiler_params=pltpu.CompilerParams(
-            vmem_limit_bytes=56 * 1024 * 1024, dimension_semantics=("arbitrary",)
+            vmem_limit_bytes=VMEM_LIMIT, dimension_semantics=("arbitrary",)
         ),
-        cost_estimate=pl.CostEstimate(
-            flops=18 * total * width * hidden_count,
-            bytes_accessed=20 * total * width,
-            transcendentals=total * hidden_count,
-        ),
+        cost_estimate=SMALL_COST,
     )(own, nffn, go, *weights, *(() if first else totals))
     return (outs[0], outs[1]), outs[2:]
 
@@ -415,8 +423,8 @@
         + [vmem_spec if outward else any_spec] * len(arrays),
         out_specs=[any_spec if outward else vmem_spec] * len(shapes),
         scratch_shapes=[pltpu.SemaphoreType.DMA((len(plan) * len(segments),))],
-        compiler_params=pltpu.CompilerParams(vmem_limit_bytes=24 * 1024 * 1024),
-        cost_estimate=pl.CostEstimate(flops=0, bytes_accessed=1 << 24, transcendentals=0),
+        compiler_params=pltpu.CompilerParams(vmem_limit_bytes=VMEM_LIMIT),
+        cost_estimate=SMALL_COST,
     )(own, *arrays)
 
 
@@ -499,7 +507,7 @@
 
 def in_grad_kernel(
     geometry, count, own_ref, grad_conv_ref, behind_ref, before_ref, projected_ref, grad_c_ref,
-    normed_ref, taps_ref, grad_out_ref, grad_projected_ref, grad_taps_ref, *refs
+    normed_ref, taps_ref, grad_projected_ref, grad_taps_ref, *refs
 ):
     parts, (total_ref, low_ref, sems) = refs[:count], refs[count:]
     plan, segments, n_ctx = geometry
@@ -530,11 +538,11 @@
     @pl.when(step == pl.num_programs(0) - 1)
     def _():
         low_ref[...] = total_ref[...].astype(bf16)
-        pairs = slot_pairs(own_ref[0], plan, parts, segments, n_ctx, (low_ref, grad_out_ref))
+        pairs = slot_pairs(own_ref[0], plan, parts, segments, n_ctx, (low_ref,))
         copy_all([(b, a) for a, b in pairs], sems)
 
 
-def row_call(body, steps, ins, outs, scratch=(), flops=0, limit=48):
+def row_call(body, steps, ins, outs, scratch=()):
     return pl.pallas_call(
         body,
         grid=(steps,),
@@ -549,13 +557,9 @@
         out_shape=[jax.ShapeDtypeStruct(shape, dtype) for shape, dtype, _, _ in outs],
         scratch_shapes=list(scratch),
         compiler_params=pltpu.CompilerParams(
-            vmem_limit_bytes=limit * 1024 * 1024, dimension_semantics=("arbitrary",)
+            vmem_limit_bytes=VMEM_LIMIT, dimension_semantics=("arbitrary",)
         ),
-        cost_estimate=pl.CostEstimate(
-            flops=flops,
-            bytes_accessed=sum(a.size * a.dtype.itemsize for a, _, _ in ins),
-            transcendentals=0,
-        ),
+        cost_estimate=SMALL_COST,
     )(*[a for a, _, _ in ins])
 
 
@@ -641,7 +645,7 @@
         for k in range(in_parts)
     ]
     out_segments = [
-        (in_rows + k * depth, depth, 0, 256, 1, depth, 0, wide, 256 * k) for k in range(out_parts)
+        (k * depth, depth, 0, 256, 0, depth, 0, wide, 256 * k) for k in range(out_parts)
     ]
     small_segment = (in_rows, 16, 0, 256, 1, 16, 0, 256, 0)
     mix_plan = gather_plan(mix_cut, mix_rows)
@@ -659,11 +663,7 @@
     whole_geometry = (whole_plan, chunk_segments, n_ctx)
     step_geometry = (gather_plan(chunk_cut, chunk_rows), chunk_segments, n_ctx)
 
-    first_block = jnp.concatenate(
-        [chunk_blocks[0], jnp.pad(out_block, ((0, 0), (0, lanes - 256)))], axis=0
-    )
-    first_all = lax.all_gather(first_block, ("chip", "ctx"))
-    last_all = lax.all_gather(chunk_blocks[2], ("chip", "ctx"))
+    out_all = lax.all_gather(out_block, ("chip", "ctx"))
 
     far, first_order, second_order = bit_masks()
 
@@ -674,7 +674,10 @@
     for mask in far:
         hold = doubled(hold, across(hold, mask))
     mix_halves = [hold[:, :mix_cut], hold[:, mix_cut:]]
-    next_hold = after(chunk_blocks[1][None], hold)
+    next_hold = after(chunk_blocks[0][None], hold)
+    chunk_all = [
+        lax.all_gather(after(block, hold), ("chip", "ctx")) for block in chunk_blocks[1:]
+    ]
     far_left = list(far)
     mix_parts = []
     for step in range(len(first_order)):
@@ -701,25 +704,18 @@
     )
     (out_half,) = move(
         own,
-        [first_all],
+        [out_all],
         [(channels, width)],
-        (
-            [(0, i, None, 0, chunk_rows + out_parts * depth) for i in range(slots)],
-            [
-                (chunk_rows + k * depth, depth, 0, 256, 0, depth, 0, wide, 256 * k)
-                for k in range(out_parts)
-            ],
-            n_ctx,
-        ),
+        ([(0, i, None, 0, out_parts * depth) for i in range(slots)], out_segments, n_ctx),
         1,
         False,
     )
     next_halves = [next_hold[:, :chunk_cut], next_hold[:, chunk_cut:]]
     next_orders = (first_order, second_order)
 
-    def next_step(step, *done):
-        got = [across(after(h, *done), o[step]) for h, o in zip(next_halves, next_orders)]
-        return got
+    def next_step(step, done):
+        got = [across(h, o[step]) for h, o in zip(next_halves, next_orders)]
+        return [after(g, done) for g in got]
 
     small_all = small_all.reshape(n_chip, 16, n_ctx * 256)[:, :5, : 2 * depth].astype(f32)
     first_gain = small_all[:, 0].reshape(width)
@@ -745,7 +741,6 @@
 
     wide_rows, thin_rows = (piece, width), (piece, channels)
     taps = jnp.pad(taps, ((0, 5), (0, 0)))
-    next_got = next_step(0, in_half)
     normed_low, projected = row_call(
         in_kernel,
         blocks,
@@ -758,8 +753,8 @@
             ((2 * rows, width), bf16, wide_rows, at),
             ((2 * rows, 3 * channels), f32, (piece, 3 * channels), at),
         ],
-        flops=12 * rows * width * channels,
-    )
+    )
+    next_got = next_step(0, projected)
     tail = projected.reshape(blocks, piece, 3 * channels)[:, piece - 2 :]
     tail = (tail[:, :, :channels] * tail[:, :, 2 * channels :]).astype(bf16)
     before = passed_along(tail, "ctx", 1)
@@ -782,13 +777,7 @@
             ((2 * rows, channels), f32, thin_rows, at),
             ((2 * rows, width), bf16, wide_rows, at),
         ],
-        flops=4 * rows * width * channels,
-    )
-    branch = after(branch, *next_got)
-    for step in range(1, len(first_order)):
-        next_halves = [doubled(h, g) for h, g in zip(next_halves, next_got)]
-        next_got = next_step(step, branch)
-    next_parts = [next_halves[0], next_got[0], next_halves[1], next_got[1]]
+    )
     residual, nffn_low = row_call(
         norm_kernel,
         blocks,
@@ -801,16 +790,19 @@
         [((2 * rows, width), f32, wide_rows, at), ((2 * rows, width), bf16, wide_rows, at)],
     )
 
+    for step in range(1, len(first_order)):
+        next_halves = [doubled(h, g) for h, g in zip(next_halves, next_got)]
+        next_got = next_step(step, nffn_low)
+    next_parts = [next_halves[0], next_got[0], next_halves[1], next_got[1]]
     totals, first_grads = ffn_chunk(
-        own, nffn_low, go, [first_all], None, whole_geometry, step_geometry, hidden_count
-    )
-    first_total = totals[1]
-    totals, next_grads = ffn_chunk(
-        own, nffn_low, go, next_parts, totals, step_geometry, step_geometry, hidden_count
-    )
-    next_total = totals[1]
+        own, nffn_low, go, next_parts, None, step_geometry, step_geometry, hidden_count
+    )
+    totals, second_grads = ffn_chunk(
+        own, nffn_low, go, [chunk_all[0]], totals, whole_geometry, step_geometry, hidden_count
+    )
+    second_total = totals[1]
     totals, last_grads = ffn_chunk(
-        own, nffn_low, go, [last_all], totals, whole_geometry, step_geometry, hidden_count
+        own, nffn_low, go, [chunk_all[1]], totals, whole_geometry, step_geometry, hidden_count
     )
     ffn_out, grad_nffn = totals
     grad_got = swap(grad_nffn.astype(bf16))
@@ -850,17 +842,16 @@
             ((1, width), f32, (1, width), still),
         ],
         scratch=[pltpu.VMEM((channels, width), f32)],
-        flops=8 * rows * width * channels,
     )
     grad_gain_ffn = grad_gain_ffn[0]
     head = grad_conv.reshape(blocks, piece, channels)[:, :2].astype(bf16)
     behind = passed_along(head, "ctx", -1)
-    sum_rows = in_rows + out_parts * depth
-    sum_cut = sum_rows // 2
-    sum_plan = gather_plan(sum_cut, sum_rows)
-    sum_segments = mix_segments + out_segments
+    grad_out_slots = grad_w_out.reshape(n_chip, depth, n_ctx, out_parts, 256)
+    grad_out_slots = grad_out_slots.transpose(0, 2, 3, 1, 4).reshape(slots, out_parts * depth, 256)
+    out_sum = lax.psum_scatter(grad_out_slots, ("chip", "ctx"), scatter_dimension=0).astype(f32)
+    sum_plan = gather_plan(mix_cut, in_rows)
     grad_projected, grad_kernel, *mix_grad_parts = row_call(
-        functools.partial(in_grad_kernel, (sum_plan, sum_segments, n_ctx), 4),
+        functools.partial(in_grad_kernel, (sum_plan, mix_segments, n_ctx), 4),
         blocks,
         [
             (own, None, None),
@@ -871,7 +862,6 @@
             (grad_c, thin_rows, at),
             (normed_low, wide_rows, at),
             (taps, taps.shape, still),
-            (grad_w_out, grad_w_out.shape, still),
         ],
         [
             ((2 * rows, 3 * channels), bf16, (piece, 3 * channels), at),
@@ -881,14 +871,15 @@
         scratch=[
             pltpu.VMEM((width, 3 * channels), f32),
             pltpu.VMEM((width, 3 * channels), bf16),
-            pltpu.SemaphoreType.DMA((len(sum_plan) * len(sum_segments),)),
-        ],
-        flops=12 * rows * width * channels,
+            pltpu.SemaphoreType.DMA((len(sum_plan) * len(mix_segments),)),
+        ],
     )
     grad_kernel = grad_kernel[:3]
-    first_sum = scatter_sum(first_grads, (None, next_total, grad_got, grad_c))
-    next_sum = scatter_sum(next_grads, (None, grad_got, grad_c, grad_projected))
-    last_sum = scatter_sum(last_grads, (None, grad_c, grad_projected, grad_projected))
+    first_sum = scatter_sum(
+        first_grads, (second_total, grad_nffn, grad_c, grad_projected, grad_projected)
+    )
+    second_sum = scatter_sum(second_grads, (grad_nffn, grad_c, grad_projected))
+    last_sum = scatter_sum(last_grads, (grad_c, grad_projected))
     mix_sum = scatter_sum(mix_grad_parts)
     late_projected = after(grad_projected, mix_grad_parts[1])
     grad_normed = cross_cols(late_projected[rows:], in_half).astype(bf16)
@@ -900,7 +891,7 @@
     grad_in_norm, grad_gain_mix = norm_backward(own_inputs, scale_mix, first_gain, grad_normed)
     grad_tokens = (grad_residual + grad_in_norm).reshape(seqs, piece, width)
 
-    chunk_sum = jnp.stack([first_sum, next_sum, last_sum])
+    chunk_sum = jnp.stack([first_sum, second_sum, last_sum])
     both_sum = chunk_sum[:, : 4 * depth].reshape(CHUNKS, 2, 2, depth, lanes).transpose(2, 0, 1, 3, 4)
     both_mine, both_other = mine_other(both_sum)
     both_got = swap(both_other)
@@ -912,12 +903,12 @@
     final_down = jnp.concatenate([chunk_sum[:, 4 * depth : 4 * depth + sub], down_rest], axis=2)
     final_down = final_down.reshape(CHUNKS * sub, wide)
 
-    in_sum = mix_sum[:in_rows].reshape(in_parts, 2, depth, 256).transpose(1, 0, 2, 3)
+    in_sum = mix_sum.reshape(in_parts, 2, depth, 256).transpose(1, 0, 2, 3)
     in_mine, in_other = mine_other(in_sum)
     in_sum = in_core_order(in_mine[None], swap(in_other)[None], 0)
     in_sum = in_sum.transpose(0, 2, 1, 3).reshape(2, depth, in_cols // depth, depth)
     final_in = in_sum.transpose(1, 2, 0, 3).reshape(depth, 2 * in_cols)
-    final_out = mix_sum[in_rows:].reshape(out_parts, depth, 256).transpose(1, 0, 2)
+    final_out = out_sum.reshape(out_parts, depth, 256).transpose(1, 0, 2)
     final_out = final_out.reshape(depth, wide)
 
     grad_taps = grad_kernel.reshape(3, n_chip, 1, depth)

time: 617 us -> 632 us (1.024)
  starting transfers between devices: 52.6 us -> 66.5 us
  Pallas kernels: 193 us -> 202 us
  local copies, waits for them, and re-layouts: 52.9 us -> 45 us
    ppermute x0 -> x28, waiting for transfers between devices: none -> 69.5 us  [got(): lax.ppermute(block.astype(bf16), ('chip', 'ctx'), [(i, i ^ mask) for i in...]
    ppermute x40 -> x16, waiting for transfers between devices: 199 us -> 131 us  [across(): lax.ppermute(block, ('chip', 'ctx'), [(i, i ^ mask) for i in range(count)])]
    ppermute x0 -> x28, starting transfers between devices: none -> 41.2 us  [got(): lax.ppermute(block.astype(bf16), ('chip', 'ctx'), [(i, i ^ mask) for i in...]
    ppermute x40 -> x16, starting transfers between devices: 44.8 us -> 18.8 us  [across(): lax.ppermute(block, ('chip', 'ctx'), [(i, i ^ mask) for i in range(count)])]
    ppermute x11, waiting for transfers between devices: 10.8 us -> 0.86 us  [swap(): return lax.ppermute(block, 'core', [(0, 1), (1, 0)])]
    convert_element_type x0 -> x16, other arithmetic: none -> 7.38 us  [the longest x8 4.07 us: got(): return block.astype(f32)]
    all_gather x2 -> x3, waiting for transfers between devices: 8.4 us -> 14.9 us  [the longest x1 14.9 us: fast_shards(): out_all = lax.all_gather(out_block, ('chip', 'ctx'))]
    unnamed x115 -> x105, local copies, waits for them, and re-layouts: 15.2 us -> 10.1 us
  transfers between devices with their start and end apart: 55 -> 61, of which waited for: 24 -> 25; matrix products, arithmetic and copies ran while one was open for 16% -> 15% of each run, Pallas kernels for 25% -> 26%
where the time goes in v3:
time: 632 us; the launch traced here: 624 us
  waiting for transfers between devices  218 us (34%)
  Pallas kernels  202 us (32%)
  starting transfers between devices  66.5 us (11%)
  other arithmetic  63.3 us (10%)
  local copies, waits for them, and re-layouts  45 us (7%)
  between operations  15.7 us (2%)
  matrix products  13.8 us (2%)
    ppermute x16, waiting for transfers between devices, across(): lax.ppermute(block, ('chip', 'ctx'), [(i, i ^ mask) for i in range(count)])  131 us
    pallas_call x3, Pallas kernels, ffn_chunk(): pl.pallas_call(functools.partial(ffn_kernel, geometry, out_geometry, firs...  126 us
    ppermute x28, waiting for transfers between devices, got(): lax.ppermute(block.astype(bf16), ('chip', 'ctx'), [(i, i ^ mask) for i in...  69.5 us
    pallas_call x5, Pallas kernels, row_call(): pl.pallas_call(body, grid=(steps,), in_specs=[pl.BlockSpec(memory_space=p...  68.7 us
    ppermute x28, starting transfers between devices, got(): lax.ppermute(block.astype(bf16), ('chip', 'ctx'), [(i, i ^ mask) for i in...  41.2 us
    ppermute x16, starting transfers between devices, across(): lax.ppermute(block, ('chip', 'ctx'), [(i, i ^ mask) for i in range(count)])  18.8 us
    all_gather x1, waiting for transfers between devices, fast_shards(): out_all = lax.all_gather(out_block, ('chip', 'ctx'))  14.9 us
    dot_general x2, matrix products, cross_cols(): lax.dot_general(left_operand, right_operand, (((1,), (1,)), ((), ())), pr...  13.8 us
  transfers between devices with their start and end apart: 61, of which 25 were waited for; matrix products, arithmetic and copies ran while one was open for 15% of the time, Pallas kernels for 26%

profile of v3, /device:TPU:0, one launch (start us, length us, event | category | flops | bytes accessed | tf_op | source)
XLA Modules:
  0.0 623.8 jit_solution(2595236186362464593)
XLA Ops:
  14.1 2.7 collective-permute-start.2
  18.5 4.0 collective-permute-done.2
  22.5 2.8 collective-permute-start.3
  27.6 17.4 %collective-permute-done.3 = bf16[2,400,256]{2,1,0:T(8,128)(2,1)S(1)} collective-permute-done((bf16[2,400,256]{2,1,0:T(8,128)(2,1)S(1)}, bf16[2,400,256]{2,1,0:T(8,128)(2,1)S(1)}, u32[]{:S(2)}, u32[]{:S(2)}) %collective-permute-start.3) | collective-permute-done | bytes 409632 | tf_op jit(solution)/shard_map/ppermute | solution.py:191
  50.2 9.9 %collective-permute-done.6 = bf16[1,384,384]{2,1,0:T(8,128)(2,1)S(1)} collective-permute-done((bf16[1,384,384]{2,1,0:T(8,128)(2,1)S(1)}, bf16[1,384,384]{2,1,0:T(8,128)(2,1)S(1)}, u32[]{:S(2)}, u32[]{:S(2)}) %collective-permute-start.6) | collective-permute-done | bytes 294944 | tf_op jit(solution)/shard_map/ppermute | solution.py:191
  63.6 14.9 %all-gather.6.cloned.1.call-done.refs_0_ = bf16[16,128,256]{2,1,0:T(8,128)(2,1)} async-done(((bf16[1,128,256]{2,1,0:T(8,128)(2,1)}), bf16[16,128,256]{2,1,0:T(8,128)(2,1)}) %all-gather.6.cloned.1.call-update) | async-done | bytes 1048592 | tf_op jit(solution)/shard_map/all_gather | solution.py:666
  78.5 2.4 shard_map.179.w_ref
  81.0 3.8 collective-permute-done.7.refs_1_
  85.0 4.8 shard_map.177
  91.3 4.0 pad_maximum_fusion.x_ref
  95.3 11.9 %shard_map.178 = (bf16[2048,1024]{1,0:T(8,128)(2,1)}, f32[2048,1536]{1,0:T(8,128)}) custom-call(bf16[2048,1024]{1,0:T(8,128)(2,1)} %pad_maximum_fusion.x_ref, f32[1,1024]{1,0:T(1,128)} %bitcast.154, bf16[1024,1536]{1,0:T(8,128)(2,1)} %get-tuple-element.79.w_ref), custom_call_target="tpu_custom_call" | custom-call | flops 65536 | bytes 65536 | tf_op jit(solution)/shard_map/pallas_call | solution.py:546
  108.1 2.9 collective-permute-start.10
  112.8 9.5 %shard_map.180 = (bf16[2048,512]{1,0:T(8,128)(2,1)}, f32[2048,512]{1,0:T(8,128)}, bf16[2048,1024]{1,0:T(8,128)(2,1)}) custom-call(f32[2048,1536]{1,0:T(8,128)} %get-tuple-element.80.projected_ref.gate_c_ref, bf16[4,2,512]{2,1,0:T(2,128)(2,1)} %copy-done.39, f32[8,512]{1,0:T(8,128)} %pad.14.taps_ref, bf16[512,1024]{1,0:T(8,128)(2,1)} %shard_map.179.w_ref), custom_call_target="tpu_custom_call" | custom-call | flops 65536 | bytes 65536 | tf_op jit(solution)/shard_map/pallas_call | solution.py:546
  124.8 52.5 %collective-permute-done.13 = bf16[2,384,384]{2,1,0:T(8,128)(2,1)S(1)} collective-permute-done((bf16[2,384,384]{2,1,0:T(8,128)(2,1)S(1)}, bf16[2,384,384]{2,1,0:T(8,128)(2,1)S(1)}, u32[]{:S(2)}, u32[]{:S(2)}) %collective-permute-start.13) | collective-permute-done | bytes 589856 | tf_op jit(solution)/shard_map/ppermute | solution.py:191
  180.6 12.0 %collective-permute-done.16 = bf16[4,192,384]{2,1,0:T(8,128)(2,1)S(1)} collective-permute-done((bf16[4,192,384]{2,1,0:T(8,128)(2,1)S(1)}, bf16[4,192,384]{2,1,0:T(8,128)(2,1)S(1)}, u32[]{:S(2)}, u32[]{:S(2)}) %collective-permute-start.16) | collective-permute-done | bytes 589856 | tf_op jit(solution)/shard_map/ppermute | solution.py:191
  200.6 9.7 %shard_map.181 = (f32[2048,1024]{1,0:T(8,128)}, bf16[2048,1024]{1,0:T(8,128)(2,1)}) custom-call(bf16[2048,1024]{1,0:T(8,128)(2,1)} %pad_maximum_fusion.x_ref, bf16[2048,1024]{1,0:T(8,128)(2,1)} %get-tuple-element.81.branch_ref, bf16[2048,1024]{1,0:T(8,128)(2,1)} %copy-done.18, f32[1,1024]{1,0:T(1,128)} %bitcast.148), custom_call_target="tpu_custom_call" | custom-call | flops 65536 | bytes 65536 | tf_op jit(solution)/shard_map/pallas_call | solution.py:546
  210.3 19.5 %collective-permute-done.17.refs_3_ = bf16[8,192,384]{2,1,0:T(8,128)(2,1)} collective-permute-done((bf16[8,192,384]{2,1,0:T(8,128)(2,1)S(1)}, bf16[8,192,384]{2,1,0:T(8,128)(2,1)}, u32[]{:S(2)}, u32[]{:S(2)}) %collective-permute-start.17) | collective-permute-done | bytes 1179680 | tf_op jit(solution)/shard_map/ppermute | solution.py:191
  229.8 41.2 %shard_map.182 = (f32[2048,1024]{1,0:T(8,128)}, f32[2048,1024]{1,0:T(8,128)}, bf16[8,192,384]{2,1,0:T(8,128)(2,1)}, bf16[8,192,384]{2,1,0:T(8,128)(2,1)}, bf16[8...) custom-call(s32[1]{0:T(128)} %bitcast.1.own_ref, bf16[2048,1024]{1,0:T(8,128)(2,1)} %get-tuple-element.83.n_ref, ...), custom_call_target="tpu_custom_call" | custom-call | flops 65536 | bytes 65536 | tf_op jit(solution)/shard_map/pallas_call | solution.py:372
  273.0 42.5 %shard_map.183 = (f32[2048,1024]{1,0:T(8,128)}, f32[2048,1024]{1,0:T(8,128)}, bf16[8,192,384]{2,1,0:T(8,128)(2,1)}, bf16[8,192,384]{2,1,0:T(8,128)(2,1)}, bf16[8...) custom-call(s32[1]{0:T(128)} %bitcast.1.own_ref, ...), custom_call_target="tpu_custom_call", output_to_operand_aliasing={{0}: (4, {}), {1}: (5, {})} | custom-call | flops 65536 | bytes 65536 | tf_op jit(solution)/shard_map/pallas_call | solution.py:372
  315.5 42.2 %shard_map.184 = (f32[2048,1024]{1,0:T(8,128)}, f32[2048,1024]{1,0:T(8,128)}, bf16[8,192,384]{2,1,0:T(8,128)(2,1)}, bf16[8,192,384]{2,1,0:T(8,128)(2,1)}, bf16[8...) custom-call(s32[1]{0:T(128)} %bitcast.1.own_ref, ...), custom_call_target="tpu_custom_call", output_to_operand_aliasing={{0}: (4, {}), {1}: (5, {})} | custom-call | flops 65536 | bytes 65536 | tf_op jit(solution)/shard_map/pallas_call | solution.py:372
  357.8 6.2 convert_element_type.188
  368.3 3.9 slice.536
  376.3 6.5 %collective-permute-done.31 = bf16[4,192,384]{2,1,0:T(8,128)(2,1)} collective-permute-done((bf16[4,192,384]{2,1,0:T(8,128)(2,1)S(1)}, bf16[4,192,384]{2,1,0:T(8,128)(2,1)}, u32[]{:S(2)}, u32[]{:S(2)}) %collective-permute-start.31) | collective-permute-done | bytes 589856 | tf_op jit(solution)/shard_map/ppermute | solution.py:238
  384.8 5.6 collective-permute-done.33
  394.3 21.5 %collective-permute-done.37 = bf16[8,192,384]{2,1,0:T(8,128)(2,1)} collective-permute-done((bf16[8,192,384]{2,1,0:T(8,128)(2,1)}, bf16[8,192,384]{2,1,0:T(8,128)(2,1)}, u32[]{:S(2)}, u32[]{:S(2)}) %collective-permute-start.37) | collective-permute-done | bytes 1179680 | tf_op jit(solution)/shard_map/ppermute | solution.py:238
  416.5 4.3 collective-permute-start.34
  428.4 5.4 add_convert_fusion
  433.8 19.5 %shard_map.185 = (f32[1024,1024]{1,0:T(8,128)}, f32[2048,512]{1,0:T(8,128)}, bf16[2048,512]{1,0:T(8,128)(2,1)}, bf16[512,1024]{1,0:T(8,128)(2,1)}, f32[1,1024]{1,0:T(1,128)}) custom-call(f32[2048,1024]{1,0:T(8,128)} %get-tuple-element.96.gn_ref, bf16[2048,1024]{1,0:T(8,128)(2,1)} %collective-permute-done.19.got_ref, ...), custom_call_target="tpu_custom_call" | custom-call | flops 65536 | bytes 65536 | tf_op jit(solution)/shard_map/pallas_call | solution.py:546
  453.2 2.5 convert.47
  472.4 2.6 collective-permute-start.47
  475.1 2.8 reshape.232
  477.9 2.4 copy.88
  480.9 18.1 %shard_map.186 = (bf16[2048,1536]{1,0:T(8,128)(2,1)}, f32[8,512]{1,0:T(8,128)}, bf16[8,192,256]{2,1,0:T(8,128)(2,1)}, bf16[8,192,256]{2,1,0:T(8,128)(2,1)}, bf16...) custom-call(s32[1]{0:T(128)} %bitcast.1.own_ref, f32[2048,512]{1,0:T(8,128)} %get-tuple-element.100.grad_conv_ref, ...), custom_call_target="tpu_custom_call" | custom-call | flops 65536 | bytes 65536 | tf_op jit(solution)/shard_map/pallas_call | solution.py:546
  499.1 7.7 %fusion.12 = bf16[1024,1024]{1,0:T(8,128)(2,1)} fusion(bf16[1024,1536]{1,0:T(8,128)(2,1)} %get-tuple-element.79.w_ref, bf16[2048,1536]{1,0:T(8,128)(2,1)} %get-tuple-element.105), kind=kOutput, calls=%fused_computation.31 | convolution fusion | flops 3222274048 | bytes 8388608 | tf_op jit(solution)/shard_map/dot_general | solution.py:29
  515.9 11.1 %collective-permute-done.24 = bf16[8,192,256]{2,1,0:T(8,128)(2,1)S(1)} collective-permute-done((bf16[8,192,256]{2,1,0:T(8,128)(2,1)}, bf16[8,192,256]{2,1,0:T(8,128)(2,1)S(1)}, u32[]{:S(2)}, u32[]{:S(2)}) %collective-permute-start.24) | collective-permute-done | bytes 786464 | tf_op jit(solution)/shard_map/ppermute | solution.py:238
  528.6 5.6 collective-permute-done.22
  536.3 3.9 collective-permute-done.48
  541.2 4.2 collective-permute-done.25
  545.7 2.9 collective-permute-start.26
  548.9 9.6 %collective-permute-done.26 = bf16[2,384,256]{2,1,0:T(8,128)(2,1)S(1)} collective-permute-done((bf16[2,384,256]{2,1,0:T(8,128)(2,1)S(1)}, bf16[2,384,256]{2,1,0:T(8,128)(2,1)S(1)}, u32[]{:S(2)}, u32[]{:S(2)}) %collective-permute-start.26) | collective-permute-done | bytes 393248 | tf_op jit(solution)/shard_map/ppermute | solution.py:238
  559.7 3.8 collective-permute-start.50
  565.8 6.0 collective-permute-start.28
  574.7 6.2 fusion.5
  581.0 3.6 collective-permute-done.52
  586.4 2.9 collective-permute-done.53
  593.1 3.6 collective-permute-done.55
  596.9 5.5 fusion.2
  608.2 2.4 concatenate.135
  (354 shorter events, 117.2 us)
Async XLA Ops:
  7.2 71.3 %all-gather.6.cloned.1.call-start = ((), (), s32[]{:S(2)}) async-start(), calls=%async_computation.1 | async-start | bytes 1114112 | tf_op jit(solution)/shard_map/all_gather | solution.py:666
  8.8 264.2 %all-gather.10.cloned.1.call-start = ((), (), s32[]{:S(2)}) async-start(), calls=%async_computation.4 | async-start | bytes 5013504 | tf_op jit(solution)/shard_map/all_gather | solution.py:679
  22.5 22.4 %collective-permute-start.3 = (bf16[2,400,256]{2,1,0:T(8,128)(2,1)S(1)}, bf16[2,400,256]{2,1,0:T(8,128)(2,1)S(1)}, u32[]{:S(2)}, u32[]{:S(2)}) collective-permute-start(bf16[2,400,256]{2,1,0:T(8,128)(2,1)S(1)} %pad_maximum_fusion.16), channel_id=1, source_target_pairs={{0,16},{1,17},{4,20},{5,21},{8,24},{9,25},{12,28},{13,29},{16,0},{... | collective-permute-start | bytes 1228808 | tf_op jit(solution)/shard_map/ppermute | solution.py:191
  46.0 269.5 %all-gather.8.cloned.1.call-start = ((), (), s32[]{:S(2)}) async-start(), calls=%async_computation.3 | async-start | bytes 5013504 | tf_op jit(solution)/shard_map/all_gather | solution.py:679
  46.7 543.5 %reduce-scatter.2.cloned.1.call-start = ((), (), s32[]{:S(2)}) async-start(), calls=%async_computation.2 | async-start | bytes 1114112 | tf_op jit(solution)/shard_map/reduce_scatter | solution.py:851
  46.8 44.5 %collective-permute-start = (bf16[1024,1024]{1,0:T(8,128)(2,1)S(1)}, bf16[1024,1024]{1,0:T(8,128)(2,1)}, u32[]{:S(2)}, u32[]{:S(2)}) collective-permute-start(bf16[1024,1024]{1,0:T(8,128)(2,1)S(1)} %bitcast.115), channel_id=1, source_target_pairs={{0,2},{2,0},{1,3},{3,1},{4,6},{6,4},{5,7},{7,5},{8,10},{10,8},{9,1... | collective-permute-start | bytes 6291464 | tf_op jit(solution)/shard_map/ppermute | solution.py:186
  46.9 14.0 %collective-permute-start.8 = (bf16[4,208,256]{2,1,0:T(8,128)(2,1)S(1)}, bf16[4,208,256]{2,1,0:T(8,128)(2,1)S(1)}, u32[]{:S(2)}, u32[]{:S(2)}) collective-permute-start(bf16[4,208,256]{2,1,0:T(8,128)(2,1)S(1)} %slice.370), channel_id=1, source_target_pairs={{0,1},{1,0},{4,5},{5,4},{8,9},{9,8},{12,13},{13,12},{16,17},{17,16... | collective-permute-start | bytes 1277960 | tf_op jit(solution)/shard_map/ppermute | solution.py:191
  48.5 11.7 %collective-permute-start.4 = (bf16[4,192,256]{2,1,0:T(8,128)(2,1)S(1)}, bf16[4,192,256]{2,1,0:T(8,128)(2,1)S(1)}, u32[]{:S(2)}, u32[]{:S(2)}) collective-permute-start(bf16[4,192,256]{2,1,0:T(8,128)(2,1)S(1)} %slice.364), channel_id=1, source_target_pairs={{0,4},{1,5},{4,0},{5,1},{8,12},{9,13},{12,8},{13,9},{16,20},{17,21... | collective-permute-start | bytes 1179656 | tf_op jit(solution)/shard_map/ppermute | solution.py:191
  61.0 24.0 %collective-permute-start.9 = (bf16[8,208,256]{2,1,0:T(8,128)(2,1)S(1)}, bf16[8,208,256]{2,1,0:T(8,128)(2,1)}, u32[]{:S(2)}, u32[]{:S(2)}) collective-permute-start(bf16[8,208,256]{2,1,0:T(8,128)(2,1)S(1)} %pad_maximum_fusion.9.refs_2_), channel_id=1, source_target_pairs={{0,4},{1,5},{4,0},{5,1},{8,12},{9,13},{12,8},{13,9},{16,20},{17,21... | collective-permute-start | bytes 2555912 | tf_op jit(solution)/shard_map/ppermute | solution.py:191
  62.8 22.0 %collective-permute-start.7 = (bf16[8,192,256]{2,1,0:T(8,128)(2,1)}, bf16[8,192,256]{2,1,0:T(8,128)(2,1)}, u32[]{:S(2)}, u32[]{:S(2)}) collective-permute-start(bf16[8,192,256]{2,1,0:T(8,128)(2,1)} %pad_maximum_fusion.12.refs_0_), channel_id=1, source_target_pairs={{0,1},{1,0},{4,5},{5,4},{8,9},{9,8},{12,13},{13,12},{16,17},{17,16... | collective-permute-start | bytes 2359304 | tf_op jit(solution)/shard_map/ppermute | solution.py:191
  122.3 76.3 %collective-permute-start.11 = (bf16[2048,1024]{1,0:T(8,128)(2,1)}, bf16[2048,1024]{1,0:T(8,128)(2,1)S(1)}, u32[]{:S(2)}, u32[]{:S(2)}) collective-permute-start(bf16[2048,1024]{1,0:T(8,128)(2,1)} %get-tuple-element.81.branch_ref), channel_id=1, source_target_pairs={{0,2},{2,0},{1,3},{3,1},{4,6},{6,4},{5,7},{7,5},{8,10},{10,8},{9,1... | collective-permute-start | bytes 12582920 | tf_op jit(solution)/shard_map/ppermute | solution.py:186
  122.4 54.9 %collective-permute-start.13 = (bf16[2,384,384]{2,1,0:T(8,128)(2,1)S(1)}, bf16[2,384,384]{2,1,0:T(8,128)(2,1)S(1)}, u32[]{:S(2)}, u32[]{:S(2)}) collective-permute-start(bf16[2,384,384]{2,1,0:T(8,128)(2,1)S(1)} %pad_maximum_fusion.13), channel_id=1, source_target_pairs={{0,16},{1,17},{4,20},{5,21},{8,24},{9,25},{12,28},{13,29},{16,0},{... | collective-permute-start | bytes 1769480 | tf_op jit(solution)/shard_map/ppermute | solution.py:191
  124.5 71.7 %collective-permute-start.12 = (bf16[1024,1024]{1,0:T(8,128)(2,1)}, bf16[1024,1024]{1,0:T(8,128)(2,1)S(1)}, u32[]{:S(2)}, u32[]{:S(2)}) collective-permute-start(bf16[1024,1024]{1,0:T(8,128)(2,1)} %bitcast.127), channel_id=1, source_target_pairs={{0,2},{2,0},{1,3},{3,1},{4,6},{6,4},{5,7},{7,5},{8,10},{10,8},{9,1... | collective-permute-start | bytes 6291464 | tf_op jit(solution)/shard_map/ppermute | solution.py:186
  177.6 15.0 %collective-permute-start.16 = (bf16[4,192,384]{2,1,0:T(8,128)(2,1)S(1)}, bf16[4,192,384]{2,1,0:T(8,128)(2,1)S(1)}, u32[]{:S(2)}, u32[]{:S(2)}) collective-permute-start(bf16[4,192,384]{2,1,0:T(8,128)(2,1)S(1)} %get-tuple-element.146), channel_id=1, source_target_pairs={{0,1},{1,0},{4,5},{5,4},{8,9},{9,8},{12,13},{13,12},{16,17},{17,16... | collective-permute-start | bytes 1769480 | tf_op jit(solution)/shard_map/ppermute | solution.py:191
  179.8 14.0 %collective-permute-start.14 = (bf16[4,192,384]{2,1,0:T(8,128)(2,1)S(1)}, bf16[4,192,384]{2,1,0:T(8,128)(2,1)S(1)}, u32[]{:S(2)}, u32[]{:S(2)}) collective-permute-start(bf16[4,192,384]{2,1,0:T(8,128)(2,1)S(1)} %get-tuple-element.147), channel_id=1, source_target_pairs={{0,4},{1,5},{4,0},{5,1},{8,12},{9,13},{12,8},{13,9},{16,20},{17,21... | collective-permute-start | bytes 1769480 | tf_op jit(solution)/shard_map/ppermute | solution.py:191
  192.7 37.0 %collective-permute-start.17 = (bf16[8,192,384]{2,1,0:T(8,128)(2,1)S(1)}, bf16[8,192,384]{2,1,0:T(8,128)(2,1)}, u32[]{:S(2)}, u32[]{:S(2)}) collective-permute-start(bf16[8,192,384]{2,1,0:T(8,128)(2,1)S(1)} %pad_maximum_fusion.7.refs_2_), channel_id=1, source_target_pairs={{0,4},{1,5},{4,0},{5,1},{8,12},{9,13},{12,8},{13,9},{16,20},{17,21... | collective-permute-start | bytes 3538952 | tf_op jit(solution)/shard_map/ppermute | solution.py:191
  195.0 34.8 %collective-permute-start.15 = (bf16[8,192,384]{2,1,0:T(8,128)(2,1)}, bf16[8,192,384]{2,1,0:T(8,128)(2,1)}, u32[]{:S(2)}, u32[]{:S(2)}) collective-permute-start(bf16[8,192,384]{2,1,0:T(8,128)(2,1)} %pad_maximum_fusion.6.refs_0_), channel_id=1, source_target_pairs={{0,1},{1,0},{4,5},{5,4},{8,9},{9,8},{12,13},{13,12},{16,17},{17,16... | collective-permute-start | bytes 3538952 | tf_op jit(solution)/shard_map/ppermute | solution.py:191
  271.0 44.5 %collective-permute-start.30 = (bf16[8,192,384]{2,1,0:T(8,128)(2,1)}, bf16[8,192,384]{2,1,0:T(8,128)(2,1)}, u32[]{:S(2)}, u32[]{:S(2)}) collective-permute-start(bf16[8,192,384]{2,1,0:T(8,128)(2,1)} %get-tuple-element.111), channel_id=1, source_target_pairs={{0,1},{1,0},{4,5},{5,4},{8,9},{9,8},{12,13},{13,12},{16,17},{17,16... | collective-permute-start | bytes 3538952 | tf_op jit(solution)/shard_map/ppermute | solution.py:238
  272.3 43.2 %collective-permute-start.32 = (bf16[8,192,384]{2,1,0:T(8,128)(2,1)}, bf16[8,192,384]{2,1,0:T(8,128)(2,1)S(1)}, u32[]{:S(2)}, u32[]{:S(2)}) collective-permute-start(bf16[8,192,384]{2,1,0:T(8,128)(2,1)} %get-tuple-element.115), channel_id=1, source_target_pairs={{0,4},{1,5},{4,0},{5,1},{8,12},{9,13},{12,8},{13,9},{16,20},{17,21... | collective-permute-start | bytes 3538952 | tf_op jit(solution)/shard_map/ppermute | solution.py:238
  363.9 63.8 %collective-permute-start.19 = (bf16[2048,1024]{1,0:T(8,128)(2,1)}, bf16[2048,1024]{1,0:T(8,128)(2,1)}, u32[]{:S(2)}, u32[]{:S(2)}) collective-permute-start(bf16[2048,1024]{1,0:T(8,128)(2,1)} %convert_element_type.188), channel_id=1, source_target_pairs={{0,2},{2,0},{1,3},{3,1},{4,6},{6,4},{5,7},{7,5},{8,10},{10,8},{9,1... | collective-permute-start | bytes 12582920 | tf_op jit(solution)/shard_map/ppermute | solution.py:186
  366.9 15.9 %collective-permute-start.31 = (bf16[4,192,384]{2,1,0:T(8,128)(2,1)S(1)}, bf16[4,192,384]{2,1,0:T(8,128)(2,1)}, u32[]{:S(2)}, u32[]{:S(2)}) collective-permute-start(bf16[4,192,384]{2,1,0:T(8,128)(2,1)S(1)} %slice.542), channel_id=1, source_target_pairs={{0,4},{1,5},{4,0},{5,1},{8,12},{9,13},{12,8},{13,9},{16,20},{17,21... | collective-permute-start | bytes 1769480 | tf_op jit(solution)/shard_map/ppermute | solution.py:238
  372.2 54.5 %collective-permute-start.18 = (bf16[1024,1024]{1,0:T(8,128)(2,1)}, bf16[1024,1024]{1,0:T(8,128)(2,1)}, u32[]{:S(2)}, u32[]{:S(2)}) collective-permute-start(bf16[1024,1024]{1,0:T(8,128)(2,1)} %slice.536), channel_id=1, source_target_pairs={{0,2},{2,0},{1,3},{3,1},{4,6},{6,4},{5,7},{7,5},{8,10},{10,8},{9,1... | collective-permute-start | bytes 6291464 | tf_op jit(solution)/shard_map/ppermute | solution.py:186
  374.2 16.2 %collective-permute-start.33 = (bf16[4,192,384]{2,1,0:T(8,128)(2,1)S(1)}, bf16[4,192,384]{2,1,0:T(8,128)(2,1)S(1)}, u32[]{:S(2)}, u32[]{:S(2)}) collective-permute-start(bf16[4,192,384]{2,1,0:T(8,128)(2,1)S(1)} %slice.541), channel_id=1, source_target_pairs={{0,1},{1,0},{4,5},{5,4},{8,9},{9,8},{12,13},{13,12},{16,17},{17,16... | collective-permute-start | bytes 1769480 | tf_op jit(solution)/shard_map/ppermute | solution.py:238
  375.0 40.8 %collective-permute-start.37 = (bf16[8,192,384]{2,1,0:T(8,128)(2,1)}, bf16[8,192,384]{2,1,0:T(8,128)(2,1)}, u32[]{:S(2)}, u32[]{:S(2)}) collective-permute-start(bf16[8,192,384]{2,1,0:T(8,128)(2,1)} %get-tuple-element.122), channel_id=1, source_target_pairs={{0,1},{1,0},{4,5},{5,4},{8,9},{9,8},{12,13},{13,12},{16,17},{17,16... | collective-permute-start | bytes 3538952 | tf_op jit(solution)/shard_map/ppermute | solution.py:238
  382.8 33.7 %collective-permute-start.39 = (bf16[8,192,384]{2,1,0:T(8,128)(2,1)}, bf16[8,192,384]{2,1,0:T(8,128)(2,1)}, u32[]{:S(2)}, u32[]{:S(2)}) collective-permute-start(bf16[8,192,384]{2,1,0:T(8,128)(2,1)} %get-tuple-element.126), channel_id=1, source_target_pairs={{0,4},{1,5},{4,0},{5,1},{8,12},{9,13},{12,8},{13,9},{16,20},{17,21... | collective-permute-start | bytes 3538952 | tf_op jit(solution)/shard_map/ppermute | solution.py:238
  390.4 75.2 %collective-permute-start.44 = (bf16[8,192,384]{2,1,0:T(8,128)(2,1)}, bf16[8,192,384]{2,1,0:T(8,128)(2,1)}, u32[]{:S(2)}, u32[]{:S(2)}) collective-permute-start(bf16[8,192,384]{2,1,0:T(8,128)(2,1)} %get-tuple-element.131), channel_id=1, source_target_pairs={{0,1},{1,0},{4,5},{5,4},{8,9},{9,8},{12,13},{13,12},{16,17},{17,16... | collective-permute-start | bytes 3538952 | tf_op jit(solution)/shard_map/ppermute | solution.py:238
  415.8 53.5 %collective-permute-start.46 = (bf16[8,192,384]{2,1,0:T(8,128)(2,1)}, bf16[8,192,384]{2,1,0:T(8,128)(2,1)}, u32[]{:S(2)}, u32[]{:S(2)}) collective-permute-start(bf16[8,192,384]{2,1,0:T(8,128)(2,1)} %get-tuple-element.135), channel_id=1, source_target_pairs={{0,4},{1,5},{4,0},{5,1},{8,12},{9,13},{12,8},{13,9},{16,20},{17,21... | collective-permute-start | bytes 3538952 | tf_op jit(solution)/shard_map/ppermute | solution.py:238
  416.5 39.2 %collective-permute-start.34 = (bf16[2,384,384]{2,1,0:T(8,128)(2,1)}, bf16[2,384,384]{2,1,0:T(8,128)(2,1)}, u32[]{:S(2)}, u32[]{:S(2)}) collective-permute-start(bf16[2,384,384]{2,1,0:T(8,128)(2,1)} %fusion.25), channel_id=1, source_target_pairs={{0,8},{1,9},{4,12},{5,13},{24,16},{25,17},{28,20},{29,21},{2,10},{... | collective-permute-start | bytes 1769480 | tf_op jit(solution)/shard_map/ppermute | solution.py:238
  426.8 32.7 %collective-permute-start.38 = (bf16[4,192,384]{2,1,0:T(8,128)(2,1)}, bf16[4,192,384]{2,1,0:T(8,128)(2,1)S(1)}, u32[]{:S(2)}, u32[]{:S(2)}) collective-permute-start(bf16[4,192,384]{2,1,0:T(8,128)(2,1)} %slice.540), channel_id=1, source_target_pairs={{0,4},{1,5},{4,0},{5,1},{8,12},{9,13},{12,8},{13,9},{16,20},{17,21... | collective-permute-start | bytes 1769480 | tf_op jit(solution)/shard_map/ppermute | solution.py:238
  427.8 33.2 %collective-permute-start.40 = (bf16[4,192,384]{2,1,0:T(8,128)(2,1)}, bf16[4,192,384]{2,1,0:T(8,128)(2,1)}, u32[]{:S(2)}, u32[]{:S(2)}) collective-permute-start(bf16[4,192,384]{2,1,0:T(8,128)(2,1)} %slice.539), channel_id=1, source_target_pairs={{0,1},{1,0},{4,5},{5,4},{8,9},{9,8},{12,13},{13,12},{16,17},{17,16... | collective-permute-start | bytes 1769480 | tf_op jit(solution)/shard_map/ppermute | solution.py:238
  455.7 24.6 %collective-permute-start.20 = (bf16[4,2,512]{2,1,0:T(2,128)(2,1)S(1)}, bf16[4,2,512]{2,1,0:T(2,128)(2,1)S(1)}, u32[]{:S(2)}, u32[]{:S(2)}) collective-permute-start(bf16[4,2,512]{2,1,0:T(2,128)(2,1)S(1)} %slice.382), channel_id=1, source_target_pairs={{1,0},{3,2},{5,4},{7,6},{9,8},{11,10},{13,12},{15,14},{17,16},{19,... | collective-permute-start | bytes 24584 | tf_op jit(solution)/shard_map/ppermute | solution.py:19
  459.5 48.7 %collective-permute-start.35 = (bf16[2,384,384]{2,1,0:T(8,128)(2,1)}, bf16[2,384,384]{2,1,0:T(8,128)(2,1)}, u32[]{:S(2)}, u32[]{:S(2)}) collective-permute-start(bf16[2,384,384]{2,1,0:T(8,128)(2,1)} %add_convert_fusion.3), channel_id=1, source_target_pairs={{8,16},{9,17},{12,20},{13,21},{16,8},{17,9},{20,12},{21,13},{10,18... | collective-permute-start | bytes 1769480 | tf_op jit(solution)/shard_map/ppermute | solution.py:238
  463.4 47.4 %collective-permute-start.41 = (bf16[2,384,384]{2,1,0:T(8,128)(2,1)}, bf16[2,384,384]{2,1,0:T(8,128)(2,1)}, u32[]{:S(2)}, u32[]{:S(2)}) collective-permute-start(bf16[2,384,384]{2,1,0:T(8,128)(2,1)} %fusion.26), channel_id=1, source_target_pairs={{0,8},{1,9},{4,12},{5,13},{24,16},{25,17},{28,20},{29,21},{2,10},{... | collective-permute-start | bytes 1769480 | tf_op jit(solution)/shard_map/ppermute | solution.py:238
  468.1 44.4 %collective-permute-start.45 = (bf16[4,192,384]{2,1,0:T(8,128)(2,1)}, bf16[4,192,384]{2,1,0:T(8,128)(2,1)}, u32[]{:S(2)}, u32[]{:S(2)}) collective-permute-start(bf16[4,192,384]{2,1,0:T(8,128)(2,1)} %slice.538), channel_id=1, source_target_pairs={{0,4},{1,5},{4,0},{5,1},{8,12},{9,13},{12,8},{13,9},{16,20},{17,21... | collective-permute-start | bytes 1769480 | tf_op jit(solution)/shard_map/ppermute | solution.py:238
  472.4 40.3 %collective-permute-start.47 = (bf16[4,192,384]{2,1,0:T(8,128)(2,1)}, bf16[4,192,384]{2,1,0:T(8,128)(2,1)}, u32[]{:S(2)}, u32[]{:S(2)}) collective-permute-start(bf16[4,192,384]{2,1,0:T(8,128)(2,1)} %slice.537), channel_id=1, source_target_pairs={{0,1},{1,0},{4,5},{5,4},{8,9},{9,8},{12,13},{13,12},{16,17},{17,16... | collective-permute-start | bytes 1769480 | tf_op jit(solution)/shard_map/ppermute | solution.py:238
  506.9 20.1 %collective-permute-start.24 = (bf16[8,192,256]{2,1,0:T(8,128)(2,1)}, bf16[8,192,256]{2,1,0:T(8,128)(2,1)S(1)}, u32[]{:S(2)}, u32[]{:S(2)}) collective-permute-start(bf16[8,192,256]{2,1,0:T(8,128)(2,1)} %get-tuple-element.108), channel_id=1, source_target_pairs={{0,4},{1,5},{4,0},{5,1},{8,12},{9,13},{12,8},{13,9},{16,20},{17,21... | collective-permute-start | bytes 2359304 | tf_op jit(solution)/shard_map/ppermute | solution.py:238
  508.2 26.0 %collective-permute-start.22 = (bf16[8,192,256]{2,1,0:T(8,128)(2,1)}, bf16[8,192,256]{2,1,0:T(8,128)(2,1)S(1)}, u32[]{:S(2)}, u32[]{:S(2)}) collective-permute-start(bf16[8,192,256]{2,1,0:T(8,128)(2,1)} %get-tuple-element.104), channel_id=1, source_target_pairs={{0,1},{1,0},{4,5},{5,4},{8,9},{9,8},{12,13},{13,12},{16,17},{17,16... | collective-permute-start | bytes 2359304 | tf_op jit(solution)/shard_map/ppermute | solution.py:238
  511.2 62.0 %collective-permute-start.21 = (bf16[1024,1024]{1,0:T(8,128)(2,1)S(1)}, bf16[1024,1024]{1,0:T(8,128)(2,1)S(1)}, u32[]{:S(2)}, u32[]{:S(2)}) collective-permute-start(bf16[1024,1024]{1,0:T(8,128)(2,1)S(1)} %copy-done.46), channel_id=1, source_target_pairs={{0,2},{2,0},{1,3},{3,1},{4,6},{6,4},{5,7},{7,5},{8,10},{10,8},{9,1... | collective-permute-start | bytes 6291464 | tf_op jit(solution)/shard_map/ppermute | solution.py:186
  512.5 22.1 %collective-permute-start.36 = (bf16[1,384,384]{2,1,0:T(8,128)(2,1)S(1)}, bf16[1,384,384]{2,1,0:T(8,128)(2,1)S(1)}, u32[]{:S(2)}, u32[]{:S(2)}) collective-permute-start(bf16[1,384,384]{2,1,0:T(8,128)(2,1)S(1)} %slice.547), channel_id=1, source_target_pairs={{0,8},{1,9},{4,12},{5,13},{8,0},{9,1},{12,4},{13,5},{16,24},{17,25... | collective-permute-start | bytes 884744 | tf_op jit(solution)/shard_map/ppermute | solution.py:238
  512.7 28.4 %collective-permute-start.42 = (bf16[2,384,384]{2,1,0:T(8,128)(2,1)S(1)}, bf16[2,384,384]{2,1,0:T(8,128)(2,1)S(1)}, u32[]{:S(2)}, u32[]{:S(2)}) collective-permute-start(bf16[2,384,384]{2,1,0:T(8,128)(2,1)S(1)} %add_convert_fusion.2), channel_id=1, source_target_pairs={{8,16},{9,17},{12,20},{13,21},{16,8},{17,9},{20,12},{21,13},{10,18... | collective-permute-start | bytes 1769480 | tf_op jit(solution)/shard_map/ppermute | solution.py:238
  527.0 13.2 %collective-permute-start.48 = (bf16[2,384,384]{2,1,0:T(8,128)(2,1)S(1)}, bf16[2,384,384]{2,1,0:T(8,128)(2,1)S(1)}, u32[]{:S(2)}, u32[]{:S(2)}) collective-permute-start(bf16[2,384,384]{2,1,0:T(8,128)(2,1)S(1)} %fusion.27), channel_id=1, source_target_pairs={{0,8},{1,9},{4,12},{5,13},{24,16},{25,17},{28,20},{29,21},{2,10},{... | collective-permute-start | bytes 1769480 | tf_op jit(solution)/shard_map/ppermute | solution.py:238
  534.2 11.2 %collective-permute-start.25 = (bf16[4,192,256]{2,1,0:T(8,128)(2,1)S(1)}, bf16[4,192,256]{2,1,0:T(8,128)(2,1)S(1)}, u32[]{:S(2)}, u32[]{:S(2)}) collective-permute-start(bf16[4,192,256]{2,1,0:T(8,128)(2,1)S(1)} %slice.543), channel_id=1, source_target_pairs={{0,1},{1,0},{4,5},{5,4},{8,9},{9,8},{12,13},{13,12},{16,17},{17,16... | collective-permute-start | bytes 1179656 | tf_op jit(solution)/shard_map/ppermute | solution.py:238
  540.4 19.0 %collective-permute-start.49 = (bf16[2,384,384]{2,1,0:T(8,128)(2,1)S(1)}, bf16[2,384,384]{2,1,0:T(8,128)(2,1)S(1)}, u32[]{:S(2)}, u32[]{:S(2)}) collective-permute-start(bf16[2,384,384]{2,1,0:T(8,128)(2,1)S(1)} %add_convert_fusion.1), channel_id=1, source_target_pairs={{8,16},{9,17},{12,20},{13,21},{16,8},{17,9},{20,12},{21,13},{10,18... | collective-permute-start | bytes 1769480 | tf_op jit(solution)/shard_map/ppermute | solution.py:238
  545.7 12.9 %collective-permute-start.26 = (bf16[2,384,256]{2,1,0:T(8,128)(2,1)S(1)}, bf16[2,384,256]{2,1,0:T(8,128)(2,1)S(1)}, u32[]{:S(2)}, u32[]{:S(2)}) collective-permute-start(bf16[2,384,256]{2,1,0:T(8,128)(2,1)S(1)} %fusion.28), channel_id=1, source_target_pairs={{0,8},{1,9},{4,12},{5,13},{24,16},{25,17},{28,20},{29,21},{2,10},{... | collective-permute-start | bytes 1179656 | tf_op jit(solution)/shard_map/ppermute | solution.py:238
  548.8 16.1 %collective-permute-start.43 = (bf16[1,384,384]{2,1,0:T(8,128)(2,1)S(1)}, bf16[1,384,384]{2,1,0:T(8,128)(2,1)S(1)}, u32[]{:S(2)}, u32[]{:S(2)}) collective-permute-start(bf16[1,384,384]{2,1,0:T(8,128)(2,1)S(1)} %slice.546), channel_id=1, source_target_pairs={{0,8},{1,9},{4,12},{5,13},{8,0},{9,1},{12,4},{13,5},{16,24},{17,25... | collective-permute-start | bytes 884744 | tf_op jit(solution)/shard_map/ppermute | solution.py:238
  559.7 12.1 %collective-permute-start.50 = (bf16[1,384,384]{2,1,0:T(8,128)(2,1)S(1)}, bf16[1,384,384]{2,1,0:T(8,128)(2,1)S(1)}, u32[]{:S(2)}, u32[]{:S(2)}) collective-permute-start(bf16[1,384,384]{2,1,0:T(8,128)(2,1)S(1)} %slice.545), channel_id=1, source_target_pairs={{0,8},{1,9},{4,12},{5,13},{8,0},{9,1},{12,4},{13,5},{16,24},{17,25... | collective-permute-start | bytes 884744 | tf_op jit(solution)/shard_map/ppermute | solution.py:238
  565.8 37.1 %collective-permute-start.28 = (bf16[1,384,256]{2,1,0:T(8,128)(2,1)}, bf16[1,384,256]{2,1,0:T(8,128)(2,1)}, u32[]{:S(2)}, u32[]{:S(2)}) collective-permute-start(bf16[1,384,256]{2,1,0:T(8,128)(2,1)} %slice.548), channel_id=1, source_target_pairs={{0,8},{1,9},{4,12},{5,13},{8,0},{9,1},{12,4},{13,5},{16,24},{17,25... | collective-permute-start | bytes 589832 | tf_op jit(solution)/shard_map/ppermute | solution.py:238
  581.0 27.3 %collective-permute-start.51 = (f32[3,2,64,384]{3,2,1,0:T(8,128)}, f32[3,2,64,384]{3,2,1,0:T(8,128)}, u32[]{:S(2)}, u32[]{:S(2)}) collective-permute-start(f32[3,2,64,384]{3,2,1,0:T(8,128)} %get-tuple-element.145), channel_id=1, source_target_pairs={{0,2},{2,0},{1,3},{3,1},{4,6},{6,4},{5,7},{7,5},{8,10},{10,8},{9,1... | collective-permute-start | bytes 1769480 | tf_op jit(solution)/shard_map/ppermute | solution.py:186
  (64 other events, 475.3 us)
Sparse Core Ops, SparseCore 0:
  11.4 67.0 all-gather.5
  81.9 96.1 all-gather.9
  181.4 90.8 all-gather.7
  480.5 78.3 reduce-scatter.1

commit v4 on v3

--- a/solution.py
+++ b/solution.py
@@ -229,38 +229,49 @@
     return parts
 
 
-def scatter_sum(parts, ties=()):
+def scatter_steps(parts):
     far, first_order, second_order = bit_masks()
     n_slots = lax.axis_size("chip") * lax.axis_size("ctx")
-    ties = dict(enumerate(ties))
-
-    def got(block, mask, step, senders=range(n_slots)):
-        block = lax.ppermute(block.astype(bf16), ("chip", "ctx"), [(i, i ^ mask) for i in senders])
-        if ties.get(step) is not None:
-            block = after(block, ties[step])
-        return block.astype(f32)
-
-    halves = []
-    for order, keep, send in ((first_order, parts[0], parts[1]), (second_order, parts[2], parts[3])):
-        keep = keep.astype(f32) + got(send, order[-1], 0)
-        for step, mask in enumerate(reversed(order[:-1])):
-            mid = keep.shape[0] // 2
-            keep = keep[:mid] + got(keep[mid:], mask, step + 1)
-        halves.append(keep)
-    keep = jnp.concatenate(halves, axis=1)
-    step = len(first_order)
+
+    def send(block, mask, senders=range(n_slots)):
+        route = [(i, i ^ mask) for i in senders]
+        return lax.ppermute(block.astype(bf16), ("chip", "ctx"), route)
+
+    orders = (first_order, second_order)
+    got = yield [send(parts[1], first_order[-1]), send(parts[3], second_order[-1])]
+    keeps = [k.astype(f32) + g.astype(f32) for k, g in zip((parts[0], parts[2]), got)]
+    for step in range(len(first_order) - 2, -1, -1):
+        mid = keeps[0].shape[0] // 2
+        got = yield [send(k[mid:], order[step]) for k, order in zip(keeps, orders)]
+        keeps = [k[:mid] + g.astype(f32) for k, g in zip(keeps, got)]
+    keep = jnp.concatenate(keeps, axis=1)
     if len(far) == 2:
         low, high = far
         outer = [i for i in range(n_slots) if (i & low == 0) == (i & high == 0)]
         inner = [i for i in range(n_slots) if i not in outer]
-        distant = keep[2:] + got(keep[2:], low, step, outer)[::-1]
-        keep = keep[:2] + got(distant, low | high, step + 1, inner)[::-1]
-        return keep[0] + got(keep[1:], low, step + 2)[0]
+        (got,) = yield [send(keep[2:], low, outer)]
+        distant = keep[2:] + got.astype(f32)[::-1]
+        (got,) = yield [send(distant, low | high, inner)]
+        keep = keep[:2] + got.astype(f32)[::-1]
+        far = far[:1]
     for mask in reversed(far):
         mid = keep.shape[0] // 2
-        keep = keep[:mid] + got(keep[mid:], mask, step)
-        step += 1
+        (got,) = yield [send(keep[mid:], mask)]
+        keep = keep[:mid] + got.astype(f32)
     return keep[0]
+
+
+class Stages:
+    def __init__(self, parts):
+        self.steps = scatter_steps(parts)
+        self.got = next(self.steps)
+        self.total = None
+
+    def advance(self, *done):
+        try:
+            self.got = self.steps.send([after(g, *done) for g in self.got])
+        except StopIteration as end:
+            self.got, self.total = [], end.value
 
 
 def slot_pairs(own, plan, refs, segments, n_ctx, targets):
@@ -304,7 +315,7 @@
     return [shapes[operand] for operand in sorted(shapes)]
 
 
-def ffn_kernel(geometry, out_geometry, first, own_ref, n_ref, go_ref, *refs):
+def ffn_kernel(geometry, out_geometry, first, last, own_ref, n_ref, go_ref, *refs):
     plan, segments, n_ctx = geometry
     out_plan = out_geometry[0]
     count, out_count = part_count(plan), part_count(out_plan)
@@ -313,7 +324,11 @@
         res_in, gn_in = refs[:2]
         refs = refs[2:]
     res_ref, gn_ref = refs[:2]
-    grads, refs = refs[2 : 2 + out_count], refs[2 + out_count :]
+    refs = refs[2:]
+    if last:
+        res_low_ref, gn_low_ref = refs[:2]
+        refs = refs[2:]
+    grads, refs = refs[:out_count], refs[out_count:]
     gate_m, up_m, down_m, d_gate, d_up, d_down, h_m, gg_m, gu_m, sems = refs
     own = own_ref[0]
     targets = (gate_m, up_m, down_m)
@@ -347,6 +362,9 @@
         gn = gn_in[...] + gn
     res_ref[...] = res
     gn_ref[...] = gn
+    if last:
+        res_low_ref[...] = res.astype(bf16)
+        gn_low_ref[...] = gn.astype(bf16)
     d_gate[...] += lax.dot_general(n, gg_m[...], TN, preferred_element_type=f32)
     d_up[...] += lax.dot_general(n, gu_m[...], TN, preferred_element_type=f32)
     d_down[...] += lax.dot_general(h_m[...], go, TN, preferred_element_type=f32)
@@ -360,7 +378,9 @@
         copy_all([(b, a) for a, b in pairs], sems)
 
 
-def ffn_chunk(own, nffn, go, weights, totals, geometry, out_geometry, hidden_count, rows=256):
+def ffn_chunk(
+    own, nffn, go, weights, totals, geometry, out_geometry, hidden_count, last=False, rows=256
+):
     total, width = nffn.shape
     first = totals is None
     plan, segments, _ = geometry
@@ -370,14 +390,15 @@
     row_spec = pl.BlockSpec((rows, width), lambda i, o: (i, 0))
     any_spec = pl.BlockSpec(memory_space=pl.ANY)
     outs = pl.pallas_call(
-        functools.partial(ffn_kernel, geometry, out_geometry, first),
+        functools.partial(ffn_kernel, geometry, out_geometry, first, last),
         out_shape=[jax.ShapeDtypeStruct((total, width), f32)] * 2
+        + [jax.ShapeDtypeStruct((total, width), bf16)] * (2 if last else 0)
         + [jax.ShapeDtypeStruct(s, bf16) for s in part_shapes(out_plan, lanes)],
         grid_spec=pltpu.PrefetchScalarGridSpec(
             num_scalar_prefetch=1,
             grid=(total // rows,),
             in_specs=[row_spec] * 2 + [any_spec] * count + [row_spec] * (0 if first else 2),
-            out_specs=[row_spec] * 2 + [any_spec] * out_count,
+            out_specs=[row_spec] * (4 if last else 2) + [any_spec] * out_count,
             scratch_shapes=[
                 pltpu.VMEM((width, hidden_count), bf16),
                 pltpu.VMEM((width, hidden_count), bf16),
@@ -397,7 +418,9 @@
         ),
         cost_estimate=SMALL_COST,
     )(own, nffn, go, *weights, *(() if first else totals))
-    return (outs[0], outs[1]), outs[2:]
+    if last:
+        return outs[:4], outs[4:]
+    return outs[:2], outs[2:]
 
 
 def move_kernel(geometry, count, outward, own_ref, *refs):
@@ -582,6 +605,8 @@
         and (w_in.shape[1] // n_ctx) % (2 * depth) == 0
         and width % (2 * depth) == 0
         and tokens.shape[1] % n_ctx == 0
+        and n_ctx == 2
+        and n_dp >= 16
     )
 
 
@@ -665,7 +690,13 @@
 
     out_all = lax.all_gather(out_block, ("chip", "ctx"))
 
+    token_rows = tokens.reshape(rows, width)
+    inputs = jnp.concatenate([token_rows, swap(token_rows)], axis=0)
+    go_rows = cotangent.reshape(rows, width)
+    go = jnp.concatenate([go_rows, swap(go_rows)], axis=0)
+
     far, first_order, second_order = bit_masks()
+    orders = (first_order, second_order)
 
     def doubled(hold, got):
         return jnp.concatenate([hold, got], axis=0)
@@ -673,27 +704,27 @@
     hold = mix_block[None]
     for mask in far:
         hold = doubled(hold, across(hold, mask))
+    chunk_all = lax.all_gather(after(chunk_blocks[1], hold), ("chip", "ctx"))
     mix_halves = [hold[:, :mix_cut], hold[:, mix_cut:]]
     next_hold = after(chunk_blocks[0][None], hold)
-    chunk_all = [
-        lax.all_gather(after(block, hold), ("chip", "ctx")) for block in chunk_blocks[1:]
-    ]
     far_left = list(far)
-    mix_parts = []
+    early = [inputs, go]
     for step in range(len(first_order)):
-        got = [across(h, order[step]) for h, order in zip(mix_halves, (first_order, second_order))]
+        got = [across(h, order[step]) for h, order in zip(mix_halves, orders)]
         if far_left:
             next_got = across(next_hold, far_left.pop(0))
             next_hold = doubled(next_hold, next_got)
-            if step + 1 < len(first_order):
-                got = [after(g, next_got) for g in got]
+        if early:
+            got = [after(g, early[0]) for g in got]
+            early = early[1:]
         if step + 1 < len(first_order):
+            got = [after(g, next_got) for g in got]
             mix_halves = [doubled(h, g) for h, g in zip(mix_halves, got)]
             next_hold = after(next_hold, *got)
-        else:
-            mix_parts = [mix_halves[0], got[0], mix_halves[1], got[1]]
+    mix_parts = [mix_halves[0], got[0], mix_halves[1], got[1]]
     for mask in far_left:
-        next_hold = doubled(next_hold, across(next_hold, mask))
+        next_got = across(next_hold, mask)
+        next_hold = doubled(next_hold, next_got)
     in_half, small_all = move(
         own,
         mix_parts,
@@ -702,20 +733,15 @@
         4,
         False,
     )
-    (out_half,) = move(
-        own,
-        [out_all],
-        [(channels, width)],
-        ([(0, i, None, 0, out_parts * depth) for i in range(slots)], out_segments, n_ctx),
-        1,
-        False,
-    )
+    in_half = after(in_half, next_got)
     next_halves = [next_hold[:, :chunk_cut], next_hold[:, chunk_cut:]]
-    next_orders = (first_order, second_order)
-
-    def next_step(step, done):
-        got = [across(h, o[step]) for h, o in zip(next_halves, next_orders)]
-        return [after(g, done) for g in got]
+    last_hold = after(chunk_blocks[2][None], next_got)
+
+    def step_of(halves, step):
+        return [across(h, order[step]) for h, order in zip(halves, orders)]
+
+    def all_after(blocks, *done):
+        return [after(block, *done) for block in blocks]
 
     small_all = small_all.reshape(n_chip, 16, n_ctx * 256)[:, :5, : 2 * depth].astype(f32)
     first_gain = small_all[:, 0].reshape(width)
@@ -724,10 +750,6 @@
     taps = jnp.where(core == 0, taps[:, :, 0], taps[:, :, 1]).transpose(1, 0, 2)
     taps = taps.reshape(3, channels)
 
-    token_rows = tokens.reshape(rows, width)
-    inputs = jnp.concatenate([token_rows, swap(token_rows)], axis=0)
-    go_rows = cotangent.reshape(rows, width)
-    go = jnp.concatenate([go_rows, swap(go_rows)], axis=0)
     blocks = 2 * seqs
 
     def at(i):
@@ -741,6 +763,8 @@
 
     wide_rows, thin_rows = (piece, width), (piece, channels)
     taps = jnp.pad(taps, ((0, 5), (0, 0)))
+    next_got = step_of(next_halves, 0)
+    last_got = across(last_hold, far[0])
     normed_low, projected = row_call(
         in_kernel,
         blocks,
@@ -754,7 +778,14 @@
             ((2 * rows, 3 * channels), f32, (piece, 3 * channels), at),
         ],
     )
-    next_got = next_step(0, projected)
+    (out_half,) = move(
+        own,
+        [after(out_all, projected)],
+        [(channels, width)],
+        ([(0, i, None, 0, out_parts * depth) for i in range(slots)], out_segments, n_ctx),
+        1,
+        False,
+    )
     tail = projected.reshape(blocks, piece, 3 * channels)[:, piece - 2 :]
     tail = (tail[:, :, :channels] * tail[:, :, 2 * channels :]).astype(bf16)
     before = passed_along(tail, "ctx", 1)
@@ -763,13 +794,20 @@
     def halo_at(i):
         return (i, 0, 0)
 
+    conv_taps = after(taps, last_got, *next_got)
+    next_halves = [
+        doubled(h, g) for h, g in zip(next_halves, all_after(next_got, projected))
+    ]
+    last_hold = doubled(last_hold, after(last_got, projected))
+    next_got = step_of(next_halves, 1)
+    last_got = across(last_hold, far[1])
     mixer_out, convolved, branch = row_call(
         conv_kernel,
         blocks,
         [
             (projected, (piece, 3 * channels), at),
             (before, halo, halo_at),
-            (taps, taps.shape, still),
+            (conv_taps, taps.shape, still),
             (out_half, out_half.shape, still),
         ],
         [
@@ -790,23 +828,38 @@
         [((2 * rows, width), f32, wide_rows, at), ((2 * rows, width), bf16, wide_rows, at)],
     )
 
-    for step in range(1, len(first_order)):
-        next_halves = [doubled(h, g) for h, g in zip(next_halves, next_got)]
-        next_got = next_step(step, nffn_low)
     next_parts = [next_halves[0], next_got[0], next_halves[1], next_got[1]]
+    next_parts = all_after(next_parts, nffn_low)
+    last_hold = doubled(last_hold, after(last_got, nffn_low))
+    last_halves = [last_hold[:, :chunk_cut], last_hold[:, chunk_cut:]]
+    last_got_halves = step_of(last_halves, 0)
+
     totals, first_grads = ffn_chunk(
-        own, nffn_low, go, next_parts, None, step_geometry, step_geometry, hidden_count
-    )
+        own, nffn_low, after(go, last_got), next_parts, None, step_geometry, step_geometry,
+        hidden_count,
+    )
+    first_stages = Stages(first_grads)
+    nffn_then = after(nffn_low, *last_got_halves)
+    last_halves = [
+        doubled(h, g) for h, g in zip(last_halves, all_after(last_got_halves, totals[1]))
+    ]
+    last_got_halves = step_of(last_halves, 1)
     totals, second_grads = ffn_chunk(
-        own, nffn_low, go, [chunk_all[0]], totals, whole_geometry, step_geometry, hidden_count
-    )
-    second_total = totals[1]
+        own, nffn_then, go, [chunk_all], totals, whole_geometry, step_geometry, hidden_count
+    )
+    second_stages = Stages(second_grads)
+    nffn_then = after(nffn_low, *first_stages.got)
+    first_stages.advance(totals[1])
+    last_got_halves = all_after(last_got_halves, totals[1])
+    last_parts = [last_halves[0], last_got_halves[0], last_halves[1], last_got_halves[1]]
     totals, last_grads = ffn_chunk(
-        own, nffn_low, go, [chunk_all[1]], totals, whole_geometry, step_geometry, hidden_count
-    )
-    ffn_out, grad_nffn = totals
-    grad_got = swap(grad_nffn.astype(bf16))
-    ffn_got = swap(ffn_out[rows:].astype(bf16))
+        own, nffn_then, go, last_parts, totals, step_geometry, step_geometry, hidden_count, last=True
+    )
+    ffn_out, grad_nffn, ffn_low, grad_low = totals
+    last_stages = Stages(last_grads)
+    grad_got = swap(after(grad_low, *first_stages.got, *second_stages.got))
+    first_stages.advance(grad_low)
+    second_stages.advance(grad_low)
 
     def turned(i):
         return ((i + seqs) % blocks, 0)
@@ -844,6 +897,10 @@
         scratch=[pltpu.VMEM((channels, width), f32)],
     )
     grad_gain_ffn = grad_gain_ffn[0]
+    stages = (first_stages, second_stages, last_stages)
+    grad_c_then = after(grad_c, *(g for s in stages for g in s.got))
+    for s in stages:
+        s.advance(grad_c)
     head = grad_conv.reshape(blocks, piece, channels)[:, :2].astype(bf16)
     behind = passed_along(head, "ctx", -1)
     grad_out_slots = grad_w_out.reshape(n_chip, depth, n_ctx, out_parts, 256)
@@ -859,7 +916,7 @@
             (behind, halo, halo_at),
             (before, halo, halo_at),
             (projected, (piece, 3 * channels), at),
-            (grad_c, thin_rows, at),
+            (grad_c_then, thin_rows, at),
             (normed_low, wide_rows, at),
             (taps, taps.shape, still),
         ],
@@ -875,23 +932,31 @@
         ],
     )
     grad_kernel = grad_kernel[:3]
-    first_sum = scatter_sum(
-        first_grads, (second_total, grad_nffn, grad_c, grad_projected, grad_projected)
-    )
-    second_sum = scatter_sum(second_grads, (grad_nffn, grad_c, grad_projected))
-    last_sum = scatter_sum(last_grads, (grad_c, grad_projected))
-    mix_sum = scatter_sum(mix_grad_parts)
-    late_projected = after(grad_projected, mix_grad_parts[1])
-    grad_normed = cross_cols(late_projected[rows:], in_half).astype(bf16)
-    grad_normed = cross_cols(late_projected[:rows], in_half) + swap(grad_normed).astype(f32)
-    result = residual[:rows] + (ffn_out[:rows] + ffn_got.astype(f32))
+    mix_stages = Stages(mix_grad_parts)
+    for s in stages:
+        s.advance(grad_projected)
+    grad_other = cross_cols(grad_projected[rows:], in_half).astype(bf16)
+    for s in (mix_stages, *stages):
+        s.advance(grad_other)
+    other_got = swap(grad_other)
+    grad_mine = cross_cols(after(grad_projected[:rows], other_got), in_half)
+    for s in (mix_stages, second_stages, last_stages):
+        s.advance(grad_mine)
+    grad_normed = grad_mine + other_got.astype(f32)
+    ffn_got = swap(after(ffn_low[rows:], grad_other))
+    result = residual[:rows] + (after(ffn_out[:rows], grad_mine) + ffn_got.astype(f32))
     result = result.astype(bf16).reshape(seqs, piece, width)
     own_inputs = token_rows.astype(f32)
     scale_mix = lax.rsqrt(jnp.mean(own_inputs * own_inputs, axis=-1, keepdims=True) + EPSILON)
     grad_in_norm, grad_gain_mix = norm_backward(own_inputs, scale_mix, first_gain, grad_normed)
     grad_tokens = (grad_residual + grad_in_norm).reshape(seqs, piece, width)
 
-    chunk_sum = jnp.stack([first_sum, second_sum, last_sum])
+    mix_stages.advance(grad_tokens)
+    last_stages.advance(grad_tokens)
+    while mix_stages.total is None:
+        mix_stages.advance()
+
+    chunk_sum = jnp.stack([s.total for s in stages])
     both_sum = chunk_sum[:, : 4 * depth].reshape(CHUNKS, 2, 2, depth, lanes).transpose(2, 0, 1, 3, 4)
     both_mine, both_other = mine_other(both_sum)
     both_got = swap(both_other)
@@ -903,7 +968,7 @@
     final_down = jnp.concatenate([chunk_sum[:, 4 * depth : 4 * depth + sub], down_rest], axis=2)
     final_down = final_down.reshape(CHUNKS * sub, wide)
 
-    in_sum = mix_sum.reshape(in_parts, 2, depth, 256).transpose(1, 0, 2, 3)
+    in_sum = mix_stages.total.reshape(in_parts, 2, depth, 256).transpose(1, 0, 2, 3)
     in_mine, in_other = mine_other(in_sum)
     in_sum = in_core_order(in_mine[None], swap(in_other)[None], 0)
     in_sum = in_sum.transpose(0, 2, 1, 3).reshape(2, depth, in_cols // depth, depth)

time: 632 us -> 642 us (1.016)
  waiting for transfers between devices: 218 us -> 149 us
  local copies, waits for them, and re-layouts: 45 us -> 75.3 us
  starting transfers between devices: 66.5 us -> 86.9 us
  other arithmetic: 63.3 us -> 78.9 us
  Pallas kernels: 202 us -> 211 us
    ppermute x28, waiting for transfers between devices: 69.5 us -> 28.2 us  [send(): return lax.ppermute(block.astype(bf16), ('chip', 'ctx'), route)]
    all_gather x1, waiting for transfers between devices: 14.9 us -> 0.02 us  [fast_shards(): out_all = lax.all_gather(out_block, ('chip', 'ctx'))]
    slice x13 -> x16, local copies, waits for them, and re-layouts: 8.73 us -> 21.4 us  [the longest x8 8.41 us: scatter_steps(): k[mid:]]
    ppermute x16 -> x22, starting transfers between devices: 18.8 us -> 29.7 us  [across(): lax.ppermute(block, ('chip', 'ctx'), [(i, i ^ mask) for i in range(count)])]
    ppermute x16 -> x22, waiting for transfers between devices: 131 us -> 121 us  [across(): lax.ppermute(block, ('chip', 'ctx'), [(i, i ^ mask) for i in range(count)])]
    ppermute x28, starting transfers between devices: 41.2 us -> 50.4 us  [send(): return lax.ppermute(block.astype(bf16), ('chip', 'ctx'), route)]
    pallas_call x3, Pallas kernels: 126 us -> 135 us  [ffn_chunk(): pl.pallas_call(functools.partial(ffn_kernel, geometry, out_geometry, firs...]
    concatenate x7 -> x10, other arithmetic: 3.43 us -> 10.4 us  [doubled(): return jnp.concatenate([hold, got], axis=0)]
  transfers between devices with their start and end apart: 61 -> 66, of which waited for: 25 -> 13; matrix products, arithmetic and copies ran while one was open for 15% -> 23% of each run, Pallas kernels for 26% -> 33%
where the time goes in v4:
time: 642 us; the launch traced here: 632 us
  Pallas kernels  211 us (33%)
  waiting for transfers between devices  149 us (23%)
  starting transfers between devices  86.9 us (14%)
  other arithmetic  78.9 us (12%)
  local copies, waits for them, and re-layouts  75.3 us (12%)
  between operations  15.9 us (2%)
  matrix products  15.2 us (2%)
    pallas_call x3, Pallas kernels, ffn_chunk(): pl.pallas_call(functools.partial(ffn_kernel, geometry, out_geometry, firs...  135 us
    ppermute x22, waiting for transfers between devices, across(): lax.ppermute(block, ('chip', 'ctx'), [(i, i ^ mask) for i in range(count)])  121 us
    pallas_call x5, Pallas kernels, row_call(): pl.pallas_call(body, grid=(steps,), in_specs=[pl.BlockSpec(memory_space=p...  69 us
    ppermute x28, starting transfers between devices, send(): return lax.ppermute(block.astype(bf16), ('chip', 'ctx'), route)  50.4 us
    ppermute x22, starting transfers between devices, across(): lax.ppermute(block, ('chip', 'ctx'), [(i, i ^ mask) for i in range(count)])  29.7 us
    ppermute x28, waiting for transfers between devices, send(): return lax.ppermute(block.astype(bf16), ('chip', 'ctx'), route)  28.2 us
    unnamed x143, local copies, waits for them, and re-layouts  16.9 us
    dot_general x2, matrix products, cross_cols(): lax.dot_general(left_operand, right_operand, (((1,), (1,)), ((), ())), pr...  15.2 us
  transfers between devices with their start and end apart: 66, of which 13 were waited for; matrix products, arithmetic and copies ran while one was open for 23% of the time, Pallas kernels for 33%

profile of v4, /device:TPU:0, one launch (start us, length us, event | category | flops | bytes accessed | tf_op | source)
XLA Modules:
  0.0 632.2 jit_solution(3146400895167853409)
XLA Ops:
  15.5 2.1 maximum_bitcast_fusion
  22.4 3.1 collective-permute-start.2
  32.4 2.9 collective-permute-start.3
  37.6 18.3 %collective-permute-done.3 = bf16[2,400,256]{2,1,0:T(8,128)(2,1)S(1)} collective-permute-done((bf16[2,400,256]{2,1,0:T(8,128)(2,1)S(1)}, bf16[2,400,256]{2,1,0:T(8,128)(2,1)S(1)}, u32[]{:S(2)}, u32[]{:S(2)}) %collective-permute-start.3) | collective-permute-done | bytes 409632 | tf_op jit(solution)/shard_map/ppermute | solution.py:191
  60.9 5.5 collective-permute-done.6
  67.4 4.0 pad_maximum_fusion.x_ref
  73.4 3.4 collective-permute-start.11
  79.8 4.0 pad_maximum_fusion.1.go_ref
  83.8 19.7 %collective-permute-done.11 = bf16[2,384,384]{2,1,0:T(8,128)(2,1)S(1)} collective-permute-done((bf16[2,384,384]{2,1,0:T(8,128)(2,1)S(1)}, bf16[2,384,384]{2,1,0:T(8,128)(2,1)S(1)}, u32[]{:S(2)}, u32[]{:S(2)}) %collective-permute-start.11) | collective-permute-done | bytes 589856 | tf_op jit(solution)/shard_map/ppermute | solution.py:191
  109.0 4.8 shard_map.177
  115.2 12.0 %shard_map.178 = (bf16[2048,1024]{1,0:T(8,128)(2,1)}, f32[2048,1536]{1,0:T(8,128)}) custom-call(bf16[2048,1024]{1,0:T(8,128)(2,1)} %pad_maximum_fusion.x_ref, f32[1,1024]{1,0:T(1,128)} %bitcast.151, bf16[1024,1536]{1,0:T(8,128)(2,1)} %get-tuple-element.119.w_ref), custom_call_target="tpu_custom_call" | custom-call | flops 65536 | bytes 65536 | tf_op jit(solution)/shard_map/pallas_call | solution.py:569
  128.1 3.3 collective-permute-start.12
  131.5 2.4 shard_map.179.w_ref
  135.3 9.5 %shard_map.180 = (bf16[2048,512]{1,0:T(8,128)(2,1)}, f32[2048,512]{1,0:T(8,128)}, bf16[2048,1024]{1,0:T(8,128)(2,1)}) custom-call(f32[2048,1536]{1,0:T(8,128)} %get-tuple-element.120.projected_ref.gate_c_ref, bf16[4,2,512]{2,1,0:T(2,128)(2,1)} %copy-done.59, f32[8,512]{1,0:T(8,128)} %pad.14.taps_ref, bf16[512,1024]{1,0:T(8,128)(2,1)} %shard_map.179.w_ref), custom_call_target="tpu_custom_call" | custom-call | flops 65536 | bytes 65536 | tf_op jit(solution)/shard_map/pallas_call | solution.py:569
  146.8 2.5 pad_maximum_fusion.6.refs_0_
  150.2 2.2 collective-permute-start.17
  153.9 9.9 %shard_map.181 = (f32[2048,1024]{1,0:T(8,128)}, bf16[2048,1024]{1,0:T(8,128)(2,1)}) custom-call(bf16[2048,1024]{1,0:T(8,128)(2,1)} %pad_maximum_fusion.x_ref, bf16[2048,1024]{1,0:T(8,128)(2,1)} %get-tuple-element.124.branch_ref, bf16[2048,1024]{1,0:T(8,128)(2,1)} %collective-permute-done.16.got_ref, f32[1,1024]{1,0:T(1,128)} %bitcast.145), custom_call_target="tpu_custom_call" | custom-call | flops 65536 | bytes 65536 | tf_op jit(solution)/shard_map/pallas_call | solution.py:569
  163.8 36.5 %collective-permute-done.17 = bf16[2,384,384]{2,1,0:T(8,128)(2,1)} collective-permute-done((bf16[2,384,384]{2,1,0:T(8,128)(2,1)}, bf16[2,384,384]{2,1,0:T(8,128)(2,1)}, u32[]{:S(2)}, u32[]{:S(2)}) %collective-permute-start.17) | collective-permute-done | bytes 589856 | tf_op jit(solution)/shard_map/ppermute | solution.py:191
  202.2 2.4 fusion.43
  206.1 41.3 %shard_map.182 = (f32[2048,1024]{1,0:T(8,128)}, f32[2048,1024]{1,0:T(8,128)}, bf16[8,192,384]{2,1,0:T(8,128)(2,1)}, bf16[8,192,384]{2,1,0:T(8,128)(2,1)}, bf16[8...) custom-call(s32[1]{0:T(128)} %bitcast.1.own_ref, bf16[2048,1024]{1,0:T(8,128)(2,1)} %get-tuple-element.137.n_ref, ...), custom_call_target="tpu_custom_call" | custom-call | flops 65536 | bytes 65536 | tf_op jit(solution)/shard_map/pallas_call | solution.py:392
  252.9 36.8 %collective-permute-done.22 = bf16[4,192,384]{2,1,0:T(8,128)(2,1)S(1)} collective-permute-done((bf16[4,192,384]{2,1,0:T(8,128)(2,1)}, bf16[4,192,384]{2,1,0:T(8,128)(2,1)S(1)}, u32[]{:S(2)}, u32[]{:S(2)}) %collective-permute-start.22) | collective-permute-done | bytes 589856 | tf_op jit(solution)/shard_map/ppermute | solution.py:191
  292.4 42.2 %shard_map.183 = (f32[2048,1024]{1,0:T(8,128)}, f32[2048,1024]{1,0:T(8,128)}, bf16[8,192,384]{2,1,0:T(8,128)(2,1)}, bf16[8,192,384]{2,1,0:T(8,128)(2,1)}, bf16[8...) custom-call(s32[1]{0:T(128)} %bitcast.1.own_ref, ...), custom_call_target="tpu_custom_call", output_to_operand_aliasing={{0}: (4, {}), {1}: (5, {})} | custom-call | flops 65536 | bytes 65536 | tf_op jit(solution)/shard_map/pallas_call | solution.py:392
  346.8 51.2 %shard_map.184 = (f32[2048,1024]{1,0:T(8,128)}, f32[2048,1024]{1,0:T(8,128)}, bf16[2048,1024]{1,0:T(8,128)(2,1)}, bf16[2048,1024]{1,0:T(8,128)(2,1)}, bf16[8,192...) custom-call(s32[1]{0:T(128)} %bitcast.1.own_ref, ...), custom_call_target="tpu_custom_call", output_to_operand_aliasing={{0}: (7, {}), {1}: (8, {})} | custom-call | flops 65536 | bytes 65536 | tf_op jit(solution)/shard_map/pallas_call | solution.py:392
  400.2 2.2 slice_add_fusion.4
  403.3 2.2 collective-permute-start.32
  412.5 2.1 copy-done.29
  415.8 3.1 slice.325
  418.9 4.8 slice.314
  423.7 19.4 %shard_map.185 = (f32[1024,1024]{1,0:T(8,128)}, f32[2048,512]{1,0:T(8,128)}, bf16[2048,512]{1,0:T(8,128)(2,1)}, bf16[512,1024]{1,0:T(8,128)(2,1)}, f32[1,1024]{1,0:T(1,128)}) custom-call(f32[2048,1024]{1,0:T(8,128)} %get-tuple-element.150.gn_ref, bf16[2048,1024]{1,0:T(8,128)(2,1)} %copy-done.29, f32[2048,1024]{1,0:T(8,128)} %get-tuple-element.125.residual_ref, ...), custom_call_target="tpu_custom_call" | custom-call | flops 65536 | bytes 65536 | tf_op jit(solution)/shard_map/pallas_call | solution.py:569
  443.2 2.5 convert.45
  453.5 2.7 collective-permute-start.49
  456.2 2.9 convert_add_fusion.1
  459.1 2.2 slice.552
  461.3 2.6 collective-permute-start.53
  469.2 2.6 reshape.228
  471.8 2.4 copy.88
  474.8 18.2 %shard_map.186 = (bf16[2048,1536]{1,0:T(8,128)(2,1)}, f32[8,512]{1,0:T(8,128)}, bf16[8,192,256]{2,1,0:T(8,128)(2,1)}, bf16[8,192,256]{2,1,0:T(8,128)(2,1)}, bf16...) custom-call(s32[1]{0:T(128)} %bitcast.1.own_ref, f32[2048,512]{1,0:T(8,128)} %get-tuple-element.161.grad_conv_ref, ...), custom_call_target="tpu_custom_call" | custom-call | flops 65536 | bytes 65536 | tf_op jit(solution)/shard_map/pallas_call | solution.py:569
  493.0 7.8 %fusion.8 = bf16[1024,1024]{1,0:T(8,128)(2,1)} fusion(bf16[1024,1536]{1,0:T(8,128)(2,1)} %get-tuple-element.119.w_ref, bf16[2048,1536]{1,0:T(8,128)(2,1)} %get-tuple-element.173), kind=kOutput, calls=%fused_computation.28 | convolution fusion | flops 3222274048 | bytes 8388608 | tf_op jit(solution)/shard_map/dot_general | solution.py:29
  512.8 13.4 %collective-permute-done.41 = bf16[8,192,256]{2,1,0:T(8,128)(2,1)S(1)} collective-permute-done((bf16[8,192,256]{2,1,0:T(8,128)(2,1)}, bf16[8,192,256]{2,1,0:T(8,128)(2,1)S(1)}, u32[]{:S(2)}, u32[]{:S(2)}) %collective-permute-start.41) | collective-permute-done | bytes 786464 | tf_op jit(solution)/shard_map/ppermute | solution.py:238
  527.9 5.5 collective-permute-done.39
  539.8 8.3 %collective-permute-done.54 = bf16[2,384,384]{2,1,0:T(8,128)(2,1)S(1)} collective-permute-done((bf16[2,384,384]{2,1,0:T(8,128)(2,1)S(1)}, bf16[2,384,384]{2,1,0:T(8,128)(2,1)S(1)}, u32[]{:S(2)}, u32[]{:S(2)}) %collective-permute-start.54) | collective-permute-done | bytes 589856 | tf_op jit(solution)/shard_map/ppermute | solution.py:238
  548.1 2.5 collective-permute-start.51
  554.1 7.5 %fusion.5 = (f32[1024]{0:T(1024)S(1)}, f32[1024]{0:T(1024)S(1)}, f32[1024,1024]{1,0:T(8,128)S(1)}) fusion(f32[1024]{0:T(1024)S(1)} %bitcast.148, bf16[1024,1024]{1,0:T(8,128)(2,1)} %collective-permute-done.37, bf16[2,512,1024]{2,1,0:T(8,128)(2,1)S(1)} %copy-done, f32[1024]{0:T(1024)S(1)} %get-tuple-element.227, bf16[1024,1536]{1,0:T(8,128)(2,1)} %slice.323, ...), kind=kOutput, calls=%fused_computation.8 | convolution fusion | flops 3230660608 | bytes 14696448 | tf_op jit(solution)/shard_map/dot_general | solution.py:29
  563.1 7.2 %collective-permute-start.56 = (bf16[1,384,384]{2,1,0:T(8,128)(2,1)S(1)}, bf16[1,384,384]{2,1,0:T(8,128)(2,1)S(1)}, u32[]{:S(2)}, u32[]{:S(2)}) collective-permute-start(bf16[1,384,384]{2,1,0:T(8,128)(2,1)S(1)} %slice.560), channel_id=1, source_target_pairs={{0,8},{1,9},{4,12},{5,13},{8,0},{9,1},{12,4},{13,5},{16,24},{17,25... | collective-permute-start | bytes 884744 | tf_op jit(solution)/shard_map/ppermute | solution.py:238
  574.9 3.2 collective-permute-start.43
  579.0 4.3 fusion.2
  585.8 4.2 add_convert_fusion
  604.5 9.7 %collective-permute-start.45 = (bf16[1,384,256]{2,1,0:T(8,128)(2,1)S(1)}, bf16[1,384,256]{2,1,0:T(8,128)(2,1)S(1)}, u32[]{:S(2)}, u32[]{:S(2)}) collective-permute-start(bf16[1,384,256]{2,1,0:T(8,128)(2,1)S(1)} %slice.563), channel_id=1, source_target_pairs={{0,8},{1,9},{4,12},{5,13},{8,0},{9,1},{12,4},{13,5},{16,24},{17,25... | collective-permute-start | bytes 589832 | tf_op jit(solution)/shard_map/ppermute | solution.py:238
  (407 shorter events, 153.1 us)
Async XLA Ops:
  7.2 124.2 %all-gather.4.cloned.1.call-start = ((), (), s32[]{:S(2)}) async-start(), calls=%async_computation.1 | async-start | bytes 1114112 | tf_op jit(solution)/shard_map/all_gather | solution.py:691
  8.9 283.5 %all-gather.6.cloned.1.call-start = ((), (), s32[]{:S(2)}) async-start(), calls=%async_computation.3 | async-start | bytes 5013504 | tf_op jit(solution)/shard_map/all_gather | solution.py:707
  12.6 54.7 %collective-permute-start = (bf16[1024,1024]{1,0:T(8,128)(2,1)S(1)}, bf16[1024,1024]{1,0:T(8,128)(2,1)}, u32[]{:S(2)}, u32[]{:S(2)}) collective-permute-start(bf16[1024,1024]{1,0:T(8,128)(2,1)S(1)} %bitcast.111), channel_id=1, source_target_pairs={{0,2},{2,0},{1,3},{3,1},{4,6},{6,4},{5,7},{7,5},{8,10},{10,8},{9,1... | collective-permute-start | bytes 6291464 | tf_op jit(solution)/shard_map/ppermute | solution.py:186
  27.8 52.0 %collective-permute-start.8 = (bf16[1024,1024]{1,0:T(8,128)(2,1)}, bf16[1024,1024]{1,0:T(8,128)(2,1)}, u32[]{:S(2)}, u32[]{:S(2)}) collective-permute-start(bf16[1024,1024]{1,0:T(8,128)(2,1)} %bitcast.124), channel_id=1, source_target_pairs={{0,2},{2,0},{1,3},{3,1},{4,6},{6,4},{5,7},{7,5},{8,10},{10,8},{9,1... | collective-permute-start | bytes 6291464 | tf_op jit(solution)/shard_map/ppermute | solution.py:186
  32.4 23.5 %collective-permute-start.3 = (bf16[2,400,256]{2,1,0:T(8,128)(2,1)S(1)}, bf16[2,400,256]{2,1,0:T(8,128)(2,1)S(1)}, u32[]{:S(2)}, u32[]{:S(2)}) collective-permute-start(bf16[2,400,256]{2,1,0:T(8,128)(2,1)S(1)} %pad_maximum_fusion.19), channel_id=1, source_target_pairs={{0,16},{1,17},{4,20},{5,21},{8,24},{9,25},{12,28},{13,29},{16,0},{... | collective-permute-start | bytes 1228808 | tf_op jit(solution)/shard_map/ppermute | solution.py:191
  56.9 494.7 %reduce-scatter.2.cloned.1.call-start = ((), (), s32[]{:S(2)}) async-start(), calls=%async_computation.2 | async-start | bytes 1114112 | tf_op jit(solution)/shard_map/reduce_scatter | solution.py:908
  57.7 15.2 %collective-permute-start.9 = (bf16[4,208,256]{2,1,0:T(8,128)(2,1)S(1)}, bf16[4,208,256]{2,1,0:T(8,128)(2,1)S(1)}, u32[]{:S(2)}, u32[]{:S(2)}) collective-permute-start(bf16[4,208,256]{2,1,0:T(8,128)(2,1)S(1)} %slice.382), channel_id=1, source_target_pairs={{0,1},{1,0},{4,5},{5,4},{8,9},{9,8},{12,13},{13,12},{16,17},{17,16... | collective-permute-start | bytes 1277960 | tf_op jit(solution)/shard_map/ppermute | solution.py:191
  73.4 30.1 %collective-permute-start.11 = (bf16[2,384,384]{2,1,0:T(8,128)(2,1)S(1)}, bf16[2,384,384]{2,1,0:T(8,128)(2,1)S(1)}, u32[]{:S(2)}, u32[]{:S(2)}) collective-permute-start(bf16[2,384,384]{2,1,0:T(8,128)(2,1)S(1)} %pad_maximum_fusion.15), channel_id=1, source_target_pairs={{0,16},{1,17},{4,20},{5,21},{8,24},{9,25},{12,28},{13,29},{16,0},{... | collective-permute-start | bytes 1769480 | tf_op jit(solution)/shard_map/ppermute | solution.py:191
  76.9 30.3 %collective-permute-start.10 = (bf16[8,208,256]{2,1,0:T(8,128)(2,1)S(1)}, bf16[8,208,256]{2,1,0:T(8,128)(2,1)S(1)}, u32[]{:S(2)}, u32[]{:S(2)}) collective-permute-start(bf16[8,208,256]{2,1,0:T(8,128)(2,1)S(1)} %pad_maximum_fusion.11.refs_2_), channel_id=1, source_target_pairs={{0,4},{1,5},{4,0},{5,1},{8,12},{9,13},{12,8},{13,9},{16,20},{17,21... | collective-permute-start | bytes 2555912 | tf_op jit(solution)/shard_map/ppermute | solution.py:191
  78.7 28.6 %collective-permute-start.7 = (bf16[8,192,256]{2,1,0:T(8,128)(2,1)S(1)}, bf16[8,192,256]{2,1,0:T(8,128)(2,1)S(1)}, u32[]{:S(2)}, u32[]{:S(2)}) collective-permute-start(bf16[8,192,256]{2,1,0:T(8,128)(2,1)S(1)} %pad_maximum_fusion.14.refs_0_), channel_id=1, source_target_pairs={{0,1},{1,0},{4,5},{5,4},{8,9},{9,8},{12,13},{13,12},{16,17},{17,16... | collective-permute-start | bytes 2359304 | tf_op jit(solution)/shard_map/ppermute | solution.py:191
  104.7 29.8 %collective-permute-start.15 = (bf16[4,192,384]{2,1,0:T(8,128)(2,1)}, bf16[4,192,384]{2,1,0:T(8,128)(2,1)}, u32[]{:S(2)}, u32[]{:S(2)}) collective-permute-start(bf16[4,192,384]{2,1,0:T(8,128)(2,1)} %get-tuple-element.216), channel_id=1, source_target_pairs={{0,1},{1,0},{4,5},{5,4},{8,9},{9,8},{12,13},{13,12},{16,17},{17,16... | collective-permute-start | bytes 1769480 | tf_op jit(solution)/shard_map/ppermute | solution.py:191
  105.8 28.8 %collective-permute-start.14 = (bf16[4,192,384]{2,1,0:T(8,128)(2,1)}, bf16[4,192,384]{2,1,0:T(8,128)(2,1)}, u32[]{:S(2)}, u32[]{:S(2)}) collective-permute-start(bf16[4,192,384]{2,1,0:T(8,128)(2,1)} %get-tuple-element.217), channel_id=1, source_target_pairs={{0,4},{1,5},{4,0},{5,1},{8,12},{9,13},{12,8},{13,9},{16,20},{17,21... | collective-permute-start | bytes 1769480 | tf_op jit(solution)/shard_map/ppermute | solution.py:191
  107.2 27.4 %collective-permute-start.13 = (bf16[1,384,384]{2,1,0:T(8,128)(2,1)S(1)}, bf16[1,384,384]{2,1,0:T(8,128)(2,1)S(1)}, u32[]{:S(2)}, u32[]{:S(2)}) collective-permute-start(bf16[1,384,384]{2,1,0:T(8,128)(2,1)S(1)} %get-tuple-element.121), channel_id=1, source_target_pairs={{0,8},{1,9},{4,12},{5,13},{8,0},{9,1},{12,4},{13,5},{16,24},{17,25... | collective-permute-start | bytes 884744 | tf_op jit(solution)/shard_map/ppermute | solution.py:191
  146.2 59.9 %collective-permute-start.19 = (bf16[8,192,384]{2,1,0:T(8,128)(2,1)S(1)}, bf16[8,192,384]{2,1,0:T(8,128)(2,1)}, u32[]{:S(2)}, u32[]{:S(2)}) collective-permute-start(bf16[8,192,384]{2,1,0:T(8,128)(2,1)S(1)} %pad_maximum_fusion.7.refs_2_), channel_id=1, source_target_pairs={{0,4},{1,5},{4,0},{5,1},{8,12},{9,13},{12,8},{13,9},{16,20},{17,21... | collective-permute-start | bytes 3538952 | tf_op jit(solution)/shard_map/ppermute | solution.py:191
  149.3 56.8 %collective-permute-start.18 = (bf16[8,192,384]{2,1,0:T(8,128)(2,1)}, bf16[8,192,384]{2,1,0:T(8,128)(2,1)}, u32[]{:S(2)}, u32[]{:S(2)}) collective-permute-start(bf16[8,192,384]{2,1,0:T(8,128)(2,1)} %pad_maximum_fusion.6.refs_0_), channel_id=1, source_target_pairs={{0,1},{1,0},{4,5},{5,4},{8,9},{9,8},{12,13},{13,12},{16,17},{17,16... | collective-permute-start | bytes 3538952 | tf_op jit(solution)/shard_map/ppermute | solution.py:191
  150.2 50.0 %collective-permute-start.17 = (bf16[2,384,384]{2,1,0:T(8,128)(2,1)}, bf16[2,384,384]{2,1,0:T(8,128)(2,1)}, u32[]{:S(2)}, u32[]{:S(2)}) collective-permute-start(bf16[2,384,384]{2,1,0:T(8,128)(2,1)} %pad_maximum_fusion.16), channel_id=1, source_target_pairs={{0,16},{1,17},{4,20},{5,21},{8,24},{9,25},{12,28},{13,29},{16,0},{... | collective-permute-start | bytes 1769480 | tf_op jit(solution)/shard_map/ppermute | solution.py:191
  204.6 45.4 %collective-permute-start.24 = (bf16[4,192,384]{2,1,0:T(8,128)(2,1)}, bf16[4,192,384]{2,1,0:T(8,128)(2,1)}, u32[]{:S(2)}, u32[]{:S(2)}) collective-permute-start(bf16[4,192,384]{2,1,0:T(8,128)(2,1)} %get-tuple-element.214), channel_id=1, source_target_pairs={{0,1},{1,0},{4,5},{5,4},{8,9},{9,8},{12,13},{13,12},{16,17},{17,16... | collective-permute-start | bytes 1769480 | tf_op jit(solution)/shard_map/ppermute | solution.py:191
  247.4 87.2 %collective-permute-start.20 = (bf16[8,192,384]{2,1,0:T(8,128)(2,1)}, bf16[8,192,384]{2,1,0:T(8,128)(2,1)}, u32[]{:S(2)}, u32[]{:S(2)}) collective-permute-start(bf16[8,192,384]{2,1,0:T(8,128)(2,1)} %get-tuple-element.135), channel_id=1, source_target_pairs={{0,1},{1,0},{4,5},{5,4},{8,9},{9,8},{12,13},{13,12},{16,17},{17,16... | collective-permute-start | bytes 3538952 | tf_op jit(solution)/shard_map/ppermute | solution.py:238
  248.0 86.6 %collective-permute-start.21 = (bf16[8,192,384]{2,1,0:T(8,128)(2,1)}, bf16[8,192,384]{2,1,0:T(8,128)(2,1)}, u32[]{:S(2)}, u32[]{:S(2)}) collective-permute-start(bf16[8,192,384]{2,1,0:T(8,128)(2,1)} %get-tuple-element.136), channel_id=1, source_target_pairs={{0,4},{1,5},{4,0},{5,1},{8,12},{9,13},{12,8},{13,9},{16,20},{17,21... | collective-permute-start | bytes 3538952 | tf_op jit(solution)/shard_map/ppermute | solution.py:238
  249.5 40.3 %collective-permute-start.22 = (bf16[4,192,384]{2,1,0:T(8,128)(2,1)}, bf16[4,192,384]{2,1,0:T(8,128)(2,1)S(1)}, u32[]{:S(2)}, u32[]{:S(2)}) collective-permute-start(bf16[4,192,384]{2,1,0:T(8,128)(2,1)} %get-tuple-element.215), channel_id=1, source_target_pairs={{0,4},{1,5},{4,0},{5,1},{8,12},{9,13},{12,8},{13,9},{16,20},{17,21... | collective-permute-start | bytes 1769480 | tf_op jit(solution)/shard_map/ppermute | solution.py:191
  251.4 93.9 %collective-permute-start.25 = (bf16[8,192,384]{2,1,0:T(8,128)(2,1)S(1)}, bf16[8,192,384]{2,1,0:T(8,128)(2,1)}, u32[]{:S(2)}, u32[]{:S(2)}) collective-permute-start(bf16[8,192,384]{2,1,0:T(8,128)(2,1)S(1)} %pad_maximum_fusion.9.refs_2_), channel_id=1, source_target_pairs={{0,4},{1,5},{4,0},{5,1},{8,12},{9,13},{12,8},{13,9},{16,20},{17,21... | collective-permute-start | bytes 3538952 | tf_op jit(solution)/shard_map/ppermute | solution.py:191
  290.9 55.8 %collective-permute-start.23 = (bf16[8,192,384]{2,1,0:T(8,128)(2,1)}, bf16[8,192,384]{2,1,0:T(8,128)(2,1)}, u32[]{:S(2)}, u32[]{:S(2)}) collective-permute-start(bf16[8,192,384]{2,1,0:T(8,128)(2,1)} %pad_maximum_fusion.8.refs_0_), channel_id=1, source_target_pairs={{0,1},{1,0},{4,5},{5,4},{8,9},{9,8},{12,13},{13,12},{16,17},{17,16... | collective-permute-start | bytes 3538952 | tf_op jit(solution)/shard_map/ppermute | solution.py:191
  334.6 63.4 %collective-permute-start.29 = (bf16[8,192,384]{2,1,0:T(8,128)(2,1)}, bf16[8,192,384]{2,1,0:T(8,128)(2,1)}, u32[]{:S(2)}, u32[]{:S(2)}) collective-permute-start(bf16[8,192,384]{2,1,0:T(8,128)(2,1)} %get-tuple-element.157), channel_id=1, source_target_pairs={{0,4},{1,5},{4,0},{5,1},{8,12},{9,13},{12,8},{13,9},{16,20},{17,21... | collective-permute-start | bytes 3538952 | tf_op jit(solution)/shard_map/ppermute | solution.py:238
  336.2 61.8 %collective-permute-start.28 = (bf16[8,192,384]{2,1,0:T(8,128)(2,1)}, bf16[8,192,384]{2,1,0:T(8,128)(2,1)}, u32[]{:S(2)}, u32[]{:S(2)}) collective-permute-start(bf16[8,192,384]{2,1,0:T(8,128)(2,1)} %get-tuple-element.156), channel_id=1, source_target_pairs={{0,1},{1,0},{4,5},{5,4},{8,9},{9,8},{12,13},{13,12},{16,17},{17,16... | collective-permute-start | bytes 3538952 | tf_op jit(solution)/shard_map/ppermute | solution.py:238
  340.9 57.1 %collective-permute-start.26 = (bf16[4,192,384]{2,1,0:T(8,128)(2,1)}, bf16[4,192,384]{2,1,0:T(8,128)(2,1)}, u32[]{:S(2)}, u32[]{:S(2)}) collective-permute-start(bf16[4,192,384]{2,1,0:T(8,128)(2,1)} %slice.557), channel_id=1, source_target_pairs={{0,4},{1,5},{4,0},{5,1},{8,12},{9,13},{12,8},{13,9},{16,20},{17,21... | collective-permute-start | bytes 1769480 | tf_op jit(solution)/shard_map/ppermute | solution.py:238
  345.3 52.7 %collective-permute-start.27 = (bf16[4,192,384]{2,1,0:T(8,128)(2,1)}, bf16[4,192,384]{2,1,0:T(8,128)(2,1)S(1)}, u32[]{:S(2)}, u32[]{:S(2)}) collective-permute-start(bf16[4,192,384]{2,1,0:T(8,128)(2,1)} %slice.556), channel_id=1, source_target_pairs={{0,1},{1,0},{4,5},{5,4},{8,9},{9,8},{12,13},{13,12},{16,17},{17,16... | collective-permute-start | bytes 1769480 | tf_op jit(solution)/shard_map/ppermute | solution.py:238
  398.1 45.0 %collective-permute-start.35 = (bf16[8,192,384]{2,1,0:T(8,128)(2,1)}, bf16[8,192,384]{2,1,0:T(8,128)(2,1)}, u32[]{:S(2)}, u32[]{:S(2)}) collective-permute-start(bf16[8,192,384]{2,1,0:T(8,128)(2,1)} %get-tuple-element.169), channel_id=1, source_target_pairs={{0,1},{1,0},{4,5},{5,4},{8,9},{9,8},{12,13},{13,12},{16,17},{17,16... | collective-permute-start | bytes 3538952 | tf_op jit(solution)/shard_map/ppermute | solution.py:238
  398.8 44.3 %collective-permute-start.36 = (bf16[8,192,384]{2,1,0:T(8,128)(2,1)}, bf16[8,192,384]{2,1,0:T(8,128)(2,1)}, u32[]{:S(2)}, u32[]{:S(2)}) collective-permute-start(bf16[8,192,384]{2,1,0:T(8,128)(2,1)} %get-tuple-element.170), channel_id=1, source_target_pairs={{0,4},{1,5},{4,0},{5,1},{8,12},{9,13},{12,8},{13,9},{16,20},{17,21... | collective-permute-start | bytes 3538952 | tf_op jit(solution)/shard_map/ppermute | solution.py:238
  403.3 39.8 %collective-permute-start.32 = (bf16[2,384,384]{2,1,0:T(8,128)(2,1)}, bf16[2,384,384]{2,1,0:T(8,128)(2,1)}, u32[]{:S(2)}, u32[]{:S(2)}) collective-permute-start(bf16[2,384,384]{2,1,0:T(8,128)(2,1)} %fusion.26), channel_id=1, source_target_pairs={{0,8},{1,9},{4,12},{5,13},{24,16},{25,17},{28,20},{29,21},{2,10},{... | collective-permute-start | bytes 1769480 | tf_op jit(solution)/shard_map/ppermute | solution.py:238
  408.0 35.2 %collective-permute-start.34 = (bf16[4,192,384]{2,1,0:T(8,128)(2,1)}, bf16[4,192,384]{2,1,0:T(8,128)(2,1)}, u32[]{:S(2)}, u32[]{:S(2)}) collective-permute-start(bf16[4,192,384]{2,1,0:T(8,128)(2,1)} %slice.554), channel_id=1, source_target_pairs={{0,1},{1,0},{4,5},{5,4},{8,9},{9,8},{12,13},{13,12},{16,17},{17,16... | collective-permute-start | bytes 1769480 | tf_op jit(solution)/shard_map/ppermute | solution.py:238
  414.6 28.6 %collective-permute-start.33 = (bf16[4,192,384]{2,1,0:T(8,128)(2,1)}, bf16[4,192,384]{2,1,0:T(8,128)(2,1)}, u32[]{:S(2)}, u32[]{:S(2)}) collective-permute-start(bf16[4,192,384]{2,1,0:T(8,128)(2,1)} %slice.555), channel_id=1, source_target_pairs={{0,4},{1,5},{4,0},{5,1},{8,12},{9,13},{12,8},{13,9},{16,20},{17,21... | collective-permute-start | bytes 1769480 | tf_op jit(solution)/shard_map/ppermute | solution.py:238
  445.7 28.5 %collective-permute-start.31 = (bf16[4,2,512]{2,1,0:T(2,128)(2,1)S(1)}, bf16[4,2,512]{2,1,0:T(2,128)(2,1)S(1)}, u32[]{:S(2)}, u32[]{:S(2)}) collective-permute-start(bf16[4,2,512]{2,1,0:T(2,128)(2,1)S(1)} %slice.399), channel_id=1, source_target_pairs={{1,0},{3,2},{5,4},{7,6},{9,8},{11,10},{13,12},{15,14},{17,16},{19,... | collective-permute-start | bytes 24584 | tf_op jit(solution)/shard_map/ppermute | solution.py:19
  449.4 55.7 %collective-permute-start.47 = (bf16[2,384,384]{2,1,0:T(8,128)(2,1)}, bf16[2,384,384]{2,1,0:T(8,128)(2,1)}, u32[]{:S(2)}, u32[]{:S(2)}) collective-permute-start(bf16[2,384,384]{2,1,0:T(8,128)(2,1)} %add_convert_fusion.3), channel_id=1, source_target_pairs={{8,16},{9,17},{12,20},{13,21},{16,8},{17,9},{20,12},{21,13},{10,18... | collective-permute-start | bytes 1769480 | tf_op jit(solution)/shard_map/ppermute | solution.py:238
  453.5 53.3 %collective-permute-start.49 = (bf16[2,384,384]{2,1,0:T(8,128)(2,1)}, bf16[2,384,384]{2,1,0:T(8,128)(2,1)}, u32[]{:S(2)}, u32[]{:S(2)}) collective-permute-start(bf16[2,384,384]{2,1,0:T(8,128)(2,1)} %fusion.21), channel_id=1, source_target_pairs={{0,8},{1,9},{4,12},{5,13},{24,16},{25,17},{28,20},{29,21},{2,10},{... | collective-permute-start | bytes 1769480 | tf_op jit(solution)/shard_map/ppermute | solution.py:238
  461.3 41.5 %collective-permute-start.53 = (bf16[4,192,384]{2,1,0:T(8,128)(2,1)}, bf16[4,192,384]{2,1,0:T(8,128)(2,1)}, u32[]{:S(2)}, u32[]{:S(2)}) collective-permute-start(bf16[4,192,384]{2,1,0:T(8,128)(2,1)} %slice.552), channel_id=1, source_target_pairs={{0,1},{1,0},{4,5},{5,4},{8,9},{9,8},{12,13},{13,12},{16,17},{17,16... | collective-permute-start | bytes 1769480 | tf_op jit(solution)/shard_map/ppermute | solution.py:238
  467.8 42.3 %collective-permute-start.52 = (bf16[4,192,384]{2,1,0:T(8,128)(2,1)}, bf16[4,192,384]{2,1,0:T(8,128)(2,1)}, u32[]{:S(2)}, u32[]{:S(2)}) collective-permute-start(bf16[4,192,384]{2,1,0:T(8,128)(2,1)} %slice.553), channel_id=1, source_target_pairs={{0,4},{1,5},{4,0},{5,1},{8,12},{9,13},{12,8},{13,9},{16,20},{17,21... | collective-permute-start | bytes 1769480 | tf_op jit(solution)/shard_map/ppermute | solution.py:238
  502.6 50.5 %collective-permute-start.37 = (bf16[1024,1024]{1,0:T(8,128)(2,1)}, bf16[1024,1024]{1,0:T(8,128)(2,1)}, u32[]{:S(2)}, u32[]{:S(2)}) collective-permute-start(bf16[1024,1024]{1,0:T(8,128)(2,1)} %fusion.8), channel_id=1, source_target_pairs={{0,2},{2,0},{1,3},{3,1},{4,6},{6,4},{5,7},{7,5},{8,10},{10,8},{9,1... | collective-permute-start | bytes 6291464 | tf_op jit(solution)/shard_map/ppermute | solution.py:186
  502.8 23.4 %collective-permute-start.41 = (bf16[8,192,256]{2,1,0:T(8,128)(2,1)}, bf16[8,192,256]{2,1,0:T(8,128)(2,1)S(1)}, u32[]{:S(2)}, u32[]{:S(2)}) collective-permute-start(bf16[8,192,256]{2,1,0:T(8,128)(2,1)} %get-tuple-element.184), channel_id=1, source_target_pairs={{0,4},{1,5},{4,0},{5,1},{8,12},{9,13},{12,8},{13,9},{16,20},{17,21... | collective-permute-start | bytes 2359304 | tf_op jit(solution)/shard_map/ppermute | solution.py:238
  505.1 28.4 %collective-permute-start.39 = (bf16[8,192,256]{2,1,0:T(8,128)(2,1)S(1)}, bf16[8,192,256]{2,1,0:T(8,128)(2,1)S(1)}, u32[]{:S(2)}, u32[]{:S(2)}) collective-permute-start(bf16[8,192,256]{2,1,0:T(8,128)(2,1)S(1)} %copy-done.66), channel_id=1, source_target_pairs={{0,1},{1,0},{4,5},{5,4},{8,9},{9,8},{12,13},{13,12},{16,17},{17,16... | collective-permute-start | bytes 2359304 | tf_op jit(solution)/shard_map/ppermute | solution.py:238
  506.8 79.0 %collective-permute-start.38 = (bf16[1024,1024]{1,0:T(8,128)(2,1)}, bf16[1024,1024]{1,0:T(8,128)(2,1)}, u32[]{:S(2)}, u32[]{:S(2)}) collective-permute-start(bf16[1024,1024]{1,0:T(8,128)(2,1)} %slice.325), channel_id=1, source_target_pairs={{0,2},{2,0},{1,3},{3,1},{4,6},{6,4},{5,7},{7,5},{8,10},{10,8},{9,1... | collective-permute-start | bytes 6291464 | tf_op jit(solution)/shard_map/ppermute | solution.py:186
  510.1 26.2 %collective-permute-start.48 = (bf16[1,384,384]{2,1,0:T(8,128)(2,1)S(1)}, bf16[1,384,384]{2,1,0:T(8,128)(2,1)S(1)}, u32[]{:S(2)}, u32[]{:S(2)}) collective-permute-start(bf16[1,384,384]{2,1,0:T(8,128)(2,1)S(1)} %slice.562), channel_id=1, source_target_pairs={{0,8},{1,9},{4,12},{5,13},{8,0},{9,1},{12,4},{13,5},{16,24},{17,25... | collective-permute-start | bytes 884744 | tf_op jit(solution)/shard_map/ppermute | solution.py:238
  533.4 14.7 %collective-permute-start.54 = (bf16[2,384,384]{2,1,0:T(8,128)(2,1)S(1)}, bf16[2,384,384]{2,1,0:T(8,128)(2,1)S(1)}, u32[]{:S(2)}, u32[]{:S(2)}) collective-permute-start(bf16[2,384,384]{2,1,0:T(8,128)(2,1)S(1)} %fusion.22), channel_id=1, source_target_pairs={{0,8},{1,9},{4,12},{5,13},{24,16},{25,17},{28,20},{29,21},{2,10},{... | collective-permute-start | bytes 1769480 | tf_op jit(solution)/shard_map/ppermute | solution.py:238
  536.3 26.8 %collective-permute-start.42 = (bf16[4,192,256]{2,1,0:T(8,128)(2,1)}, bf16[4,192,256]{2,1,0:T(8,128)(2,1)}, u32[]{:S(2)}, u32[]{:S(2)}) collective-permute-start(bf16[4,192,256]{2,1,0:T(8,128)(2,1)} %slice.558), channel_id=1, source_target_pairs={{0,1},{1,0},{4,5},{5,4},{8,9},{9,8},{12,13},{13,12},{16,17},{17,16... | collective-permute-start | bytes 1179656 | tf_op jit(solution)/shard_map/ppermute | solution.py:238
  537.2 34.3 %collective-permute-start.40 = (bf16[4,192,256]{2,1,0:T(8,128)(2,1)}, bf16[4,192,256]{2,1,0:T(8,128)(2,1)}, u32[]{:S(2)}, u32[]{:S(2)}) collective-permute-start(bf16[4,192,256]{2,1,0:T(8,128)(2,1)} %slice.559), channel_id=1, source_target_pairs={{0,4},{1,5},{4,0},{5,1},{8,12},{9,13},{12,8},{13,9},{16,20},{17,21... | collective-permute-start | bytes 1179656 | tf_op jit(solution)/shard_map/ppermute | solution.py:238
  548.1 41.9 %collective-permute-start.51 = (bf16[1,384,384]{2,1,0:T(8,128)(2,1)}, bf16[1,384,384]{2,1,0:T(8,128)(2,1)}, u32[]{:S(2)}, u32[]{:S(2)}) collective-permute-start(bf16[1,384,384]{2,1,0:T(8,128)(2,1)} %slice.561), channel_id=1, source_target_pairs={{0,8},{1,9},{4,12},{5,13},{8,0},{9,1},{12,4},{13,5},{16,24},{17,25... | collective-permute-start | bytes 884744 | tf_op jit(solution)/shard_map/ppermute | solution.py:238
  563.1 28.3 %collective-permute-start.56 = (bf16[1,384,384]{2,1,0:T(8,128)(2,1)S(1)}, bf16[1,384,384]{2,1,0:T(8,128)(2,1)S(1)}, u32[]{:S(2)}, u32[]{:S(2)}) collective-permute-start(bf16[1,384,384]{2,1,0:T(8,128)(2,1)S(1)} %slice.560), channel_id=1, source_target_pairs={{0,8},{1,9},{4,12},{5,13},{8,0},{9,1},{12,4},{13,5},{16,24},{17,25... | collective-permute-start | bytes 884744 | tf_op jit(solution)/shard_map/ppermute | solution.py:238
  574.9 20.4 %collective-permute-start.43 = (bf16[2,384,256]{2,1,0:T(8,128)(2,1)}, bf16[2,384,256]{2,1,0:T(8,128)(2,1)}, u32[]{:S(2)}, u32[]{:S(2)}) collective-permute-start(bf16[2,384,256]{2,1,0:T(8,128)(2,1)} %fusion.23), channel_id=1, source_target_pairs={{0,8},{1,9},{4,12},{5,13},{24,16},{25,17},{28,20},{29,21},{2,10},{... | collective-permute-start | bytes 1179656 | tf_op jit(solution)/shard_map/ppermute | solution.py:238
  594.8 20.7 %collective-permute-start.57 = (f32[3,2,64,384]{3,2,1,0:T(8,128)}, f32[3,2,64,384]{3,2,1,0:T(8,128)}, u32[]{:S(2)}, u32[]{:S(2)}) collective-permute-start(f32[3,2,64,384]{3,2,1,0:T(8,128)} %get-tuple-element.213), channel_id=1, source_target_pairs={{0,2},{2,0},{1,3},{3,1},{4,6},{6,4},{5,7},{7,5},{8,10},{10,8},{9,1... | collective-permute-start | bytes 1769480 | tf_op jit(solution)/shard_map/ppermute | solution.py:186
  (87 other events, 682.7 us)
Sparse Core Ops, SparseCore 0:
  10.8 81.7 all-gather.3
  96.0 103.4 all-gather.5
  474.3 76.3 reduce-scatter.1

commit v5 on v4

--- a/solution.py
+++ b/solution.py
@@ -231,11 +231,9 @@
 
 def scatter_steps(parts):
     far, first_order, second_order = bit_masks()
-    n_slots = lax.axis_size("chip") * lax.axis_size("ctx")
-
-    def send(block, mask, senders=range(n_slots)):
-        route = [(i, i ^ mask) for i in senders]
-        return lax.ppermute(block.astype(bf16), ("chip", "ctx"), route)
+
+    def send(block, mask):
+        return across(block.astype(bf16), mask)
 
     orders = (first_order, second_order)
     got = yield [send(parts[1], first_order[-1]), send(parts[3], second_order[-1])]
@@ -245,15 +243,6 @@
         got = yield [send(k[mid:], order[step]) for k, order in zip(keeps, orders)]
         keeps = [k[:mid] + g.astype(f32) for k, g in zip(keeps, got)]
     keep = jnp.concatenate(keeps, axis=1)
-    if len(far) == 2:
-        low, high = far
-        outer = [i for i in range(n_slots) if (i & low == 0) == (i & high == 0)]
-        inner = [i for i in range(n_slots) if i not in outer]
-        (got,) = yield [send(keep[2:], low, outer)]
-        distant = keep[2:] + got.astype(f32)[::-1]
-        (got,) = yield [send(distant, low | high, inner)]
-        keep = keep[:2] + got.astype(f32)[::-1]
-        far = far[:1]
     for mask in reversed(far):
         mid = keep.shape[0] // 2
         (got,) = yield [send(keep[mid:], mask)]
@@ -268,6 +257,8 @@
         self.total = None
 
     def advance(self, *done):
+        if self.total is not None:
+            return
         try:
             self.got = self.steps.send([after(g, *done) for g in self.got])
         except StopIteration as end:
@@ -315,7 +306,7 @@
     return [shapes[operand] for operand in sorted(shapes)]
 
 
-def ffn_kernel(geometry, out_geometry, first, last, own_ref, n_ref, go_ref, *refs):
+def ffn_kernel(geometry, out_geometry, first, own_ref, n_ref, go_ref, *refs):
     plan, segments, n_ctx = geometry
     out_plan = out_geometry[0]
     count, out_count = part_count(plan), part_count(out_plan)
@@ -325,9 +316,6 @@
         refs = refs[2:]
     res_ref, gn_ref = refs[:2]
     refs = refs[2:]
-    if last:
-        res_low_ref, gn_low_ref = refs[:2]
-        refs = refs[2:]
     grads, refs = refs[:out_count], refs[out_count:]
     gate_m, up_m, down_m, d_gate, d_up, d_down, h_m, gg_m, gu_m, sems = refs
     own = own_ref[0]
@@ -361,10 +349,7 @@
         res = res_in[...] + res
         gn = gn_in[...] + gn
     res_ref[...] = res
-    gn_ref[...] = gn
-    if last:
-        res_low_ref[...] = res.astype(bf16)
-        gn_low_ref[...] = gn.astype(bf16)
+    gn_ref[...] = gn.astype(gn_ref.dtype)
     d_gate[...] += lax.dot_general(n, gg_m[...], TN, preferred_element_type=f32)
     d_up[...] += lax.dot_general(n, gu_m[...], TN, preferred_element_type=f32)
     d_down[...] += lax.dot_general(h_m[...], go, TN, preferred_element_type=f32)
@@ -390,15 +375,14 @@
     row_spec = pl.BlockSpec((rows, width), lambda i, o: (i, 0))
     any_spec = pl.BlockSpec(memory_space=pl.ANY)
     outs = pl.pallas_call(
-        functools.partial(ffn_kernel, geometry, out_geometry, first, last),
-        out_shape=[jax.ShapeDtypeStruct((total, width), f32)] * 2
-        + [jax.ShapeDtypeStruct((total, width), bf16)] * (2 if last else 0)
+        functools.partial(ffn_kernel, geometry, out_geometry, first),
+        out_shape=[jax.ShapeDtypeStruct((total, width), d) for d in (f32, bf16 if last else f32)]
         + [jax.ShapeDtypeStruct(s, bf16) for s in part_shapes(out_plan, lanes)],
         grid_spec=pltpu.PrefetchScalarGridSpec(
             num_scalar_prefetch=1,
             grid=(total // rows,),
             in_specs=[row_spec] * 2 + [any_spec] * count + [row_spec] * (0 if first else 2),
-            out_specs=[row_spec] * (4 if last else 2) + [any_spec] * out_count,
+            out_specs=[row_spec] * 2 + [any_spec] * out_count,
             scratch_shapes=[
                 pltpu.VMEM((width, hidden_count), bf16),
                 pltpu.VMEM((width, hidden_count), bf16),
@@ -412,14 +396,12 @@
                 pltpu.SemaphoreType.DMA((max(len(plan), len(out_plan)) * len(segments),)),
             ],
         ),
-        input_output_aliases={} if first else {3 + count: 0, 4 + count: 1},
+        input_output_aliases={} if first else {3 + count: 0} if last else {3 + count: 0, 4 + count: 1},
         compiler_params=pltpu.CompilerParams(
             vmem_limit_bytes=VMEM_LIMIT, dimension_semantics=("arbitrary",)
         ),
         cost_estimate=SMALL_COST,
     )(own, nffn, go, *weights, *(() if first else totals))
-    if last:
-        return outs[:4], outs[4:]
     return outs[:2], outs[2:]
 
 
@@ -493,9 +475,11 @@
 
 
 def branch_grad_kernel(
-    own_first, gn_ref, got_ref, residual_ref, go_ref, gain_ref, mixer_ref, conv_ref, gate_c_ref,
-    w_ref, grad_residual_ref, grad_conv_ref, grad_c_ref, grad_w_ref, grad_gain_ref, total_ref,
+    own_first, geometry, own_ref, gn_ref, got_ref, residual_ref, go_ref, gain_ref, mixer_ref,
+    conv_ref, gate_c_ref, w_ref, grad_residual_ref, grad_conv_ref, grad_c_ref, grad_gain_ref,
+    part_ref, total_ref, low_ref, sems,
 ):
+    plan, segments, n_ctx = geometry
     step = pl.program_id(0)
 
     @pl.when(step == 0)
@@ -503,7 +487,7 @@
         total_ref[...] = jnp.zeros_like(total_ref)
         grad_gain_ref[...] = jnp.zeros_like(grad_gain_ref)
 
-    incoming = gn_ref[...] + got_ref[...].astype(f32)
+    incoming = gn_ref[...].astype(f32) + got_ref[...].astype(f32)
     residual = residual_ref[...]
     scale = lax.rsqrt(jnp.mean(residual * residual, axis=-1, keepdims=True) + EPSILON)
     weighted = incoming * gain_ref[...]
@@ -525,7 +509,9 @@
 
     @pl.when(step == pl.num_programs(0) - 1)
     def _():
-        grad_w_ref[...] = total_ref[...].astype(bf16)
+        low_ref[...] = total_ref[...].astype(bf16)
+        pairs = slot_pairs(own_ref[0], plan, (part_ref,), segments, n_ctx, (low_ref,))
+        copy_all([(b, a) for a, b in pairs], sems)
 
 
 def in_grad_kernel(
@@ -649,7 +635,7 @@
     small_block = in_core_order(small, swapped[in_parts * depth :][:5, :depth], 1)
     small_block = jnp.pad(small_block, ((0, 11), (0, 256 - 2 * depth)))
     out_block = w_out.reshape(depth, out_parts, 256).transpose(1, 0, 2).reshape(-1, 256)
-    mix_block = jnp.concatenate([in_block, small_block], axis=0)
+    mix_block = jnp.concatenate([in_block, out_block, small_block], axis=0)
 
     both = jnp.stack([w_gate, w_up]).reshape(2, depth, groups, 2, CHUNKS, sub)
     both = both.transpose(3, 4, 0, 1, 2, 5).reshape(2, CHUNKS, 2, depth, lanes)
@@ -663,16 +649,19 @@
     )
 
     mix_rows = mix_block.shape[0]
-    mix_cut = in_parts * depth
+    mix_cut = -(-mix_rows // 32) * 16
     in_rows = in_parts * 2 * depth
     mix_segments = [
         (k * 2 * depth, 2 * depth, 0, 256, 0, 2 * depth, 0, in_cols, 256 * k)
         for k in range(in_parts)
     ]
-    out_segments = [
-        (k * depth, depth, 0, 256, 0, depth, 0, wide, 256 * k) for k in range(out_parts)
-    ]
-    small_segment = (in_rows, 16, 0, 256, 1, 16, 0, 256, 0)
+    def out_segments(base, target):
+        return [
+            (base + k * depth, depth, 0, 256, target, depth, 0, wide, 256 * k)
+            for k in range(out_parts)
+        ]
+
+    small_segment = (in_rows + out_parts * depth, 16, 0, 256, 2, 16, 0, 256, 0)
     mix_plan = gather_plan(mix_cut, mix_rows)
     chunk_rows = chunk_blocks.shape[1]
     chunk_cut = chunk_rows // 2
@@ -688,8 +677,6 @@
     whole_geometry = (whole_plan, chunk_segments, n_ctx)
     step_geometry = (gather_plan(chunk_cut, chunk_rows), chunk_segments, n_ctx)
 
-    out_all = lax.all_gather(out_block, ("chip", "ctx"))
-
     token_rows = tokens.reshape(rows, width)
     inputs = jnp.concatenate([token_rows, swap(token_rows)], axis=0)
     go_rows = cotangent.reshape(rows, width)
@@ -704,7 +691,9 @@
     hold = mix_block[None]
     for mask in far:
         hold = doubled(hold, across(hold, mask))
-    chunk_all = lax.all_gather(after(chunk_blocks[1], hold), ("chip", "ctx"))
+    second_all, last_all = [
+        lax.all_gather(after(block, hold), ("chip", "ctx")) for block in chunk_blocks[1:]
+    ]
     mix_halves = [hold[:, :mix_cut], hold[:, mix_cut:]]
     next_hold = after(chunk_blocks[0][None], hold)
     far_left = list(far)
@@ -725,17 +714,16 @@
     for mask in far_left:
         next_got = across(next_hold, mask)
         next_hold = doubled(next_hold, next_got)
-    in_half, small_all = move(
+    in_half, out_half, small_all = move(
         own,
         mix_parts,
-        [(width, n_ctx * in_cols), (n_chip * 16, n_ctx * 256)],
-        (mix_plan, mix_segments + [small_segment], n_ctx),
+        [(width, n_ctx * in_cols), (channels, width), (n_chip * 16, n_ctx * 256)],
+        (mix_plan, mix_segments + out_segments(in_rows, 1) + [small_segment], n_ctx),
         4,
         False,
     )
     in_half = after(in_half, next_got)
     next_halves = [next_hold[:, :chunk_cut], next_hold[:, chunk_cut:]]
-    last_hold = after(chunk_blocks[2][None], next_got)
 
     def step_of(halves, step):
         return [across(h, order[step]) for h, order in zip(halves, orders)]
@@ -764,7 +752,6 @@
     wide_rows, thin_rows = (piece, width), (piece, channels)
     taps = jnp.pad(taps, ((0, 5), (0, 0)))
     next_got = step_of(next_halves, 0)
-    last_got = across(last_hold, far[0])
     normed_low, projected = row_call(
         in_kernel,
         blocks,
@@ -778,14 +765,6 @@
             ((2 * rows, 3 * channels), f32, (piece, 3 * channels), at),
         ],
     )
-    (out_half,) = move(
-        own,
-        [after(out_all, projected)],
-        [(channels, width)],
-        ([(0, i, None, 0, out_parts * depth) for i in range(slots)], out_segments, n_ctx),
-        1,
-        False,
-    )
     tail = projected.reshape(blocks, piece, 3 * channels)[:, piece - 2 :]
     tail = (tail[:, :, :channels] * tail[:, :, 2 * channels :]).astype(bf16)
     before = passed_along(tail, "ctx", 1)
@@ -794,13 +773,11 @@
     def halo_at(i):
         return (i, 0, 0)
 
-    conv_taps = after(taps, last_got, *next_got)
+    conv_taps = after(taps, *next_got)
     next_halves = [
         doubled(h, g) for h, g in zip(next_halves, all_after(next_got, projected))
     ]
-    last_hold = doubled(last_hold, after(last_got, projected))
     next_got = step_of(next_halves, 1)
-    last_got = across(last_hold, far[1])
     mixer_out, convolved, branch = row_call(
         conv_kernel,
         blocks,
@@ -830,32 +807,21 @@
 
     next_parts = [next_halves[0], next_got[0], next_halves[1], next_got[1]]
     next_parts = all_after(next_parts, nffn_low)
-    last_hold = doubled(last_hold, after(last_got, nffn_low))
-    last_halves = [last_hold[:, :chunk_cut], last_hold[:, chunk_cut:]]
-    last_got_halves = step_of(last_halves, 0)
 
     totals, first_grads = ffn_chunk(
-        own, nffn_low, after(go, last_got), next_parts, None, step_geometry, step_geometry,
-        hidden_count,
+        own, nffn_low, go, next_parts, None, step_geometry, step_geometry, hidden_count
     )
     first_stages = Stages(first_grads)
-    nffn_then = after(nffn_low, *last_got_halves)
-    last_halves = [
-        doubled(h, g) for h, g in zip(last_halves, all_after(last_got_halves, totals[1]))
-    ]
-    last_got_halves = step_of(last_halves, 1)
     totals, second_grads = ffn_chunk(
-        own, nffn_then, go, [chunk_all], totals, whole_geometry, step_geometry, hidden_count
+        own, nffn_low, go, [second_all], totals, whole_geometry, step_geometry, hidden_count
     )
     second_stages = Stages(second_grads)
     nffn_then = after(nffn_low, *first_stages.got)
     first_stages.advance(totals[1])
-    last_got_halves = all_after(last_got_halves, totals[1])
-    last_parts = [last_halves[0], last_got_halves[0], last_halves[1], last_got_halves[1]]
     totals, last_grads = ffn_chunk(
-        own, nffn_then, go, last_parts, totals, step_geometry, step_geometry, hidden_count, last=True
-    )
-    ffn_out, grad_nffn, ffn_low, grad_low = totals
+        own, nffn_then, go, [last_all], totals, whole_geometry, step_geometry, hidden_count, last=True
+    )
+    ffn_out, grad_low = totals
     last_stages = Stages(last_grads)
     grad_got = swap(after(grad_low, *first_stages.got, *second_stages.got))
     first_stages.advance(grad_low)
@@ -873,11 +839,13 @@
     def gate_c_place(i):
         return ((i + seqs) % blocks, 1)
 
-    grad_residual, grad_conv, grad_c, grad_w_out, grad_gain_ffn = row_call(
-        functools.partial(branch_grad_kernel, seqs),
+    out_plan = [(0, i, None, 0, out_parts * depth) for i in range(slots)]
+    grad_residual, grad_conv, grad_c, grad_gain_ffn, grad_out_slots = row_call(
+        functools.partial(branch_grad_kernel, seqs, (out_plan, out_segments(0, 0), n_ctx)),
         blocks,
         [
-            (grad_nffn, wide_rows, turned),
+            (own, None, None),
+            (grad_low, wide_rows, turned),
             (grad_got, wide_rows, turned_back),
             (residual, wide_rows, turned),
             (go, wide_rows, turned),
@@ -891,10 +859,14 @@
             ((rows, width), f32, wide_rows, own_place),
             ((2 * rows, channels), f32, thin_rows, turned),
             ((2 * rows, channels), bf16, thin_rows, turned),
-            ((channels, width), bf16, (channels, width), still),
             ((1, width), f32, (1, width), still),
-        ],
-        scratch=[pltpu.VMEM((channels, width), f32)],
+            ((slots, out_parts * depth, 256), bf16, None, None),
+        ],
+        scratch=[
+            pltpu.VMEM((channels, width), f32),
+            pltpu.VMEM((channels, width), bf16),
+            pltpu.SemaphoreType.DMA((slots * out_parts,)),
+        ],
     )
     grad_gain_ffn = grad_gain_ffn[0]
     stages = (first_stages, second_stages, last_stages)
@@ -903,10 +875,8 @@
         s.advance(grad_c)
     head = grad_conv.reshape(blocks, piece, channels)[:, :2].astype(bf16)
     behind = passed_along(head, "ctx", -1)
-    grad_out_slots = grad_w_out.reshape(n_chip, depth, n_ctx, out_parts, 256)
-    grad_out_slots = grad_out_slots.transpose(0, 2, 3, 1, 4).reshape(slots, out_parts * depth, 256)
     out_sum = lax.psum_scatter(grad_out_slots, ("chip", "ctx"), scatter_dimension=0).astype(f32)
-    sum_plan = gather_plan(mix_cut, in_rows)
+    sum_plan = gather_plan(in_rows // 2, in_rows)
     grad_projected, grad_kernel, *mix_grad_parts = row_call(
         functools.partial(in_grad_kernel, (sum_plan, mix_segments, n_ctx), 4),
         blocks,
@@ -943,8 +913,9 @@
     for s in (mix_stages, second_stages, last_stages):
         s.advance(grad_mine)
     grad_normed = grad_mine + other_got.astype(f32)
-    ffn_got = swap(after(ffn_low[rows:], grad_other))
-    result = residual[:rows] + (after(ffn_out[:rows], grad_mine) + ffn_got.astype(f32))
+    ffn_late = after(ffn_out, grad_other)
+    ffn_got = swap(ffn_late[rows:].astype(bf16))
+    result = after(residual, grad_mine)[:rows] + (ffn_late[:rows] + ffn_got.astype(f32))
     result = result.astype(bf16).reshape(seqs, piece, width)
     own_inputs = token_rows.astype(f32)
     scale_mix = lax.rsqrt(jnp.mean(own_inputs * own_inputs, axis=-1, keepdims=True) + EPSILON)

time: 642 us -> 574 us (0.89)
  starting transfers between devices: 86.9 us -> 54.1 us
  local copies, waits for them, and re-layouts: 75.3 us -> 50.2 us
  other arithmetic: 78.9 us -> 65.6 us
    ppermute x28 -> x0, starting transfers between devices: 50.4 us -> none  [send(): return lax.ppermute(block.astype(bf16), ('chip', 'ctx'), route)]
    ppermute x22 -> x40, waiting for transfers between devices: 121 us -> 153 us  [across(): lax.ppermute(block, ('chip', 'ctx'), [(i, i ^ mask) for i in range(count)])]
    ppermute x28 -> x0, waiting for transfers between devices: 28.2 us -> none  [send(): return lax.ppermute(block.astype(bf16), ('chip', 'ctx'), route)]
    ppermute x22 -> x40, starting transfers between devices: 29.7 us -> 47.2 us  [across(): lax.ppermute(block, ('chip', 'ctx'), [(i, i ^ mask) for i in range(count)])]
    convert_element_type x16 -> x0, other arithmetic: 11.9 us -> none  [the longest x8 5.49 us: send(): return lax.ppermute(block.astype(bf16), ('chip', 'ctx'), route)]
    unnamed x143 -> x121, local copies, waits for them, and re-layouts: 16.9 us -> 13.7 us
  transfers between devices with their start and end apart: 66 -> 56, of which waited for: 13 -> 16; matrix products, arithmetic and copies ran while one was open for 23% -> 20% of each run, Pallas kernels for 33% -> 37%
where the time goes in v5:
time: 574 us; the launch traced here: 565 us
  Pallas kernels  210 us (37%)
  waiting for transfers between devices  154 us (27%)
  other arithmetic  65.6 us (11%)
  starting transfers between devices  54.1 us (9%)
  local copies, waits for them, and re-layouts  50.2 us (9%)
  between operations  15.6 us (3%)
  matrix products  15.3 us (3%)
    ppermute x40, waiting for transfers between devices, across(): lax.ppermute(block, ('chip', 'ctx'), [(i, i ^ mask) for i in range(count)])  153 us
    pallas_call x3, Pallas kernels, ffn_chunk(): pl.pallas_call(functools.partial(ffn_kernel, geometry, out_geometry, firs...  134 us
    pallas_call x5, Pallas kernels, row_call(): pl.pallas_call(body, grid=(steps,), in_specs=[pl.BlockSpec(memory_space=p...  69.9 us
    ppermute x40, starting transfers between devices, across(): lax.ppermute(block, ('chip', 'ctx'), [(i, i ^ mask) for i in range(count)])  47.2 us
    dot_general x2, matrix products, cross_cols(): lax.dot_general(left_operand, right_operand, (((1,), (1,)), ((), ())), pr...  15.3 us
    unnamed x121, local copies, waits for them, and re-layouts  13.7 us
  transfers between devices with their start and end apart: 56, of which 16 were waited for; matrix products, arithmetic and copies ran while one was open for 20% of the time, Pallas kernels for 37%

profile of v5, /device:TPU:0, one launch (start us, length us, event | category | flops | bytes accessed | tf_op | source)
XLA Modules:
  0.0 565.1 jit_solution(4041755703078708809)
XLA Ops:
  12.6 2.7 collective-permute-start.2
  16.3 6.0 %collective-permute-done.2 = bf16[1,528,256]{2,1,0:T(8,128)(2,1)S(1)} collective-permute-done((bf16[1,528,256]{2,1,0:T(8,128)(2,1)S(1)}, bf16[1,528,256]{2,1,0:T(8,128)(2,1)S(1)}, u32[]{:S(2)}, u32[]{:S(2)}) %collective-permute-start.2) | collective-permute-done | bytes 270368 | tf_op jit(solution)/shard_map/ppermute | solution.py:191
  22.4 2.8 collective-permute-start.3
  28.2 21.0 %collective-permute-done.3 = bf16[2,528,256]{2,1,0:T(8,128)(2,1)} collective-permute-done((bf16[2,528,256]{2,1,0:T(8,128)(2,1)S(1)}, bf16[2,528,256]{2,1,0:T(8,128)(2,1)}, u32[]{:S(2)}, u32[]{:S(2)}) %collective-permute-start.3) | collective-permute-done | bytes 540704 | tf_op jit(solution)/shard_map/ppermute | solution.py:191
  57.0 4.0 pad_maximum_fusion.x_ref
  61.0 7.8 %collective-permute-done.4 = bf16[4,272,256]{2,1,0:T(8,128)(2,1)} collective-permute-done((bf16[4,272,256]{2,1,0:T(8,128)(2,1)}, bf16[4,272,256]{2,1,0:T(8,128)(2,1)}, u32[]{:S(2)}, u32[]{:S(2)}) %collective-permute-start.4) | collective-permute-done | bytes 557088 | tf_op jit(solution)/shard_map/ppermute | solution.py:191
  71.8 2.3 pad_maximum_fusion.10.refs_2_
  78.6 4.9 pad_maximum_fusion.1.go_ref
  83.5 34.4 %collective-permute-done.11 = bf16[2,384,384]{2,1,0:T(8,128)(2,1)} collective-permute-done((bf16[2,384,384]{2,1,0:T(8,128)(2,1)}, bf16[2,384,384]{2,1,0:T(8,128)(2,1)}, u32[]{:S(2)}, u32[]{:S(2)}) %collective-permute-start.11) | collective-permute-done | bytes 589856 | tf_op jit(solution)/shard_map/ppermute | solution.py:191
  121.3 6.1 %shard_map.177 = (bf16[1024,1536]{1,0:T(8,128)(2,1)}, bf16[512,1024]{1,0:T(8,128)(2,1)}, bf16[128,512]{1,0:T(8,128)(2,1)}) custom-call(s32[1]{0:T(128)} %bitcast.1.own_ref, bf16[8,272,256]{2,1,0:T(8,128)(2,1)} %copy-done.23, bf16[8,272,256]{2,1,0:T(8,128)(2,1)} %collective-permute-done.7.refs_1_, bf16[8,256,256]{2,1,0:T(8,128)(2,1)} %pad_maximum_fusion.10.refs_2_, ...), custom_call_target="tpu_custom_call" | custom-call | flops 65536 | bytes 65536 | tf_op jit(solution)/shard_map/pallas_call | solution.py:424
  128.7 12.0 %shard_map.178 = (bf16[2048,1024]{1,0:T(8,128)(2,1)}, f32[2048,1536]{1,0:T(8,128)}) custom-call(bf16[2048,1024]{1,0:T(8,128)(2,1)} %pad_maximum_fusion.x_ref, f32[1,1024]{1,0:T(1,128)} %bitcast.153, bf16[1024,1536]{1,0:T(8,128)(2,1)} %get-tuple-element.106.w_ref), custom_call_target="tpu_custom_call" | custom-call | flops 65536 | bytes 65536 | tf_op jit(solution)/shard_map/pallas_call | solution.py:555
  141.7 3.6 collective-permute-start.12
  147.0 9.4 %shard_map.179 = (bf16[2048,512]{1,0:T(8,128)(2,1)}, f32[2048,512]{1,0:T(8,128)}, bf16[2048,1024]{1,0:T(8,128)(2,1)}) custom-call(f32[2048,1536]{1,0:T(8,128)} %get-tuple-element.107.projected_ref.gate_c_ref, bf16[4,2,512]{2,1,0:T(2,128)(2,1)} %copy-done.47, f32[8,512]{1,0:T(8,128)} %pad.14.taps_ref, bf16[512,1024]{1,0:T(8,128)(2,1)} %get-tuple-element.109.w_ref), custom_call_target="tpu_custom_call" | custom-call | flops 65536 | bytes 65536 | tf_op jit(solution)/shard_map/pallas_call | solution.py:555
  159.3 2.4 pad_maximum_fusion.6.refs_0_
  161.8 2.3 collective-permute-start.16
  164.0 9.8 %shard_map.180 = (f32[2048,1024]{1,0:T(8,128)}, bf16[2048,1024]{1,0:T(8,128)(2,1)}) custom-call(bf16[2048,1024]{1,0:T(8,128)(2,1)} %pad_maximum_fusion.x_ref, bf16[2048,1024]{1,0:T(8,128)(2,1)} %get-tuple-element.110.branch_ref, bf16[2048,1024]{1,0:T(8,128)(2,1)} %collective-permute-done.15.got_ref, f32[1,1024]{1,0:T(1,128)} %bitcast.147), custom_call_target="tpu_custom_call" | custom-call | flops 65536 | bytes 65536 | tf_op jit(solution)/shard_map/pallas_call | solution.py:555
  173.8 14.6 %collective-permute-done.17.refs_3_ = bf16[8,192,384]{2,1,0:T(8,128)(2,1)} collective-permute-done((bf16[8,192,384]{2,1,0:T(8,128)(2,1)S(1)}, bf16[8,192,384]{2,1,0:T(8,128)(2,1)}, u32[]{:S(2)}, u32[]{:S(2)}) %collective-permute-start.17) | collective-permute-done | bytes 1179680 | tf_op jit(solution)/shard_map/ppermute | solution.py:191
  188.4 7.1 %collective-permute-done.16.refs_1_ = bf16[8,192,384]{2,1,0:T(8,128)(2,1)} collective-permute-done((bf16[8,192,384]{2,1,0:T(8,128)(2,1)}, bf16[8,192,384]{2,1,0:T(8,128)(2,1)}, u32[]{:S(2)}, u32[]{:S(2)}) %collective-permute-start.16) | collective-permute-done | bytes 1179680 | tf_op jit(solution)/shard_map/ppermute | solution.py:191
  195.6 41.2 %shard_map.181 = (f32[2048,1024]{1,0:T(8,128)}, f32[2048,1024]{1,0:T(8,128)}, bf16[8,192,384]{2,1,0:T(8,128)(2,1)}, bf16[8,192,384]{2,1,0:T(8,128)(2,1)}, bf16[8...) custom-call(s32[1]{0:T(128)} %bitcast.1.own_ref, bf16[2048,1024]{1,0:T(8,128)(2,1)} %get-tuple-element.121.n_ref, ...), custom_call_target="tpu_custom_call" | custom-call | flops 65536 | bytes 65536 | tf_op jit(solution)/shard_map/pallas_call | solution.py:377
  236.8 2.6 collective-permute-start.18
  239.3 42.0 %shard_map.182 = (f32[2048,1024]{1,0:T(8,128)}, f32[2048,1024]{1,0:T(8,128)}, bf16[8,192,384]{2,1,0:T(8,128)(2,1)}, bf16[8,192,384]{2,1,0:T(8,128)(2,1)}, bf16[8...) custom-call(s32[1]{0:T(128)} %bitcast.1.own_ref, ...), custom_call_target="tpu_custom_call", output_to_operand_aliasing={{0}: (4, {}), {1}: (5, {})} | custom-call | flops 65536 | bytes 65536 | tf_op jit(solution)/shard_map/pallas_call | solution.py:377
  281.4 2.1 collective-permute-start.23
  290.7 2.0 collective-permute-start.21
  292.6 51.0 %shard_map.183 = (f32[2048,1024]{1,0:T(8,128)}, bf16[2048,1024]{1,0:T(8,128)(2,1)}, bf16[8,192,384]{2,1,0:T(8,128)(2,1)}, bf16[8,192,384]{2,1,0:T(8,128)(2,1)}, ...) custom-call(s32[1]{0:T(128)} %bitcast.1.own_ref, ...), custom_call_target="tpu_custom_call", output_to_operand_aliasing={{0}: (4, {})} | custom-call | flops 65536 | bytes 65536 | tf_op jit(solution)/shard_map/pallas_call | solution.py:377
  345.4 2.2 slice_add_fusion.4
  355.2 2.0 copy-done.25
  359.1 20.4 %shard_map.184 = (f32[1024,1024]{1,0:T(8,128)}, f32[2048,512]{1,0:T(8,128)}, bf16[2048,512]{1,0:T(8,128)(2,1)}, f32[1,1024]{1,0:T(1,128)}, bf16[16,128,256]{2,1,0:T(8,128)(2,1)}) custom-call(s32[1]{0:T(128)} %bitcast.1.own_ref, bf16[2048,1024]{1,0:T(8,128)(2,1)} %get-tuple-element.135.gn_ref, bf16[2048,1024]{1,0:T(8,128)(2,1)} %copy-done.25, ...), custom_call_target="tpu_custom_call" | custom-call | flops 65536 | bytes 65536 | tf_op jit(solution)/shard_map/pallas_call | solution.py:555
  379.5 5.6 collective-permute-done.28
  385.1 2.6 convert.60
  397.4 2.6 collective-permute-start.44
  405.3 18.3 %shard_map.185 = (bf16[2048,1536]{1,0:T(8,128)(2,1)}, f32[8,512]{1,0:T(8,128)}, bf16[8,192,256]{2,1,0:T(8,128)(2,1)}, bf16[8,192,256]{2,1,0:T(8,128)(2,1)}, bf16...) custom-call(s32[1]{0:T(128)} %bitcast.1.own_ref, f32[2048,512]{1,0:T(8,128)} %get-tuple-element.138.grad_conv_ref, ...), custom_call_target="tpu_custom_call" | custom-call | flops 65536 | bytes 65536 | tf_op jit(solution)/shard_map/pallas_call | solution.py:555
  423.7 7.7 %fusion.8 = bf16[1024,1024]{1,0:T(8,128)(2,1)} fusion(bf16[1024,1536]{1,0:T(8,128)(2,1)} %get-tuple-element.106.w_ref, bf16[2048,1536]{1,0:T(8,128)(2,1)} %get-tuple-element.150), kind=kOutput, calls=%fused_computation.29 | convolution fusion | flops 3222274048 | bytes 8388608 | tf_op jit(solution)/shard_map/dot_general | solution.py:29
  431.4 1.9 slice.309
  433.5 4.0 slice.532
  444.5 2.1 collective-permute-start.42
  448.0 12.9 %collective-permute-done.35 = bf16[8,192,256]{2,1,0:T(8,128)(2,1)S(1)} collective-permute-done((bf16[8,192,256]{2,1,0:T(8,128)(2,1)}, bf16[8,192,256]{2,1,0:T(8,128)(2,1)S(1)}, u32[]{:S(2)}, u32[]{:S(2)}) %collective-permute-start.35) | collective-permute-done | bytes 786464 | tf_op jit(solution)/shard_map/ppermute | solution.py:191
  460.8 2.2 collective-permute-start.45
  463.3 5.4 collective-permute-done.33
  470.9 19.3 %collective-permute-done.45 = bf16[2,384,384]{2,1,0:T(8,128)(2,1)S(1)} collective-permute-done((bf16[2,384,384]{2,1,0:T(8,128)(2,1)S(1)}, bf16[2,384,384]{2,1,0:T(8,128)(2,1)S(1)}, u32[]{:S(2)}, u32[]{:S(2)}) %collective-permute-start.45) | collective-permute-done | bytes 589856 | tf_op jit(solution)/shard_map/ppermute | solution.py:191
  494.6 7.5 %fusion.5 = (f32[1024]{0:T(1024)S(1)}, f32[1024]{0:T(1024)S(1)}, f32[1024,1024]{1,0:T(8,128)S(1)}) fusion(f32[1024]{0:T(1024)S(1)} %bitcast.150, bf16[1024,1024]{1,0:T(8,128)(2,1)} %collective-permute-done.31, bf16[2,512,1024]{2,1,0:T(8,128)(2,1)S(1)} %copy-done, f32[1024]{0:T(1024)S(1)} %get-tuple-element.199, bf16[1024,1536]{1,0:T(8,128)(2,1)} %slice.309, ...), kind=kOutput, calls=%fused_computation.8 | convolution fusion | flops 3230660608 | bytes 14696448 | tf_op jit(solution)/shard_map/dot_general | solution.py:29
  505.6 1.9 slice_add_fusion.6
  509.5 3.4 collective-permute-start.37
  512.9 4.5 fusion.2
  519.7 4.2 add_convert_fusion
  523.9 6.8 %collective-permute-done.49 = f32[4,5,128]{2,0,1:T(4,128)S(1)} collective-permute-done((f32[4,5,128]{2,0,1:T(4,128)S(1)}, f32[4,5,128]{2,0,1:T(4,128)S(1)}, u32[]{:S(2)}, u32[]{:S(2)}) %collective-permute-start.49) | collective-permute-done | bytes 10272 | tf_op jit(solution)/shard_map/ppermute | solution.py:191
  530.9 3.6 collective-permute-done.50
  536.1 2.0 collective-permute-done.51
  543.0 6.2 %collective-permute-done.38 = bf16[1,384,256]{2,1,0:T(8,128)(2,1)S(1)} collective-permute-done((bf16[1,384,256]{2,1,0:T(8,128)(2,1)S(1)}, bf16[1,384,256]{2,1,0:T(8,128)(2,1)S(1)}, u32[]{:S(2)}, u32[]{:S(2)}) %collective-permute-start.38) | collective-permute-done | bytes 196640 | tf_op jit(solution)/shard_map/ppermute | solution.py:191
  (345 shorter events, 106.1 us)
Async XLA Ops:
  7.2 232.1 %all-gather.7.cloned.1.call-start = ((), (), s32[]{:S(2)}) async-start(), calls=%async_computation.3 | async-start | bytes 5013504 | tf_op jit(solution)/shard_map/all_gather | solution.py:695
  12.6 9.8 %collective-permute-start.2 = (bf16[1,528,256]{2,1,0:T(8,128)(2,1)S(1)}, bf16[1,528,256]{2,1,0:T(8,128)(2,1)S(1)}, u32[]{:S(2)}, u32[]{:S(2)}) collective-permute-start(bf16[1,528,256]{2,1,0:T(8,128)(2,1)S(1)} %fusion.26), channel_id=1, source_target_pairs={{0,8},{1,9},{4,12},{5,13},{8,0},{9,1},{12,4},{13,5},{16,24},{17,25... | collective-permute-start | bytes 811016 | tf_op jit(solution)/shard_map/ppermute | solution.py:191
  16.1 9.8 %collective-permute-start.5 = (bf16[3,2,64,384]{3,2,1,0:T(8,128)(2,1)S(1)}, bf16[3,2,64,384]{3,2,1,0:T(8,128)(2,1)}, u32[]{:S(2)}, u32[]{:S(2)}) collective-permute-start(bf16[3,2,64,384]{3,2,1,0:T(8,128)(2,1)S(1)} %select_n.202), channel_id=1, source_target_pairs={{0,2},{2,0},{1,3},{3,1},{4,6},{6,4},{5,7},{7,5},{8,10},{10,8},{9,1... | collective-permute-start | bytes 884744 | tf_op jit(solution)/shard_map/ppermute | solution.py:186
  22.4 26.7 %collective-permute-start.3 = (bf16[2,528,256]{2,1,0:T(8,128)(2,1)S(1)}, bf16[2,528,256]{2,1,0:T(8,128)(2,1)}, u32[]{:S(2)}, u32[]{:S(2)}) collective-permute-start(bf16[2,528,256]{2,1,0:T(8,128)(2,1)S(1)} %pad_maximum_fusion.15), channel_id=1, source_target_pairs={{0,16},{1,17},{4,20},{5,21},{8,24},{9,25},{12,28},{13,29},{16,0},{... | collective-permute-start | bytes 1622024 | tf_op jit(solution)/shard_map/ppermute | solution.py:191
  50.4 242.3 %all-gather.5.cloned.1.call-start = ((), (), s32[]{:S(2)}) async-start(), calls=%async_computation.2 | async-start | bytes 5013504 | tf_op jit(solution)/shard_map/all_gather | solution.py:695
  50.5 28.1 %collective-permute-start.8 = (bf16[1024,1024]{1,0:T(8,128)(2,1)}, bf16[1024,1024]{1,0:T(8,128)(2,1)}, u32[]{:S(2)}, u32[]{:S(2)}) collective-permute-start(bf16[1024,1024]{1,0:T(8,128)(2,1)} %bitcast.126), channel_id=1, source_target_pairs={{0,2},{2,0},{1,3},{3,1},{4,6},{6,4},{5,7},{7,5},{8,10},{10,8},{9,1... | collective-permute-start | bytes 6291464 | tf_op jit(solution)/shard_map/ppermute | solution.py:186
  51.9 17.0 %collective-permute-start.4 = (bf16[4,272,256]{2,1,0:T(8,128)(2,1)}, bf16[4,272,256]{2,1,0:T(8,128)(2,1)}, u32[]{:S(2)}, u32[]{:S(2)}) collective-permute-start(bf16[4,272,256]{2,1,0:T(8,128)(2,1)} %slice.364), channel_id=1, source_target_pairs={{0,4},{1,5},{4,0},{5,1},{8,12},{9,13},{12,8},{13,9},{16,20},{17,21... | collective-permute-start | bytes 1671176 | tf_op jit(solution)/shard_map/ppermute | solution.py:191
  54.1 16.1 %collective-permute-start.9 = (bf16[4,256,256]{2,1,0:T(8,128)(2,1)}, bf16[4,256,256]{2,1,0:T(8,128)(2,1)}, u32[]{:S(2)}, u32[]{:S(2)}) collective-permute-start(bf16[4,256,256]{2,1,0:T(8,128)(2,1)} %slice.370), channel_id=1, source_target_pairs={{0,1},{1,0},{4,5},{5,4},{8,9},{9,8},{12,13},{13,12},{16,17},{17,16... | collective-permute-start | bytes 1572872 | tf_op jit(solution)/shard_map/ppermute | solution.py:191
  55.7 13.2 %collective-permute-start.6 = (bf16[1,384,384]{2,1,0:T(8,128)(2,1)S(1)}, bf16[1,384,384]{2,1,0:T(8,128)(2,1)}, u32[]{:S(2)}, u32[]{:S(2)}) collective-permute-start(bf16[1,384,384]{2,1,0:T(8,128)(2,1)S(1)} %copy-done.31), channel_id=1, source_target_pairs={{0,8},{1,9},{4,12},{5,13},{8,0},{9,1},{12,4},{13,5},{16,24},{17,25... | collective-permute-start | bytes 884744 | tf_op jit(solution)/shard_map/ppermute | solution.py:191
  56.2 436.8 %reduce-scatter.2.cloned.1.call-start = ((), (), s32[]{:S(2)}) async-start(), calls=%async_computation.1 | async-start | bytes 1114112 | tf_op jit(solution)/shard_map/reduce_scatter | solution.py:878
  70.2 51.0 %collective-permute-start.7 = (bf16[8,272,256]{2,1,0:T(8,128)(2,1)S(1)}, bf16[8,272,256]{2,1,0:T(8,128)(2,1)}, u32[]{:S(2)}, u32[]{:S(2)}) collective-permute-start(bf16[8,272,256]{2,1,0:T(8,128)(2,1)S(1)} %pad_maximum_fusion.8.refs_0_), channel_id=1, source_target_pairs={{0,1},{1,0},{4,5},{5,4},{8,9},{9,8},{12,13},{13,12},{16,17},{17,16... | collective-permute-start | bytes 3342344 | tf_op jit(solution)/shard_map/ppermute | solution.py:191
  74.1 47.2 %collective-permute-start.10 = (bf16[8,256,256]{2,1,0:T(8,128)(2,1)}, bf16[8,256,256]{2,1,0:T(8,128)(2,1)}, u32[]{:S(2)}, u32[]{:S(2)}) collective-permute-start(bf16[8,256,256]{2,1,0:T(8,128)(2,1)} %pad_maximum_fusion.10.refs_2_), channel_id=1, source_target_pairs={{0,4},{1,5},{4,0},{5,1},{8,12},{9,13},{12,8},{13,9},{16,20},{17,21... | collective-permute-start | bytes 3145736 | tf_op jit(solution)/shard_map/ppermute | solution.py:191
  77.4 40.5 %collective-permute-start.11 = (bf16[2,384,384]{2,1,0:T(8,128)(2,1)}, bf16[2,384,384]{2,1,0:T(8,128)(2,1)}, u32[]{:S(2)}, u32[]{:S(2)}) collective-permute-start(bf16[2,384,384]{2,1,0:T(8,128)(2,1)} %pad_maximum_fusion.13), channel_id=1, source_target_pairs={{0,16},{1,17},{4,20},{5,21},{8,24},{9,25},{12,28},{13,29},{16,0},{... | collective-permute-start | bytes 1769480 | tf_op jit(solution)/shard_map/ppermute | solution.py:191
  120.2 26.2 %collective-permute-start.14 = (bf16[4,192,384]{2,1,0:T(8,128)(2,1)}, bf16[4,192,384]{2,1,0:T(8,128)(2,1)}, u32[]{:S(2)}, u32[]{:S(2)}) collective-permute-start(bf16[4,192,384]{2,1,0:T(8,128)(2,1)} %get-tuple-element.188), channel_id=1, source_target_pairs={{0,1},{1,0},{4,5},{5,4},{8,9},{9,8},{12,13},{13,12},{16,17},{17,16... | collective-permute-start | bytes 1769480 | tf_op jit(solution)/shard_map/ppermute | solution.py:191
  120.7 25.7 %collective-permute-start.13 = (bf16[4,192,384]{2,1,0:T(8,128)(2,1)}, bf16[4,192,384]{2,1,0:T(8,128)(2,1)}, u32[]{:S(2)}, u32[]{:S(2)}) collective-permute-start(bf16[4,192,384]{2,1,0:T(8,128)(2,1)} %get-tuple-element.189), channel_id=1, source_target_pairs={{0,4},{1,5},{4,0},{5,1},{8,12},{9,13},{12,8},{13,9},{16,20},{17,21... | collective-permute-start | bytes 1769480 | tf_op jit(solution)/shard_map/ppermute | solution.py:191
  156.4 7.6 %collective-permute-start.15 = (bf16[2048,1024]{1,0:T(8,128)(2,1)}, bf16[2048,1024]{1,0:T(8,128)(2,1)}, u32[]{:S(2)}, u32[]{:S(2)}) collective-permute-start(bf16[2048,1024]{1,0:T(8,128)(2,1)} %get-tuple-element.110.branch_ref), channel_id=1, source_target_pairs={{0,2},{2,0},{1,3},{3,1},{4,6},{6,4},{5,7},{7,5},{8,10},{10,8},{9,1... | collective-permute-start | bytes 12582920 | tf_op jit(solution)/shard_map/ppermute | solution.py:186
  157.8 30.7 %collective-permute-start.17 = (bf16[8,192,384]{2,1,0:T(8,128)(2,1)S(1)}, bf16[8,192,384]{2,1,0:T(8,128)(2,1)}, u32[]{:S(2)}, u32[]{:S(2)}) collective-permute-start(bf16[8,192,384]{2,1,0:T(8,128)(2,1)S(1)} %pad_maximum_fusion.7.refs_2_), channel_id=1, source_target_pairs={{0,4},{1,5},{4,0},{5,1},{8,12},{9,13},{12,8},{13,9},{16,20},{17,21... | collective-permute-start | bytes 3538952 | tf_op jit(solution)/shard_map/ppermute | solution.py:191
  161.8 33.8 %collective-permute-start.16 = (bf16[8,192,384]{2,1,0:T(8,128)(2,1)}, bf16[8,192,384]{2,1,0:T(8,128)(2,1)}, u32[]{:S(2)}, u32[]{:S(2)}) collective-permute-start(bf16[8,192,384]{2,1,0:T(8,128)(2,1)} %pad_maximum_fusion.6.refs_0_), channel_id=1, source_target_pairs={{0,1},{1,0},{4,5},{5,4},{8,9},{9,8},{12,13},{13,12},{16,17},{17,16... | collective-permute-start | bytes 3538952 | tf_op jit(solution)/shard_map/ppermute | solution.py:191
  236.8 46.8 %collective-permute-start.18 = (bf16[8,192,384]{2,1,0:T(8,128)(2,1)}, bf16[8,192,384]{2,1,0:T(8,128)(2,1)}, u32[]{:S(2)}, u32[]{:S(2)}) collective-permute-start(bf16[8,192,384]{2,1,0:T(8,128)(2,1)} %get-tuple-element.119), channel_id=1, source_target_pairs={{0,1},{1,0},{4,5},{5,4},{8,9},{9,8},{12,13},{13,12},{16,17},{17,16... | collective-permute-start | bytes 3538952 | tf_op jit(solution)/shard_map/ppermute | solution.py:191
  239.3 47.1 %collective-permute-start.19 = (bf16[8,192,384]{2,1,0:T(8,128)(2,1)}, bf16[8,192,384]{2,1,0:T(8,128)(2,1)}, u32[]{:S(2)}, u32[]{:S(2)}) collective-permute-start(bf16[8,192,384]{2,1,0:T(8,128)(2,1)} %get-tuple-element.120), channel_id=1, source_target_pairs={{0,4},{1,5},{4,0},{5,1},{8,12},{9,13},{12,8},{13,9},{16,20},{17,21... | collective-permute-start | bytes 3538952 | tf_op jit(solution)/shard_map/ppermute | solution.py:191
  281.4 62.2 %collective-permute-start.23 = (bf16[8,192,384]{2,1,0:T(8,128)(2,1)}, bf16[8,192,384]{2,1,0:T(8,128)(2,1)}, u32[]{:S(2)}, u32[]{:S(2)}) collective-permute-start(bf16[8,192,384]{2,1,0:T(8,128)(2,1)} %get-tuple-element.134), channel_id=1, source_target_pairs={{0,4},{1,5},{4,0},{5,1},{8,12},{9,13},{12,8},{13,9},{16,20},{17,21... | collective-permute-start | bytes 3538952 | tf_op jit(solution)/shard_map/ppermute | solution.py:191
  283.5 60.1 %collective-permute-start.22 = (bf16[8,192,384]{2,1,0:T(8,128)(2,1)}, bf16[8,192,384]{2,1,0:T(8,128)(2,1)S(1)}, u32[]{:S(2)}, u32[]{:S(2)}) collective-permute-start(bf16[8,192,384]{2,1,0:T(8,128)(2,1)} %get-tuple-element.133), channel_id=1, source_target_pairs={{0,1},{1,0},{4,5},{5,4},{8,9},{9,8},{12,13},{13,12},{16,17},{17,16... | collective-permute-start | bytes 3538952 | tf_op jit(solution)/shard_map/ppermute | solution.py:191
  286.3 57.3 %collective-permute-start.20 = (bf16[4,192,384]{2,1,0:T(8,128)(2,1)}, bf16[4,192,384]{2,1,0:T(8,128)(2,1)}, u32[]{:S(2)}, u32[]{:S(2)}) collective-permute-start(bf16[4,192,384]{2,1,0:T(8,128)(2,1)} %slice.538), channel_id=1, source_target_pairs={{0,4},{1,5},{4,0},{5,1},{8,12},{9,13},{12,8},{13,9},{16,20},{17,21... | collective-permute-start | bytes 1769480 | tf_op jit(solution)/shard_map/ppermute | solution.py:191
  290.7 52.9 %collective-permute-start.21 = (bf16[4,192,384]{2,1,0:T(8,128)(2,1)}, bf16[4,192,384]{2,1,0:T(8,128)(2,1)}, u32[]{:S(2)}, u32[]{:S(2)}) collective-permute-start(bf16[4,192,384]{2,1,0:T(8,128)(2,1)} %slice.537), channel_id=1, source_target_pairs={{0,1},{1,0},{4,5},{5,4},{8,9},{9,8},{12,13},{13,12},{16,17},{17,16... | collective-permute-start | bytes 1769480 | tf_op jit(solution)/shard_map/ppermute | solution.py:191
  343.7 11.6 %collective-permute-start.24 = (bf16[2048,1024]{1,0:T(8,128)(2,1)}, bf16[2048,1024]{1,0:T(8,128)(2,1)S(1)}, u32[]{:S(2)}, u32[]{:S(2)}) collective-permute-start(bf16[2048,1024]{1,0:T(8,128)(2,1)} %get-tuple-element.135.gn_ref), channel_id=1, source_target_pairs={{0,2},{2,0},{1,3},{3,1},{4,6},{6,4},{5,7},{7,5},{8,10},{10,8},{9,1... | collective-permute-start | bytes 12582920 | tf_op jit(solution)/shard_map/ppermute | solution.py:186
  343.7 35.8 %collective-permute-start.29 = (bf16[8,192,384]{2,1,0:T(8,128)(2,1)}, bf16[8,192,384]{2,1,0:T(8,128)(2,1)}, u32[]{:S(2)}, u32[]{:S(2)}) collective-permute-start(bf16[8,192,384]{2,1,0:T(8,128)(2,1)} %get-tuple-element.146), channel_id=1, source_target_pairs={{0,1},{1,0},{4,5},{5,4},{8,9},{9,8},{12,13},{13,12},{16,17},{17,16... | collective-permute-start | bytes 3538952 | tf_op jit(solution)/shard_map/ppermute | solution.py:191
  344.6 34.9 %collective-permute-start.30 = (bf16[8,192,384]{2,1,0:T(8,128)(2,1)}, bf16[8,192,384]{2,1,0:T(8,128)(2,1)}, u32[]{:S(2)}, u32[]{:S(2)}) collective-permute-start(bf16[8,192,384]{2,1,0:T(8,128)(2,1)} %get-tuple-element.147), channel_id=1, source_target_pairs={{0,4},{1,5},{4,0},{5,1},{8,12},{9,13},{12,8},{13,9},{16,20},{17,21... | collective-permute-start | bytes 3538952 | tf_op jit(solution)/shard_map/ppermute | solution.py:191
  348.5 31.0 %collective-permute-start.26 = (bf16[2,384,384]{2,1,0:T(8,128)(2,1)}, bf16[2,384,384]{2,1,0:T(8,128)(2,1)}, u32[]{:S(2)}, u32[]{:S(2)}) collective-permute-start(bf16[2,384,384]{2,1,0:T(8,128)(2,1)} %fusion.17), channel_id=1, source_target_pairs={{0,16},{1,17},{4,20},{5,21},{8,24},{9,25},{12,28},{13,29},{16,0},{... | collective-permute-start | bytes 1769480 | tf_op jit(solution)/shard_map/ppermute | solution.py:191
  352.1 33.0 %collective-permute-start.28 = (bf16[4,192,384]{2,1,0:T(8,128)(2,1)}, bf16[4,192,384]{2,1,0:T(8,128)(2,1)}, u32[]{:S(2)}, u32[]{:S(2)}) collective-permute-start(bf16[4,192,384]{2,1,0:T(8,128)(2,1)} %slice.535), channel_id=1, source_target_pairs={{0,1},{1,0},{4,5},{5,4},{8,9},{9,8},{12,13},{13,12},{16,17},{17,16... | collective-permute-start | bytes 1769480 | tf_op jit(solution)/shard_map/ppermute | solution.py:191
  357.2 27.9 %collective-permute-start.27 = (bf16[4,192,384]{2,1,0:T(8,128)(2,1)}, bf16[4,192,384]{2,1,0:T(8,128)(2,1)}, u32[]{:S(2)}, u32[]{:S(2)}) collective-permute-start(bf16[4,192,384]{2,1,0:T(8,128)(2,1)} %slice.536), channel_id=1, source_target_pairs={{0,4},{1,5},{4,0},{5,1},{8,12},{9,13},{12,8},{13,9},{16,20},{17,21... | collective-permute-start | bytes 1769480 | tf_op jit(solution)/shard_map/ppermute | solution.py:191
  387.7 17.0 %collective-permute-start.25 = (bf16[4,2,512]{2,1,0:T(2,128)(2,1)S(1)}, bf16[4,2,512]{2,1,0:T(2,128)(2,1)S(1)}, u32[]{:S(2)}, u32[]{:S(2)}) collective-permute-start(bf16[4,2,512]{2,1,0:T(2,128)(2,1)S(1)} %slice.383), channel_id=1, source_target_pairs={{1,0},{3,2},{5,4},{7,6},{9,8},{11,10},{13,12},{15,14},{17,16},{19,... | collective-permute-start | bytes 24584 | tf_op jit(solution)/shard_map/ppermute | solution.py:19
  391.6 45.9 %collective-permute-start.40 = (bf16[1,384,384]{2,1,0:T(8,128)(2,1)}, bf16[1,384,384]{2,1,0:T(8,128)(2,1)}, u32[]{:S(2)}, u32[]{:S(2)}) collective-permute-start(bf16[1,384,384]{2,1,0:T(8,128)(2,1)} %slice.543), channel_id=1, source_target_pairs={{0,8},{1,9},{4,12},{5,13},{8,0},{9,1},{12,4},{13,5},{16,24},{17,25... | collective-permute-start | bytes 884744 | tf_op jit(solution)/shard_map/ppermute | solution.py:191
  394.0 49.1 %collective-permute-start.41 = (bf16[2,384,384]{2,1,0:T(8,128)(2,1)}, bf16[2,384,384]{2,1,0:T(8,128)(2,1)}, u32[]{:S(2)}, u32[]{:S(2)}) collective-permute-start(bf16[2,384,384]{2,1,0:T(8,128)(2,1)} %fusion.19), channel_id=1, source_target_pairs={{0,16},{1,17},{4,20},{5,21},{8,24},{9,25},{12,28},{13,29},{16,0},{... | collective-permute-start | bytes 1769480 | tf_op jit(solution)/shard_map/ppermute | solution.py:191
  397.4 43.2 %collective-permute-start.44 = (bf16[4,192,384]{2,1,0:T(8,128)(2,1)}, bf16[4,192,384]{2,1,0:T(8,128)(2,1)}, u32[]{:S(2)}, u32[]{:S(2)}) collective-permute-start(bf16[4,192,384]{2,1,0:T(8,128)(2,1)} %slice.533), channel_id=1, source_target_pairs={{0,1},{1,0},{4,5},{5,4},{8,9},{9,8},{12,13},{13,12},{16,17},{17,16... | collective-permute-start | bytes 1769480 | tf_op jit(solution)/shard_map/ppermute | solution.py:191
  403.9 40.6 %collective-permute-start.43 = (bf16[4,192,384]{2,1,0:T(8,128)(2,1)}, bf16[4,192,384]{2,1,0:T(8,128)(2,1)}, u32[]{:S(2)}, u32[]{:S(2)}) collective-permute-start(bf16[4,192,384]{2,1,0:T(8,128)(2,1)} %slice.534), channel_id=1, source_target_pairs={{0,4},{1,5},{4,0},{5,1},{8,12},{9,13},{12,8},{13,9},{16,20},{17,21... | collective-permute-start | bytes 1769480 | tf_op jit(solution)/shard_map/ppermute | solution.py:191
  433.3 61.3 %collective-permute-start.31 = (bf16[1024,1024]{1,0:T(8,128)(2,1)}, bf16[1024,1024]{1,0:T(8,128)(2,1)}, u32[]{:S(2)}, u32[]{:S(2)}) collective-permute-start(bf16[1024,1024]{1,0:T(8,128)(2,1)} %fusion.8), channel_id=1, source_target_pairs={{0,2},{2,0},{1,3},{3,1},{4,6},{6,4},{5,7},{7,5},{8,10},{10,8},{9,1... | collective-permute-start | bytes 6291464 | tf_op jit(solution)/shard_map/ppermute | solution.py:186
  437.5 23.3 %collective-permute-start.35 = (bf16[8,192,256]{2,1,0:T(8,128)(2,1)}, bf16[8,192,256]{2,1,0:T(8,128)(2,1)S(1)}, u32[]{:S(2)}, u32[]{:S(2)}) collective-permute-start(bf16[8,192,256]{2,1,0:T(8,128)(2,1)} %get-tuple-element.161), channel_id=1, source_target_pairs={{0,4},{1,5},{4,0},{5,1},{8,12},{9,13},{12,8},{13,9},{16,20},{17,21... | collective-permute-start | bytes 2359304 | tf_op jit(solution)/shard_map/ppermute | solution.py:191
  440.6 28.1 %collective-permute-start.33 = (bf16[8,192,256]{2,1,0:T(8,128)(2,1)S(1)}, bf16[8,192,256]{2,1,0:T(8,128)(2,1)S(1)}, u32[]{:S(2)}, u32[]{:S(2)}) collective-permute-start(bf16[8,192,256]{2,1,0:T(8,128)(2,1)S(1)} %copy-done.54), channel_id=1, source_target_pairs={{0,1},{1,0},{4,5},{5,4},{8,9},{9,8},{12,13},{13,12},{16,17},{17,16... | collective-permute-start | bytes 2359304 | tf_op jit(solution)/shard_map/ppermute | solution.py:191
  443.1 74.6 %collective-permute-start.32 = (bf16[1024,1024]{1,0:T(8,128)(2,1)}, bf16[1024,1024]{1,0:T(8,128)(2,1)}, u32[]{:S(2)}, u32[]{:S(2)}) collective-permute-start(bf16[1024,1024]{1,0:T(8,128)(2,1)} %slice.532), channel_id=1, source_target_pairs={{0,2},{2,0},{1,3},{3,1},{4,6},{6,4},{5,7},{7,5},{8,10},{10,8},{9,1... | collective-permute-start | bytes 6291464 | tf_op jit(solution)/shard_map/ppermute | solution.py:186
  444.5 25.8 %collective-permute-start.42 = (bf16[1,384,384]{2,1,0:T(8,128)(2,1)S(1)}, bf16[1,384,384]{2,1,0:T(8,128)(2,1)S(1)}, u32[]{:S(2)}, u32[]{:S(2)}) collective-permute-start(bf16[1,384,384]{2,1,0:T(8,128)(2,1)S(1)} %slice.542), channel_id=1, source_target_pairs={{0,8},{1,9},{4,12},{5,13},{8,0},{9,1},{12,4},{13,5},{16,24},{17,25... | collective-permute-start | bytes 884744 | tf_op jit(solution)/shard_map/ppermute | solution.py:191
  460.8 29.4 %collective-permute-start.45 = (bf16[2,384,384]{2,1,0:T(8,128)(2,1)S(1)}, bf16[2,384,384]{2,1,0:T(8,128)(2,1)S(1)}, u32[]{:S(2)}, u32[]{:S(2)}) collective-permute-start(bf16[2,384,384]{2,1,0:T(8,128)(2,1)S(1)} %fusion.18), channel_id=1, source_target_pairs={{0,16},{1,17},{4,20},{5,21},{8,24},{9,25},{12,28},{13,29},{16,0},{... | collective-permute-start | bytes 1769480 | tf_op jit(solution)/shard_map/ppermute | solution.py:191
  468.7 36.1 %collective-permute-start.36 = (bf16[4,192,256]{2,1,0:T(8,128)(2,1)S(1)}, bf16[4,192,256]{2,1,0:T(8,128)(2,1)}, u32[]{:S(2)}, u32[]{:S(2)}) collective-permute-start(bf16[4,192,256]{2,1,0:T(8,128)(2,1)S(1)} %slice.539), channel_id=1, source_target_pairs={{0,1},{1,0},{4,5},{5,4},{8,9},{9,8},{12,13},{13,12},{16,17},{17,16... | collective-permute-start | bytes 1179656 | tf_op jit(solution)/shard_map/ppermute | solution.py:191
  470.3 34.5 %collective-permute-start.34 = (bf16[4,192,256]{2,1,0:T(8,128)(2,1)S(1)}, bf16[4,192,256]{2,1,0:T(8,128)(2,1)}, u32[]{:S(2)}, u32[]{:S(2)}) collective-permute-start(bf16[4,192,256]{2,1,0:T(8,128)(2,1)S(1)} %slice.540), channel_id=1, source_target_pairs={{0,4},{1,5},{4,0},{5,1},{8,12},{9,13},{12,8},{13,9},{16,20},{17,21... | collective-permute-start | bytes 1179656 | tf_op jit(solution)/shard_map/ppermute | solution.py:191
  491.5 10.7 %collective-permute-start.46 = (bf16[1,384,384]{2,1,0:T(8,128)(2,1)}, bf16[1,384,384]{2,1,0:T(8,128)(2,1)}, u32[]{:S(2)}, u32[]{:S(2)}) collective-permute-start(bf16[1,384,384]{2,1,0:T(8,128)(2,1)} %slice.541), channel_id=1, source_target_pairs={{0,8},{1,9},{4,12},{5,13},{8,0},{9,1},{12,4},{13,5},{16,24},{17,25... | collective-permute-start | bytes 884744 | tf_op jit(solution)/shard_map/ppermute | solution.py:191
  502.2 15.3 %collective-permute-start.48 = (f32[8,5,128]{2,0,1:T(8,128)S(1)}, f32[8,5,128]{2,0,1:T(8,128)S(1)}, u32[]{:S(2)}, u32[]{:S(2)}) collective-permute-start(f32[8,5,128]{2,0,1:T(8,128)S(1)} %maximum_bitcast_fusion.1), channel_id=1, source_target_pairs={{0,1},{1,0},{4,5},{5,4},{8,9},{9,8},{12,13},{13,12},{16,17},{17,16... | collective-permute-start | bytes 61448 | tf_op jit(solution)/shard_map/ppermute | solution.py:191
  504.8 44.9 %collective-permute-start.47 = (f32[3,2,64,384]{3,2,1,0:T(8,128)}, f32[3,2,64,384]{3,2,1,0:T(8,128)}, u32[]{:S(2)}, u32[]{:S(2)}) collective-permute-start(f32[3,2,64,384]{3,2,1,0:T(8,128)} %get-tuple-element.187), channel_id=1, source_target_pairs={{0,2},{2,0},{1,3},{3,1},{4,6},{6,4},{5,7},{7,5},{8,10},{10,8},{9,1... | collective-permute-start | bytes 1769480 | tf_op jit(solution)/shard_map/ppermute | solution.py:186
  509.5 31.2 %collective-permute-start.37 = (bf16[2,384,256]{2,1,0:T(8,128)(2,1)}, bf16[2,384,256]{2,1,0:T(8,128)(2,1)}, u32[]{:S(2)}, u32[]{:S(2)}) collective-permute-start(bf16[2,384,256]{2,1,0:T(8,128)(2,1)} %fusion.23), channel_id=1, source_target_pairs={{0,16},{1,17},{4,20},{5,21},{8,24},{9,25},{12,28},{13,29},{16,0},{... | collective-permute-start | bytes 1179656 | tf_op jit(solution)/shard_map/ppermute | solution.py:191
  517.5 13.2 %collective-permute-start.49 = (f32[4,5,128]{2,0,1:T(4,128)S(1)}, f32[4,5,128]{2,0,1:T(4,128)S(1)}, u32[]{:S(2)}, u32[]{:S(2)}) collective-permute-start(f32[4,5,128]{2,0,1:T(4,128)S(1)} %slice_select_fusion.2), channel_id=1, source_target_pairs={{0,16},{1,17},{4,20},{5,21},{8,24},{9,25},{12,28},{13,29},{16,0},{... | collective-permute-start | bytes 30728 | tf_op jit(solution)/shard_map/ppermute | solution.py:191
  (67 other events, 349.1 us)
Sparse Core Ops, SparseCore 0:
  50.5 107.9 all-gather.6
  161.9 80.7 all-gather.4
  404.8 79.9 reduce-scatter.1

commit v6 on v5

--- a/solution.py
+++ b/solution.py
@@ -448,12 +448,16 @@
     return one, jnp.where(row == count - 1, behind[1:2], two)
 
 
-def in_kernel(x_ref, gain_ref, w_ref, normed_ref, projected_ref):
+def in_kernel(x_ref, gain_ref, w_ref, normed_ref, projected_ref, tail_ref):
     x = x_ref[...].astype(f32)
     scale = lax.rsqrt(jnp.mean(x * x, axis=-1, keepdims=True) + EPSILON)
     normed = (x * scale * gain_ref[...]).astype(bf16)
     normed_ref[...] = normed
-    projected_ref[...] = jnp.dot(normed, w_ref[...], preferred_element_type=f32)
+    projected = jnp.dot(normed, w_ref[...], preferred_element_type=f32)
+    projected_ref[...] = projected
+    channels = projected.shape[1] // 3
+    product = projected[-8:, :channels] * projected[-8:, 2 * channels :]
+    tail_ref[0] = product[6:].astype(bf16)
 
 
 def conv_kernel(projected_ref, before_ref, taps_ref, w_ref, mixer_ref, conv_ref, branch_ref):
@@ -477,7 +481,7 @@
 def branch_grad_kernel(
     own_first, geometry, own_ref, gn_ref, got_ref, residual_ref, go_ref, gain_ref, mixer_ref,
     conv_ref, gate_c_ref, w_ref, grad_residual_ref, grad_conv_ref, grad_c_ref, grad_gain_ref,
-    part_ref, total_ref, low_ref, sems,
+    head_ref, part_ref, total_ref, low_ref, sems,
 ):
     plan, segments, n_ctx = geometry
     step = pl.program_id(0)
@@ -504,7 +508,9 @@
     grad_branch = grad_residual.astype(bf16)
     grad_mix = lax.dot_general(grad_branch, w_ref[...], NT, preferred_element_type=f32)
     grad_c_ref[...] = (grad_mix * conv_ref[...]).astype(bf16)
-    grad_conv_ref[...] = grad_mix * gate_c_ref[...]
+    grad_conv = grad_mix * gate_c_ref[...]
+    grad_conv_ref[...] = grad_conv
+    head_ref[0] = grad_conv[:8][:2].astype(bf16)
     total_ref[...] += lax.dot_general(mixer_ref[...], grad_branch, TN, preferred_element_type=f32)
 
     @pl.when(step == pl.num_programs(0) - 1)
@@ -691,9 +697,6 @@
     hold = mix_block[None]
     for mask in far:
         hold = doubled(hold, across(hold, mask))
-    second_all, last_all = [
-        lax.all_gather(after(block, hold), ("chip", "ctx")) for block in chunk_blocks[1:]
-    ]
     mix_halves = [hold[:, :mix_cut], hold[:, mix_cut:]]
     next_hold = after(chunk_blocks[0][None], hold)
     far_left = list(far)
@@ -723,6 +726,9 @@
         False,
     )
     in_half = after(in_half, next_got)
+    second_all, last_all = [
+        lax.all_gather(after(block, next_got), ("chip", "ctx")) for block in chunk_blocks[1:]
+    ]
     next_halves = [next_hold[:, :chunk_cut], next_hold[:, chunk_cut:]]
 
     def step_of(halves, step):
@@ -752,7 +758,12 @@
     wide_rows, thin_rows = (piece, width), (piece, channels)
     taps = jnp.pad(taps, ((0, 5), (0, 0)))
     next_got = step_of(next_halves, 0)
-    normed_low, projected = row_call(
+    halo = (1, 2, channels)
+
+    def halo_at(i):
+        return (i, 0, 0)
+
+    normed_low, projected, tail = row_call(
         in_kernel,
         blocks,
         [
@@ -763,16 +774,10 @@
         [
             ((2 * rows, width), bf16, wide_rows, at),
             ((2 * rows, 3 * channels), f32, (piece, 3 * channels), at),
-        ],
-    )
-    tail = projected.reshape(blocks, piece, 3 * channels)[:, piece - 2 :]
-    tail = (tail[:, :, :channels] * tail[:, :, 2 * channels :]).astype(bf16)
+            ((blocks, 2, channels), bf16, (1, 2, channels), halo_at),
+        ],
+    )
     before = passed_along(tail, "ctx", 1)
-    halo = (1, 2, channels)
-
-    def halo_at(i):
-        return (i, 0, 0)
-
     conv_taps = after(taps, *next_got)
     next_halves = [
         doubled(h, g) for h, g in zip(next_halves, all_after(next_got, projected))
@@ -840,7 +845,7 @@
         return ((i + seqs) % blocks, 1)
 
     out_plan = [(0, i, None, 0, out_parts * depth) for i in range(slots)]
-    grad_residual, grad_conv, grad_c, grad_gain_ffn, grad_out_slots = row_call(
+    grad_residual, grad_conv, grad_c, grad_gain_ffn, head, grad_out_slots = row_call(
         functools.partial(branch_grad_kernel, seqs, (out_plan, out_segments(0, 0), n_ctx)),
         blocks,
         [
@@ -860,6 +865,7 @@
             ((2 * rows, channels), f32, thin_rows, turned),
             ((2 * rows, channels), bf16, thin_rows, turned),
             ((1, width), f32, (1, width), still),
+            ((blocks, 2, channels), bf16, halo, lambda i: ((i + seqs) % blocks, 0, 0)),
             ((slots, out_parts * depth, 256), bf16, None, None),
         ],
         scratch=[
@@ -870,11 +876,10 @@
     )
     grad_gain_ffn = grad_gain_ffn[0]
     stages = (first_stages, second_stages, last_stages)
-    grad_c_then = after(grad_c, *(g for s in stages for g in s.got))
-    for s in stages:
-        s.advance(grad_c)
-    head = grad_conv.reshape(blocks, piece, channels)[:, :2].astype(bf16)
     behind = passed_along(head, "ctx", -1)
+    grad_c_then = after(grad_c, *second_stages.got, *last_stages.got)
+    second_stages.advance(grad_c)
+    last_stages.advance(grad_c)
     out_sum = lax.psum_scatter(grad_out_slots, ("chip", "ctx"), scatter_dimension=0).astype(f32)
     sum_plan = gather_plan(in_rows // 2, in_rows)
     grad_projected, grad_kernel, *mix_grad_parts = row_call(
@@ -903,14 +908,17 @@
     )
     grad_kernel = grad_kernel[:3]
     mix_stages = Stages(mix_grad_parts)
+    stages = (first_stages, second_stages, last_stages)
     for s in stages:
         s.advance(grad_projected)
-    grad_other = cross_cols(grad_projected[rows:], in_half).astype(bf16)
+    late_projected = after(grad_projected, *mix_stages.got)
+    mix_stages.advance()
+    grad_other = cross_cols(late_projected[rows:], in_half).astype(bf16)
     for s in (mix_stages, *stages):
         s.advance(grad_other)
     other_got = swap(grad_other)
-    grad_mine = cross_cols(after(grad_projected[:rows], other_got), in_half)
-    for s in (mix_stages, second_stages, last_stages):
+    grad_mine = cross_cols(after(late_projected, grad_other)[:rows], in_half)
+    for s in stages:
         s.advance(grad_mine)
     grad_normed = grad_mine + other_got.astype(f32)
     ffn_late = after(ffn_out, grad_other)
@@ -922,10 +930,7 @@
     grad_in_norm, grad_gain_mix = norm_backward(own_inputs, scale_mix, first_gain, grad_normed)
     grad_tokens = (grad_residual + grad_in_norm).reshape(seqs, piece, width)
 
-    mix_stages.advance(grad_tokens)
-    last_stages.advance(grad_tokens)
-    while mix_stages.total is None:
-        mix_stages.advance()
+    mix_stages.advance(grad_mine)
 
     chunk_sum = jnp.stack([s.total for s in stages])
     both_sum = chunk_sum[:, : 4 * depth].reshape(CHUNKS, 2, 2, depth, lanes).transpose(2, 0, 1, 3, 4)
@@ -939,6 +944,7 @@
     final_down = jnp.concatenate([chunk_sum[:, 4 * depth : 4 * depth + sub], down_rest], axis=2)
     final_down = final_down.reshape(CHUNKS * sub, wide)
 
+    mix_stages.advance(both_sum, final_down)
     in_sum = mix_stages.total.reshape(in_parts, 2, depth, 256).transpose(1, 0, 2, 3)
     in_mine, in_other = mine_other(in_sum)
     in_sum = in_core_order(in_mine[None], swap(in_other)[None], 0)

time: 574 us -> 578 us (level)
  starting transfers between devices: 54.1 us -> 63.8 us
  waiting for transfers between devices: 154 us -> 148 us
    ppermute x40, starting transfers between devices: 47.2 us -> 59 us  [across(): lax.ppermute(block, ('chip', 'ctx'), [(i, i ^ mask) for i in range(count)])]
    ppermute x40, waiting for transfers between devices: 153 us -> 146 us  [across(): lax.ppermute(block, ('chip', 'ctx'), [(i, i ^ mask) for i in range(count)])]
    unnamed x121 -> x119, local copies, waits for them, and re-layouts: 13.7 us -> 7.61 us
  transfers between devices with their start and end apart: 56 -> 56, of which waited for: 16 -> 17; matrix products, arithmetic and copies ran while one was open for 20% -> 20% of each run, Pallas kernels for 37% -> 37%
where the time goes in v6:
time: 578 us; the launch traced here: 568 us
  Pallas kernels  211 us (37%)
  waiting for transfers between devices  148 us (26%)
  other arithmetic  68.8 us (12%)
  starting transfers between devices  63.8 us (11%)
  local copies, waits for them, and re-layouts  47.4 us (8%)
  between operations  15.5 us (3%)
  matrix products  14.1 us (2%)
    ppermute x40, waiting for transfers between devices, across(): lax.ppermute(block, ('chip', 'ctx'), [(i, i ^ mask) for i in range(count)])  146 us
    pallas_call x3, Pallas kernels, ffn_chunk(): pl.pallas_call(functools.partial(ffn_kernel, geometry, out_geometry, firs...  134 us
    pallas_call x5, Pallas kernels, row_call(): pl.pallas_call(body, grid=(steps,), in_specs=[pl.BlockSpec(memory_space=p...  70.4 us
    ppermute x40, starting transfers between devices, across(): lax.ppermute(block, ('chip', 'ctx'), [(i, i ^ mask) for i in range(count)])  59 us
    dot_general x2, matrix products, cross_cols(): lax.dot_general(left_operand, right_operand, (((1,), (1,)), ((), ())), pr...  14.1 us
    add x8, other arithmetic, scatter_steps(): k.astype(f32) + g.astype(f32)  11.7 us
  transfers between devices with their start and end apart: 56, of which 17 were waited for; matrix products, arithmetic and copies ran while one was open for 20% of the time, Pallas kernels for 37%

profile of v6, /device:TPU:0, one launch (start us, length us, event | category | flops | bytes accessed | tf_op | source)
XLA Modules:
  0.0 568.3 jit_solution(7735677998427921284)
XLA Ops:
  14.6 2.1 maximum_bitcast_fusion
  21.6 3.1 collective-permute-start.2
  27.0 4.5 collective-permute-done.2
  31.4 1.8 pad_maximum_fusion.16
  33.2 2.8 collective-permute-start.3
  41.3 18.3 %collective-permute-done.3 = bf16[2,528,256]{2,1,0:T(8,128)(2,1)} collective-permute-done((bf16[2,528,256]{2,1,0:T(8,128)(2,1)}, bf16[2,528,256]{2,1,0:T(8,128)(2,1)}, u32[]{:S(2)}, u32[]{:S(2)}) %collective-permute-start.3) | collective-permute-done | bytes 540704 | tf_op jit(solution)/shard_map/ppermute | solution.py:191
  64.7 4.2 collective-permute-done.6
  69.1 4.3 pad_maximum_fusion.x_ref
  73.3 3.2 collective-permute-done.9
  76.5 3.4 collective-permute-start.11
  80.0 24.7 %collective-permute-done.11 = bf16[2,384,384]{2,1,0:T(8,128)(2,1)S(1)} collective-permute-done((bf16[2,384,384]{2,1,0:T(8,128)(2,1)S(1)}, bf16[2,384,384]{2,1,0:T(8,128)(2,1)S(1)}, u32[]{:S(2)}, u32[]{:S(2)}) %collective-permute-start.11) | collective-permute-done | bytes 589856 | tf_op jit(solution)/shard_map/ppermute | solution.py:191
  112.6 4.9 pad_maximum_fusion.1.go_ref
  120.0 21.3 %collective-permute-done.10.refs_3_ = bf16[8,256,256]{2,1,0:T(8,128)(2,1)} collective-permute-done((bf16[8,256,256]{2,1,0:T(8,128)(2,1)}, bf16[8,256,256]{2,1,0:T(8,128)(2,1)}, u32[]{:S(2)}, u32[]{:S(2)}) %collective-permute-start.10) | collective-permute-done | bytes 1048608 | tf_op jit(solution)/shard_map/ppermute | solution.py:191
  141.4 6.0 %shard_map.177 = (bf16[1024,1536]{1,0:T(8,128)(2,1)}, bf16[512,1024]{1,0:T(8,128)(2,1)}, bf16[128,512]{1,0:T(8,128)(2,1)}) custom-call(s32[1]{0:T(128)} %bitcast.1.own_ref, bf16[8,272,256]{2,1,0:T(8,128)(2,1)} %copy-done.17, bf16[8,272,256]{2,1,0:T(8,128)(2,1)} %collective-permute-done.7.refs_1_, bf16[8,256,256]{2,1,0:T(8,128)(2,1)} %pad_maximum_fusion.11.refs_2_, ...), custom_call_target="tpu_custom_call" | custom-call | flops 65536 | bytes 65536 | tf_op jit(solution)/shard_map/pallas_call | solution.py:424
  148.7 12.1 %shard_map.178 = (bf16[2048,1024]{1,0:T(8,128)(2,1)}, f32[2048,1536]{1,0:T(8,128)}, bf16[4,2,512]{2,1,0:T(2,128)(2,1)}) custom-call(bf16[2048,1024]{1,0:T(8,128)(2,1)} %pad_maximum_fusion.x_ref, f32[1,1024]{1,0:T(1,128)} %bitcast.148, bf16[1024,1536]{1,0:T(8,128)(2,1)} %get-tuple-element.108.w_ref), custom_call_target="tpu_custom_call" | custom-call | flops 65536 | bytes 65536 | tf_op jit(solution)/shard_map/pallas_call | solution.py:561
  160.9 2.0 collective-permute-start.12
  164.8 9.9 %shard_map.179 = (bf16[2048,512]{1,0:T(8,128)(2,1)}, f32[2048,512]{1,0:T(8,128)}, bf16[2048,1024]{1,0:T(8,128)(2,1)}) custom-call(f32[2048,1536]{1,0:T(8,128)} %get-tuple-element.109.projected_ref.gate_c_ref, bf16[4,2,512]{2,1,0:T(2,128)(2,1)} %copy-done.47, f32[8,512]{1,0:T(8,128)} %pad.14.taps_ref, bf16[512,1024]{1,0:T(8,128)(2,1)} %get-tuple-element.112.w_ref), custom_call_target="tpu_custom_call" | custom-call | flops 65536 | bytes 65536 | tf_op jit(solution)/shard_map/pallas_call | solution.py:561
  177.7 2.4 pad_maximum_fusion.7.refs_0_
  180.1 1.9 collective-permute-start.16
  182.2 9.8 %shard_map.180 = (f32[2048,1024]{1,0:T(8,128)}, bf16[2048,1024]{1,0:T(8,128)(2,1)}) custom-call(bf16[2048,1024]{1,0:T(8,128)(2,1)} %pad_maximum_fusion.x_ref, bf16[2048,1024]{1,0:T(8,128)(2,1)} %get-tuple-element.113.branch_ref, bf16[2048,1024]{1,0:T(8,128)(2,1)} %collective-permute-done.15.got_ref, f32[1,1024]{1,0:T(1,128)} %bitcast.142), custom_call_target="tpu_custom_call" | custom-call | flops 65536 | bytes 65536 | tf_op jit(solution)/shard_map/pallas_call | solution.py:561
  191.9 17.6 %collective-permute-done.17.refs_3_ = bf16[8,192,384]{2,1,0:T(8,128)(2,1)} collective-permute-done((bf16[8,192,384]{2,1,0:T(8,128)(2,1)S(1)}, bf16[8,192,384]{2,1,0:T(8,128)(2,1)}, u32[]{:S(2)}, u32[]{:S(2)}) %collective-permute-start.17) | collective-permute-done | bytes 1179680 | tf_op jit(solution)/shard_map/ppermute | solution.py:191
  209.6 41.2 %shard_map.181 = (f32[2048,1024]{1,0:T(8,128)}, f32[2048,1024]{1,0:T(8,128)}, bf16[8,192,384]{2,1,0:T(8,128)(2,1)}, bf16[8,192,384]{2,1,0:T(8,128)(2,1)}, bf16[8...) custom-call(s32[1]{0:T(128)} %bitcast.1.own_ref, bf16[2048,1024]{1,0:T(8,128)(2,1)} %get-tuple-element.124.n_ref, ...), custom_call_target="tpu_custom_call" | custom-call | flops 65536 | bytes 65536 | tf_op jit(solution)/shard_map/pallas_call | solution.py:377
  252.8 42.8 %shard_map.182 = (f32[2048,1024]{1,0:T(8,128)}, f32[2048,1024]{1,0:T(8,128)}, bf16[8,192,384]{2,1,0:T(8,128)(2,1)}, bf16[8,192,384]{2,1,0:T(8,128)(2,1)}, bf16[8...) custom-call(s32[1]{0:T(128)} %bitcast.1.own_ref, ...), custom_call_target="tpu_custom_call", output_to_operand_aliasing={{0}: (4, {}), {1}: (5, {})} | custom-call | flops 65536 | bytes 65536 | tf_op jit(solution)/shard_map/pallas_call | solution.py:377
  306.0 50.6 %shard_map.183 = (f32[2048,1024]{1,0:T(8,128)}, bf16[2048,1024]{1,0:T(8,128)(2,1)}, bf16[8,192,384]{2,1,0:T(8,128)(2,1)}, bf16[8,192,384]{2,1,0:T(8,128)(2,1)}, ...) custom-call(s32[1]{0:T(128)} %bitcast.1.own_ref, ...), custom_call_target="tpu_custom_call", output_to_operand_aliasing={{0}: (4, {})} | custom-call | flops 65536 | bytes 65536 | tf_op jit(solution)/shard_map/pallas_call | solution.py:377
  367.0 2.2 slice_add_fusion.4
  371.1 2.4 collective-permute-start.38
  373.5 20.5 %shard_map.184 = (f32[1024,1024]{1,0:T(8,128)}, f32[2048,512]{1,0:T(8,128)}, bf16[2048,512]{1,0:T(8,128)(2,1)}, f32[1,1024]{1,0:T(1,128)}, bf16[4,2,512]{2,1,0:T(2,128)(2,1)}, /*index=5*/bf16[16,128,256]{2,1,0:T(8,128)(2,1)}) custom-call(s32[1]{0:T(128)} %bitcast.1.own_ref, bf16[2048,1024]{1,0:T(8,128)(2,1)} %get-tuple-element.138.gn_ref, ...), custom_call_target="tpu_custom_call" | custom-call | flops 65536 | bytes 65536 | tf_op jit(solution)/shard_map/pallas_call | solution.py:561
  394.0 4.6 collective-permute-done.27
  400.4 2.2 slice_add_fusion.2
  403.5 2.4 collective-permute-start.40
  412.7 2.6 collective-permute-start.43
  416.0 18.2 %shard_map.185 = (bf16[2048,1536]{1,0:T(8,128)(2,1)}, f32[8,512]{1,0:T(8,128)}, bf16[8,192,256]{2,1,0:T(8,128)(2,1)}, bf16[8,192,256]{2,1,0:T(8,128)(2,1)}, bf16...) custom-call(s32[1]{0:T(128)} %bitcast.1.own_ref, f32[2048,512]{1,0:T(8,128)} %get-tuple-element.141.grad_conv_ref, ...), custom_call_target="tpu_custom_call" | custom-call | flops 65536 | bytes 65536 | tf_op jit(solution)/shard_map/pallas_call | solution.py:561
  435.7 2.4 fusion.19
  445.0 15.7 %collective-permute-done.30 = bf16[8,192,256]{2,1,0:T(8,128)(2,1)} collective-permute-done((bf16[8,192,256]{2,1,0:T(8,128)(2,1)}, bf16[8,192,256]{2,1,0:T(8,128)(2,1)}, u32[]{:S(2)}, u32[]{:S(2)}) %collective-permute-start.30) | collective-permute-done | bytes 786464 | tf_op jit(solution)/shard_map/ppermute | solution.py:191
  460.7 6.5 %fusion.10 = bf16[1024,1024]{1,0:T(8,128)(2,1)} fusion(bf16[1024,1536]{1,0:T(8,128)(2,1)S(1)} %copy-done.22, bf16[2048,1536]{1,0:T(8,128)(2,1)} %get-tuple-element.156), kind=kOutput, calls=%fused_computation.31 | convolution fusion | flops 3222274048 | bytes 8388608 | tf_op jit(solution)/shard_map/dot_general | solution.py:29
  467.3 3.7 collective-permute-start.44
  475.3 3.9 slice.510
  479.5 18.8 %collective-permute-done.44 = bf16[2,384,384]{2,1,0:T(8,128)(2,1)S(1)} collective-permute-done((bf16[2,384,384]{2,1,0:T(8,128)(2,1)S(1)}, bf16[2,384,384]{2,1,0:T(8,128)(2,1)S(1)}, u32[]{:S(2)}, u32[]{:S(2)}) %collective-permute-start.44) | collective-permute-done | bytes 589856 | tf_op jit(solution)/shard_map/ppermute | solution.py:191
  502.8 3.4 collective-permute-start.36
  507.8 7.5 %fusion.5 = (f32[1024]{0:T(1024)S(1)}, f32[1024]{0:T(1024)S(1)}, f32[1024,1024]{1,0:T(8,128)S(1)}) fusion(f32[1024]{0:T(1024)S(1)} %bitcast.145, bf16[1024,1024]{1,0:T(8,128)(2,1)} %collective-permute-done.33, bf16[2,512,1024]{2,1,0:T(8,128)(2,1)S(1)} %copy-done, f32[1024]{0:T(1024)S(1)} %get-tuple-element.203, ...), kind=kOutput, calls=%fused_computation.8 | convolution fusion | flops 3230660608 | bytes 14696448 | tf_op jit(solution)/shard_map/dot_general | solution.py:29
  516.8 7.0 %collective-permute-done.36 = bf16[2,384,256]{2,1,0:T(8,128)(2,1)} collective-permute-done((bf16[2,384,256]{2,1,0:T(8,128)(2,1)}, bf16[2,384,256]{2,1,0:T(8,128)(2,1)}, u32[]{:S(2)}, u32[]{:S(2)}) %collective-permute-start.36) | collective-permute-done | bytes 393248 | tf_op jit(solution)/shard_map/ppermute | solution.py:191
  525.2 4.7 fusion.2
  530.8 2.9 collective-permute-start.49
  535.5 1.9 collective-permute-start.50
  537.4 4.2 add_convert_fusion
  541.8 3.5 collective-permute-done.51
  552.7 2.4 concatenate.138
  555.1 1.9 fusion.13
  (336 shorter events, 112.8 us)
Async XLA Ops:
  7.2 245.6 %all-gather.7.cloned.1.call-start = ((), (), s32[]{:S(2)}) async-start(), calls=%async_computation.3 | async-start | bytes 5013504 | tf_op jit(solution)/shard_map/all_gather | solution.py:730
  11.1 58.0 %collective-permute-start = (bf16[1024,1024]{1,0:T(8,128)(2,1)S(1)}, bf16[1024,1024]{1,0:T(8,128)(2,1)}, u32[]{:S(2)}, u32[]{:S(2)}) collective-permute-start(bf16[1024,1024]{1,0:T(8,128)(2,1)S(1)} %bitcast.109), channel_id=1, source_target_pairs={{0,2},{2,0},{1,3},{3,1},{4,6},{6,4},{5,7},{7,5},{8,10},{10,8},{9,1... | collective-permute-start | bytes 6291464 | tf_op jit(solution)/shard_map/ppermute | solution.py:186
  21.6 9.8 %collective-permute-start.2 = (bf16[1,528,256]{2,1,0:T(8,128)(2,1)S(1)}, bf16[1,528,256]{2,1,0:T(8,128)(2,1)}, u32[]{:S(2)}, u32[]{:S(2)}) collective-permute-start(bf16[1,528,256]{2,1,0:T(8,128)(2,1)S(1)} %fusion.28), channel_id=1, source_target_pairs={{0,8},{1,9},{4,12},{5,13},{8,0},{9,1},{12,4},{13,5},{16,24},{17,25... | collective-permute-start | bytes 811016 | tf_op jit(solution)/shard_map/ppermute | solution.py:191
  27.0 12.1 %collective-permute-start.5 = (bf16[3,2,64,384]{3,2,1,0:T(8,128)(2,1)}, bf16[3,2,64,384]{3,2,1,0:T(8,128)(2,1)}, u32[]{:S(2)}, u32[]{:S(2)}) collective-permute-start(bf16[3,2,64,384]{3,2,1,0:T(8,128)(2,1)} %select_n.202), channel_id=1, source_target_pairs={{0,2},{2,0},{1,3},{3,1},{4,6},{6,4},{5,7},{7,5},{8,10},{10,8},{9,1... | collective-permute-start | bytes 884744 | tf_op jit(solution)/shard_map/ppermute | solution.py:186
  33.2 26.5 %collective-permute-start.3 = (bf16[2,528,256]{2,1,0:T(8,128)(2,1)}, bf16[2,528,256]{2,1,0:T(8,128)(2,1)}, u32[]{:S(2)}, u32[]{:S(2)}) collective-permute-start(bf16[2,528,256]{2,1,0:T(8,128)(2,1)} %pad_maximum_fusion.16), channel_id=1, source_target_pairs={{0,16},{1,17},{4,20},{5,21},{8,24},{9,25},{12,28},{13,29},{16,0},{... | collective-permute-start | bytes 1622024 | tf_op jit(solution)/shard_map/ppermute | solution.py:191
  60.9 8.1 %collective-permute-start.6 = (bf16[1,384,384]{2,1,0:T(8,128)(2,1)S(1)}, bf16[1,384,384]{2,1,0:T(8,128)(2,1)S(1)}, u32[]{:S(2)}, u32[]{:S(2)}) collective-permute-start(bf16[1,384,384]{2,1,0:T(8,128)(2,1)S(1)} %get-tuple-element.99), channel_id=1, source_target_pairs={{0,8},{1,9},{4,12},{5,13},{8,0},{9,1},{12,4},{13,5},{16,24},{17,25... | collective-permute-start | bytes 884744 | tf_op jit(solution)/shard_map/ppermute | solution.py:191
  61.5 15.0 %collective-permute-start.4 = (bf16[4,272,256]{2,1,0:T(8,128)(2,1)S(1)}, bf16[4,272,256]{2,1,0:T(8,128)(2,1)S(1)}, u32[]{:S(2)}, u32[]{:S(2)}) collective-permute-start(bf16[4,272,256]{2,1,0:T(8,128)(2,1)S(1)} %slice.348), channel_id=1, source_target_pairs={{0,4},{1,5},{4,0},{5,1},{8,12},{9,13},{12,8},{13,9},{16,20},{17,21... | collective-permute-start | bytes 1671176 | tf_op jit(solution)/shard_map/ppermute | solution.py:191
  63.1 13.4 %collective-permute-start.9 = (bf16[4,256,256]{2,1,0:T(8,128)(2,1)S(1)}, bf16[4,256,256]{2,1,0:T(8,128)(2,1)S(1)}, u32[]{:S(2)}, u32[]{:S(2)}) collective-permute-start(bf16[4,256,256]{2,1,0:T(8,128)(2,1)S(1)} %slice.354), channel_id=1, source_target_pairs={{0,1},{1,0},{4,5},{5,4},{8,9},{9,8},{12,13},{13,12},{16,17},{17,16... | collective-permute-start | bytes 1572872 | tf_op jit(solution)/shard_map/ppermute | solution.py:191
  76.5 28.1 %collective-permute-start.11 = (bf16[2,384,384]{2,1,0:T(8,128)(2,1)S(1)}, bf16[2,384,384]{2,1,0:T(8,128)(2,1)S(1)}, u32[]{:S(2)}, u32[]{:S(2)}) collective-permute-start(bf16[2,384,384]{2,1,0:T(8,128)(2,1)S(1)} %pad_maximum_fusion.14), channel_id=1, source_target_pairs={{0,16},{1,17},{4,20},{5,21},{8,24},{9,25},{12,28},{13,29},{16,0},{... | collective-permute-start | bytes 1769480 | tf_op jit(solution)/shard_map/ppermute | solution.py:191
  105.5 200.5 %all-gather.5.cloned.1.call-start = ((), (), s32[]{:S(2)}) async-start(), calls=%async_computation.2 | async-start | bytes 5013504 | tf_op jit(solution)/shard_map/all_gather | solution.py:730
  106.2 400.0 %reduce-scatter.2.cloned.1.call-start = ((), (), s32[]{:S(2)}) async-start(), calls=%async_computation.1 | async-start | bytes 1114112 | tf_op jit(solution)/shard_map/reduce_scatter | solution.py:883
  107.7 33.6 %collective-permute-start.7 = (bf16[8,272,256]{2,1,0:T(8,128)(2,1)S(1)}, bf16[8,272,256]{2,1,0:T(8,128)(2,1)}, u32[]{:S(2)}, u32[]{:S(2)}) collective-permute-start(bf16[8,272,256]{2,1,0:T(8,128)(2,1)S(1)} %pad_maximum_fusion.9.refs_0_), channel_id=1, source_target_pairs={{0,1},{1,0},{4,5},{5,4},{8,9},{9,8},{12,13},{13,12},{16,17},{17,16... | collective-permute-start | bytes 3342344 | tf_op jit(solution)/shard_map/ppermute | solution.py:191
  110.4 31.0 %collective-permute-start.10 = (bf16[8,256,256]{2,1,0:T(8,128)(2,1)}, bf16[8,256,256]{2,1,0:T(8,128)(2,1)}, u32[]{:S(2)}, u32[]{:S(2)}) collective-permute-start(bf16[8,256,256]{2,1,0:T(8,128)(2,1)} %pad_maximum_fusion.11.refs_2_), channel_id=1, source_target_pairs={{0,4},{1,5},{4,0},{5,1},{8,12},{9,13},{12,8},{13,9},{16,20},{17,21... | collective-permute-start | bytes 3145736 | tf_op jit(solution)/shard_map/ppermute | solution.py:191
  118.7 44.9 %collective-permute-start.14 = (bf16[4,192,384]{2,1,0:T(8,128)(2,1)}, bf16[4,192,384]{2,1,0:T(8,128)(2,1)}, u32[]{:S(2)}, u32[]{:S(2)}) collective-permute-start(bf16[4,192,384]{2,1,0:T(8,128)(2,1)} %get-tuple-element.192), channel_id=1, source_target_pairs={{0,1},{1,0},{4,5},{5,4},{8,9},{9,8},{12,13},{13,12},{16,17},{17,16... | collective-permute-start | bytes 1769480 | tf_op jit(solution)/shard_map/ppermute | solution.py:191
  119.1 44.5 %collective-permute-start.13 = (bf16[4,192,384]{2,1,0:T(8,128)(2,1)}, bf16[4,192,384]{2,1,0:T(8,128)(2,1)}, u32[]{:S(2)}, u32[]{:S(2)}) collective-permute-start(bf16[4,192,384]{2,1,0:T(8,128)(2,1)} %get-tuple-element.193), channel_id=1, source_target_pairs={{0,4},{1,5},{4,0},{5,1},{8,12},{9,13},{12,8},{13,9},{16,20},{17,21... | collective-permute-start | bytes 1769480 | tf_op jit(solution)/shard_map/ppermute | solution.py:191
  174.7 7.5 %collective-permute-start.15 = (bf16[2048,1024]{1,0:T(8,128)(2,1)}, bf16[2048,1024]{1,0:T(8,128)(2,1)}, u32[]{:S(2)}, u32[]{:S(2)}) collective-permute-start(bf16[2048,1024]{1,0:T(8,128)(2,1)} %get-tuple-element.113.branch_ref), channel_id=1, source_target_pairs={{0,2},{2,0},{1,3},{3,1},{4,6},{6,4},{5,7},{7,5},{8,10},{10,8},{9,1... | collective-permute-start | bytes 12582920 | tf_op jit(solution)/shard_map/ppermute | solution.py:186
  176.0 33.5 %collective-permute-start.17 = (bf16[8,192,384]{2,1,0:T(8,128)(2,1)S(1)}, bf16[8,192,384]{2,1,0:T(8,128)(2,1)}, u32[]{:S(2)}, u32[]{:S(2)}) collective-permute-start(bf16[8,192,384]{2,1,0:T(8,128)(2,1)S(1)} %pad_maximum_fusion.8.refs_2_), channel_id=1, source_target_pairs={{0,4},{1,5},{4,0},{5,1},{8,12},{9,13},{12,8},{13,9},{16,20},{17,21... | collective-permute-start | bytes 3538952 | tf_op jit(solution)/shard_map/ppermute | solution.py:191
  180.1 29.4 %collective-permute-start.16 = (bf16[8,192,384]{2,1,0:T(8,128)(2,1)}, bf16[8,192,384]{2,1,0:T(8,128)(2,1)}, u32[]{:S(2)}, u32[]{:S(2)}) collective-permute-start(bf16[8,192,384]{2,1,0:T(8,128)(2,1)} %pad_maximum_fusion.7.refs_0_), channel_id=1, source_target_pairs={{0,1},{1,0},{4,5},{5,4},{8,9},{9,8},{12,13},{13,12},{16,17},{17,16... | collective-permute-start | bytes 3538952 | tf_op jit(solution)/shard_map/ppermute | solution.py:191
  250.7 46.8 %collective-permute-start.19 = (bf16[8,192,384]{2,1,0:T(8,128)(2,1)}, bf16[8,192,384]{2,1,0:T(8,128)(2,1)}, u32[]{:S(2)}, u32[]{:S(2)}) collective-permute-start(bf16[8,192,384]{2,1,0:T(8,128)(2,1)} %get-tuple-element.123), channel_id=1, source_target_pairs={{0,4},{1,5},{4,0},{5,1},{8,12},{9,13},{12,8},{13,9},{16,20},{17,21... | collective-permute-start | bytes 3538952 | tf_op jit(solution)/shard_map/ppermute | solution.py:191
  252.3 49.3 %collective-permute-start.18 = (bf16[8,192,384]{2,1,0:T(8,128)(2,1)}, bf16[8,192,384]{2,1,0:T(8,128)(2,1)}, u32[]{:S(2)}, u32[]{:S(2)}) collective-permute-start(bf16[8,192,384]{2,1,0:T(8,128)(2,1)} %get-tuple-element.122), channel_id=1, source_target_pairs={{0,1},{1,0},{4,5},{5,4},{8,9},{9,8},{12,13},{13,12},{16,17},{17,16... | collective-permute-start | bytes 3538952 | tf_op jit(solution)/shard_map/ppermute | solution.py:191
  295.6 61.0 %collective-permute-start.23 = (bf16[8,192,384]{2,1,0:T(8,128)(2,1)}, bf16[8,192,384]{2,1,0:T(8,128)(2,1)}, u32[]{:S(2)}, u32[]{:S(2)}) collective-permute-start(bf16[8,192,384]{2,1,0:T(8,128)(2,1)} %get-tuple-element.137), channel_id=1, source_target_pairs={{0,4},{1,5},{4,0},{5,1},{8,12},{9,13},{12,8},{13,9},{16,20},{17,21... | collective-permute-start | bytes 3538952 | tf_op jit(solution)/shard_map/ppermute | solution.py:191
  297.2 59.5 %collective-permute-start.22 = (bf16[8,192,384]{2,1,0:T(8,128)(2,1)}, bf16[8,192,384]{2,1,0:T(8,128)(2,1)}, u32[]{:S(2)}, u32[]{:S(2)}) collective-permute-start(bf16[8,192,384]{2,1,0:T(8,128)(2,1)} %get-tuple-element.136), channel_id=1, source_target_pairs={{0,1},{1,0},{4,5},{5,4},{8,9},{9,8},{12,13},{13,12},{16,17},{17,16... | collective-permute-start | bytes 3538952 | tf_op jit(solution)/shard_map/ppermute | solution.py:191
  299.9 56.7 %collective-permute-start.21 = (bf16[4,192,384]{2,1,0:T(8,128)(2,1)}, bf16[4,192,384]{2,1,0:T(8,128)(2,1)}, u32[]{:S(2)}, u32[]{:S(2)}) collective-permute-start(bf16[4,192,384]{2,1,0:T(8,128)(2,1)} %slice.515), channel_id=1, source_target_pairs={{0,1},{1,0},{4,5},{5,4},{8,9},{9,8},{12,13},{13,12},{16,17},{17,16... | collective-permute-start | bytes 1769480 | tf_op jit(solution)/shard_map/ppermute | solution.py:191
  304.7 51.9 %collective-permute-start.20 = (bf16[4,192,384]{2,1,0:T(8,128)(2,1)}, bf16[4,192,384]{2,1,0:T(8,128)(2,1)}, u32[]{:S(2)}, u32[]{:S(2)}) collective-permute-start(bf16[4,192,384]{2,1,0:T(8,128)(2,1)} %slice.516), channel_id=1, source_target_pairs={{0,4},{1,5},{4,0},{5,1},{8,12},{9,13},{12,8},{13,9},{16,20},{17,21... | collective-permute-start | bytes 1769480 | tf_op jit(solution)/shard_map/ppermute | solution.py:191
  356.6 14.5 %collective-permute-start.24 = (bf16[2048,1024]{1,0:T(8,128)(2,1)}, bf16[2048,1024]{1,0:T(8,128)(2,1)}, u32[]{:S(2)}, u32[]{:S(2)}) collective-permute-start(bf16[2048,1024]{1,0:T(8,128)(2,1)} %get-tuple-element.138.gn_ref), channel_id=1, source_target_pairs={{0,2},{2,0},{1,3},{3,1},{4,6},{6,4},{5,7},{7,5},{8,10},{10,8},{9,1... | collective-permute-start | bytes 12582920 | tf_op jit(solution)/shard_map/ppermute | solution.py:186
  357.2 36.8 %collective-permute-start.28 = (bf16[8,192,384]{2,1,0:T(8,128)(2,1)}, bf16[8,192,384]{2,1,0:T(8,128)(2,1)}, u32[]{:S(2)}, u32[]{:S(2)}) collective-permute-start(bf16[8,192,384]{2,1,0:T(8,128)(2,1)} %get-tuple-element.148), channel_id=1, source_target_pairs={{0,1},{1,0},{4,5},{5,4},{8,9},{9,8},{12,13},{13,12},{16,17},{17,16... | collective-permute-start | bytes 3538952 | tf_op jit(solution)/shard_map/ppermute | solution.py:191
  358.1 35.9 %collective-permute-start.29 = (bf16[8,192,384]{2,1,0:T(8,128)(2,1)}, bf16[8,192,384]{2,1,0:T(8,128)(2,1)}, u32[]{:S(2)}, u32[]{:S(2)}) collective-permute-start(bf16[8,192,384]{2,1,0:T(8,128)(2,1)} %get-tuple-element.149), channel_id=1, source_target_pairs={{0,4},{1,5},{4,0},{5,1},{8,12},{9,13},{12,8},{13,9},{16,20},{17,21... | collective-permute-start | bytes 3538952 | tf_op jit(solution)/shard_map/ppermute | solution.py:191
  361.7 36.9 %collective-permute-start.27 = (bf16[4,192,384]{2,1,0:T(8,128)(2,1)}, bf16[4,192,384]{2,1,0:T(8,128)(2,1)}, u32[]{:S(2)}, u32[]{:S(2)}) collective-permute-start(bf16[4,192,384]{2,1,0:T(8,128)(2,1)} %slice.513), channel_id=1, source_target_pairs={{0,1},{1,0},{4,5},{5,4},{8,9},{9,8},{12,13},{13,12},{16,17},{17,16... | collective-permute-start | bytes 1769480 | tf_op jit(solution)/shard_map/ppermute | solution.py:191
  366.1 33.1 %collective-permute-start.26 = (bf16[4,192,384]{2,1,0:T(8,128)(2,1)}, bf16[4,192,384]{2,1,0:T(8,128)(2,1)}, u32[]{:S(2)}, u32[]{:S(2)}) collective-permute-start(bf16[4,192,384]{2,1,0:T(8,128)(2,1)} %slice.514), channel_id=1, source_target_pairs={{0,4},{1,5},{4,0},{5,1},{8,12},{9,13},{12,8},{13,9},{16,20},{17,21... | collective-permute-start | bytes 1769480 | tf_op jit(solution)/shard_map/ppermute | solution.py:191
  371.1 63.2 %collective-permute-start.38 = (bf16[2,384,384]{2,1,0:T(8,128)(2,1)}, bf16[2,384,384]{2,1,0:T(8,128)(2,1)}, u32[]{:S(2)}, u32[]{:S(2)}) collective-permute-start(bf16[2,384,384]{2,1,0:T(8,128)(2,1)} %fusion.22), channel_id=1, source_target_pairs={{0,16},{1,17},{4,20},{5,21},{8,24},{9,25},{12,28},{13,29},{16,0},{... | collective-permute-start | bytes 1769480 | tf_op jit(solution)/shard_map/ppermute | solution.py:191
  399.1 16.3 %collective-permute-start.25 = (bf16[4,2,512]{2,1,0:T(2,128)(2,1)}, bf16[4,2,512]{2,1,0:T(2,128)(2,1)S(1)}, u32[]{:S(2)}, u32[]{:S(2)}) collective-permute-start(bf16[4,2,512]{2,1,0:T(2,128)(2,1)} %get-tuple-element.142), channel_id=1, source_target_pairs={{1,0},{3,2},{5,4},{7,6},{9,8},{11,10},{13,12},{15,14},{17,16},{19,... | collective-permute-start | bytes 24584 | tf_op jit(solution)/shard_map/ppermute | solution.py:19
  403.5 35.9 %collective-permute-start.40 = (bf16[2,384,384]{2,1,0:T(8,128)(2,1)}, bf16[2,384,384]{2,1,0:T(8,128)(2,1)}, u32[]{:S(2)}, u32[]{:S(2)}) collective-permute-start(bf16[2,384,384]{2,1,0:T(8,128)(2,1)} %fusion.21), channel_id=1, source_target_pairs={{0,16},{1,17},{4,20},{5,21},{8,24},{9,25},{12,28},{13,29},{16,0},{... | collective-permute-start | bytes 1769480 | tf_op jit(solution)/shard_map/ppermute | solution.py:191
  408.3 34.2 %collective-permute-start.42 = (bf16[4,192,384]{2,1,0:T(8,128)(2,1)}, bf16[4,192,384]{2,1,0:T(8,128)(2,1)}, u32[]{:S(2)}, u32[]{:S(2)}) collective-permute-start(bf16[4,192,384]{2,1,0:T(8,128)(2,1)} %slice.512), channel_id=1, source_target_pairs={{0,4},{1,5},{4,0},{5,1},{8,12},{9,13},{12,8},{13,9},{16,20},{17,21... | collective-permute-start | bytes 1769480 | tf_op jit(solution)/shard_map/ppermute | solution.py:191
  412.7 30.8 %collective-permute-start.43 = (bf16[4,192,384]{2,1,0:T(8,128)(2,1)}, bf16[4,192,384]{2,1,0:T(8,128)(2,1)}, u32[]{:S(2)}, u32[]{:S(2)}) collective-permute-start(bf16[4,192,384]{2,1,0:T(8,128)(2,1)} %slice.511), channel_id=1, source_target_pairs={{0,1},{1,0},{4,5},{5,4},{8,9},{9,8},{12,13},{13,12},{16,17},{17,16... | collective-permute-start | bytes 1769480 | tf_op jit(solution)/shard_map/ppermute | solution.py:191
  434.2 26.4 %collective-permute-start.30 = (bf16[8,192,256]{2,1,0:T(8,128)(2,1)}, bf16[8,192,256]{2,1,0:T(8,128)(2,1)}, u32[]{:S(2)}, u32[]{:S(2)}) collective-permute-start(bf16[8,192,256]{2,1,0:T(8,128)(2,1)} %get-tuple-element.153), channel_id=1, source_target_pairs={{0,1},{1,0},{4,5},{5,4},{8,9},{9,8},{12,13},{13,12},{16,17},{17,16... | collective-permute-start | bytes 2359304 | tf_op jit(solution)/shard_map/ppermute | solution.py:191
  434.3 26.3 %collective-permute-start.31 = (bf16[8,192,256]{2,1,0:T(8,128)(2,1)}, bf16[8,192,256]{2,1,0:T(8,128)(2,1)}, u32[]{:S(2)}, u32[]{:S(2)}) collective-permute-start(bf16[8,192,256]{2,1,0:T(8,128)(2,1)} %get-tuple-element.154), channel_id=1, source_target_pairs={{0,4},{1,5},{4,0},{5,1},{8,12},{9,13},{12,8},{13,9},{16,20},{17,21... | collective-permute-start | bytes 2359304 | tf_op jit(solution)/shard_map/ppermute | solution.py:191
  439.4 31.6 %collective-permute-start.39 = (bf16[1,384,384]{2,1,0:T(8,128)(2,1)S(1)}, bf16[1,384,384]{2,1,0:T(8,128)(2,1)S(1)}, u32[]{:S(2)}, u32[]{:S(2)}) collective-permute-start(bf16[1,384,384]{2,1,0:T(8,128)(2,1)S(1)} %slice.521), channel_id=1, source_target_pairs={{0,8},{1,9},{4,12},{5,13},{8,0},{9,1},{12,4},{13,5},{16,24},{17,25... | collective-permute-start | bytes 884744 | tf_op jit(solution)/shard_map/ppermute | solution.py:191
  442.5 36.8 %collective-permute-start.41 = (bf16[1,384,384]{2,1,0:T(8,128)(2,1)S(1)}, bf16[1,384,384]{2,1,0:T(8,128)(2,1)S(1)}, u32[]{:S(2)}, u32[]{:S(2)}) collective-permute-start(bf16[1,384,384]{2,1,0:T(8,128)(2,1)S(1)} %slice.520), channel_id=1, source_target_pairs={{0,8},{1,9},{4,12},{5,13},{8,0},{9,1},{12,4},{13,5},{16,24},{17,25... | collective-permute-start | bytes 884744 | tf_op jit(solution)/shard_map/ppermute | solution.py:191
  467.2 40.6 %collective-permute-start.33 = (bf16[1024,1024]{1,0:T(8,128)(2,1)}, bf16[1024,1024]{1,0:T(8,128)(2,1)}, u32[]{:S(2)}, u32[]{:S(2)}) collective-permute-start(bf16[1024,1024]{1,0:T(8,128)(2,1)} %fusion.10), channel_id=1, source_target_pairs={{0,2},{2,0},{1,3},{3,1},{4,6},{6,4},{5,7},{7,5},{8,10},{10,8},{9,1... | collective-permute-start | bytes 6291464 | tf_op jit(solution)/shard_map/ppermute | solution.py:186
  467.3 31.0 %collective-permute-start.44 = (bf16[2,384,384]{2,1,0:T(8,128)(2,1)S(1)}, bf16[2,384,384]{2,1,0:T(8,128)(2,1)S(1)}, u32[]{:S(2)}, u32[]{:S(2)}) collective-permute-start(bf16[2,384,384]{2,1,0:T(8,128)(2,1)S(1)} %fusion.20), channel_id=1, source_target_pairs={{0,16},{1,17},{4,20},{5,21},{8,24},{9,25},{12,28},{13,29},{16,0},{... | collective-permute-start | bytes 1769480 | tf_op jit(solution)/shard_map/ppermute | solution.py:191
  472.4 28.5 %collective-permute-start.34 = (bf16[4,192,256]{2,1,0:T(8,128)(2,1)S(1)}, bf16[4,192,256]{2,1,0:T(8,128)(2,1)S(1)}, u32[]{:S(2)}, u32[]{:S(2)}) collective-permute-start(bf16[4,192,256]{2,1,0:T(8,128)(2,1)S(1)} %slice.518), channel_id=1, source_target_pairs={{0,4},{1,5},{4,0},{5,1},{8,12},{9,13},{12,8},{13,9},{16,20},{17,21... | collective-permute-start | bytes 1179656 | tf_op jit(solution)/shard_map/ppermute | solution.py:191
  474.5 26.4 %collective-permute-start.35 = (bf16[4,192,256]{2,1,0:T(8,128)(2,1)S(1)}, bf16[4,192,256]{2,1,0:T(8,128)(2,1)S(1)}, u32[]{:S(2)}, u32[]{:S(2)}) collective-permute-start(bf16[4,192,256]{2,1,0:T(8,128)(2,1)S(1)} %slice.517), channel_id=1, source_target_pairs={{0,1},{1,0},{4,5},{5,4},{8,9},{9,8},{12,13},{13,12},{16,17},{17,16... | collective-permute-start | bytes 1179656 | tf_op jit(solution)/shard_map/ppermute | solution.py:191
  479.3 58.0 %collective-permute-start.32 = (bf16[1024,1024]{1,0:T(8,128)(2,1)}, bf16[1024,1024]{1,0:T(8,128)(2,1)}, u32[]{:S(2)}, u32[]{:S(2)}) collective-permute-start(bf16[1024,1024]{1,0:T(8,128)(2,1)} %slice.510), channel_id=1, source_target_pairs={{0,2},{2,0},{1,3},{3,1},{4,6},{6,4},{5,7},{7,5},{8,10},{10,8},{9,1... | collective-permute-start | bytes 6291464 | tf_op jit(solution)/shard_map/ppermute | solution.py:186
  499.2 16.2 %collective-permute-start.45 = (bf16[1,384,384]{2,1,0:T(8,128)(2,1)}, bf16[1,384,384]{2,1,0:T(8,128)(2,1)}, u32[]{:S(2)}, u32[]{:S(2)}) collective-permute-start(bf16[1,384,384]{2,1,0:T(8,128)(2,1)} %slice.519), channel_id=1, source_target_pairs={{0,8},{1,9},{4,12},{5,13},{8,0},{9,1},{12,4},{13,5},{16,24},{17,25... | collective-permute-start | bytes 884744 | tf_op jit(solution)/shard_map/ppermute | solution.py:191
  502.8 20.9 %collective-permute-start.36 = (bf16[2,384,256]{2,1,0:T(8,128)(2,1)}, bf16[2,384,256]{2,1,0:T(8,128)(2,1)}, u32[]{:S(2)}, u32[]{:S(2)}) collective-permute-start(bf16[2,384,256]{2,1,0:T(8,128)(2,1)} %fusion.25), channel_id=1, source_target_pairs={{0,16},{1,17},{4,20},{5,21},{8,24},{9,25},{12,28},{13,29},{16,0},{... | collective-permute-start | bytes 1179656 | tf_op jit(solution)/shard_map/ppermute | solution.py:191
  515.3 15.5 %collective-permute-start.48 = (f32[8,5,128]{2,0,1:T(8,128)S(1)}, f32[8,5,128]{2,0,1:T(8,128)S(1)}, u32[]{:S(2)}, u32[]{:S(2)}) collective-permute-start(f32[8,5,128]{2,0,1:T(8,128)S(1)} %maximum_bitcast_fusion.1), channel_id=1, source_target_pairs={{0,1},{1,0},{4,5},{5,4},{8,9},{9,8},{12,13},{13,12},{16,17},{17,16... | collective-permute-start | bytes 61448 | tf_op jit(solution)/shard_map/ppermute | solution.py:191
  525.0 22.4 %collective-permute-start.37 = (bf16[1,384,256]{2,1,0:T(8,128)(2,1)S(1)}, bf16[1,384,256]{2,1,0:T(8,128)(2,1)}, u32[]{:S(2)}, u32[]{:S(2)}) collective-permute-start(bf16[1,384,256]{2,1,0:T(8,128)(2,1)S(1)} %slice.522), channel_id=1, source_target_pairs={{0,8},{1,9},{4,12},{5,13},{8,0},{9,1},{12,4},{13,5},{16,24},{17,25... | collective-permute-start | bytes 589832 | tf_op jit(solution)/shard_map/ppermute | solution.py:191
  533.7 19.0 %collective-permute-start.47 = (f32[3,2,64,384]{3,2,1,0:T(8,128)}, f32[3,2,64,384]{3,2,1,0:T(8,128)}, u32[]{:S(2)}, u32[]{:S(2)}) collective-permute-start(f32[3,2,64,384]{3,2,1,0:T(8,128)} %get-tuple-element.191), channel_id=1, source_target_pairs={{0,2},{2,0},{1,3},{3,1},{4,6},{6,4},{5,7},{7,5},{8,10},{10,8},{9,1... | collective-permute-start | bytes 1769480 | tf_op jit(solution)/shard_map/ppermute | solution.py:186
  (66 other events, 421.5 us)
Sparse Core Ops, SparseCore 0:
  105.6 99.0 all-gather.6
  207.5 96.4 all-gather.4
  415.5 78.3 reduce-scatter.1

commit v7 on v6

--- a/solution.py
+++ b/solution.py
@@ -233,7 +233,8 @@
     far, first_order, second_order = bit_masks()
 
     def send(block, mask):
-        return across(block.astype(bf16), mask)
+        block = block.astype(bf16)
+        return across(block, mask), block
 
     orders = (first_order, second_order)
     got = yield [send(parts[1], first_order[-1]), send(parts[3], second_order[-1])]
@@ -253,16 +254,17 @@
 class Stages:
     def __init__(self, parts):
         self.steps = scatter_steps(parts)
-        self.got = next(self.steps)
+        self.got, self.sent = zip(*next(self.steps))
         self.total = None
 
     def advance(self, *done):
         if self.total is not None:
             return
         try:
-            self.got = self.steps.send([after(g, *done) for g in self.got])
+            pairs = self.steps.send([after(g, *done) for g in self.got])
+            self.got, self.sent = zip(*pairs)
         except StopIteration as end:
-            self.got, self.total = [], end.value
+            self.got, self.sent, self.total = (), (), end.value
 
 
 def slot_pairs(own, plan, refs, segments, n_ctx, targets):
@@ -643,7 +645,7 @@
     out_block = w_out.reshape(depth, out_parts, 256).transpose(1, 0, 2).reshape(-1, 256)
     mix_block = jnp.concatenate([in_block, out_block, small_block], axis=0)
 
-    both = jnp.stack([w_gate, w_up]).reshape(2, depth, groups, 2, CHUNKS, sub)
+    both = jnp.stack([after(w_gate, mix_block), after(w_up, mix_block)]).reshape(2, depth, groups, 2, CHUNKS, sub)
     both = both.transpose(3, 4, 0, 1, 2, 5).reshape(2, CHUNKS, 2, depth, lanes)
     both_mine, both_other = mine_other(both)
     both_block = in_core_order(both_mine, swap(both_other), 2)
@@ -697,6 +699,9 @@
     hold = mix_block[None]
     for mask in far:
         hold = doubled(hold, across(hold, mask))
+    second_all, last_all = [
+        lax.all_gather(after(block, hold), ("chip", "ctx")) for block in chunk_blocks[1:]
+    ]
     mix_halves = [hold[:, :mix_cut], hold[:, mix_cut:]]
     next_hold = after(chunk_blocks[0][None], hold)
     far_left = list(far)
@@ -709,10 +714,9 @@
         if early:
             got = [after(g, early[0]) for g in got]
             early = early[1:]
+        got = [after(g, next_got) for g in got]
         if step + 1 < len(first_order):
-            got = [after(g, next_got) for g in got]
             mix_halves = [doubled(h, g) for h, g in zip(mix_halves, got)]
-            next_hold = after(next_hold, *got)
     mix_parts = [mix_halves[0], got[0], mix_halves[1], got[1]]
     for mask in far_left:
         next_got = across(next_hold, mask)
@@ -726,9 +730,6 @@
         False,
     )
     in_half = after(in_half, next_got)
-    second_all, last_all = [
-        lax.all_gather(after(block, next_got), ("chip", "ctx")) for block in chunk_blocks[1:]
-    ]
     next_halves = [next_hold[:, :chunk_cut], next_hold[:, chunk_cut:]]
 
     def step_of(halves, step):
@@ -877,9 +878,9 @@
     grad_gain_ffn = grad_gain_ffn[0]
     stages = (first_stages, second_stages, last_stages)
     behind = passed_along(head, "ctx", -1)
-    grad_c_then = after(grad_c, *second_stages.got, *last_stages.got)
     second_stages.advance(grad_c)
     last_stages.advance(grad_c)
+    grad_c_then = after(grad_c, *second_stages.sent, *last_stages.sent)
     out_sum = lax.psum_scatter(grad_out_slots, ("chip", "ctx"), scatter_dimension=0).astype(f32)
     sum_plan = gather_plan(in_rows // 2, in_rows)
     grad_projected, grad_kernel, *mix_grad_parts = row_call(
@@ -911,14 +912,15 @@
     stages = (first_stages, second_stages, last_stages)
     for s in stages:
         s.advance(grad_projected)
+    mix_stages.advance()
     late_projected = after(grad_projected, *mix_stages.got)
     mix_stages.advance()
     grad_other = cross_cols(late_projected[rows:], in_half).astype(bf16)
-    for s in (mix_stages, *stages):
+    for s in stages:
         s.advance(grad_other)
     other_got = swap(grad_other)
     grad_mine = cross_cols(after(late_projected, grad_other)[:rows], in_half)
-    for s in stages:
+    for s in (*stages, mix_stages):
         s.advance(grad_mine)
     grad_normed = grad_mine + other_got.astype(f32)
     ffn_late = after(ffn_out, grad_other)
@@ -929,8 +931,6 @@
     scale_mix = lax.rsqrt(jnp.mean(own_inputs * own_inputs, axis=-1, keepdims=True) + EPSILON)
     grad_in_norm, grad_gain_mix = norm_backward(own_inputs, scale_mix, first_gain, grad_normed)
     grad_tokens = (grad_residual + grad_in_norm).reshape(seqs, piece, width)
-
-    mix_stages.advance(grad_mine)
 
     chunk_sum = jnp.stack([s.total for s in stages])
     both_sum = chunk_sum[:, : 4 * depth].reshape(CHUNKS, 2, 2, depth, lanes).transpose(2, 0, 1, 3, 4)

time: 578 us -> 548 us (0.948)
  waiting for transfers between devices: 148 us -> 123 us
    ppermute x40, waiting for transfers between devices: 146 us -> 119 us  [across(): lax.ppermute(block, ('chip', 'ctx'), [(i, i ^ mask) for i in range(count)])]
    unnamed x119 -> x148, local copies, waits for them, and re-layouts: 7.61 us -> 15.7 us
    ppermute x40, starting transfers between devices: 59 us -> 52.5 us  [across(): lax.ppermute(block, ('chip', 'ctx'), [(i, i ^ mask) for i in range(count)])]
  transfers between devices with their start and end apart: 56 -> 56, of which waited for: 17 -> 19; matrix products, arithmetic and copies ran while one was open for 20% -> 19% of each run, Pallas kernels for 37% -> 39%
where the time goes in v7:
time: 548 us; the launch traced here: 538 us
  Pallas kernels  209 us (38%)
  waiting for transfers between devices  123 us (22%)
  other arithmetic  66.7 us (12%)
  starting transfers between devices  58.5 us (11%)
  local copies, waits for them, and re-layouts  50.6 us (9%)
  between operations  15.6 us (3%)
  matrix products  14.1 us (3%)
    pallas_call x3, Pallas kernels, ffn_chunk(): pl.pallas_call(functools.partial(ffn_kernel, geometry, out_geometry, firs...  134 us
    ppermute x40, waiting for transfers between devices, across(): lax.ppermute(block, ('chip', 'ctx'), [(i, i ^ mask) for i in range(count)])  119 us
    pallas_call x5, Pallas kernels, row_call(): pl.pallas_call(body, grid=(steps,), in_specs=[pl.BlockSpec(memory_space=p...  69.7 us
    ppermute x40, starting transfers between devices, across(): lax.ppermute(block, ('chip', 'ctx'), [(i, i ^ mask) for i in range(count)])  52.5 us
    unnamed x148, local copies, waits for them, and re-layouts  15.7 us
    dot_general x2, matrix products, cross_cols(): lax.dot_general(left_operand, right_operand, (((1,), (1,)), ((), ())), pr...  14.1 us
    concatenate x7, other arithmetic, doubled(): return jnp.concatenate([hold, got], axis=0)  11.4 us
  transfers between devices with their start and end apart: 56, of which 19 were waited for; matrix products, arithmetic and copies ran while one was open for 19% of the time, Pallas kernels for 39%

profile of v7, /device:TPU:0, one launch (start us, length us, event | category | flops | bytes accessed | tf_op | source)
XLA Modules:
  0.0 538.4 jit_solution(6663894216930415862)
XLA Ops:
  12.6 3.0 collective-permute-start.2
  17.4 5.0 collective-permute-done.2
  23.3 2.8 collective-permute-start.3
  27.9 22.0 %collective-permute-done.3 = bf16[2,528,256]{2,1,0:T(8,128)(2,1)} collective-permute-done((bf16[2,528,256]{2,1,0:T(8,128)(2,1)}, bf16[2,528,256]{2,1,0:T(8,128)(2,1)}, u32[]{:S(2)}, u32[]{:S(2)}) %collective-permute-start.3) | collective-permute-done | bytes 540704 | tf_op jit(solution)/shard_map/ppermute | solution.py:191
  57.0 3.8 collective-permute-done.6
  60.8 1.9 pad_maximum_fusion.14
  62.7 2.2 collective-permute-start.9
  64.8 4.0 pad_maximum_fusion.x_ref
  68.9 2.2 collective-permute-done.10
  74.9 2.2 pad_maximum_fusion.11.refs_2_
  78.6 21.7 %collective-permute-done.9 = bf16[2,384,384]{2,1,0:T(8,128)(2,1)} collective-permute-done((bf16[2,384,384]{2,1,0:T(8,128)(2,1)}, bf16[2,384,384]{2,1,0:T(8,128)(2,1)}, u32[]{:S(2)}, u32[]{:S(2)}) %collective-permute-start.9) | collective-permute-done | bytes 589856 | tf_op jit(solution)/shard_map/ppermute | solution.py:191
  105.7 4.0 pad_maximum_fusion.1.go_ref
  111.1 6.1 %shard_map.177 = (bf16[1024,1536]{1,0:T(8,128)(2,1)}, bf16[512,1024]{1,0:T(8,128)(2,1)}, bf16[128,512]{1,0:T(8,128)(2,1)}) custom-call(s32[1]{0:T(128)} %bitcast.1.own_ref, bf16[8,272,256]{2,1,0:T(8,128)(2,1)} %copy-done.26, bf16[8,272,256]{2,1,0:T(8,128)(2,1)} %collective-permute-done.7.refs_1_, bf16[8,256,256]{2,1,0:T(8,128)(2,1)} %pad_maximum_fusion.11.refs_2_, ...), custom_call_target="tpu_custom_call" | custom-call | flops 65536 | bytes 65536 | tf_op jit(solution)/shard_map/pallas_call | solution.py:426
  118.5 12.0 %shard_map.178 = (bf16[2048,1024]{1,0:T(8,128)(2,1)}, f32[2048,1536]{1,0:T(8,128)}, bf16[4,2,512]{2,1,0:T(2,128)(2,1)}) custom-call(bf16[2048,1024]{1,0:T(8,128)(2,1)} %pad_maximum_fusion.x_ref, f32[1,1024]{1,0:T(1,128)} %bitcast.148, bf16[1024,1536]{1,0:T(8,128)(2,1)} %get-tuple-element.112.w_ref), custom_call_target="tpu_custom_call" | custom-call | flops 65536 | bytes 65536 | tf_op jit(solution)/shard_map/pallas_call | solution.py:563
  130.6 2.5 collective-permute-start.12
  135.0 9.4 %shard_map.179 = (bf16[2048,512]{1,0:T(8,128)(2,1)}, f32[2048,512]{1,0:T(8,128)}, bf16[2048,1024]{1,0:T(8,128)(2,1)}) custom-call(f32[2048,1536]{1,0:T(8,128)} %get-tuple-element.113.projected_ref.gate_c_ref, bf16[4,2,512]{2,1,0:T(2,128)(2,1)} %copy-done.60, f32[8,512]{1,0:T(8,128)} %pad.14.taps_ref, bf16[512,1024]{1,0:T(8,128)(2,1)} %get-tuple-element.116.w_ref), custom_call_target="tpu_custom_call" | custom-call | flops 65536 | bytes 65536 | tf_op jit(solution)/shard_map/pallas_call | solution.py:563
  146.1 2.6 pad_maximum_fusion.7.refs_0_
  148.6 2.4 collective-permute-start.16
  151.9 9.7 %shard_map.180 = (f32[2048,1024]{1,0:T(8,128)}, bf16[2048,1024]{1,0:T(8,128)(2,1)}) custom-call(bf16[2048,1024]{1,0:T(8,128)(2,1)} %pad_maximum_fusion.x_ref, bf16[2048,1024]{1,0:T(8,128)(2,1)} %get-tuple-element.117.branch_ref, bf16[2048,1024]{1,0:T(8,128)(2,1)} %collective-permute-done.15.got_ref, f32[1,1024]{1,0:T(1,128)} %bitcast.142), custom_call_target="tpu_custom_call" | custom-call | flops 65536 | bytes 65536 | tf_op jit(solution)/shard_map/pallas_call | solution.py:563
  161.6 14.8 %collective-permute-done.17.refs_3_ = bf16[8,192,384]{2,1,0:T(8,128)(2,1)} collective-permute-done((bf16[8,192,384]{2,1,0:T(8,128)(2,1)S(1)}, bf16[8,192,384]{2,1,0:T(8,128)(2,1)}, u32[]{:S(2)}, u32[]{:S(2)}) %collective-permute-start.17) | collective-permute-done | bytes 1179680 | tf_op jit(solution)/shard_map/ppermute | solution.py:191
  176.5 3.7 collective-permute-done.16.refs_1_
  180.1 41.2 %shard_map.181 = (f32[2048,1024]{1,0:T(8,128)}, f32[2048,1024]{1,0:T(8,128)}, bf16[8,192,384]{2,1,0:T(8,128)(2,1)}, bf16[8,192,384]{2,1,0:T(8,128)(2,1)}, bf16[8...) custom-call(s32[1]{0:T(128)} %bitcast.1.own_ref, bf16[2048,1024]{1,0:T(8,128)(2,1)} %get-tuple-element.128.n_ref, ...), custom_call_target="tpu_custom_call" | custom-call | flops 65536 | bytes 65536 | tf_op jit(solution)/shard_map/pallas_call | solution.py:379
  224.5 42.2 %shard_map.182 = (f32[2048,1024]{1,0:T(8,128)}, f32[2048,1024]{1,0:T(8,128)}, bf16[8,192,384]{2,1,0:T(8,128)(2,1)}, bf16[8,192,384]{2,1,0:T(8,128)(2,1)}, bf16[8...) custom-call(s32[1]{0:T(128)} %bitcast.1.own_ref, ...), custom_call_target="tpu_custom_call", output_to_operand_aliasing={{0}: (4, {}), {1}: (5, {})} | custom-call | flops 65536 | bytes 65536 | tf_op jit(solution)/shard_map/pallas_call | solution.py:379
  268.4 1.9 convert_add_fusion.5
  276.9 50.2 %shard_map.183 = (f32[2048,1024]{1,0:T(8,128)}, bf16[2048,1024]{1,0:T(8,128)(2,1)}, bf16[8,192,384]{2,1,0:T(8,128)(2,1)}, bf16[8,192,384]{2,1,0:T(8,128)(2,1)}, ...) custom-call(s32[1]{0:T(128)} %bitcast.1.own_ref, ...), custom_call_target="tpu_custom_call", output_to_operand_aliasing={{0}: (4, {})} | custom-call | flops 65536 | bytes 65536 | tf_op jit(solution)/shard_map/pallas_call | solution.py:379
  329.5 2.2 slice_add_fusion.2
  332.6 4.6 collective-permute-start.38
  342.9 1.9 copy-done.28
  345.8 20.5 %shard_map.184 = (f32[1024,1024]{1,0:T(8,128)}, f32[2048,512]{1,0:T(8,128)}, bf16[2048,512]{1,0:T(8,128)(2,1)}, f32[1,1024]{1,0:T(1,128)}, bf16[4,2,512]{2,1,0:T(2,128)(2,1)}, /*index=5*/bf16[16,128,256]{2,1,0:T(8,128)(2,1)}) custom-call(s32[1]{0:T(128)} %bitcast.1.own_ref, bf16[2048,1024]{1,0:T(8,128)(2,1)} %get-tuple-element.142.gn_ref, ...), custom_call_target="tpu_custom_call" | custom-call | flops 65536 | bytes 65536 | tf_op jit(solution)/shard_map/pallas_call | solution.py:563
  366.3 1.9 convert_add_fusion.1
  379.5 2.6 collective-permute-start.43
  384.0 18.1 %shard_map.185 = (bf16[2048,1536]{1,0:T(8,128)(2,1)}, f32[8,512]{1,0:T(8,128)}, bf16[8,192,256]{2,1,0:T(8,128)(2,1)}, bf16[8,192,256]{2,1,0:T(8,128)(2,1)}, bf16...) custom-call(s32[1]{0:T(128)} %bitcast.1.own_ref, f32[2048,512]{1,0:T(8,128)} %get-tuple-element.145.grad_conv_ref, ...), custom_call_target="tpu_custom_call" | custom-call | flops 65536 | bytes 65536 | tf_op jit(solution)/shard_map/pallas_call | solution.py:563
  406.8 16.2 %collective-permute-done.32 = bf16[8,192,256]{2,1,0:T(8,128)(2,1)} collective-permute-done((bf16[8,192,256]{2,1,0:T(8,128)(2,1)}, bf16[8,192,256]{2,1,0:T(8,128)(2,1)}, u32[]{:S(2)}, u32[]{:S(2)}) %collective-permute-start.32) | collective-permute-done | bytes 786464 | tf_op jit(solution)/shard_map/ppermute | solution.py:191
  424.5 4.8 collective-permute-done.30
  430.6 4.3 collective-permute-start.31
  438.2 3.5 collective-permute-start.44
  442.5 6.5 %fusion.10 = bf16[1024,1024]{1,0:T(8,128)(2,1)} fusion(bf16[1024,1536]{1,0:T(8,128)(2,1)S(1)} %copy-done.35, bf16[2048,1536]{1,0:T(8,128)(2,1)} %get-tuple-element.168), kind=kOutput, calls=%fused_computation.31 | convolution fusion | flops 3222274048 | bytes 8388608 | tf_op jit(solution)/shard_map/dot_general | solution.py:29
  452.5 14.8 %collective-permute-done.41 = bf16[1,384,384]{2,1,0:T(8,128)(2,1)} collective-permute-done((bf16[1,384,384]{2,1,0:T(8,128)(2,1)}, bf16[1,384,384]{2,1,0:T(8,128)(2,1)}, u32[]{:S(2)}, u32[]{:S(2)}) %collective-permute-start.41) | collective-permute-done | bytes 294944 | tf_op jit(solution)/shard_map/ppermute | solution.py:191
  473.4 4.0 slice.510
  482.6 7.5 %fusion.5 = (f32[1024]{0:T(1024)S(1)}, f32[1024]{0:T(1024)S(1)}, f32[1024,1024]{1,0:T(8,128)S(1)}) fusion(f32[1024]{0:T(1024)S(1)} %bitcast.145, bf16[1024,1024]{1,0:T(8,128)(2,1)} %collective-permute-done.35, bf16[2,512,1024]{2,1,0:T(8,128)(2,1)S(1)} %copy-done, f32[1024]{0:T(1024)S(1)} %get-tuple-element.207, ...), kind=kOutput, calls=%fused_computation.8 | convolution fusion | flops 3230660608 | bytes 14696448 | tf_op jit(solution)/shard_map/dot_general | solution.py:29
  491.6 2.1 collective-permute-done.36
  495.1 4.7 fusion.2
  502.6 2.8 collective-permute-done.49
  505.4 1.9 collective-permute-start.50
  507.4 4.2 add_convert_fusion
  511.8 3.5 collective-permute-done.51
  522.7 2.4 concatenate.139
  525.1 2.0 fusion.13
  (367 shorter events, 112.4 us)
Async XLA Ops:
  7.2 217.3 %all-gather.7.cloned.1.call-start = ((), (), s32[]{:S(2)}) async-start(), calls=%async_computation.3 | async-start | bytes 5013504 | tf_op jit(solution)/shard_map/all_gather | solution.py:703
  12.6 9.8 %collective-permute-start.2 = (bf16[1,528,256]{2,1,0:T(8,128)(2,1)S(1)}, bf16[1,528,256]{2,1,0:T(8,128)(2,1)S(1)}, u32[]{:S(2)}, u32[]{:S(2)}) collective-permute-start(bf16[1,528,256]{2,1,0:T(8,128)(2,1)S(1)} %fusion.27), channel_id=1, source_target_pairs={{0,8},{1,9},{4,12},{5,13},{8,0},{9,1},{12,4},{13,5},{16,24},{17,25... | collective-permute-start | bytes 811016 | tf_op jit(solution)/shard_map/ppermute | solution.py:191
  17.3 9.4 %collective-permute-start.5 = (bf16[3,2,64,384]{3,2,1,0:T(8,128)(2,1)S(1)}, bf16[3,2,64,384]{3,2,1,0:T(8,128)(2,1)S(1)}, u32[]{:S(2)}, u32[]{:S(2)}) collective-permute-start(bf16[3,2,64,384]{3,2,1,0:T(8,128)(2,1)S(1)} %select_n.202), channel_id=1, source_target_pairs={{0,2},{2,0},{1,3},{3,1},{4,6},{6,4},{5,7},{7,5},{8,10},{10,8},{9,1... | collective-permute-start | bytes 884744 | tf_op jit(solution)/shard_map/ppermute | solution.py:186
  23.3 26.6 %collective-permute-start.3 = (bf16[2,528,256]{2,1,0:T(8,128)(2,1)}, bf16[2,528,256]{2,1,0:T(8,128)(2,1)}, u32[]{:S(2)}, u32[]{:S(2)}) collective-permute-start(bf16[2,528,256]{2,1,0:T(8,128)(2,1)} %pad_maximum_fusion.16), channel_id=1, source_target_pairs={{0,16},{1,17},{4,20},{5,21},{8,24},{9,25},{12,28},{13,29},{16,0},{... | collective-permute-start | bytes 1622024 | tf_op jit(solution)/shard_map/ppermute | solution.py:191
  51.1 225.8 %all-gather.5.cloned.1.call-start = ((), (), s32[]{:S(2)}) async-start(), calls=%async_computation.2 | async-start | bytes 5013504 | tf_op jit(solution)/shard_map/all_gather | solution.py:703
  51.1 13.7 %collective-permute-start = (bf16[1024,1024]{1,0:T(8,128)(2,1)S(1)}, bf16[1024,1024]{1,0:T(8,128)(2,1)}, u32[]{:S(2)}, u32[]{:S(2)}) collective-permute-start(bf16[1024,1024]{1,0:T(8,128)(2,1)S(1)} %bitcast.109), channel_id=1, source_target_pairs={{0,2},{2,0},{1,3},{3,1},{4,6},{6,4},{5,7},{7,5},{8,10},{10,8},{9,1... | collective-permute-start | bytes 6291464 | tf_op jit(solution)/shard_map/ppermute | solution.py:186
  51.2 54.5 %collective-permute-start.8 = (bf16[1024,1024]{1,0:T(8,128)(2,1)}, bf16[1024,1024]{1,0:T(8,128)(2,1)}, u32[]{:S(2)}, u32[]{:S(2)}) collective-permute-start(bf16[1024,1024]{1,0:T(8,128)(2,1)} %bitcast.121), channel_id=1, source_target_pairs={{0,2},{2,0},{1,3},{3,1},{4,6},{6,4},{5,7},{7,5},{8,10},{10,8},{9,1... | collective-permute-start | bytes 6291464 | tf_op jit(solution)/shard_map/ppermute | solution.py:186
  51.7 9.1 %collective-permute-start.6 = (bf16[1,384,384]{2,1,0:T(8,128)(2,1)S(1)}, bf16[1,384,384]{2,1,0:T(8,128)(2,1)}, u32[]{:S(2)}, u32[]{:S(2)}) collective-permute-start(bf16[1,384,384]{2,1,0:T(8,128)(2,1)S(1)} %get-tuple-element.102), channel_id=1, source_target_pairs={{0,8},{1,9},{4,12},{5,13},{8,0},{9,1},{12,4},{13,5},{16,24},{17,25... | collective-permute-start | bytes 884744 | tf_op jit(solution)/shard_map/ppermute | solution.py:191
  53.1 18.8 %collective-permute-start.4 = (bf16[4,272,256]{2,1,0:T(8,128)(2,1)}, bf16[4,272,256]{2,1,0:T(8,128)(2,1)}, u32[]{:S(2)}, u32[]{:S(2)}) collective-permute-start(bf16[4,272,256]{2,1,0:T(8,128)(2,1)} %slice.348), channel_id=1, source_target_pairs={{0,4},{1,5},{4,0},{5,1},{8,12},{9,13},{12,8},{13,9},{16,20},{17,21... | collective-permute-start | bytes 1671176 | tf_op jit(solution)/shard_map/ppermute | solution.py:191
  55.4 15.7 %collective-permute-start.10 = (bf16[4,256,256]{2,1,0:T(8,128)(2,1)}, bf16[4,256,256]{2,1,0:T(8,128)(2,1)S(1)}, u32[]{:S(2)}, u32[]{:S(2)}) collective-permute-start(bf16[4,256,256]{2,1,0:T(8,128)(2,1)} %slice.354), channel_id=1, source_target_pairs={{0,1},{1,0},{4,5},{5,4},{8,9},{9,8},{12,13},{13,12},{16,17},{17,16... | collective-permute-start | bytes 1572872 | tf_op jit(solution)/shard_map/ppermute | solution.py:191
  56.9 424.1 %reduce-scatter.2.cloned.1.call-start = ((), (), s32[]{:S(2)}) async-start(), calls=%async_computation.1 | async-start | bytes 1114112 | tf_op jit(solution)/shard_map/reduce_scatter | solution.py:884
  62.7 37.7 %collective-permute-start.9 = (bf16[2,384,384]{2,1,0:T(8,128)(2,1)}, bf16[2,384,384]{2,1,0:T(8,128)(2,1)}, u32[]{:S(2)}, u32[]{:S(2)}) collective-permute-start(bf16[2,384,384]{2,1,0:T(8,128)(2,1)} %pad_maximum_fusion.14), channel_id=1, source_target_pairs={{0,16},{1,17},{4,20},{5,21},{8,24},{9,25},{12,28},{13,29},{16,0},{... | collective-permute-start | bytes 1769480 | tf_op jit(solution)/shard_map/ppermute | solution.py:191
  73.3 37.8 %collective-permute-start.7 = (bf16[8,272,256]{2,1,0:T(8,128)(2,1)S(1)}, bf16[8,272,256]{2,1,0:T(8,128)(2,1)}, u32[]{:S(2)}, u32[]{:S(2)}) collective-permute-start(bf16[8,272,256]{2,1,0:T(8,128)(2,1)S(1)} %pad_maximum_fusion.9.refs_0_), channel_id=1, source_target_pairs={{0,1},{1,0},{4,5},{5,4},{8,9},{9,8},{12,13},{13,12},{16,17},{17,16... | collective-permute-start | bytes 3342344 | tf_op jit(solution)/shard_map/ppermute | solution.py:191
  77.0 34.0 %collective-permute-start.11 = (bf16[8,256,256]{2,1,0:T(8,128)(2,1)}, bf16[8,256,256]{2,1,0:T(8,128)(2,1)}, u32[]{:S(2)}, u32[]{:S(2)}) collective-permute-start(bf16[8,256,256]{2,1,0:T(8,128)(2,1)} %pad_maximum_fusion.11.refs_2_), channel_id=1, source_target_pairs={{0,4},{1,5},{4,0},{5,1},{8,12},{9,13},{12,8},{13,9},{16,20},{17,21... | collective-permute-start | bytes 3145736 | tf_op jit(solution)/shard_map/ppermute | solution.py:191
  102.6 31.1 %collective-permute-start.14 = (bf16[4,192,384]{2,1,0:T(8,128)(2,1)}, bf16[4,192,384]{2,1,0:T(8,128)(2,1)}, u32[]{:S(2)}, u32[]{:S(2)}) collective-permute-start(bf16[4,192,384]{2,1,0:T(8,128)(2,1)} %get-tuple-element.194), channel_id=1, source_target_pairs={{0,1},{1,0},{4,5},{5,4},{8,9},{9,8},{12,13},{13,12},{16,17},{17,16... | collective-permute-start | bytes 1769480 | tf_op jit(solution)/shard_map/ppermute | solution.py:191
  104.3 29.5 %collective-permute-start.13 = (bf16[4,192,384]{2,1,0:T(8,128)(2,1)}, bf16[4,192,384]{2,1,0:T(8,128)(2,1)}, u32[]{:S(2)}, u32[]{:S(2)}) collective-permute-start(bf16[4,192,384]{2,1,0:T(8,128)(2,1)} %get-tuple-element.195), channel_id=1, source_target_pairs={{0,4},{1,5},{4,0},{5,1},{8,12},{9,13},{12,8},{13,9},{16,20},{17,21... | collective-permute-start | bytes 1769480 | tf_op jit(solution)/shard_map/ppermute | solution.py:191
  145.8 30.7 %collective-permute-start.17 = (bf16[8,192,384]{2,1,0:T(8,128)(2,1)S(1)}, bf16[8,192,384]{2,1,0:T(8,128)(2,1)}, u32[]{:S(2)}, u32[]{:S(2)}) collective-permute-start(bf16[8,192,384]{2,1,0:T(8,128)(2,1)S(1)} %pad_maximum_fusion.8.refs_2_), channel_id=1, source_target_pairs={{0,4},{1,5},{4,0},{5,1},{8,12},{9,13},{12,8},{13,9},{16,20},{17,21... | collective-permute-start | bytes 3538952 | tf_op jit(solution)/shard_map/ppermute | solution.py:191
  148.6 31.5 %collective-permute-start.16 = (bf16[8,192,384]{2,1,0:T(8,128)(2,1)}, bf16[8,192,384]{2,1,0:T(8,128)(2,1)}, u32[]{:S(2)}, u32[]{:S(2)}) collective-permute-start(bf16[8,192,384]{2,1,0:T(8,128)(2,1)} %pad_maximum_fusion.7.refs_0_), channel_id=1, source_target_pairs={{0,1},{1,0},{4,5},{5,4},{8,9},{9,8},{12,13},{13,12},{16,17},{17,16... | collective-permute-start | bytes 3538952 | tf_op jit(solution)/shard_map/ppermute | solution.py:191
  221.3 45.4 %collective-permute-start.19 = (bf16[8,192,384]{2,1,0:T(8,128)(2,1)}, bf16[8,192,384]{2,1,0:T(8,128)(2,1)S(1)}, u32[]{:S(2)}, u32[]{:S(2)}) collective-permute-start(bf16[8,192,384]{2,1,0:T(8,128)(2,1)} %get-tuple-element.127), channel_id=1, source_target_pairs={{0,4},{1,5},{4,0},{5,1},{8,12},{9,13},{12,8},{13,9},{16,20},{17,21... | collective-permute-start | bytes 3538952 | tf_op jit(solution)/shard_map/ppermute | solution.py:191
  222.8 49.5 %collective-permute-start.18 = (bf16[8,192,384]{2,1,0:T(8,128)(2,1)}, bf16[8,192,384]{2,1,0:T(8,128)(2,1)}, u32[]{:S(2)}, u32[]{:S(2)}) collective-permute-start(bf16[8,192,384]{2,1,0:T(8,128)(2,1)} %get-tuple-element.126), channel_id=1, source_target_pairs={{0,1},{1,0},{4,5},{5,4},{8,9},{9,8},{12,13},{13,12},{16,17},{17,16... | collective-permute-start | bytes 3538952 | tf_op jit(solution)/shard_map/ppermute | solution.py:191
  266.8 60.4 %collective-permute-start.22 = (bf16[8,192,384]{2,1,0:T(8,128)(2,1)}, bf16[8,192,384]{2,1,0:T(8,128)(2,1)}, u32[]{:S(2)}, u32[]{:S(2)}) collective-permute-start(bf16[8,192,384]{2,1,0:T(8,128)(2,1)} %get-tuple-element.140), channel_id=1, source_target_pairs={{0,1},{1,0},{4,5},{5,4},{8,9},{9,8},{12,13},{13,12},{16,17},{17,16... | collective-permute-start | bytes 3538952 | tf_op jit(solution)/shard_map/ppermute | solution.py:191
  267.8 59.4 %collective-permute-start.23 = (bf16[8,192,384]{2,1,0:T(8,128)(2,1)}, bf16[8,192,384]{2,1,0:T(8,128)(2,1)S(1)}, u32[]{:S(2)}, u32[]{:S(2)}) collective-permute-start(bf16[8,192,384]{2,1,0:T(8,128)(2,1)} %get-tuple-element.141), channel_id=1, source_target_pairs={{0,4},{1,5},{4,0},{5,1},{8,12},{9,13},{12,8},{13,9},{16,20},{17,21... | collective-permute-start | bytes 3538952 | tf_op jit(solution)/shard_map/ppermute | solution.py:191
  271.2 55.9 %collective-permute-start.21 = (bf16[4,192,384]{2,1,0:T(8,128)(2,1)}, bf16[4,192,384]{2,1,0:T(8,128)(2,1)}, u32[]{:S(2)}, u32[]{:S(2)}) collective-permute-start(bf16[4,192,384]{2,1,0:T(8,128)(2,1)} %slice.515), channel_id=1, source_target_pairs={{0,1},{1,0},{4,5},{5,4},{8,9},{9,8},{12,13},{13,12},{16,17},{17,16... | collective-permute-start | bytes 1769480 | tf_op jit(solution)/shard_map/ppermute | solution.py:191
  275.5 51.6 %collective-permute-start.20 = (bf16[4,192,384]{2,1,0:T(8,128)(2,1)}, bf16[4,192,384]{2,1,0:T(8,128)(2,1)}, u32[]{:S(2)}, u32[]{:S(2)}) collective-permute-start(bf16[4,192,384]{2,1,0:T(8,128)(2,1)} %slice.516), channel_id=1, source_target_pairs={{0,4},{1,5},{4,0},{5,1},{8,12},{9,13},{12,8},{13,9},{16,20},{17,21... | collective-permute-start | bytes 1769480 | tf_op jit(solution)/shard_map/ppermute | solution.py:191
  327.1 15.8 %collective-permute-start.24 = (bf16[2048,1024]{1,0:T(8,128)(2,1)}, bf16[2048,1024]{1,0:T(8,128)(2,1)S(1)}, u32[]{:S(2)}, u32[]{:S(2)}) collective-permute-start(bf16[2048,1024]{1,0:T(8,128)(2,1)} %get-tuple-element.142.gn_ref), channel_id=1, source_target_pairs={{0,2},{2,0},{1,3},{3,1},{4,6},{6,4},{5,7},{7,5},{8,10},{10,8},{9,1... | collective-permute-start | bytes 12582920 | tf_op jit(solution)/shard_map/ppermute | solution.py:186
  327.7 38.6 %collective-permute-start.29 = (bf16[8,192,384]{2,1,0:T(8,128)(2,1)}, bf16[8,192,384]{2,1,0:T(8,128)(2,1)}, u32[]{:S(2)}, u32[]{:S(2)}) collective-permute-start(bf16[8,192,384]{2,1,0:T(8,128)(2,1)} %get-tuple-element.158), channel_id=1, source_target_pairs={{0,4},{1,5},{4,0},{5,1},{8,12},{9,13},{12,8},{13,9},{16,20},{17,21... | collective-permute-start | bytes 3538952 | tf_op jit(solution)/shard_map/ppermute | solution.py:191
  328.5 40.6 %collective-permute-start.28 = (bf16[8,192,384]{2,1,0:T(8,128)(2,1)}, bf16[8,192,384]{2,1,0:T(8,128)(2,1)}, u32[]{:S(2)}, u32[]{:S(2)}) collective-permute-start(bf16[8,192,384]{2,1,0:T(8,128)(2,1)} %get-tuple-element.155), channel_id=1, source_target_pairs={{0,1},{1,0},{4,5},{5,4},{8,9},{9,8},{12,13},{13,12},{16,17},{17,16... | collective-permute-start | bytes 3538952 | tf_op jit(solution)/shard_map/ppermute | solution.py:191
  332.6 70.4 %collective-permute-start.38 = (bf16[2,384,384]{2,1,0:T(8,128)(2,1)}, bf16[2,384,384]{2,1,0:T(8,128)(2,1)}, u32[]{:S(2)}, u32[]{:S(2)}) collective-permute-start(bf16[2,384,384]{2,1,0:T(8,128)(2,1)} %fusion.22), channel_id=1, source_target_pairs={{0,16},{1,17},{4,20},{5,21},{8,24},{9,25},{12,28},{13,29},{16,0},{... | collective-permute-start | bytes 1769480 | tf_op jit(solution)/shard_map/ppermute | solution.py:191
  339.8 33.1 %collective-permute-start.26 = (bf16[4,192,384]{2,1,0:T(8,128)(2,1)}, bf16[4,192,384]{2,1,0:T(8,128)(2,1)}, u32[]{:S(2)}, u32[]{:S(2)}) collective-permute-start(bf16[4,192,384]{2,1,0:T(8,128)(2,1)} %slice.514), channel_id=1, source_target_pairs={{0,4},{1,5},{4,0},{5,1},{8,12},{9,13},{12,8},{13,9},{16,20},{17,21... | collective-permute-start | bytes 1769480 | tf_op jit(solution)/shard_map/ppermute | solution.py:191
  344.9 28.0 %collective-permute-start.27 = (bf16[4,192,384]{2,1,0:T(8,128)(2,1)}, bf16[4,192,384]{2,1,0:T(8,128)(2,1)}, u32[]{:S(2)}, u32[]{:S(2)}) collective-permute-start(bf16[4,192,384]{2,1,0:T(8,128)(2,1)} %slice.513), channel_id=1, source_target_pairs={{0,1},{1,0},{4,5},{5,4},{8,9},{9,8},{12,13},{13,12},{16,17},{17,16... | collective-permute-start | bytes 1769480 | tf_op jit(solution)/shard_map/ppermute | solution.py:191
  373.6 9.8 %collective-permute-start.25 = (bf16[4,2,512]{2,1,0:T(2,128)(2,1)S(1)}, bf16[4,2,512]{2,1,0:T(2,128)(2,1)S(1)}, u32[]{:S(2)}, u32[]{:S(2)}) collective-permute-start(bf16[4,2,512]{2,1,0:T(2,128)(2,1)S(1)} %copy-done.67), channel_id=1, source_target_pairs={{1,0},{3,2},{5,4},{7,6},{9,8},{11,10},{13,12},{15,14},{17,16},{19,... | collective-permute-start | bytes 24584 | tf_op jit(solution)/shard_map/ppermute | solution.py:19
  378.5 26.9 %collective-permute-start.40 = (bf16[2,384,384]{2,1,0:T(8,128)(2,1)}, bf16[2,384,384]{2,1,0:T(8,128)(2,1)}, u32[]{:S(2)}, u32[]{:S(2)}) collective-permute-start(bf16[2,384,384]{2,1,0:T(8,128)(2,1)} %fusion.19), channel_id=1, source_target_pairs={{0,16},{1,17},{4,20},{5,21},{8,24},{9,25},{12,28},{13,29},{16,0},{... | collective-permute-start | bytes 1769480 | tf_op jit(solution)/shard_map/ppermute | solution.py:191
  379.5 25.9 %collective-permute-start.43 = (bf16[4,192,384]{2,1,0:T(8,128)(2,1)}, bf16[4,192,384]{2,1,0:T(8,128)(2,1)}, u32[]{:S(2)}, u32[]{:S(2)}) collective-permute-start(bf16[4,192,384]{2,1,0:T(8,128)(2,1)} %slice.511), channel_id=1, source_target_pairs={{0,1},{1,0},{4,5},{5,4},{8,9},{9,8},{12,13},{13,12},{16,17},{17,16... | collective-permute-start | bytes 1769480 | tf_op jit(solution)/shard_map/ppermute | solution.py:191
  382.2 23.3 %collective-permute-start.42 = (bf16[4,192,384]{2,1,0:T(8,128)(2,1)}, bf16[4,192,384]{2,1,0:T(8,128)(2,1)}, u32[]{:S(2)}, u32[]{:S(2)}) collective-permute-start(bf16[4,192,384]{2,1,0:T(8,128)(2,1)} %slice.512), channel_id=1, source_target_pairs={{0,4},{1,5},{4,0},{5,1},{8,12},{9,13},{12,8},{13,9},{16,20},{17,21... | collective-permute-start | bytes 1769480 | tf_op jit(solution)/shard_map/ppermute | solution.py:191
  402.1 20.8 %collective-permute-start.32 = (bf16[8,192,256]{2,1,0:T(8,128)(2,1)}, bf16[8,192,256]{2,1,0:T(8,128)(2,1)}, u32[]{:S(2)}, u32[]{:S(2)}) collective-permute-start(bf16[8,192,256]{2,1,0:T(8,128)(2,1)} %get-tuple-element.166), channel_id=1, source_target_pairs={{0,4},{1,5},{4,0},{5,1},{8,12},{9,13},{12,8},{13,9},{16,20},{17,21... | collective-permute-start | bytes 2359304 | tf_op jit(solution)/shard_map/ppermute | solution.py:191
  403.0 26.2 %collective-permute-start.30 = (bf16[8,192,256]{2,1,0:T(8,128)(2,1)}, bf16[8,192,256]{2,1,0:T(8,128)(2,1)S(1)}, u32[]{:S(2)}, u32[]{:S(2)}) collective-permute-start(bf16[8,192,256]{2,1,0:T(8,128)(2,1)} %get-tuple-element.164), channel_id=1, source_target_pairs={{0,1},{1,0},{4,5},{5,4},{8,9},{9,8},{12,13},{13,12},{16,17},{17,16... | collective-permute-start | bytes 2359304 | tf_op jit(solution)/shard_map/ppermute | solution.py:191
  405.5 47.0 %collective-permute-start.39 = (bf16[1,384,384]{2,1,0:T(8,128)(2,1)}, bf16[1,384,384]{2,1,0:T(8,128)(2,1)}, u32[]{:S(2)}, u32[]{:S(2)}) collective-permute-start(bf16[1,384,384]{2,1,0:T(8,128)(2,1)} %slice.521), channel_id=1, source_target_pairs={{0,8},{1,9},{4,12},{5,13},{8,0},{9,1},{12,4},{13,5},{16,24},{17,25... | collective-permute-start | bytes 884744 | tf_op jit(solution)/shard_map/ppermute | solution.py:191
  424.4 17.3 %collective-permute-start.33 = (bf16[4,192,256]{2,1,0:T(8,128)(2,1)S(1)}, bf16[4,192,256]{2,1,0:T(8,128)(2,1)S(1)}, u32[]{:S(2)}, u32[]{:S(2)}) collective-permute-start(bf16[4,192,256]{2,1,0:T(8,128)(2,1)S(1)} %slice.517), channel_id=1, source_target_pairs={{0,1},{1,0},{4,5},{5,4},{8,9},{9,8},{12,13},{13,12},{16,17},{17,16... | collective-permute-start | bytes 1179656 | tf_op jit(solution)/shard_map/ppermute | solution.py:191
  430.6 11.9 %collective-permute-start.31 = (bf16[4,192,256]{2,1,0:T(8,128)(2,1)S(1)}, bf16[4,192,256]{2,1,0:T(8,128)(2,1)}, u32[]{:S(2)}, u32[]{:S(2)}) collective-permute-start(bf16[4,192,256]{2,1,0:T(8,128)(2,1)S(1)} %slice.518), channel_id=1, source_target_pairs={{0,4},{1,5},{4,0},{5,1},{8,12},{9,13},{12,8},{13,9},{16,20},{17,21... | collective-permute-start | bytes 1179656 | tf_op jit(solution)/shard_map/ppermute | solution.py:191
  438.2 29.1 %collective-permute-start.44 = (bf16[2,384,384]{2,1,0:T(8,128)(2,1)}, bf16[2,384,384]{2,1,0:T(8,128)(2,1)}, u32[]{:S(2)}, u32[]{:S(2)}) collective-permute-start(bf16[2,384,384]{2,1,0:T(8,128)(2,1)} %fusion.20), channel_id=1, source_target_pairs={{0,16},{1,17},{4,20},{5,21},{8,24},{9,25},{12,28},{13,29},{16,0},{... | collective-permute-start | bytes 1769480 | tf_op jit(solution)/shard_map/ppermute | solution.py:191
  449.0 33.5 %collective-permute-start.35 = (bf16[1024,1024]{1,0:T(8,128)(2,1)}, bf16[1024,1024]{1,0:T(8,128)(2,1)}, u32[]{:S(2)}, u32[]{:S(2)}) collective-permute-start(bf16[1024,1024]{1,0:T(8,128)(2,1)} %fusion.10), channel_id=1, source_target_pairs={{0,2},{2,0},{1,3},{3,1},{4,6},{6,4},{5,7},{7,5},{8,10},{10,8},{9,1... | collective-permute-start | bytes 6291464 | tf_op jit(solution)/shard_map/ppermute | solution.py:186
  452.1 15.2 %collective-permute-start.41 = (bf16[1,384,384]{2,1,0:T(8,128)(2,1)}, bf16[1,384,384]{2,1,0:T(8,128)(2,1)}, u32[]{:S(2)}, u32[]{:S(2)}) collective-permute-start(bf16[1,384,384]{2,1,0:T(8,128)(2,1)} %slice.520), channel_id=1, source_target_pairs={{0,8},{1,9},{4,12},{5,13},{8,0},{9,1},{12,4},{13,5},{16,24},{17,25... | collective-permute-start | bytes 884744 | tf_op jit(solution)/shard_map/ppermute | solution.py:191
  469.5 20.7 %collective-permute-start.45 = (bf16[1,384,384]{2,1,0:T(8,128)(2,1)}, bf16[1,384,384]{2,1,0:T(8,128)(2,1)}, u32[]{:S(2)}, u32[]{:S(2)}) collective-permute-start(bf16[1,384,384]{2,1,0:T(8,128)(2,1)} %slice.519), channel_id=1, source_target_pairs={{0,8},{1,9},{4,12},{5,13},{8,0},{9,1},{12,4},{13,5},{16,24},{17,25... | collective-permute-start | bytes 884744 | tf_op jit(solution)/shard_map/ppermute | solution.py:191
  472.9 20.8 %collective-permute-start.36 = (bf16[2,384,256]{2,1,0:T(8,128)(2,1)}, bf16[2,384,256]{2,1,0:T(8,128)(2,1)}, u32[]{:S(2)}, u32[]{:S(2)}) collective-permute-start(bf16[2,384,256]{2,1,0:T(8,128)(2,1)} %fusion.25), channel_id=1, source_target_pairs={{0,16},{1,17},{4,20},{5,21},{8,24},{9,25},{12,28},{13,29},{16,0},{... | collective-permute-start | bytes 1179656 | tf_op jit(solution)/shard_map/ppermute | solution.py:191
  477.3 30.0 %collective-permute-start.34 = (bf16[1024,1024]{1,0:T(8,128)(2,1)}, bf16[1024,1024]{1,0:T(8,128)(2,1)}, u32[]{:S(2)}, u32[]{:S(2)}) collective-permute-start(bf16[1024,1024]{1,0:T(8,128)(2,1)} %slice.510), channel_id=1, source_target_pairs={{0,2},{2,0},{1,3},{3,1},{4,6},{6,4},{5,7},{7,5},{8,10},{10,8},{9,1... | collective-permute-start | bytes 6291464 | tf_op jit(solution)/shard_map/ppermute | solution.py:186
  490.1 10.6 %collective-permute-start.48 = (f32[8,5,128]{2,0,1:T(8,128)S(1)}, f32[8,5,128]{2,0,1:T(8,128)S(1)}, u32[]{:S(2)}, u32[]{:S(2)}) collective-permute-start(f32[8,5,128]{2,0,1:T(8,128)S(1)} %maximum_bitcast_fusion.1), channel_id=1, source_target_pairs={{0,1},{1,0},{4,5},{5,4},{8,9},{9,8},{12,13},{13,12},{16,17},{17,16... | collective-permute-start | bytes 61448 | tf_op jit(solution)/shard_map/ppermute | solution.py:191
  495.0 22.4 %collective-permute-start.37 = (bf16[1,384,256]{2,1,0:T(8,128)(2,1)S(1)}, bf16[1,384,256]{2,1,0:T(8,128)(2,1)}, u32[]{:S(2)}, u32[]{:S(2)}) collective-permute-start(bf16[1,384,256]{2,1,0:T(8,128)(2,1)S(1)} %slice.522), channel_id=1, source_target_pairs={{0,8},{1,9},{4,12},{5,13},{8,0},{9,1},{12,4},{13,5},{16,24},{17,25... | collective-permute-start | bytes 589832 | tf_op jit(solution)/shard_map/ppermute | solution.py:191
  502.5 20.2 %collective-permute-start.47 = (f32[3,2,64,384]{3,2,1,0:T(8,128)}, f32[3,2,64,384]{3,2,1,0:T(8,128)}, u32[]{:S(2)}, u32[]{:S(2)}) collective-permute-start(f32[3,2,64,384]{3,2,1,0:T(8,128)} %get-tuple-element.193), channel_id=1, source_target_pairs={{0,2},{2,0},{1,3},{3,1},{4,6},{6,4},{5,7},{7,5},{8,10},{10,8},{9,1... | collective-permute-start | bytes 1769480 | tf_op jit(solution)/shard_map/ppermute | solution.py:186
  (80 other events, 455.4 us)
Sparse Core Ops, SparseCore 0:
  51.2 102.6 all-gather.6
  156.7 81.2 all-gather.4
  403.2 77.8 reduce-scatter.1
